TPU v7x, 32 devices: a whole 2x2x4 slice. The times are simulated.
32 devices in a mesh: groups: 2 (over x), seq: 16 (over z, y, core).
Axes of the slice: x: 2, y: 2, z: 4, core: 2. Of those that a mesh axis runs over, the one named last changes fastest.
Arguments:
- tower_in: bfloat16 [8, 4096, 768], P('groups', 'seq'), parts along dimension 0, may hold values from -6 to 6
- first_norm_scale: float32 [4, 768], replicated, may hold values from 0.5 to 2
- first_norm_shift: float32 [4, 768], replicated, may hold values from -0.5 to 0.5
- conv_weight: bfloat16 [4, 3, 768, 384], replicated, may hold values from -0.125 to 0.125
- mid_scale: float32 [4, 384], replicated, may hold values from 0.5 to 2
- second_norm_shift: float32 [4, 384], replicated, may hold values from -0.5 to 0.5
- point_weight: bfloat16 [4, 384, 768], replicated, may hold values from -0.3125 to 0.3125
Outputs:
- tower_out: bfloat16 [8, 4096, 768], P('groups', 'seq'), parts along dimension 0
There are 2 independent parts, one for each index of `groups`. A program takes and returns all parts, laid end to end along the dimension named above; an argument that names none is the same for every part. Nothing has to cross between parts.
All inputs are finite; a program needn't handle non-finite values.
Results may differ from a plain program's by a relative error of at most 0.017.
Values may be sent and summed in bfloat16 or wider, within the bound.
No kernel may reach another device: no remote copies, remote signals or barrier semaphores. Data moves between devices by JAX's collectives and lax.ppermute only.
A program may use at most 64 MiB of HBM per device.

v0:
```python
import jax
import jax.numpy as jnp
from jax import lax
from jax.sharding import PartitionSpec as P

FILTERS = 384
BLOCKS = 4
FIRST_DILATION = 32


def from_behind(value, axis, by):
    count = lax.axis_size(axis)
    pairs = [(i, i + by) for i in range(count) if 0 <= i + by < count]
    return lax.ppermute(value, axis, pairs)


def padded(block, sides, width):
    for axis, dim in sides:
        count = lax.axis_size(axis)
        forward = [(i, i + 1) for i in range(count - 1)]
        backward = [(target, source) for source, target in forward]
        low = lax.ppermute(
            lax.slice_in_dim(block, block.shape[dim] - width, None, axis=dim), axis, forward
        )
        high = lax.ppermute(lax.slice_in_dim(block, 0, width, axis=dim), axis, backward)
        block = jnp.concatenate([low, block, high], axis=dim)
    return block


def normalize(stream, scale_vector, shift_vec):
    return jnp.maximum(stream.astype(jnp.float32) * scale_vector + shift_vec, 0.0)


def local(
    tower_in,
    first_norm_scale,
    first_norm_shift,
    conv_weight,
    mid_scale,
    second_norm_shift,
    point_weight,
):
    stream = tower_in
    tracks, rows_here, channels = stream.shape
    devices = lax.axis_size("seq")
    first_bin = lax.axis_index("seq") * rows_here
    bin_count = devices * rows_here
    for block_number in range(BLOCKS):
        receptive_span = FIRST_DILATION * 2**block_number
        source = stream
        if block_number == BLOCKS - 1:
            before = from_behind(source, "seq", 1)
            after = from_behind(source, "seq", -1)
            extended = jnp.concatenate([before, source, after], axis=1)
        else:
            extended = padded(source, (("seq", 1),), receptive_span)
        extended = normalize(
            extended, first_norm_scale[block_number], first_norm_shift[block_number]
        ).astype(jnp.bfloat16)
        position = (
            first_bin + jnp.arange(rows_here + 2 * receptive_span, dtype=jnp.int32) - receptive_span
        )
        inside = ((position >= 0) & (position < bin_count))[None, :, None]
        extended = jnp.where(inside, extended, jnp.zeros_like(extended))
        summed = jnp.zeros((tracks * rows_here, FILTERS), jnp.float32)
        for kernel_tap_index in range(3):
            window = extended[
                :,
                kernel_tap_index * receptive_span : kernel_tap_index * receptive_span + rows_here,
                :,
            ]
            window = window.reshape(tracks * rows_here, channels)
            summed = summed + jnp.dot(
                window,
                conv_weight[block_number, kernel_tap_index],
                preferred_element_type=jnp.float32,
            )
        middle = jnp.maximum(
            summed * mid_scale[block_number] + second_norm_shift[block_number], 0.0
        ).astype(jnp.bfloat16)
        update = jnp.dot(middle, point_weight[block_number], preferred_element_type=jnp.float32)
        flat = stream.reshape(tracks * rows_here, channels).astype(jnp.float32)
        stream = (flat + update).astype(jnp.bfloat16).reshape(tracks, rows_here, channels)
    return stream


def solution(mesh):
    placed = (P("groups", "seq", None), P(), P(), P(), P(), P(), P())
    return jax.shard_map(
        local, mesh=mesh, in_specs=placed, out_specs=P("groups", "seq", None), check_vma=False
    )
```

profile of v0, /device:TPU:25, one launch (start us, length us, event | category | flops | bytes accessed | tf_op | source)
XLA Modules:
  0.0 144.7 jit_solution(12098692960789311480)
XLA Ops:
  1.1 3.7 %collective-permute-start = (bf16[4,32,768]{2,1,0:T(8,128)(2,1)S(1)}, bf16[4,32,768]{2,1,0:T(8,128)(2,1)S(1)}, u32[]{:S(2)}, u32[]{:S(2)}) collective-permute-start(bf16[4,32,768]{2,1,0:T(8,128)(2,1)S(1)} %get-tuple-element.37), channel_id=1, source_target_pairs={{0,1},{1,2},{2,3},{3,4},{4,5},{5,6},{6,7},{7,8},{8,9},{9,10},{10,1... | collective-permute-start | bytes 589832 | tf_op jit(solution)/shard_map/ppermute | solution.py:22
  4.8 1.9 %collective-permute-start.1 = (bf16[4,32,768]{2,1,0:T(8,128)(2,1)S(1)}, bf16[4,32,768]{2,1,0:T(8,128)(2,1)S(1)}, u32[]{:S(2)}, u32[]{:S(2)}) collective-permute-start(bf16[4,32,768]{2,1,0:T(8,128)(2,1)S(1)} %get-tuple-element.38), channel_id=1, source_target_pairs={{1,0},{2,1},{3,2},{4,3},{5,4},{6,5},{7,6},{8,7},{9,8},{10,9},{11,1... | collective-permute-start | bytes 589832 | tf_op jit(solution)/shard_map/ppermute | solution.py:25
  8.7 3.0 %collective-permute-done.1 = bf16[4,32,768]{2,1,0:T(8,128)(2,1)S(1)} collective-permute-done((bf16[4,32,768]{2,1,0:T(8,128)(2,1)S(1)}, bf16[4,32,768]{2,1,0:T(8,128)(2,1)S(1)}, u32[]{:S(2)}, u32[]{:S(2)}) %collective-permute-start.1) | collective-permute-done | bytes 196640 | tf_op jit(solution)/shard_map/ppermute | solution.py:25
  11.8 2.3 %fusion.4 = bf16[4,320,768]{2,1,0:T(8,128)(2,1)S(1)} fusion(bf16[4,32,768]{2,1,0:T(8,128)(2,1)S(1)} %collective-permute-done.1, bf16[4,256,768]{2,1,0:T(8,128)(2,1)} %param.7, bf16[4,32,768]{2,1,0:T(8,128)(2,1)S(1)} %collective-permute-done, f32[768]{0:T(1024)S(1)} %get-tuple-element.11, f32[768]{0:T(1024)S(1)} %get-tuple-element.40, ...), kind=kLoop, calls=%fused_computation.12 | loop fusion | flops 10813440 | bytes 3938624 | tf_op jit(solution)/shard_map/jit(_where)/select_n | solution.py:64
  14.0 1.5 %fusion.84 = (bf16[4,256,768]{2,1,0:T(8,128)(2,1)}, bf16[4,256,768]{2,1,0:T(8,128)(2,1)S(1)}, bf16[4,256,768]{2,1,0:T(8,128)(2,1)S(1)}) fusion(bf16[4,320,768]{2,1,0:T(8,128)(2,1)S(1)} %fusion.4), kind=kLoop, calls=%fused_computation.108 | loop fusion | bytes 9437184 | tf_op jit(solution)/shard_map/slice | solution.py:67
  15.6 3.2 %fusion.41 = f32[1024,384]{1,0:T(8,128)} fusion(bf16[1024,768]{1,0:T(8,128)(2,1)S(1)} %bitcast.95, bf16[4,3,768,384]{3,2,1,0:T(8,128)(2,1)} %param.10), kind=kOutput, calls=%fused_computation.49 | convolution fusion | flops 603979776 | bytes 3735552 | tf_op jit(solution)/shard_map/dot_general | solution.py:73
  18.7 3.3 %fusion.43 = f32[1024,384]{1,0:T(8,128)} fusion(bf16[1024,768]{1,0:T(8,128)(2,1)S(1)} %bitcast.91, bf16[4,3,768,384]{3,2,1,0:T(8,128)(2,1)} %param.10), kind=kOutput, calls=%fused_computation.51 | convolution fusion | flops 603979776 | bytes 3735552 | tf_op jit(solution)/shard_map/dot_general | solution.py:73
  22.1 4.6 %fusion.2 = bf16[1024,768]{1,0:T(8,128)(2,1)S(1)} fusion(bf16[1024,768]{1,0:T(8,128)(2,1)S(1)} %bitcast.86, f32[1024,384]{1,0:T(8,128)} %fusion.43, f32[1024,384]{1,0:T(8,128)} %fusion.41, bf16[1024,768]{1,0:T(8,128)(2,1)} %bitcast.90, f32[384]{0:T(512)S(1)} %get-tuple-element.19, f32[384]{0:T(512)S(1)} %get-tuple-element.44, ...), kind=kOutput, calls=%fused_computation.7 | convolution fusion | flops 1212678144 | bytes 9047040 | tf_op jit(solution)/shard_map/dot_general | solution.py:81
  26.7 1.9 %collective-permute-start.2 = (bf16[4,64,768]{2,1,0:T(8,128)(2,1)S(1)}, bf16[4,64,768]{2,1,0:T(8,128)(2,1)S(1)}, u32[]{:S(2)}, u32[]{:S(2)}) collective-permute-start(bf16[4,64,768]{2,1,0:T(8,128)(2,1)S(1)} %get-tuple-element.35), channel_id=1, source_target_pairs={{0,1},{1,2},{2,3},{3,4},{4,5},{5,6},{6,7},{7,8},{8,9},{9,10},{10,1... | collective-permute-start | bytes 1179656 | tf_op jit(solution)/shard_map/ppermute | solution.py:22
  28.6 2.4 %collective-permute-start.3 = (bf16[4,64,768]{2,1,0:T(8,128)(2,1)S(1)}, bf16[4,64,768]{2,1,0:T(8,128)(2,1)S(1)}, u32[]{:S(2)}, u32[]{:S(2)}) collective-permute-start(bf16[4,64,768]{2,1,0:T(8,128)(2,1)S(1)} %get-tuple-element.36), channel_id=1, source_target_pairs={{1,0},{2,1},{3,2},{4,3},{5,4},{6,5},{7,6},{8,7},{9,8},{10,9},{11,1... | collective-permute-start | bytes 1179656 | tf_op jit(solution)/shard_map/ppermute | solution.py:25
  31.1 2.3 %collective-permute-done.2 = bf16[4,64,768]{2,1,0:T(8,128)(2,1)S(1)} collective-permute-done((bf16[4,64,768]{2,1,0:T(8,128)(2,1)S(1)}, bf16[4,64,768]{2,1,0:T(8,128)(2,1)S(1)}, u32[]{:S(2)}, u32[]{:S(2)}) %collective-permute-start.2) | collective-permute-done | bytes 393248 | tf_op jit(solution)/shard_map/ppermute | solution.py:22
  33.3 6.7 %collective-permute-done.3 = bf16[4,64,768]{2,1,0:T(8,128)(2,1)S(1)} collective-permute-done((bf16[4,64,768]{2,1,0:T(8,128)(2,1)S(1)}, bf16[4,64,768]{2,1,0:T(8,128)(2,1)S(1)}, u32[]{:S(2)}, u32[]{:S(2)}) %collective-permute-start.3) | collective-permute-done | bytes 393248 | tf_op jit(solution)/shard_map/ppermute | solution.py:25
  40.0 2.1 %fusion.3 = bf16[4,384,768]{2,1,0:T(8,128)(2,1)S(1)} fusion(bf16[4,64,768]{2,1,0:T(8,128)(2,1)S(1)} %collective-permute-done.3, bf16[4,256,768]{2,1,0:T(8,128)(2,1)S(1)} %bitcast.85, bf16[4,64,768]{2,1,0:T(8,128)(2,1)S(1)} %collective-permute-done.2, f32[768]{0:T(1024)S(1)} %get-tuple-element.10, f32[768]{0:T(1024)S(1)} %get-tuple-element.41, ...), kind=kLoop, calls=%fused_computation.11 | loop fusion | flops 12976128 | bytes 4725120 | tf_op jit(solution)/shard_map/jit(_where)/select_n | solution.py:64
  42.2 1.5 %fusion.83 = (bf16[4,256,768]{2,1,0:T(8,128)(2,1)}, bf16[4,256,768]{2,1,0:T(8,128)(2,1)S(1)}, bf16[4,256,768]{2,1,0:T(8,128)(2,1)S(1)}) fusion(bf16[4,384,768]{2,1,0:T(8,128)(2,1)S(1)} %fusion.3), kind=kLoop, calls=%fused_computation.107 | loop fusion | bytes 9437184 | tf_op jit(solution)/shard_map/slice | solution.py:67
  43.7 3.2 %fusion.34 = f32[1024,384]{1,0:T(8,128)} fusion(bf16[1024,768]{1,0:T(8,128)(2,1)S(1)} %bitcast.96, bf16[4,3,768,384]{3,2,1,0:T(8,128)(2,1)} %param.10), kind=kOutput, calls=%fused_computation.43 | convolution fusion | flops 603979776 | bytes 3735552 | tf_op jit(solution)/shard_map/dot_general | solution.py:73
  46.9 3.2 %fusion.36 = f32[1024,384]{1,0:T(8,128)} fusion(bf16[1024,768]{1,0:T(8,128)(2,1)S(1)} %bitcast.92, bf16[4,3,768,384]{3,2,1,0:T(8,128)(2,1)} %param.10), kind=kOutput, calls=%fused_computation.45 | convolution fusion | flops 603979776 | bytes 3735552 | tf_op jit(solution)/shard_map/dot_general | solution.py:73
  50.1 4.6 %add_convert_fusion.2 = bf16[1024,768]{1,0:T(8,128)(2,1)S(1)} fusion(bf16[1024,768]{1,0:T(8,128)(2,1)S(1)} %fusion.2, f32[1024,384]{1,0:T(8,128)} %fusion.36, f32[1024,384]{1,0:T(8,128)} %fusion.34, bf16[1024,768]{1,0:T(8,128)(2,1)} %bitcast.88, f32[384]{0:T(512)S(1)} %get-tuple-element.18, f32[384]{0:T(512)S(1)} %get-tuple-element.45, ...), kind=kOutput, calls=%fused_computation.10 | convolution fusion | flops 1212678144 | bytes 9047040 | tf_op jit(solution)/shard_map/dot_general | solution.py:81
  54.8 1.9 %collective-permute-start.4 = (bf16[4,128,768]{2,1,0:T(8,128)(2,1)S(1)}, bf16[4,128,768]{2,1,0:T(8,128)(2,1)S(1)}, u32[]{:S(2)}, u32[]{:S(2)}) collective-permute-start(bf16[4,128,768]{2,1,0:T(8,128)(2,1)S(1)} %get-tuple-element.33), channel_id=1, source_target_pairs={{0,1},{1,2},{2,3},{3,4},{4,5},{5,6},{6,7},{7,8},{8,9},{9,10},{10,1... | collective-permute-start | bytes 2359304 | tf_op jit(solution)/shard_map/ppermute | solution.py:22
  56.7 2.6 %collective-permute-start.5 = (bf16[4,128,768]{2,1,0:T(8,128)(2,1)S(1)}, bf16[4,128,768]{2,1,0:T(8,128)(2,1)S(1)}, u32[]{:S(2)}, u32[]{:S(2)}) collective-permute-start(bf16[4,128,768]{2,1,0:T(8,128)(2,1)S(1)} %get-tuple-element.34), channel_id=1, source_target_pairs={{1,0},{2,1},{3,2},{4,3},{5,4},{6,5},{7,6},{8,7},{9,8},{10,9},{11,1... | collective-permute-start | bytes 2359304 | tf_op jit(solution)/shard_map/ppermute | solution.py:25
  59.3 6.3 %collective-permute-done.4 = bf16[4,128,768]{2,1,0:T(8,128)(2,1)S(1)} collective-permute-done((bf16[4,128,768]{2,1,0:T(8,128)(2,1)S(1)}, bf16[4,128,768]{2,1,0:T(8,128)(2,1)S(1)}, u32[]{:S(2)}, u32[]{:S(2)}) %collective-permute-start.4) | collective-permute-done | bytes 786464 | tf_op jit(solution)/shard_map/ppermute | solution.py:22
  65.6 9.5 %collective-permute-done.5 = bf16[4,128,768]{2,1,0:T(8,128)(2,1)S(1)} collective-permute-done((bf16[4,128,768]{2,1,0:T(8,128)(2,1)S(1)}, bf16[4,128,768]{2,1,0:T(8,128)(2,1)S(1)}, u32[]{:S(2)}, u32[]{:S(2)}) %collective-permute-start.5) | collective-permute-done | bytes 786464 | tf_op jit(solution)/shard_map/ppermute | solution.py:25
  75.1 3.3 %fusion.1 = bf16[4,512,768]{2,1,0:T(8,128)(2,1)S(1)} fusion(bf16[4,128,768]{2,1,0:T(8,128)(2,1)S(1)} %collective-permute-done.5, bf16[4,256,768]{2,1,0:T(8,128)(2,1)S(1)} %bitcast.83, bf16[4,128,768]{2,1,0:T(8,128)(2,1)S(1)} %collective-permute-done.4, f32[768]{0:T(1024)S(1)} %get-tuple-element.12, f32[768]{0:T(1024)S(1)} %get-tuple-element.39, ...), kind=kLoop, calls=%fused_computation.5 | loop fusion | flops 17301504 | bytes 6298112 | tf_op jit(solution)/shard_map/jit(_where)/select_n | solution.py:64
  78.8 3.2 %fusion.27 = f32[1024,384]{1,0:T(8,128)} fusion(bf16[1024,768]{1,0:T(8,128)(2,1)S(1)} %bitcast.97, bf16[4,3,768,384]{3,2,1,0:T(8,128)(2,1)} %param.10), kind=kOutput, calls=%fused_computation.37 | convolution fusion | flops 603979776 | bytes 3735552 | tf_op jit(solution)/shard_map/dot_general | solution.py:73
  82.0 3.2 %fusion.29 = f32[1024,384]{1,0:T(8,128)} fusion(bf16[1024,768]{1,0:T(8,128)(2,1)S(1)} %bitcast.93, bf16[4,3,768,384]{3,2,1,0:T(8,128)(2,1)} %param.10), kind=kOutput, calls=%fused_computation.39 | convolution fusion | flops 603979776 | bytes 3735552 | tf_op jit(solution)/shard_map/dot_general | solution.py:73
  85.2 5.3 %add_convert_fusion.1 = bf16[1024,768]{1,0:T(8,128)(2,1)} fusion(bf16[1024,768]{1,0:T(8,128)(2,1)S(1)} %add_convert_fusion.2, f32[1024,384]{1,0:T(8,128)} %fusion.29, f32[1024,384]{1,0:T(8,128)} %fusion.27, bf16[1024,768]{1,0:T(8,128)(2,1)S(1)} %bitcast.89, f32[384]{0:T(512)S(1)} %get-tuple-element.20, f32[384]{0:T(512)S(1)} %get-tuple-element.43, ...), kind=kOutput, calls=%fused_computation.9 | convolution fusion | flops 1212678144 | bytes 9047040 | tf_op jit(solution)/shard_map/dot_general | solution.py:81
  90.5 1.9 %collective-permute-start.7 = (bf16[4,256,768]{2,1,0:T(8,128)(2,1)}, bf16[4,256,768]{2,1,0:T(8,128)(2,1)S(1)}, u32[]{:S(2)}, u32[]{:S(2)}) collective-permute-start(bf16[4,256,768]{2,1,0:T(8,128)(2,1)} %bitcast.99), channel_id=1, source_target_pairs={{1,0},{2,1},{3,2},{4,3},{5,4},{6,5},{7,6},{8,7},{9,8},{10,9},{11,1... | collective-permute-start | bytes 4718600 | tf_op jit(solution)/shard_map/ppermute | solution.py:14
  92.4 3.6 %collective-permute-start.6 = (bf16[4,256,768]{2,1,0:T(8,128)(2,1)}, bf16[4,256,768]{2,1,0:T(8,128)(2,1)S(1)}, u32[]{:S(2)}, u32[]{:S(2)}) collective-permute-start(bf16[4,256,768]{2,1,0:T(8,128)(2,1)} %bitcast.100), channel_id=1, source_target_pairs={{0,1},{1,2},{2,3},{3,4},{4,5},{5,6},{6,7},{7,8},{8,9},{9,10},{10,1... | collective-permute-start | bytes 4718600 | tf_op jit(solution)/shard_map/ppermute | solution.py:14
  96.1 33.2 %collective-permute-done.7 = bf16[4,256,768]{2,1,0:T(8,128)(2,1)S(1)} collective-permute-done((bf16[4,256,768]{2,1,0:T(8,128)(2,1)}, bf16[4,256,768]{2,1,0:T(8,128)(2,1)S(1)}, u32[]{:S(2)}, u32[]{:S(2)}) %collective-permute-start.7) | collective-permute-done | bytes 1572896 | tf_op jit(solution)/shard_map/ppermute | solution.py:14
  129.3 3.3 %fusion = bf16[4,768,768]{2,1,0:T(8,128)(2,1)S(1)} fusion(bf16[4,256,768]{2,1,0:T(8,128)(2,1)S(1)} %collective-permute-done.7, bf16[4,256,768]{2,1,0:T(8,128)(2,1)} %bitcast.101, bf16[4,256,768]{2,1,0:T(8,128)(2,1)S(1)} %collective-permute-done.6, f32[768]{0:T(1024)S(1)} %get-tuple-element.9, f32[768]{0:T(1024)S(1)} %get-tuple-element.42, ...), kind=kLoop, calls=%fused_computation.2 | loop fusion | flops 25952256 | bytes 9444096 | tf_op jit(solution)/shard_map/jit(_where)/select_n | solution.py:64
  132.9 3.2 %fusion.20 = f32[1024,384]{1,0:T(8,128)} fusion(bf16[1024,768]{1,0:T(8,128)(2,1)S(1)} %bitcast.98, bf16[4,3,768,384]{3,2,1,0:T(8,128)(2,1)} %param.10), kind=kOutput, calls=%fused_computation.31 | convolution fusion | flops 603979776 | bytes 3735552 | tf_op jit(solution)/shard_map/dot_general | solution.py:73
  136.1 3.3 %fusion.22 = f32[1024,384]{1,0:T(8,128)} fusion(bf16[1024,768]{1,0:T(8,128)(2,1)S(1)} %bitcast.94, bf16[4,3,768,384]{3,2,1,0:T(8,128)(2,1)} %param.10), kind=kOutput, calls=%fused_computation.33 | convolution fusion | flops 603979776 | bytes 3735552 | tf_op jit(solution)/shard_map/dot_general | solution.py:73
  139.4 5.3 %add_convert_fusion = bf16[1024,768]{1,0:T(8,128)(2,1)} fusion(bf16[1024,768]{1,0:T(8,128)(2,1)S(1)} %copy-done.1, f32[1024,384]{1,0:T(8,128)} %fusion.22, f32[1024,384]{1,0:T(8,128)} %fusion.20, bf16[1024,768]{1,0:T(8,128)(2,1)S(1)} %bitcast.87, f32[384]{0:T(512)S(1)} %get-tuple-element.17, f32[384]{0:T(512)S(1)} %get-tuple-element.46, ...), kind=kOutput, calls=%fused_computation.8 | convolution fusion | flops 1212678144 | bytes 9047040 | tf_op jit(solution)/shard_map/dot_general | solution.py:81
  (17 shorter events, 4.0 us)
Async XLA Ops:
  1.1 7.7 %collective-permute-start = (bf16[4,32,768]{2,1,0:T(8,128)(2,1)S(1)}, bf16[4,32,768]{2,1,0:T(8,128)(2,1)S(1)}, u32[]{:S(2)}, u32[]{:S(2)}) collective-permute-start(bf16[4,32,768]{2,1,0:T(8,128)(2,1)S(1)} %get-tuple-element.37), channel_id=1, source_target_pairs={{0,1},{1,2},{2,3},{3,4},{4,5},{5,6},{6,7},{7,8},{8,9},{9,10},{10,1... | collective-permute-start | bytes 589832 | tf_op jit(solution)/shard_map/ppermute | solution.py:22
  4.8 7.0 %collective-permute-start.1 = (bf16[4,32,768]{2,1,0:T(8,128)(2,1)S(1)}, bf16[4,32,768]{2,1,0:T(8,128)(2,1)S(1)}, u32[]{:S(2)}, u32[]{:S(2)}) collective-permute-start(bf16[4,32,768]{2,1,0:T(8,128)(2,1)S(1)} %get-tuple-element.38), channel_id=1, source_target_pairs={{1,0},{2,1},{3,2},{4,3},{5,4},{6,5},{7,6},{8,7},{9,8},{10,9},{11,1... | collective-permute-start | bytes 589832 | tf_op jit(solution)/shard_map/ppermute | solution.py:25
  18.7 3.3 %copy-start = (bf16[4,256,768]{2,1,0:T(8,128)(2,1)S(1)}, bf16[4,256,768]{2,1,0:T(8,128)(2,1)}, u32[]{:S(2)}) copy-start(bf16[4,256,768]{2,1,0:T(8,128)(2,1)} %param.7) | copy-start | bytes 4718596
  26.7 6.6 %collective-permute-start.2 = (bf16[4,64,768]{2,1,0:T(8,128)(2,1)S(1)}, bf16[4,64,768]{2,1,0:T(8,128)(2,1)S(1)}, u32[]{:S(2)}, u32[]{:S(2)}) collective-permute-start(bf16[4,64,768]{2,1,0:T(8,128)(2,1)S(1)} %get-tuple-element.35), channel_id=1, source_target_pairs={{0,1},{1,2},{2,3},{3,4},{4,5},{5,6},{6,7},{7,8},{8,9},{9,10},{10,1... | collective-permute-start | bytes 1179656 | tf_op jit(solution)/shard_map/ppermute | solution.py:22
  28.6 11.4 %collective-permute-start.3 = (bf16[4,64,768]{2,1,0:T(8,128)(2,1)S(1)}, bf16[4,64,768]{2,1,0:T(8,128)(2,1)S(1)}, u32[]{:S(2)}, u32[]{:S(2)}) collective-permute-start(bf16[4,64,768]{2,1,0:T(8,128)(2,1)S(1)} %get-tuple-element.36), channel_id=1, source_target_pairs={{1,0},{2,1},{3,2},{4,3},{5,4},{6,5},{7,6},{8,7},{9,8},{10,9},{11,1... | collective-permute-start | bytes 1179656 | tf_op jit(solution)/shard_map/ppermute | solution.py:25
  54.8 10.8 %collective-permute-start.4 = (bf16[4,128,768]{2,1,0:T(8,128)(2,1)S(1)}, bf16[4,128,768]{2,1,0:T(8,128)(2,1)S(1)}, u32[]{:S(2)}, u32[]{:S(2)}) collective-permute-start(bf16[4,128,768]{2,1,0:T(8,128)(2,1)S(1)} %get-tuple-element.33), channel_id=1, source_target_pairs={{0,1},{1,2},{2,3},{3,4},{4,5},{5,6},{6,7},{7,8},{8,9},{9,10},{10,1... | collective-permute-start | bytes 2359304 | tf_op jit(solution)/shard_map/ppermute | solution.py:22
  56.7 18.4 %collective-permute-start.5 = (bf16[4,128,768]{2,1,0:T(8,128)(2,1)S(1)}, bf16[4,128,768]{2,1,0:T(8,128)(2,1)S(1)}, u32[]{:S(2)}, u32[]{:S(2)}) collective-permute-start(bf16[4,128,768]{2,1,0:T(8,128)(2,1)S(1)} %get-tuple-element.34), channel_id=1, source_target_pairs={{1,0},{2,1},{3,2},{4,3},{5,4},{6,5},{7,6},{8,7},{9,8},{10,9},{11,1... | collective-permute-start | bytes 2359304 | tf_op jit(solution)/shard_map/ppermute | solution.py:25
  90.5 38.8 %collective-permute-start.7 = (bf16[4,256,768]{2,1,0:T(8,128)(2,1)}, bf16[4,256,768]{2,1,0:T(8,128)(2,1)S(1)}, u32[]{:S(2)}, u32[]{:S(2)}) collective-permute-start(bf16[4,256,768]{2,1,0:T(8,128)(2,1)} %bitcast.99), channel_id=1, source_target_pairs={{1,0},{2,1},{3,2},{4,3},{5,4},{6,5},{7,6},{8,7},{9,8},{10,9},{11,1... | collective-permute-start | bytes 4718600 | tf_op jit(solution)/shard_map/ppermute | solution.py:14
  92.4 36.9 %collective-permute-start.6 = (bf16[4,256,768]{2,1,0:T(8,128)(2,1)}, bf16[4,256,768]{2,1,0:T(8,128)(2,1)S(1)}, u32[]{:S(2)}, u32[]{:S(2)}) collective-permute-start(bf16[4,256,768]{2,1,0:T(8,128)(2,1)} %bitcast.100), channel_id=1, source_target_pairs={{0,1},{1,2},{2,3},{3,4},{4,5},{5,6},{6,7},{7,8},{8,9},{9,10},{10,1... | collective-permute-start | bytes 4718600 | tf_op jit(solution)/shard_map/ppermute | solution.py:14
  136.1 3.3 %copy-start.1 = (bf16[1024,768]{1,0:T(8,128)(2,1)S(1)}, bf16[1024,768]{1,0:T(8,128)(2,1)}, u32[]{:S(2)}) copy-start(bf16[1024,768]{1,0:T(8,128)(2,1)} %add_convert_fusion.1) | copy-start | bytes 4718596
where the time goes:
time: 146 us; the launch traced here: 145 us
  waiting for transfers between devices  61 us (42%)
  matrix products  45.4 us (31%)
  starting transfers between devices  20 us (14%)
  other arithmetic  11 us (8%)
  local copies, waits for them, and re-layouts  7.04 us (5%)
    ppermute x2, waiting for transfers between devices, from_behind(): return lax.ppermute(value, axis, pairs)  33.2 us
    dot_general x8, matrix products, local(): jnp.dot(window, conv_weight[block_number, kernel_tap_index], preferred_el...  25.7 us
    dot_general x4, matrix products, local(): jnp.dot(middle, point_weight[block_number], preferred_element_type=jnp.fl...  19.7 us
    ppermute x3, waiting for transfers between devices, padded(): lax.ppermute(lax.slice_in_dim(block, 0, width, axis=dim), axis, backward)  19.2 us
    select_n x4, other arithmetic, local(): extended = jnp.where(inside, extended, jnp.zeros_like(extended))  11 us
    ppermute x3, waiting for transfers between devices, padded(): lax.ppermute(lax.slice_in_dim(block, block.shape[dim] - width, None, axis...  8.58 us
    ppermute x3, starting transfers between devices, padded(): lax.ppermute(lax.slice_in_dim(block, block.shape[dim] - width, None, axis...  7.55 us
    ppermute x3, starting transfers between devices, padded(): lax.ppermute(lax.slice_in_dim(block, 0, width, axis=dim), axis, backward)  6.91 us
  transfers between devices with their start and end apart: 8, of which 6 were waited for; matrix products, arithmetic and copies ran while one was open for 1% of the time, Pallas kernels for 0%

commit v1 on v0

v1 whole, which is shorter than its diff:
```python
import functools

import jax
import jax.numpy as jnp
from jax import lax
from jax.experimental import pallas as pl
from jax.experimental.pallas import tpu as pltpu
from jax.sharding import PartitionSpec as P

FIRST_DILATION = 32
CHUNKS = 2
VMEM_LIMIT = 48 * 1024 * 1024


def finish(stream, conv, scale, shift, point):
    middle = jnp.maximum(conv * scale + shift, 0.0).astype(jnp.bfloat16)
    update = jnp.dot(middle, point, preferred_element_type=jnp.float32)
    return (stream.astype(jnp.float32) + update).astype(jnp.bfloat16)


def begin(stream, scale, shift, weight, span, even, t, local_ref, intra_ref, inter_ref):
    rows = stream.shape[0]
    normed = jnp.maximum(stream.astype(jnp.float32) * scale + shift, 0.0).astype(jnp.bfloat16)
    behind, here, ahead = (
        jnp.dot(normed, weight[0, k], preferred_element_type=jnp.float32) for k in range(3)
    )
    to_next = behind[rows - span :].astype(jnp.bfloat16)
    to_last = ahead[:span].astype(jnp.bfloat16)

    @pl.when(even)
    def _():
        intra_ref[t] = to_next
        inter_ref[t] = to_last

    @pl.when(jnp.logical_not(even))
    def _():
        intra_ref[t] = to_last
        inter_ref[t] = to_next

    if span == rows:
        local_ref[t] = here
    else:
        zeros = jnp.zeros((span, here.shape[1]), jnp.float32)
        low = jnp.concatenate([zeros, behind[: rows - span]], axis=0)
        high = jnp.concatenate([ahead[span:], zeros], axis=0)
        local_ref[t] = here + low + high


def with_halo(local_ref, intra_ref, inter_ref, even, t, span):
    local = local_ref[t]
    rows = local.shape[0]
    intra = intra_ref[t].astype(jnp.float32)
    inter = inter_ref[t].astype(jnp.float32)
    head = jnp.where(even, inter, intra)
    tail = jnp.where(even, intra, inter)
    if span == rows:
        return local + head + tail
    zeros = jnp.zeros((rows - span, local.shape[1]), jnp.float32)
    return local + jnp.concatenate([head, zeros], axis=0) + jnp.concatenate([zeros, tail], axis=0)


def first_kernel(span, stream_ref, scale_ref, shift_ref, weight_ref, local_ref, intra_ref, inter_ref):
    even = lax.rem(lax.axis_index("seq"), 2) == 0
    for t in range(stream_ref.shape[0]):
        begin(
            stream_ref[t], scale_ref[...], shift_ref[...], weight_ref, span, even, t,
            local_ref, intra_ref, inter_ref,
        )


def middle_kernel(
    span, next_span,
    stream_ref, local_ref, intra_ref, inter_ref, mid_scale_ref, mid_shift_ref, point_ref,
    scale_ref, shift_ref, weight_ref,
    out_ref, next_local_ref, next_intra_ref, next_inter_ref,
):
    even = lax.rem(lax.axis_index("seq"), 2) == 0
    for t in range(stream_ref.shape[0]):
        conv = with_halo(local_ref, intra_ref, inter_ref, even, t, span)
        stream = finish(stream_ref[t], conv, mid_scale_ref[...], mid_shift_ref[...], point_ref[0])
        out_ref[t] = stream
        begin(
            stream, scale_ref[...], shift_ref[...], weight_ref, next_span, even, t,
            next_local_ref, next_intra_ref, next_inter_ref,
        )


def last_kernel(
    span, stream_ref, local_ref, intra_ref, inter_ref, mid_scale_ref, mid_shift_ref, point_ref, out_ref
):
    even = lax.rem(lax.axis_index("seq"), 2) == 0
    for t in range(stream_ref.shape[0]):
        conv = with_halo(local_ref, intra_ref, inter_ref, even, t, span)
        out_ref[t] = finish(stream_ref[t], conv, mid_scale_ref[...], mid_shift_ref[...], point_ref[0])


def whole(shape):
    return pl.BlockSpec(shape, lambda t: (0,) * len(shape))


def pick(shape, index):
    return pl.BlockSpec(shape, lambda t: (index,) + (0,) * (len(shape) - 1))


def track(shape, base=0):
    return pl.BlockSpec((1,) + shape, lambda t: (base + t,) + (0,) * len(shape))


def local(
    tower_in, first_norm_scale, first_norm_shift, conv_weight, mid_scale, second_norm_shift, point_weight
):
    tracks, rows, channels = tower_in.shape
    blocks, _, _, filters = conv_weight.shape
    devices = lax.axis_size("seq")
    intra_pairs = [(i, i + 1) for i in range(0, devices - 1, 2)]
    inter_pairs = [(i, i + 1) for i in range(1, devices - 1, 2)]
    intra_pairs += [(b, a) for a, b in intra_pairs]
    inter_pairs += [(b, a) for a, b in inter_pairs]
    spans = [FIRST_DILATION * 2**b for b in range(blocks)]
    size = tracks // CHUNKS
    scales = [first_norm_scale[b : b + 1] for b in range(blocks)]
    shifts = [first_norm_shift[b : b + 1] for b in range(blocks)]
    mids = [mid_scale[b : b + 1] for b in range(blocks)]
    mid_shifts = [second_norm_shift[b : b + 1] for b in range(blocks)]
    params = pltpu.CompilerParams(vmem_limit_bytes=VMEM_LIMIT)

    stream_spec = track((rows, channels))
    local_spec = track((rows, filters))
    channel_spec = whole((1, channels))
    filter_spec = whole((1, filters))
    stream_shape = jax.ShapeDtypeStruct((size, rows, channels), jnp.bfloat16)
    local_shape = jax.ShapeDtypeStruct((size, rows, filters), jnp.float32)

    def halo_spec(b):
        return track((spans[b], filters))

    def halo_shape(b):
        return jax.ShapeDtypeStruct((size, spans[b], filters), jnp.bfloat16)

    def weight_spec(b):
        return pick((1, 3, channels, filters), b)

    def point_spec(b):
        return pick((1, filters, channels), b)

    conv_flops = size * rows * channels * filters * 6
    point_flops = size * rows * channels * filters * 2

    def cost(flops):
        return pl.CostEstimate(flops=2 * flops, bytes_accessed=flops // 1000, transcendentals=0)

    streams, held = [], []
    for c in range(CHUNKS):
        streams.append(lax.slice_in_dim(tower_in, c * size, (c + 1) * size, axis=0))
    for c in range(CHUNKS):
        local_sum, intra, inter = pl.pallas_call(
            functools.partial(first_kernel, spans[0]),
            grid=(size,),
            in_specs=[
                track((rows, channels), c * size), channel_spec, channel_spec, weight_spec(0)
            ],
            out_specs=[local_spec, halo_spec(0), halo_spec(0)],
            out_shape=[local_shape, halo_shape(0), halo_shape(0)],
            compiler_params=params,
            cost_estimate=cost(conv_flops),
        )(tower_in, scales[0], shifts[0], conv_weight)
        inter = lax.ppermute(inter, "seq", inter_pairs)
        intra = lax.ppermute(intra, "seq", intra_pairs)
        held.append((local_sum, intra, inter))
    for b in range(1, blocks):
        for c in range(CHUNKS):
            first = b == 1
            stream, local_sum, intra, inter = pl.pallas_call(
                functools.partial(middle_kernel, spans[b - 1], spans[b]),
                grid=(size,),
                in_specs=[
                    track((rows, channels), c * size if first else 0),
                    local_spec, halo_spec(b - 1), halo_spec(b - 1), filter_spec, filter_spec,
                    point_spec(b - 1), channel_spec, channel_spec, weight_spec(b),
                ],
                out_specs=[stream_spec, local_spec, halo_spec(b), halo_spec(b)],
                out_shape=[stream_shape, local_shape, halo_shape(b), halo_shape(b)],
                compiler_params=params,
                cost_estimate=cost(conv_flops + point_flops),
            )(
                tower_in if first else streams[c],
                *held[c], mids[b - 1], mid_shifts[b - 1], point_weight,
                scales[b], shifts[b], conv_weight,
            )
            inter = lax.ppermute(inter, "seq", inter_pairs)
            intra = lax.ppermute(intra, "seq", intra_pairs)
            streams[c] = stream
            held[c] = (local_sum, intra, inter)
    out = None
    b = blocks - 1
    outs = []
    for c in range(CHUNKS):
        outs.append(
            pl.pallas_call(
                functools.partial(last_kernel, spans[b]),
                grid=(size,),
                in_specs=[
                    stream_spec, local_spec, halo_spec(b), halo_spec(b), filter_spec, filter_spec,
                    point_spec(b),
                ],
                out_specs=stream_spec,
                out_shape=stream_shape,
                compiler_params=params,
                cost_estimate=cost(point_flops),
            )(streams[c], *held[c], mids[b], mid_shifts[b], point_weight)
        )
    return jnp.concatenate(outs, axis=0)


def solution(mesh):
    placed = (P("groups", "seq", None), P(), P(), P(), P(), P(), P())
    return jax.shard_map(
        local, mesh=mesh, in_specs=placed, out_specs=P("groups", "seq", None), check_vma=False
    )
```

time: 146 us -> 76.7 us (0.53)
  the two profiles are of different devices: /device:TPU:25 before, /device:TPU:1 now
where the time goes in v1:
time: 76.7 us; the launch traced here: 76.1 us
  Pallas kernels  33.7 us (44%)
  starting transfers between devices  29.2 us (38%)
  waiting for transfers between devices  9.24 us (12%)
  local copies, waits for them, and re-layouts  2.4 us (3%)
  other arithmetic  1.28 us (2%)
    ppermute x8, starting transfers between devices, local(): inter = lax.ppermute(inter, 'seq', inter_pairs)  28.6 us
    pallas_call x6, Pallas kernels, local(): pl.pallas_call(functools.partial(middle_kernel, spans[b - 1], spans[b]),...  25.1 us
    ppermute x8, waiting for transfers between devices, local(): inter = lax.ppermute(inter, 'seq', inter_pairs)  9.22 us
    pallas_call x2, Pallas kernels, local(): pl.pallas_call(functools.partial(first_kernel, spans[0]), grid=(size,), i...  6.91 us
    pallas_call x2, Pallas kernels, local(): pl.pallas_call(functools.partial(last_kernel, spans[b]), grid=(size,), in...  1.68 us
  transfers between devices with their start and end apart: 16, of which 2 were waited for; matrix products, arithmetic and copies ran while one was open for 0% of the time, Pallas kernels for 39%

profile of v1, /device:TPU:1, one launch (start us, length us, event | category | flops | bytes accessed | tf_op | source)
XLA Modules:
  0.0 76.1 jit_solution(5881911829593552523)
XLA Ops:
  0.0 1.0 %fusion = (f32[1,768]{1,0:T(1,128)S(1)}, f32[1,768]{1,0:T(1,128)S(1)}, f32[1,768]{1,0:T(1,128)S(1)}, f32[1,768]{1,0:T(1,128)S(1)}, f32[1,768]{1,0:T(1,128)S(1)},...) fusion(f32[4,768]{1,0:T(4,128)} %param.9, f32[4,768]{1,0:T(4,128)} %param.8), kind=kLoop, calls=%fused_computation.1 | loop fusion | bytes 49152 | tf_op jit(solution)/shard_map/slice | solution.py:122
  1.0 1.4 %copy-done.2 = bf16[4,256,768]{2,1,0:T(8,128)(2,1)S(1)} copy-done((bf16[4,256,768]{2,1,0:T(8,128)(2,1)S(1)}, bf16[4,256,768]{2,1,0:T(8,128)(2,1)}, u32[]{:S(2)}) %copy-start.2) | copy-done | bytes 1572888
  2.4 3.4 %shard_map.73 = (f32[2,256,384]{2,1,0:T(8,128)S(1)}, bf16[2,32,384]{2,1,0:T(8,128)(2,1)S(1)}, bf16[2,32,384]{2,1,0:T(8,128)(2,1)S(1)}) custom-call(bf16[4,256,768]{2,1,0:T(8,128)(2,1)S(1)} %copy-done.2, f32[1,768]{1,0:T(1,128)S(1)} %get-tuple-element.82.scale_ref, f32[1,768]{1,0:T(1,128)S(1)} %get-tuple-element.67.shift_ref, bf16[4,3,768,384]{3,2,1,0:T(8,128)(2,1)} %weight_ref.15), custom_call_target="tpu_custom_call" | custom-call | flops 1811939328 | bytes 905969 | tf_op jit(solution)/shard_map/pallas_call | solution.py:156
  5.8 0.1 collective-permute-start
  5.9 4.5 %collective-permute-start.1 = (bf16[2,32,384]{2,1,0:T(8,128)(2,1)S(1)}, bf16[2,32,384]{2,1,0:T(8,128)(2,1)S(1)}, u32[]{:S(2)}, u32[]{:S(2)}) collective-permute-start(bf16[2,32,384]{2,1,0:T(8,128)(2,1)S(1)} %get-tuple-element.37), channel_id=1, source_target_pairs={{1,2},{3,4},{5,6},{7,8},{9,10},{11,12},{13,14},{2,1},{4,3},{6,5},{... | collective-permute-start | bytes 147464 | tf_op jit(solution)/shard_map/ppermute | solution.py:167
  10.5 3.5 %shard_map.78 = (f32[2,256,384]{2,1,0:T(8,128)S(1)}, bf16[2,32,384]{2,1,0:T(8,128)(2,1)S(1)}, bf16[2,32,384]{2,1,0:T(8,128)(2,1)S(1)}) custom-call(bf16[4,256,768]{2,1,0:T(8,128)(2,1)S(1)} %copy-done.2, f32[1,768]{1,0:T(1,128)S(1)} %get-tuple-element.82.scale_ref, f32[1,768]{1,0:T(1,128)S(1)} %get-tuple-element.67.shift_ref, bf16[4,3,768,384]{3,2,1,0:T(8,128)(2,1)} %weight_ref.15), custom_call_target="tpu_custom_call" | custom-call | flops 1811939328 | bytes 905969 | tf_op jit(solution)/shard_map/pallas_call | solution.py:156
  13.9 0.1 collective-permute-start.8
  14.0 3.5 %collective-permute-start.9 = (bf16[2,32,384]{2,1,0:T(8,128)(2,1)S(1)}, bf16[2,32,384]{2,1,0:T(8,128)(2,1)S(1)}, u32[]{:S(2)}, u32[]{:S(2)}) collective-permute-start(bf16[2,32,384]{2,1,0:T(8,128)(2,1)S(1)} %get-tuple-element.52), channel_id=1, source_target_pairs={{1,2},{3,4},{5,6},{7,8},{9,10},{11,12},{13,14},{2,1},{4,3},{6,5},{... | collective-permute-start | bytes 147464 | tf_op jit(solution)/shard_map/ppermute | solution.py:167
  17.6 4.2 %shard_map.74 = (bf16[2,256,768]{2,1,0:T(8,128)(2,1)S(1)}, f32[2,256,384]{2,1,0:T(8,128)S(1)}, bf16[2,64,384]{2,1,0:T(8,128)(2,1)S(1)}, bf16[2,64,384]{2,1,0:T(8,128)(2,1)S(1)}) custom-call(bf16[4,256,768]{2,1,0:T(8,128)(2,1)S(1)} %copy-done.2, f32[2,256,384]{2,1,0:T(8,128)S(1)} %get-tuple-element.35.local_ref, ...), custom_call_target="tpu_custom_call" | custom-call | flops 2415919104 | bytes 1207959 | tf_op jit(solution)/shard_map/pallas_call | solution.py:173
  21.8 0.1 collective-permute-start.2
  21.9 3.5 %collective-permute-start.3 = (bf16[2,64,384]{2,1,0:T(8,128)(2,1)S(1)}, bf16[2,64,384]{2,1,0:T(8,128)(2,1)S(1)}, u32[]{:S(2)}, u32[]{:S(2)}) collective-permute-start(bf16[2,64,384]{2,1,0:T(8,128)(2,1)S(1)} %get-tuple-element.41), channel_id=1, source_target_pairs={{1,2},{3,4},{5,6},{7,8},{9,10},{11,12},{13,14},{2,1},{4,3},{6,5},{... | collective-permute-start | bytes 294920 | tf_op jit(solution)/shard_map/ppermute | solution.py:190
  25.5 4.4 %shard_map.79 = (bf16[2,256,768]{2,1,0:T(8,128)(2,1)S(1)}, f32[2,256,384]{2,1,0:T(8,128)S(1)}, bf16[2,64,384]{2,1,0:T(8,128)(2,1)S(1)}, bf16[2,64,384]{2,1,0:T(8,128)(2,1)S(1)}) custom-call(bf16[4,256,768]{2,1,0:T(8,128)(2,1)S(1)} %copy-done.2, f32[2,256,384]{2,1,0:T(8,128)S(1)} %get-tuple-element.50.local_ref, ...), custom_call_target="tpu_custom_call" | custom-call | flops 2415919104 | bytes 1207959 | tf_op jit(solution)/shard_map/pallas_call | solution.py:173
  29.8 0.1 collective-permute-start.10
  29.9 3.5 %collective-permute-start.11 = (bf16[2,64,384]{2,1,0:T(8,128)(2,1)S(1)}, bf16[2,64,384]{2,1,0:T(8,128)(2,1)S(1)}, u32[]{:S(2)}, u32[]{:S(2)}) collective-permute-start(bf16[2,64,384]{2,1,0:T(8,128)(2,1)S(1)} %get-tuple-element.56), channel_id=1, source_target_pairs={{1,2},{3,4},{5,6},{7,8},{9,10},{11,12},{13,14},{2,1},{4,3},{6,5},{... | collective-permute-start | bytes 294920 | tf_op jit(solution)/shard_map/ppermute | solution.py:190
  33.5 4.1 %shard_map.75 = (bf16[2,256,768]{2,1,0:T(8,128)(2,1)S(1)}, f32[2,256,384]{2,1,0:T(8,128)S(1)}, bf16[2,128,384]{2,1,0:T(8,128)(2,1)S(1)}, bf16[2,128,384]{2,1,0:T(8,128)(2,1)S(1)}) custom-call(bf16[2,256,768]{2,1,0:T(8,128)(2,1)S(1)} %get-tuple-element.38.stream_ref, f32[2,256,384]{2,1,0:T(8,128)S(1)} %get-tuple-element.39.local_ref, ...), custom_call_target="tpu_custom_call" | custom-call | flops 2415919104 | bytes 1207959 | tf_op jit(solution)/shard_map/pallas_call | solution.py:173
  37.6 0.1 collective-permute-start.4
  37.7 3.5 %collective-permute-start.5 = (bf16[2,128,384]{2,1,0:T(8,128)(2,1)S(1)}, bf16[2,128,384]{2,1,0:T(8,128)(2,1)S(1)}, u32[]{:S(2)}, u32[]{:S(2)}) collective-permute-start(bf16[2,128,384]{2,1,0:T(8,128)(2,1)S(1)} %get-tuple-element.45), channel_id=1, source_target_pairs={{1,2},{3,4},{5,6},{7,8},{9,10},{11,12},{13,14},{2,1},{4,3},{6,5},{... | collective-permute-start | bytes 589832 | tf_op jit(solution)/shard_map/ppermute | solution.py:190
  41.2 4.1 %shard_map.80 = (bf16[2,256,768]{2,1,0:T(8,128)(2,1)S(1)}, f32[2,256,384]{2,1,0:T(8,128)S(1)}, bf16[2,128,384]{2,1,0:T(8,128)(2,1)S(1)}, bf16[2,128,384]{2,1,0:T(8,128)(2,1)S(1)}) custom-call(bf16[2,256,768]{2,1,0:T(8,128)(2,1)S(1)} %get-tuple-element.53.stream_ref, f32[2,256,384]{2,1,0:T(8,128)S(1)} %get-tuple-element.54.local_ref, ...), custom_call_target="tpu_custom_call" | custom-call | flops 2415919104 | bytes 1207959 | tf_op jit(solution)/shard_map/pallas_call | solution.py:173
  45.4 0.1 collective-permute-start.12
  45.5 3.5 %collective-permute-start.13 = (bf16[2,128,384]{2,1,0:T(8,128)(2,1)S(1)}, bf16[2,128,384]{2,1,0:T(8,128)(2,1)S(1)}, u32[]{:S(2)}, u32[]{:S(2)}) collective-permute-start(bf16[2,128,384]{2,1,0:T(8,128)(2,1)S(1)} %get-tuple-element.60), channel_id=1, source_target_pairs={{1,2},{3,4},{5,6},{7,8},{9,10},{11,12},{13,14},{2,1},{4,3},{6,5},{... | collective-permute-start | bytes 589832 | tf_op jit(solution)/shard_map/ppermute | solution.py:190
  49.0 4.0 %shard_map.76 = (bf16[2,256,768]{2,1,0:T(8,128)(2,1)S(1)}, f32[2,256,384]{2,1,0:T(8,128)S(1)}, bf16[2,256,384]{2,1,0:T(8,128)(2,1)S(1)}, bf16[2,256,384]{2,1,0:T(8,128)(2,1)S(1)}) custom-call(bf16[2,256,768]{2,1,0:T(8,128)(2,1)S(1)} %get-tuple-element.42.stream_ref, f32[2,256,384]{2,1,0:T(8,128)S(1)} %get-tuple-element.43.local_ref, ...), custom_call_target="tpu_custom_call" | custom-call | flops 2415919104 | bytes 1207959 | tf_op jit(solution)/shard_map/pallas_call | solution.py:173
  53.1 0.1 collective-permute-start.6
  53.1 3.5 %collective-permute-start.7 = (bf16[2,256,384]{2,1,0:T(8,128)(2,1)S(1)}, bf16[2,256,384]{2,1,0:T(8,128)(2,1)S(1)}, u32[]{:S(2)}, u32[]{:S(2)}) collective-permute-start(bf16[2,256,384]{2,1,0:T(8,128)(2,1)S(1)} %get-tuple-element.49), channel_id=1, source_target_pairs={{1,2},{3,4},{5,6},{7,8},{9,10},{11,12},{13,14},{2,1},{4,3},{6,5},{... | collective-permute-start | bytes 1179656 | tf_op jit(solution)/shard_map/ppermute | solution.py:190
  56.7 0.0 copy-start.1
  56.7 4.2 %shard_map.81 = (bf16[2,256,768]{2,1,0:T(8,128)(2,1)S(1)}, f32[2,256,384]{2,1,0:T(8,128)S(1)}, bf16[2,256,384]{2,1,0:T(8,128)(2,1)S(1)}, bf16[2,256,384]{2,1,0:T(8,128)(2,1)S(1)}) custom-call(bf16[2,256,768]{2,1,0:T(8,128)(2,1)S(1)} %get-tuple-element.57.stream_ref, f32[2,256,384]{2,1,0:T(8,128)S(1)} %get-tuple-element.58.local_ref, ...), custom_call_target="tpu_custom_call" | custom-call | flops 2415919104 | bytes 1207959 | tf_op jit(solution)/shard_map/pallas_call | solution.py:173
  60.9 0.1 collective-permute-start.14
  61.0 3.0 %collective-permute-start.15 = (bf16[2,256,384]{2,1,0:T(8,128)(2,1)S(1)}, bf16[2,256,384]{2,1,0:T(8,128)(2,1)S(1)}, u32[]{:S(2)}, u32[]{:S(2)}) collective-permute-start(bf16[2,256,384]{2,1,0:T(8,128)(2,1)S(1)} %get-tuple-element.64), channel_id=1, source_target_pairs={{1,2},{3,4},{5,6},{7,8},{9,10},{11,12},{13,14},{2,1},{4,3},{6,5},{... | collective-permute-start | bytes 1179656 | tf_op jit(solution)/shard_map/ppermute | solution.py:190
  63.9 1.6 %collective-permute-done.7.inter_ref = bf16[2,256,384]{2,1,0:T(8,128)(2,1)S(1)} collective-permute-done((bf16[2,256,384]{2,1,0:T(8,128)(2,1)S(1)}, bf16[2,256,384]{2,1,0:T(8,128)(2,1)S(1)}, u32[]{:S(2)}, u32[]{:S(2)}) %collective-permute-start.7) | collective-permute-done | bytes 393248 | tf_op jit(solution)/shard_map/ppermute | solution.py:190
  65.6 0.8 %shard_map.77 = bf16[2,256,768]{2,1,0:T(8,128)(2,1)S(1)} custom-call(bf16[2,256,768]{2,1,0:T(8,128)(2,1)S(1)} %get-tuple-element.46.stream_ref, f32[2,256,384]{2,1,0:T(8,128)S(1)} %get-tuple-element.47.local_ref, bf16[2,256,384]{2,1,0:T(8,128)(2,1)S(1)} %collective-permute-done.6.intra_ref, bf16[2,256,384]{2,1,0:T(8,128)(2,1)S(1)} %collective-permute-done.7.inter_ref, ...), custom_call_target="tpu_custom_call" | custom-call | flops 603979776 | bytes 301989 | tf_op jit(solution)/shard_map/pallas_call | solution.py:199
  66.4 7.6 %collective-permute-done.15.inter_ref = bf16[2,256,384]{2,1,0:T(8,128)(2,1)S(1)} collective-permute-done((bf16[2,256,384]{2,1,0:T(8,128)(2,1)S(1)}, bf16[2,256,384]{2,1,0:T(8,128)(2,1)S(1)}, u32[]{:S(2)}, u32[]{:S(2)}) %collective-permute-start.15) | collective-permute-done | bytes 393248 | tf_op jit(solution)/shard_map/ppermute | solution.py:190
  74.0 0.8 %shard_map.82 = bf16[2,256,768]{2,1,0:T(8,128)(2,1)S(1)} custom-call(bf16[2,256,768]{2,1,0:T(8,128)(2,1)S(1)} %get-tuple-element.61.stream_ref, f32[2,256,384]{2,1,0:T(8,128)S(1)} %get-tuple-element.62.local_ref, bf16[2,256,384]{2,1,0:T(8,128)(2,1)S(1)} %collective-permute-done.14.intra_ref, bf16[2,256,384]{2,1,0:T(8,128)(2,1)S(1)} %collective-permute-done.15.inter_ref, ...), custom_call_target="tpu_custom_call" | custom-call | flops 603979776 | bytes 301989 | tf_op jit(solution)/shard_map/pallas_call | solution.py:199
  74.9 1.3 %pad_maximum_fusion = bf16[4,256,768]{2,1,0:T(8,128)(2,1)} fusion(bf16[2,256,768]{2,1,0:T(8,128)(2,1)S(1)} %shard_map.82, bf16[2,256,768]{2,1,0:T(8,128)(2,1)S(1)} %shard_map.77), kind=kLoop, calls=%fused_computation | loop fusion | flops 786432 | bytes 3145728 | tf_op jit(solution)/shard_map/concatenate | solution.py:212
  (23 shorter events, 0.1 us)
Async XLA Ops:
  1.0 1.4 %copy-start.2 = (bf16[4,256,768]{2,1,0:T(8,128)(2,1)S(1)}, bf16[4,256,768]{2,1,0:T(8,128)(2,1)}, u32[]{:S(2)}) copy-start(bf16[4,256,768]{2,1,0:T(8,128)(2,1)} %stream_ref.7) | copy-start | bytes 4718596
  5.8 11.8 %collective-permute-start = (bf16[2,32,384]{2,1,0:T(8,128)(2,1)S(1)}, bf16[2,32,384]{2,1,0:T(8,128)(2,1)S(1)}, u32[]{:S(2)}, u32[]{:S(2)}) collective-permute-start(bf16[2,32,384]{2,1,0:T(8,128)(2,1)S(1)} %get-tuple-element.36), channel_id=1, source_target_pairs={{0,1},{2,3},{4,5},{6,7},{8,9},{10,11},{12,13},{14,15},{1,0},{3,2},... | collective-permute-start | bytes 147464 | tf_op jit(solution)/shard_map/ppermute | solution.py:168
  5.9 11.6 %copy-start.3 = (f32[4,384]{1,0:T(4,128)S(1)}, f32[4,384]{1,0:T(4,128)}, u32[]{:S(2)}) copy-start(f32[4,384]{1,0:T(4,128)} %param.12) | copy-start | bytes 18436
  5.9 11.6 %copy-start.4 = (f32[4,384]{1,0:T(4,128)S(1)}, f32[4,384]{1,0:T(4,128)}, u32[]{:S(2)}) copy-start(f32[4,384]{1,0:T(4,128)} %param.11) | copy-start | bytes 18436
  5.9 11.7 %collective-permute-start.1 = (bf16[2,32,384]{2,1,0:T(8,128)(2,1)S(1)}, bf16[2,32,384]{2,1,0:T(8,128)(2,1)S(1)}, u32[]{:S(2)}, u32[]{:S(2)}) collective-permute-start(bf16[2,32,384]{2,1,0:T(8,128)(2,1)S(1)} %get-tuple-element.37), channel_id=1, source_target_pairs={{1,2},{3,4},{5,6},{7,8},{9,10},{11,12},{13,14},{2,1},{4,3},{6,5},{... | collective-permute-start | bytes 147464 | tf_op jit(solution)/shard_map/ppermute | solution.py:167
  13.9 11.5 %collective-permute-start.8 = (bf16[2,32,384]{2,1,0:T(8,128)(2,1)S(1)}, bf16[2,32,384]{2,1,0:T(8,128)(2,1)S(1)}, u32[]{:S(2)}, u32[]{:S(2)}) collective-permute-start(bf16[2,32,384]{2,1,0:T(8,128)(2,1)S(1)} %get-tuple-element.51), channel_id=1, source_target_pairs={{0,1},{2,3},{4,5},{6,7},{8,9},{10,11},{12,13},{14,15},{1,0},{3,2},... | collective-permute-start | bytes 147464 | tf_op jit(solution)/shard_map/ppermute | solution.py:168
  14.0 11.4 %collective-permute-start.9 = (bf16[2,32,384]{2,1,0:T(8,128)(2,1)S(1)}, bf16[2,32,384]{2,1,0:T(8,128)(2,1)S(1)}, u32[]{:S(2)}, u32[]{:S(2)}) collective-permute-start(bf16[2,32,384]{2,1,0:T(8,128)(2,1)S(1)} %get-tuple-element.52), channel_id=1, source_target_pairs={{1,2},{3,4},{5,6},{7,8},{9,10},{11,12},{13,14},{2,1},{4,3},{6,5},{... | collective-permute-start | bytes 147464 | tf_op jit(solution)/shard_map/ppermute | solution.py:167
  21.8 11.6 %collective-permute-start.2 = (bf16[2,64,384]{2,1,0:T(8,128)(2,1)S(1)}, bf16[2,64,384]{2,1,0:T(8,128)(2,1)S(1)}, u32[]{:S(2)}, u32[]{:S(2)}) collective-permute-start(bf16[2,64,384]{2,1,0:T(8,128)(2,1)S(1)} %get-tuple-element.40), channel_id=1, source_target_pairs={{0,1},{2,3},{4,5},{6,7},{8,9},{10,11},{12,13},{14,15},{1,0},{3,2},... | collective-permute-start | bytes 294920 | tf_op jit(solution)/shard_map/ppermute | solution.py:191
  21.9 11.5 %collective-permute-start.3 = (bf16[2,64,384]{2,1,0:T(8,128)(2,1)S(1)}, bf16[2,64,384]{2,1,0:T(8,128)(2,1)S(1)}, u32[]{:S(2)}, u32[]{:S(2)}) collective-permute-start(bf16[2,64,384]{2,1,0:T(8,128)(2,1)S(1)} %get-tuple-element.41), channel_id=1, source_target_pairs={{1,2},{3,4},{5,6},{7,8},{9,10},{11,12},{13,14},{2,1},{4,3},{6,5},{... | collective-permute-start | bytes 294920 | tf_op jit(solution)/shard_map/ppermute | solution.py:190
  25.5 8.0 %copy-start = (bf16[4,384,768]{2,1,0:T(8,128)(2,1)S(1)}, bf16[4,384,768]{2,1,0:T(8,128)(2,1)}, u32[]{:S(2)}) copy-start(bf16[4,384,768]{2,1,0:T(8,128)(2,1)} %point_ref.15) | copy-start | bytes 7077892
  29.8 11.4 %collective-permute-start.10 = (bf16[2,64,384]{2,1,0:T(8,128)(2,1)S(1)}, bf16[2,64,384]{2,1,0:T(8,128)(2,1)S(1)}, u32[]{:S(2)}, u32[]{:S(2)}) collective-permute-start(bf16[2,64,384]{2,1,0:T(8,128)(2,1)S(1)} %get-tuple-element.55), channel_id=1, source_target_pairs={{0,1},{2,3},{4,5},{6,7},{8,9},{10,11},{12,13},{14,15},{1,0},{3,2},... | collective-permute-start | bytes 294920 | tf_op jit(solution)/shard_map/ppermute | solution.py:191
  29.9 11.3 %collective-permute-start.11 = (bf16[2,64,384]{2,1,0:T(8,128)(2,1)S(1)}, bf16[2,64,384]{2,1,0:T(8,128)(2,1)S(1)}, u32[]{:S(2)}, u32[]{:S(2)}) collective-permute-start(bf16[2,64,384]{2,1,0:T(8,128)(2,1)S(1)} %get-tuple-element.56), channel_id=1, source_target_pairs={{1,2},{3,4},{5,6},{7,8},{9,10},{11,12},{13,14},{2,1},{4,3},{6,5},{... | collective-permute-start | bytes 294920 | tf_op jit(solution)/shard_map/ppermute | solution.py:190
  37.6 11.4 %collective-permute-start.4 = (bf16[2,128,384]{2,1,0:T(8,128)(2,1)S(1)}, bf16[2,128,384]{2,1,0:T(8,128)(2,1)S(1)}, u32[]{:S(2)}, u32[]{:S(2)}) collective-permute-start(bf16[2,128,384]{2,1,0:T(8,128)(2,1)S(1)} %get-tuple-element.44), channel_id=1, source_target_pairs={{0,1},{2,3},{4,5},{6,7},{8,9},{10,11},{12,13},{14,15},{1,0},{3,2},... | collective-permute-start | bytes 589832 | tf_op jit(solution)/shard_map/ppermute | solution.py:191
  37.7 11.3 %collective-permute-start.5 = (bf16[2,128,384]{2,1,0:T(8,128)(2,1)S(1)}, bf16[2,128,384]{2,1,0:T(8,128)(2,1)S(1)}, u32[]{:S(2)}, u32[]{:S(2)}) collective-permute-start(bf16[2,128,384]{2,1,0:T(8,128)(2,1)S(1)} %get-tuple-element.45), channel_id=1, source_target_pairs={{1,2},{3,4},{5,6},{7,8},{9,10},{11,12},{13,14},{2,1},{4,3},{6,5},{... | collective-permute-start | bytes 589832 | tf_op jit(solution)/shard_map/ppermute | solution.py:190
  45.4 11.3 %collective-permute-start.12 = (bf16[2,128,384]{2,1,0:T(8,128)(2,1)S(1)}, bf16[2,128,384]{2,1,0:T(8,128)(2,1)S(1)}, u32[]{:S(2)}, u32[]{:S(2)}) collective-permute-start(bf16[2,128,384]{2,1,0:T(8,128)(2,1)S(1)} %get-tuple-element.59), channel_id=1, source_target_pairs={{0,1},{2,3},{4,5},{6,7},{8,9},{10,11},{12,13},{14,15},{1,0},{3,2},... | collective-permute-start | bytes 589832 | tf_op jit(solution)/shard_map/ppermute | solution.py:191
  45.5 11.2 %collective-permute-start.13 = (bf16[2,128,384]{2,1,0:T(8,128)(2,1)S(1)}, bf16[2,128,384]{2,1,0:T(8,128)(2,1)S(1)}, u32[]{:S(2)}, u32[]{:S(2)}) collective-permute-start(bf16[2,128,384]{2,1,0:T(8,128)(2,1)S(1)} %get-tuple-element.60), channel_id=1, source_target_pairs={{1,2},{3,4},{5,6},{7,8},{9,10},{11,12},{13,14},{2,1},{4,3},{6,5},{... | collective-permute-start | bytes 589832 | tf_op jit(solution)/shard_map/ppermute | solution.py:190
  53.1 10.9 %collective-permute-start.6 = (bf16[2,256,384]{2,1,0:T(8,128)(2,1)S(1)}, bf16[2,256,384]{2,1,0:T(8,128)(2,1)S(1)}, u32[]{:S(2)}, u32[]{:S(2)}) collective-permute-start(bf16[2,256,384]{2,1,0:T(8,128)(2,1)S(1)} %get-tuple-element.48), channel_id=1, source_target_pairs={{0,1},{2,3},{4,5},{6,7},{8,9},{10,11},{12,13},{14,15},{1,0},{3,2},... | collective-permute-start | bytes 1179656 | tf_op jit(solution)/shard_map/ppermute | solution.py:191
  53.1 12.4 %collective-permute-start.7 = (bf16[2,256,384]{2,1,0:T(8,128)(2,1)S(1)}, bf16[2,256,384]{2,1,0:T(8,128)(2,1)S(1)}, u32[]{:S(2)}, u32[]{:S(2)}) collective-permute-start(bf16[2,256,384]{2,1,0:T(8,128)(2,1)S(1)} %get-tuple-element.49), channel_id=1, source_target_pairs={{1,2},{3,4},{5,6},{7,8},{9,10},{11,12},{13,14},{2,1},{4,3},{6,5},{... | collective-permute-start | bytes 1179656 | tf_op jit(solution)/shard_map/ppermute | solution.py:190
  56.7 8.9 %copy-start.1 = (bf16[4,384,768]{2,1,0:T(8,128)(2,1)S(1)}, bf16[4,384,768]{2,1,0:T(8,128)(2,1)}, u32[]{:S(2)}) copy-start(bf16[4,384,768]{2,1,0:T(8,128)(2,1)} %point_ref.15) | copy-start | bytes 7077892
  60.9 5.5 %collective-permute-start.14 = (bf16[2,256,384]{2,1,0:T(8,128)(2,1)S(1)}, bf16[2,256,384]{2,1,0:T(8,128)(2,1)S(1)}, u32[]{:S(2)}, u32[]{:S(2)}) collective-permute-start(bf16[2,256,384]{2,1,0:T(8,128)(2,1)S(1)} %get-tuple-element.63), channel_id=1, source_target_pairs={{0,1},{2,3},{4,5},{6,7},{8,9},{10,11},{12,13},{14,15},{1,0},{3,2},... | collective-permute-start | bytes 1179656 | tf_op jit(solution)/shard_map/ppermute | solution.py:191
  61.0 13.0 %collective-permute-start.15 = (bf16[2,256,384]{2,1,0:T(8,128)(2,1)S(1)}, bf16[2,256,384]{2,1,0:T(8,128)(2,1)S(1)}, u32[]{:S(2)}, u32[]{:S(2)}) collective-permute-start(bf16[2,256,384]{2,1,0:T(8,128)(2,1)S(1)} %get-tuple-element.64), channel_id=1, source_target_pairs={{1,2},{3,4},{5,6},{7,8},{9,10},{11,12},{13,14},{2,1},{4,3},{6,5},{... | collective-permute-start | bytes 1179656 | tf_op jit(solution)/shard_map/ppermute | solution.py:190

commit v2 on v1

--- a/solution.py
+++ b/solution.py
@@ -46,11 +46,11 @@
         local_ref[t] = here + low + high
 
 
-def with_halo(local_ref, intra_ref, inter_ref, even, t, span):
+def with_halo(local_ref, intra_ref, inter_ref, even, edge, t, span):
     local = local_ref[t]
     rows = local.shape[0]
     intra = intra_ref[t].astype(jnp.float32)
-    inter = inter_ref[t].astype(jnp.float32)
+    inter = jnp.where(edge, 0.0, inter_ref[t].astype(jnp.float32))
     head = jnp.where(even, inter, intra)
     tail = jnp.where(even, intra, inter)
     if span == rows:
@@ -60,7 +60,7 @@
 
 
 def first_kernel(span, stream_ref, scale_ref, shift_ref, weight_ref, local_ref, intra_ref, inter_ref):
-    even = lax.rem(lax.axis_index("seq"), 2) == 0
+    even, edge = place()
     for t in range(stream_ref.shape[0]):
         begin(
             stream_ref[t], scale_ref[...], shift_ref[...], weight_ref, span, even, t,
@@ -74,9 +74,9 @@
     scale_ref, shift_ref, weight_ref,
     out_ref, next_local_ref, next_intra_ref, next_inter_ref,
 ):
-    even = lax.rem(lax.axis_index("seq"), 2) == 0
+    even, edge = place()
     for t in range(stream_ref.shape[0]):
-        conv = with_halo(local_ref, intra_ref, inter_ref, even, t, span)
+        conv = with_halo(local_ref, intra_ref, inter_ref, even, edge, t, span)
         stream = finish(stream_ref[t], conv, mid_scale_ref[...], mid_shift_ref[...], point_ref[0])
         out_ref[t] = stream
         begin(
@@ -88,9 +88,9 @@
 def last_kernel(
     span, stream_ref, local_ref, intra_ref, inter_ref, mid_scale_ref, mid_shift_ref, point_ref, out_ref
 ):
-    even = lax.rem(lax.axis_index("seq"), 2) == 0
+    even, edge = place()
     for t in range(stream_ref.shape[0]):
-        conv = with_halo(local_ref, intra_ref, inter_ref, even, t, span)
+        conv = with_halo(local_ref, intra_ref, inter_ref, even, edge, t, span)
         out_ref[t] = finish(stream_ref[t], conv, mid_scale_ref[...], mid_shift_ref[...], point_ref[0])
 
 
@@ -104,6 +104,29 @@
 
 def track(shape, base=0):
     return pl.BlockSpec((1,) + shape, lambda t: (base + t,) + (0,) * len(shape))
+
+
+def swaps(groups, devices):
+    intra, inter = [], []
+    for g in range(groups):
+        base = g * devices
+        intra += [(base + i, base + i + 1) for i in range(0, devices - 1, 2)]
+        inter += [(base + i, base + i + 1) for i in range(1, devices - 1, 2)]
+    for g in range(0, groups - 1, 2):
+        for end in (0, devices - 1):
+            inter.append((g * devices + end, (g + 1) * devices + end))
+    return tuple(pairs + [(b, a) for a, b in pairs] for pairs in (intra, inter))
+
+
+def swap(value, pairs):
+    return lax.ppermute(value, ("groups", "seq"), pairs)
+
+
+def place():
+    index = lax.axis_index("seq")
+    even = lax.rem(index, 2) == 0
+    edge = jnp.logical_or(index == 0, index == lax.axis_size("seq") - 1)
+    return even, edge
 
 
 def local(
@@ -112,10 +135,7 @@
     tracks, rows, channels = tower_in.shape
     blocks, _, _, filters = conv_weight.shape
     devices = lax.axis_size("seq")
-    intra_pairs = [(i, i + 1) for i in range(0, devices - 1, 2)]
-    inter_pairs = [(i, i + 1) for i in range(1, devices - 1, 2)]
-    intra_pairs += [(b, a) for a, b in intra_pairs]
-    inter_pairs += [(b, a) for a, b in inter_pairs]
+    intra_pairs, inter_pairs = swaps(lax.axis_size("groups"), devices)
     spans = [FIRST_DILATION * 2**b for b in range(blocks)]
     size = tracks // CHUNKS
     scales = [first_norm_scale[b : b + 1] for b in range(blocks)]
@@ -164,8 +184,8 @@
             compiler_params=params,
             cost_estimate=cost(conv_flops),
         )(tower_in, scales[0], shifts[0], conv_weight)
-        inter = lax.ppermute(inter, "seq", inter_pairs)
-        intra = lax.ppermute(intra, "seq", intra_pairs)
+        inter = swap(inter, inter_pairs)
+        intra = swap(intra, intra_pairs)
         held.append((local_sum, intra, inter))
     for b in range(1, blocks):
         for c in range(CHUNKS):
@@ -187,8 +207,8 @@
                 *held[c], mids[b - 1], mid_shifts[b - 1], point_weight,
                 scales[b], shifts[b], conv_weight,
             )
-            inter = lax.ppermute(inter, "seq", inter_pairs)
-            intra = lax.ppermute(intra, "seq", intra_pairs)
+            inter = swap(inter, inter_pairs)
+            intra = swap(intra, intra_pairs)
             streams[c] = stream
             held[c] = (local_sum, intra, inter)
     out = None

time: 76.7 us -> 63.2 us (0.82)
  the two profiles are of different devices: /device:TPU:1 before, /device:TPU:25 now
where the time goes in v2:
time: 63.2 us; the launch traced here: 62.5 us
  Pallas kernels  33.6 us (53%)
  waiting for transfers between devices  15.2 us (24%)
  starting transfers between devices  9.84 us (16%)
  local copies, waits for them, and re-layouts  2.39 us (4%)
  other arithmetic  1.28 us (2%)
    pallas_call x6, Pallas kernels, local(): pl.pallas_call(functools.partial(middle_kernel, spans[b - 1], spans[b]),...  25 us
    ppermute x16, waiting for transfers between devices, swap(): return lax.ppermute(value, ('groups', 'seq'), pairs)  15.2 us
    ppermute x16, starting transfers between devices, swap(): return lax.ppermute(value, ('groups', 'seq'), pairs)  9.84 us
    pallas_call x2, Pallas kernels, local(): pl.pallas_call(functools.partial(first_kernel, spans[0]), grid=(size,), i...  6.89 us
    pallas_call x2, Pallas kernels, local(): pl.pallas_call(functools.partial(last_kernel, spans[b]), grid=(size,), in...  1.71 us
    unnamed x10, local copies, waits for them, and re-layouts  1.42 us
    concatenate x1, other arithmetic, local(): return jnp.concatenate(outs, axis=0)  1.28 us
  transfers between devices with their start and end apart: 16, of which 4 were waited for; matrix products, arithmetic and copies ran while one was open for 0% of the time, Pallas kernels for 47%

profile of v2, /device:TPU:25, one launch (start us, length us, event | category | flops | bytes accessed | tf_op | source)
XLA Modules:
  0.0 62.5 jit_solution(12571527213738108645)
XLA Ops:
  0.0 1.0 %fusion = (f32[1,768]{1,0:T(1,128)S(1)}, f32[1,768]{1,0:T(1,128)S(1)}, f32[1,768]{1,0:T(1,128)S(1)}, f32[1,768]{1,0:T(1,128)S(1)}, f32[1,768]{1,0:T(1,128)S(1)},...) fusion(f32[4,768]{1,0:T(4,128)} %param.9, f32[4,768]{1,0:T(4,128)} %param.8), kind=kLoop, calls=%fused_computation.1 | loop fusion | bytes 49152 | tf_op jit(solution)/shard_map/slice | solution.py:142
  1.0 1.4 %copy-done.2 = bf16[4,256,768]{2,1,0:T(8,128)(2,1)S(1)} copy-done((bf16[4,256,768]{2,1,0:T(8,128)(2,1)S(1)}, bf16[4,256,768]{2,1,0:T(8,128)(2,1)}, u32[]{:S(2)}) %copy-start.2) | copy-done | bytes 1572888
  2.4 3.4 %shard_map.73 = (f32[2,256,384]{2,1,0:T(8,128)S(1)}, bf16[2,32,384]{2,1,0:T(8,128)(2,1)S(1)}, bf16[2,32,384]{2,1,0:T(8,128)(2,1)S(1)}) custom-call(bf16[4,256,768]{2,1,0:T(8,128)(2,1)S(1)} %copy-done.2, f32[1,768]{1,0:T(1,128)S(1)} %get-tuple-element.82.scale_ref, f32[1,768]{1,0:T(1,128)S(1)} %get-tuple-element.67.shift_ref, bf16[4,3,768,384]{3,2,1,0:T(8,128)(2,1)} %weight_ref.15), custom_call_target="tpu_custom_call" | custom-call | flops 1811939328 | bytes 905969 | tf_op jit(solution)/shard_map/pallas_call | solution.py:176
  5.8 0.7 %collective-permute-start = (bf16[2,32,384]{2,1,0:T(8,128)(2,1)S(1)}, bf16[2,32,384]{2,1,0:T(8,128)(2,1)S(1)}, u32[]{:S(2)}, u32[]{:S(2)}) collective-permute-start(bf16[2,32,384]{2,1,0:T(8,128)(2,1)S(1)} %get-tuple-element.36), channel_id=1, source_target_pairs={{0,1},{2,3},{4,5},{6,7},{8,9},{10,11},{12,13},{14,15},{16,17},{18,... | collective-permute-start | bytes 147464 | tf_op jit(solution)/shard_map/ppermute | solution.py:122
  6.6 1.2 %collective-permute-start.1 = (bf16[2,32,384]{2,1,0:T(8,128)(2,1)S(1)}, bf16[2,32,384]{2,1,0:T(8,128)(2,1)S(1)}, u32[]{:S(2)}, u32[]{:S(2)}) collective-permute-start(bf16[2,32,384]{2,1,0:T(8,128)(2,1)S(1)} %get-tuple-element.37), channel_id=1, source_target_pairs={{1,2},{3,4},{5,6},{7,8},{9,10},{11,12},{13,14},{17,18},{19,20},{21... | collective-permute-start | bytes 147464 | tf_op jit(solution)/shard_map/ppermute | solution.py:122
  7.8 3.4 %shard_map.78 = (f32[2,256,384]{2,1,0:T(8,128)S(1)}, bf16[2,32,384]{2,1,0:T(8,128)(2,1)S(1)}, bf16[2,32,384]{2,1,0:T(8,128)(2,1)S(1)}) custom-call(bf16[4,256,768]{2,1,0:T(8,128)(2,1)S(1)} %copy-done.2, f32[1,768]{1,0:T(1,128)S(1)} %get-tuple-element.82.scale_ref, f32[1,768]{1,0:T(1,128)S(1)} %get-tuple-element.67.shift_ref, bf16[4,3,768,384]{3,2,1,0:T(8,128)(2,1)} %weight_ref.15), custom_call_target="tpu_custom_call" | custom-call | flops 1811939328 | bytes 905969 | tf_op jit(solution)/shard_map/pallas_call | solution.py:176
  11.2 0.4 collective-permute-start.8
  11.6 1.3 %collective-permute-start.9 = (bf16[2,32,384]{2,1,0:T(8,128)(2,1)S(1)}, bf16[2,32,384]{2,1,0:T(8,128)(2,1)S(1)}, u32[]{:S(2)}, u32[]{:S(2)}) collective-permute-start(bf16[2,32,384]{2,1,0:T(8,128)(2,1)S(1)} %get-tuple-element.52), channel_id=1, source_target_pairs={{1,2},{3,4},{5,6},{7,8},{9,10},{11,12},{13,14},{17,18},{19,20},{21... | collective-permute-start | bytes 147464 | tf_op jit(solution)/shard_map/ppermute | solution.py:122
  13.0 4.2 %shard_map.74 = (bf16[2,256,768]{2,1,0:T(8,128)(2,1)S(1)}, f32[2,256,384]{2,1,0:T(8,128)S(1)}, bf16[2,64,384]{2,1,0:T(8,128)(2,1)S(1)}, bf16[2,64,384]{2,1,0:T(8,128)(2,1)S(1)}) custom-call(bf16[4,256,768]{2,1,0:T(8,128)(2,1)S(1)} %copy-done.2, f32[2,256,384]{2,1,0:T(8,128)S(1)} %get-tuple-element.35.local_ref, ...), custom_call_target="tpu_custom_call" | custom-call | flops 2415919104 | bytes 1207959 | tf_op jit(solution)/shard_map/pallas_call | solution.py:193
  17.2 0.1 collective-permute-start.2
  17.3 0.6 collective-permute-start.3
  17.9 4.4 %shard_map.79 = (bf16[2,256,768]{2,1,0:T(8,128)(2,1)S(1)}, f32[2,256,384]{2,1,0:T(8,128)S(1)}, bf16[2,64,384]{2,1,0:T(8,128)(2,1)S(1)}, bf16[2,64,384]{2,1,0:T(8,128)(2,1)S(1)}) custom-call(bf16[4,256,768]{2,1,0:T(8,128)(2,1)S(1)} %copy-done.2, f32[2,256,384]{2,1,0:T(8,128)S(1)} %get-tuple-element.50.local_ref, ...), custom_call_target="tpu_custom_call" | custom-call | flops 2415919104 | bytes 1207959 | tf_op jit(solution)/shard_map/pallas_call | solution.py:193
  22.3 1.1 %collective-permute-start.10 = (bf16[2,64,384]{2,1,0:T(8,128)(2,1)S(1)}, bf16[2,64,384]{2,1,0:T(8,128)(2,1)S(1)}, u32[]{:S(2)}, u32[]{:S(2)}) collective-permute-start(bf16[2,64,384]{2,1,0:T(8,128)(2,1)S(1)} %get-tuple-element.55), channel_id=1, source_target_pairs={{0,1},{2,3},{4,5},{6,7},{8,9},{10,11},{12,13},{14,15},{16,17},{18,... | collective-permute-start | bytes 294920 | tf_op jit(solution)/shard_map/ppermute | solution.py:122
  23.3 0.5 collective-permute-start.11
  23.8 4.1 %shard_map.75 = (bf16[2,256,768]{2,1,0:T(8,128)(2,1)S(1)}, f32[2,256,384]{2,1,0:T(8,128)S(1)}, bf16[2,128,384]{2,1,0:T(8,128)(2,1)S(1)}, bf16[2,128,384]{2,1,0:T(8,128)(2,1)S(1)}) custom-call(bf16[2,256,768]{2,1,0:T(8,128)(2,1)S(1)} %get-tuple-element.38.stream_ref, f32[2,256,384]{2,1,0:T(8,128)S(1)} %get-tuple-element.39.local_ref, ...), custom_call_target="tpu_custom_call" | custom-call | flops 2415919104 | bytes 1207959 | tf_op jit(solution)/shard_map/pallas_call | solution.py:193
  28.0 1.2 %collective-permute-start.4 = (bf16[2,128,384]{2,1,0:T(8,128)(2,1)S(1)}, bf16[2,128,384]{2,1,0:T(8,128)(2,1)S(1)}, u32[]{:S(2)}, u32[]{:S(2)}) collective-permute-start(bf16[2,128,384]{2,1,0:T(8,128)(2,1)S(1)} %get-tuple-element.44), channel_id=1, source_target_pairs={{0,1},{2,3},{4,5},{6,7},{8,9},{10,11},{12,13},{14,15},{16,17},{18,... | collective-permute-start | bytes 589832 | tf_op jit(solution)/shard_map/ppermute | solution.py:122
  29.1 0.2 collective-permute-start.5
  29.3 4.1 %shard_map.80 = (bf16[2,256,768]{2,1,0:T(8,128)(2,1)S(1)}, f32[2,256,384]{2,1,0:T(8,128)S(1)}, bf16[2,128,384]{2,1,0:T(8,128)(2,1)S(1)}, bf16[2,128,384]{2,1,0:T(8,128)(2,1)S(1)}) custom-call(bf16[2,256,768]{2,1,0:T(8,128)(2,1)S(1)} %get-tuple-element.53.stream_ref, f32[2,256,384]{2,1,0:T(8,128)S(1)} %get-tuple-element.54.local_ref, ...), custom_call_target="tpu_custom_call" | custom-call | flops 2415919104 | bytes 1207959 | tf_op jit(solution)/shard_map/pallas_call | solution.py:193
  33.5 1.0 %collective-permute-start.12 = (bf16[2,128,384]{2,1,0:T(8,128)(2,1)S(1)}, bf16[2,128,384]{2,1,0:T(8,128)(2,1)S(1)}, u32[]{:S(2)}, u32[]{:S(2)}) collective-permute-start(bf16[2,128,384]{2,1,0:T(8,128)(2,1)S(1)} %get-tuple-element.59), channel_id=1, source_target_pairs={{0,1},{2,3},{4,5},{6,7},{8,9},{10,11},{12,13},{14,15},{16,17},{18,... | collective-permute-start | bytes 589832 | tf_op jit(solution)/shard_map/ppermute | solution.py:122
  34.5 0.7 %collective-permute-start.13 = (bf16[2,128,384]{2,1,0:T(8,128)(2,1)S(1)}, bf16[2,128,384]{2,1,0:T(8,128)(2,1)S(1)}, u32[]{:S(2)}, u32[]{:S(2)}) collective-permute-start(bf16[2,128,384]{2,1,0:T(8,128)(2,1)S(1)} %get-tuple-element.60), channel_id=1, source_target_pairs={{1,2},{3,4},{5,6},{7,8},{9,10},{11,12},{13,14},{17,18},{19,20},{21... | collective-permute-start | bytes 589832 | tf_op jit(solution)/shard_map/ppermute | solution.py:122
  35.2 1.2 %collective-permute-done.5.inter_ref = bf16[2,128,384]{2,1,0:T(8,128)(2,1)S(1)} collective-permute-done((bf16[2,128,384]{2,1,0:T(8,128)(2,1)S(1)}, bf16[2,128,384]{2,1,0:T(8,128)(2,1)S(1)}, u32[]{:S(2)}, u32[]{:S(2)}) %collective-permute-start.5) | collective-permute-done | bytes 196640 | tf_op jit(solution)/shard_map/ppermute | solution.py:122
  36.3 4.0 %shard_map.76 = (bf16[2,256,768]{2,1,0:T(8,128)(2,1)S(1)}, f32[2,256,384]{2,1,0:T(8,128)S(1)}, bf16[2,256,384]{2,1,0:T(8,128)(2,1)S(1)}, bf16[2,256,384]{2,1,0:T(8,128)(2,1)S(1)}) custom-call(bf16[2,256,768]{2,1,0:T(8,128)(2,1)S(1)} %get-tuple-element.42.stream_ref, f32[2,256,384]{2,1,0:T(8,128)S(1)} %get-tuple-element.43.local_ref, ...), custom_call_target="tpu_custom_call" | custom-call | flops 2415919104 | bytes 1207959 | tf_op jit(solution)/shard_map/pallas_call | solution.py:193
  40.4 0.1 collective-permute-start.6
  40.5 1.2 %collective-permute-done.13.inter_ref = bf16[2,128,384]{2,1,0:T(8,128)(2,1)S(1)} collective-permute-done((bf16[2,128,384]{2,1,0:T(8,128)(2,1)S(1)}, bf16[2,128,384]{2,1,0:T(8,128)(2,1)S(1)}, u32[]{:S(2)}, u32[]{:S(2)}) %collective-permute-start.13) | collective-permute-done | bytes 196640 | tf_op jit(solution)/shard_map/ppermute | solution.py:122
  41.7 4.2 %shard_map.81 = (bf16[2,256,768]{2,1,0:T(8,128)(2,1)S(1)}, f32[2,256,384]{2,1,0:T(8,128)S(1)}, bf16[2,256,384]{2,1,0:T(8,128)(2,1)S(1)}, bf16[2,256,384]{2,1,0:T(8,128)(2,1)S(1)}) custom-call(bf16[2,256,768]{2,1,0:T(8,128)(2,1)S(1)} %get-tuple-element.57.stream_ref, f32[2,256,384]{2,1,0:T(8,128)S(1)} %get-tuple-element.58.local_ref, ...), custom_call_target="tpu_custom_call" | custom-call | flops 2415919104 | bytes 1207959 | tf_op jit(solution)/shard_map/pallas_call | solution.py:193
  45.9 0.4 collective-permute-start.14
  46.3 0.3 collective-permute-start.15
  46.6 9.5 %collective-permute-done.7.inter_ref = bf16[2,256,384]{2,1,0:T(8,128)(2,1)S(1)} collective-permute-done((bf16[2,256,384]{2,1,0:T(8,128)(2,1)S(1)}, bf16[2,256,384]{2,1,0:T(8,128)(2,1)S(1)}, u32[]{:S(2)}, u32[]{:S(2)}) %collective-permute-start.7) | collective-permute-done | bytes 393248 | tf_op jit(solution)/shard_map/ppermute | solution.py:122
  56.1 0.9 %shard_map.77 = bf16[2,256,768]{2,1,0:T(8,128)(2,1)S(1)} custom-call(bf16[2,256,768]{2,1,0:T(8,128)(2,1)S(1)} %get-tuple-element.46.stream_ref, f32[2,256,384]{2,1,0:T(8,128)S(1)} %get-tuple-element.47.local_ref, bf16[2,256,384]{2,1,0:T(8,128)(2,1)S(1)} %collective-permute-done.6.intra_ref, bf16[2,256,384]{2,1,0:T(8,128)(2,1)S(1)} %collective-permute-done.7.inter_ref, ...), custom_call_target="tpu_custom_call" | custom-call | flops 603979776 | bytes 301989 | tf_op jit(solution)/shard_map/pallas_call | solution.py:219
  57.0 3.3 %collective-permute-done.15.inter_ref = bf16[2,256,384]{2,1,0:T(8,128)(2,1)S(1)} collective-permute-done((bf16[2,256,384]{2,1,0:T(8,128)(2,1)S(1)}, bf16[2,256,384]{2,1,0:T(8,128)(2,1)S(1)}, u32[]{:S(2)}, u32[]{:S(2)}) %collective-permute-start.15) | collective-permute-done | bytes 393248 | tf_op jit(solution)/shard_map/ppermute | solution.py:122
  60.4 0.8 %shard_map.82 = bf16[2,256,768]{2,1,0:T(8,128)(2,1)S(1)} custom-call(bf16[2,256,768]{2,1,0:T(8,128)(2,1)S(1)} %get-tuple-element.61.stream_ref, f32[2,256,384]{2,1,0:T(8,128)S(1)} %get-tuple-element.62.local_ref, bf16[2,256,384]{2,1,0:T(8,128)(2,1)S(1)} %collective-permute-done.14.intra_ref, bf16[2,256,384]{2,1,0:T(8,128)(2,1)S(1)} %collective-permute-done.15.inter_ref, ...), custom_call_target="tpu_custom_call" | custom-call | flops 603979776 | bytes 301989 | tf_op jit(solution)/shard_map/pallas_call | solution.py:219
  61.2 1.3 %pad_maximum_fusion = bf16[4,256,768]{2,1,0:T(8,128)(2,1)} fusion(bf16[2,256,768]{2,1,0:T(8,128)(2,1)S(1)} %shard_map.82, bf16[2,256,768]{2,1,0:T(8,128)(2,1)S(1)} %shard_map.77), kind=kLoop, calls=%fused_computation | loop fusion | flops 786432 | bytes 3145728 | tf_op jit(solution)/shard_map/concatenate | solution.py:232
  (23 shorter events, 0.1 us)
Async XLA Ops:
  1.0 1.4 %copy-start.2 = (bf16[4,256,768]{2,1,0:T(8,128)(2,1)S(1)}, bf16[4,256,768]{2,1,0:T(8,128)(2,1)}, u32[]{:S(2)}) copy-start(bf16[4,256,768]{2,1,0:T(8,128)(2,1)} %stream_ref.7) | copy-start | bytes 4718596
  5.8 7.1 %collective-permute-start = (bf16[2,32,384]{2,1,0:T(8,128)(2,1)S(1)}, bf16[2,32,384]{2,1,0:T(8,128)(2,1)S(1)}, u32[]{:S(2)}, u32[]{:S(2)}) collective-permute-start(bf16[2,32,384]{2,1,0:T(8,128)(2,1)S(1)} %get-tuple-element.36), channel_id=1, source_target_pairs={{0,1},{2,3},{4,5},{6,7},{8,9},{10,11},{12,13},{14,15},{16,17},{18,... | collective-permute-start | bytes 147464 | tf_op jit(solution)/shard_map/ppermute | solution.py:122
  6.6 6.4 %copy-start.3 = (f32[4,384]{1,0:T(4,128)S(1)}, f32[4,384]{1,0:T(4,128)}, u32[]{:S(2)}) copy-start(f32[4,384]{1,0:T(4,128)} %param.12) | copy-start | bytes 18436
  6.6 6.4 %copy-start.4 = (f32[4,384]{1,0:T(4,128)S(1)}, f32[4,384]{1,0:T(4,128)}, u32[]{:S(2)}) copy-start(f32[4,384]{1,0:T(4,128)} %param.11) | copy-start | bytes 18436
  6.6 6.4 %collective-permute-start.1 = (bf16[2,32,384]{2,1,0:T(8,128)(2,1)S(1)}, bf16[2,32,384]{2,1,0:T(8,128)(2,1)S(1)}, u32[]{:S(2)}, u32[]{:S(2)}) collective-permute-start(bf16[2,32,384]{2,1,0:T(8,128)(2,1)S(1)} %get-tuple-element.37), channel_id=1, source_target_pairs={{1,2},{3,4},{5,6},{7,8},{9,10},{11,12},{13,14},{17,18},{19,20},{21... | collective-permute-start | bytes 147464 | tf_op jit(solution)/shard_map/ppermute | solution.py:122
  11.2 6.6 %collective-permute-start.8 = (bf16[2,32,384]{2,1,0:T(8,128)(2,1)S(1)}, bf16[2,32,384]{2,1,0:T(8,128)(2,1)S(1)}, u32[]{:S(2)}, u32[]{:S(2)}) collective-permute-start(bf16[2,32,384]{2,1,0:T(8,128)(2,1)S(1)} %get-tuple-element.51), channel_id=1, source_target_pairs={{0,1},{2,3},{4,5},{6,7},{8,9},{10,11},{12,13},{14,15},{16,17},{18,... | collective-permute-start | bytes 147464 | tf_op jit(solution)/shard_map/ppermute | solution.py:122
  11.6 6.3 %collective-permute-start.9 = (bf16[2,32,384]{2,1,0:T(8,128)(2,1)S(1)}, bf16[2,32,384]{2,1,0:T(8,128)(2,1)S(1)}, u32[]{:S(2)}, u32[]{:S(2)}) collective-permute-start(bf16[2,32,384]{2,1,0:T(8,128)(2,1)S(1)} %get-tuple-element.52), channel_id=1, source_target_pairs={{1,2},{3,4},{5,6},{7,8},{9,10},{11,12},{13,14},{17,18},{19,20},{21... | collective-permute-start | bytes 147464 | tf_op jit(solution)/shard_map/ppermute | solution.py:122
  17.2 6.6 %collective-permute-start.2 = (bf16[2,64,384]{2,1,0:T(8,128)(2,1)S(1)}, bf16[2,64,384]{2,1,0:T(8,128)(2,1)S(1)}, u32[]{:S(2)}, u32[]{:S(2)}) collective-permute-start(bf16[2,64,384]{2,1,0:T(8,128)(2,1)S(1)} %get-tuple-element.40), channel_id=1, source_target_pairs={{0,1},{2,3},{4,5},{6,7},{8,9},{10,11},{12,13},{14,15},{16,17},{18,... | collective-permute-start | bytes 294920 | tf_op jit(solution)/shard_map/ppermute | solution.py:122
  17.3 6.6 %collective-permute-start.3 = (bf16[2,64,384]{2,1,0:T(8,128)(2,1)S(1)}, bf16[2,64,384]{2,1,0:T(8,128)(2,1)S(1)}, u32[]{:S(2)}, u32[]{:S(2)}) collective-permute-start(bf16[2,64,384]{2,1,0:T(8,128)(2,1)S(1)} %get-tuple-element.41), channel_id=1, source_target_pairs={{1,2},{3,4},{5,6},{7,8},{9,10},{11,12},{13,14},{17,18},{19,20},{21... | collective-permute-start | bytes 294920 | tf_op jit(solution)/shard_map/ppermute | solution.py:122
  17.9 6.0 %copy-start = (bf16[4,384,768]{2,1,0:T(8,128)(2,1)S(1)}, bf16[4,384,768]{2,1,0:T(8,128)(2,1)}, u32[]{:S(2)}) copy-start(bf16[4,384,768]{2,1,0:T(8,128)(2,1)} %point_ref.15) | copy-start | bytes 7077892
  22.3 7.1 %collective-permute-start.10 = (bf16[2,64,384]{2,1,0:T(8,128)(2,1)S(1)}, bf16[2,64,384]{2,1,0:T(8,128)(2,1)S(1)}, u32[]{:S(2)}, u32[]{:S(2)}) collective-permute-start(bf16[2,64,384]{2,1,0:T(8,128)(2,1)S(1)} %get-tuple-element.55), channel_id=1, source_target_pairs={{0,1},{2,3},{4,5},{6,7},{8,9},{10,11},{12,13},{14,15},{16,17},{18,... | collective-permute-start | bytes 294920 | tf_op jit(solution)/shard_map/ppermute | solution.py:122
  23.3 6.0 %collective-permute-start.11 = (bf16[2,64,384]{2,1,0:T(8,128)(2,1)S(1)}, bf16[2,64,384]{2,1,0:T(8,128)(2,1)S(1)}, u32[]{:S(2)}, u32[]{:S(2)}) collective-permute-start(bf16[2,64,384]{2,1,0:T(8,128)(2,1)S(1)} %get-tuple-element.56), channel_id=1, source_target_pairs={{1,2},{3,4},{5,6},{7,8},{9,10},{11,12},{13,14},{17,18},{19,20},{21... | collective-permute-start | bytes 294920 | tf_op jit(solution)/shard_map/ppermute | solution.py:122
  28.0 7.2 %collective-permute-start.4 = (bf16[2,128,384]{2,1,0:T(8,128)(2,1)S(1)}, bf16[2,128,384]{2,1,0:T(8,128)(2,1)S(1)}, u32[]{:S(2)}, u32[]{:S(2)}) collective-permute-start(bf16[2,128,384]{2,1,0:T(8,128)(2,1)S(1)} %get-tuple-element.44), channel_id=1, source_target_pairs={{0,1},{2,3},{4,5},{6,7},{8,9},{10,11},{12,13},{14,15},{16,17},{18,... | collective-permute-start | bytes 589832 | tf_op jit(solution)/shard_map/ppermute | solution.py:122
  29.1 7.2 %collective-permute-start.5 = (bf16[2,128,384]{2,1,0:T(8,128)(2,1)S(1)}, bf16[2,128,384]{2,1,0:T(8,128)(2,1)S(1)}, u32[]{:S(2)}, u32[]{:S(2)}) collective-permute-start(bf16[2,128,384]{2,1,0:T(8,128)(2,1)S(1)} %get-tuple-element.45), channel_id=1, source_target_pairs={{1,2},{3,4},{5,6},{7,8},{9,10},{11,12},{13,14},{17,18},{19,20},{21... | collective-permute-start | bytes 589832 | tf_op jit(solution)/shard_map/ppermute | solution.py:122
  33.5 7.1 %collective-permute-start.12 = (bf16[2,128,384]{2,1,0:T(8,128)(2,1)S(1)}, bf16[2,128,384]{2,1,0:T(8,128)(2,1)S(1)}, u32[]{:S(2)}, u32[]{:S(2)}) collective-permute-start(bf16[2,128,384]{2,1,0:T(8,128)(2,1)S(1)} %get-tuple-element.59), channel_id=1, source_target_pairs={{0,1},{2,3},{4,5},{6,7},{8,9},{10,11},{12,13},{14,15},{16,17},{18,... | collective-permute-start | bytes 589832 | tf_op jit(solution)/shard_map/ppermute | solution.py:122
  34.5 7.2 %collective-permute-start.13 = (bf16[2,128,384]{2,1,0:T(8,128)(2,1)S(1)}, bf16[2,128,384]{2,1,0:T(8,128)(2,1)S(1)}, u32[]{:S(2)}, u32[]{:S(2)}) collective-permute-start(bf16[2,128,384]{2,1,0:T(8,128)(2,1)S(1)} %get-tuple-element.60), channel_id=1, source_target_pairs={{1,2},{3,4},{5,6},{7,8},{9,10},{11,12},{13,14},{17,18},{19,20},{21... | collective-permute-start | bytes 589832 | tf_op jit(solution)/shard_map/ppermute | solution.py:122
  40.4 6.2 %collective-permute-start.6 = (bf16[2,256,384]{2,1,0:T(8,128)(2,1)S(1)}, bf16[2,256,384]{2,1,0:T(8,128)(2,1)S(1)}, u32[]{:S(2)}, u32[]{:S(2)}) collective-permute-start(bf16[2,256,384]{2,1,0:T(8,128)(2,1)S(1)} %get-tuple-element.48), channel_id=1, source_target_pairs={{0,1},{2,3},{4,5},{6,7},{8,9},{10,11},{12,13},{14,15},{16,17},{18,... | collective-permute-start | bytes 1179656 | tf_op jit(solution)/shard_map/ppermute | solution.py:122
  40.4 15.7 %collective-permute-start.7 = (bf16[2,256,384]{2,1,0:T(8,128)(2,1)S(1)}, bf16[2,256,384]{2,1,0:T(8,128)(2,1)S(1)}, u32[]{:S(2)}, u32[]{:S(2)}) collective-permute-start(bf16[2,256,384]{2,1,0:T(8,128)(2,1)S(1)} %get-tuple-element.49), channel_id=1, source_target_pairs={{1,2},{3,4},{5,6},{7,8},{9,10},{11,12},{13,14},{17,18},{19,20},{21... | collective-permute-start | bytes 1179656 | tf_op jit(solution)/shard_map/ppermute | solution.py:122
  41.7 14.4 %copy-start.1 = (bf16[4,384,768]{2,1,0:T(8,128)(2,1)S(1)}, bf16[4,384,768]{2,1,0:T(8,128)(2,1)}, u32[]{:S(2)}) copy-start(bf16[4,384,768]{2,1,0:T(8,128)(2,1)} %point_ref.15) | copy-start | bytes 7077892
  45.9 11.1 %collective-permute-start.14 = (bf16[2,256,384]{2,1,0:T(8,128)(2,1)S(1)}, bf16[2,256,384]{2,1,0:T(8,128)(2,1)S(1)}, u32[]{:S(2)}, u32[]{:S(2)}) collective-permute-start(bf16[2,256,384]{2,1,0:T(8,128)(2,1)S(1)} %get-tuple-element.63), channel_id=1, source_target_pairs={{0,1},{2,3},{4,5},{6,7},{8,9},{10,11},{12,13},{14,15},{16,17},{18,... | collective-permute-start | bytes 1179656 | tf_op jit(solution)/shard_map/ppermute | solution.py:122
  46.3 14.0 %collective-permute-start.15 = (bf16[2,256,384]{2,1,0:T(8,128)(2,1)S(1)}, bf16[2,256,384]{2,1,0:T(8,128)(2,1)S(1)}, u32[]{:S(2)}, u32[]{:S(2)}) collective-permute-start(bf16[2,256,384]{2,1,0:T(8,128)(2,1)S(1)} %get-tuple-element.64), channel_id=1, source_target_pairs={{1,2},{3,4},{5,6},{7,8},{9,10},{11,12},{13,14},{17,18},{19,20},{21... | collective-permute-start | bytes 1179656 | tf_op jit(solution)/shard_map/ppermute | solution.py:122

commit v3 on v0

v3 whole, which is shorter than its diff:
```python
import functools

import jax
import jax.numpy as jnp
from jax import lax
from jax.experimental import pallas as pl
from jax.experimental.pallas import tpu as pltpu
from jax.sharding import PartitionSpec as P

FIRST_DILATION = 32
CHUNKS = 2
MIB = 1024 * 1024
TAPS = 3


def place():
    index = lax.axis_index("seq")
    even = lax.rem(index, 2) == 0
    edge = jnp.logical_or(index == 0, index == lax.axis_size("seq") - 1)
    return even, edge


def both_ways(body):
    even, edge = place()
    pl.when(even)(lambda: body(True, edge))
    pl.when(jnp.logical_not(even))(lambda: body(False, edge))


def normed_of(stream, scale, shift):
    return jnp.maximum(stream.astype(jnp.float32) * scale + shift, 0.0).astype(jnp.bfloat16)


def emit(products, span, even, t, rows, local_ref, intra_ref, inter_ref):
    behind, here, ahead = products
    next_ref, last_ref = (intra_ref, inter_ref) if even else (inter_ref, intra_ref)
    next_ref[t] = behind[rows - span :].astype(jnp.bfloat16)
    last_ref[t] = ahead[:span].astype(jnp.bfloat16)
    if span == rows:
        local_ref[t] = here
        return
    inner = rows - span
    if span <= inner:
        local_ref[t, :span] = here[:span] + ahead[span : 2 * span]
        if inner > span:
            local_ref[t, span:inner] = (
                here[span:inner] + behind[: inner - span] + ahead[2 * span :]
            )
        local_ref[t, inner:] = here[inner:] + behind[inner - span : inner]
    else:
        local_ref[t, :inner] = here[:inner] + ahead[span:]
        local_ref[t, inner:span] = here[inner:span]
        local_ref[t, span:] = here[span:] + behind[:inner]


def begin(streams, block, span, even, scale_ref, shift_ref, weight_ref, outs):
    tracks, rows, channels = streams.shape
    filters = weight_ref.shape[-1]
    normed = normed_of(
        streams.reshape(tracks * rows, channels),
        scale_ref[block : block + 1],
        shift_ref[block : block + 1],
    )
    weight = jnp.concatenate([weight_ref[k] for k in range(TAPS)], axis=1)
    product = jnp.dot(normed, weight, preferred_element_type=jnp.float32)
    for t in range(tracks):
        part = product[t * rows : (t + 1) * rows]
        emit(
            [part[:, k * filters : (k + 1) * filters] for k in range(TAPS)],
            span, even, t, rows, *outs,
        )


def conv_of(local_ref, intra_ref, inter_ref, even, edge, t, span):
    local = local_ref[t]
    rows = local.shape[0]
    intra = intra_ref[t].astype(jnp.float32)
    inter = jnp.where(edge, 0.0, inter_ref[t].astype(jnp.float32))
    head, tail = (inter, intra) if even else (intra, inter)
    if span == rows:
        return local + head + tail
    if 2 * span == rows:
        return local + jnp.concatenate([head, tail], axis=0)
    return jnp.concatenate(
        [local[:span] + head, local[span : rows - span], local[rows - span :] + tail], axis=0
    )


def finish(streams, block, span, even, edge, held, scale_ref, shift_ref, point_ref):
    tracks, rows, channels = streams.shape
    conv = jnp.concatenate([conv_of(*held, even, edge, t, span) for t in range(tracks)], axis=0)
    middle = jnp.maximum(
        conv * scale_ref[block : block + 1] + shift_ref[block : block + 1], 0.0
    ).astype(jnp.bfloat16)
    update = jnp.dot(middle, point_ref[block], preferred_element_type=jnp.float32)
    flat = streams.reshape(tracks * rows, channels).astype(jnp.float32)
    return (flat + update).astype(jnp.bfloat16).reshape(tracks, rows, channels)


def taps_of(weight_ref, block, weight, sems):
    copies = [
        pltpu.make_async_copy(weight_ref.at[block, k], weight.at[k], sems.at[k])
        for k in range(TAPS)
    ]
    for copy in copies:
        copy.start()
    return copies


def entry_kernel(
    base, span, tower_ref, scale_ref, shift_ref, weight_ref,
    out_ref, local_ref, intra_ref, inter_ref, scale, shift, weight, sems,
):
    tracks, rows, channels = out_ref.shape
    first = [
        pltpu.make_async_copy(tower_ref.at[base : base + tracks], out_ref, sems.at[TAPS]),
        pltpu.make_async_copy(scale_ref, scale, sems.at[TAPS + 1]),
        pltpu.make_async_copy(shift_ref, shift, sems.at[TAPS + 2]),
    ]
    for copy in first:
        copy.start()
    taps = taps_of(weight_ref, 0, weight, sems)
    for copy in first:
        copy.wait()
    normed = normed_of(out_ref[...].reshape(tracks * rows, channels), scale[0:1], shift[0:1])
    products = []
    for k in range(TAPS):
        taps[k].wait()
        products.append(jnp.dot(normed, weight[k], preferred_element_type=jnp.float32))

    def store(even, edge):
        for t in range(tracks):
            emit(
                [p[t * rows : (t + 1) * rows] for p in products],
                span, even, t, rows, local_ref, intra_ref, inter_ref,
            )

    both_ways(store)


def middle_kernel(
    block, spans,
    stream_ref, local_ref, intra_ref, inter_ref, mid_scale_ref, mid_shift_ref, point_ref,
    scale_ref, shift_ref, weight_ref,
    out_ref, next_local_ref, next_intra_ref, next_inter_ref, weight, sems,
):
    taps = taps_of(weight_ref, block + 1, weight, sems)

    def body(even, edge):
        stream = finish(
            stream_ref[...], block, spans[block], even, edge,
            (local_ref, intra_ref, inter_ref), mid_scale_ref, mid_shift_ref, point_ref,
        )
        out_ref[...] = stream
        for copy in taps:
            copy.wait()
        begin(
            stream, block + 1, spans[block + 1], even, scale_ref, shift_ref, weight,
            (next_local_ref, next_intra_ref, next_inter_ref),
        )

    both_ways(body)


def last_kernel(
    base, block, span,
    stream_ref, local_ref, intra_ref, inter_ref, mid_scale_ref, mid_shift_ref, point_ref, *rest
):
    out_ref, result, sem = rest[-3:]
    tracks = local_ref.shape[0]

    def body(even, edge):
        result[...] = finish(
            stream_ref[...], block, span, even, edge,
            (local_ref, intra_ref, inter_ref), mid_scale_ref, mid_shift_ref, point_ref,
        )

    both_ways(body)
    copy = pltpu.make_async_copy(result, out_ref.at[base : base + tracks], sem)
    copy.start()
    copy.wait()


def swaps(groups, devices):
    intra, inter = [], []
    for g in range(groups):
        base = g * devices
        intra += [(base + i, base + i + 1) for i in range(0, devices - 1, 2)]
        inter += [(base + i, base + i + 1) for i in range(1, devices - 1, 2)]
    for g in range(0, groups - 1, 2):
        for end in (0, devices - 1):
            inter.append((g * devices + end, (g + 1) * devices + end))
    return tuple(pairs + [(b, a) for a, b in pairs] for pairs in (intra, inter))


def swap(value, pairs):
    return lax.ppermute(value, ("groups", "seq"), pairs)


def local(
    tower_in, first_norm_scale, first_norm_shift, conv_weight, mid_scale, second_norm_shift, point_weight
):
    tracks, rows, channels = tower_in.shape
    blocks, _, _, filters = conv_weight.shape
    intra_pairs, inter_pairs = swaps(lax.axis_size("groups"), lax.axis_size("seq"))
    spans = [FIRST_DILATION * 2**b for b in range(blocks)]
    size = tracks // CHUNKS
    vmem = pl.BlockSpec(memory_space=pltpu.VMEM)
    hbm = pl.BlockSpec(memory_space=pltpu.HBM)

    def params(limit=24):
        return pltpu.CompilerParams(vmem_limit_bytes=limit * MIB)

    stream_shape = jax.ShapeDtypeStruct((size, rows, channels), jnp.bfloat16)
    conv_flops = size * rows * channels * filters * 6
    point_flops = size * rows * channels * filters * 2

    def emitted(b):
        halo = jax.ShapeDtypeStruct((size, spans[b], filters), jnp.bfloat16)
        return [jax.ShapeDtypeStruct((size, rows, filters), jnp.float32), halo, halo]

    def cost(flops):
        return pl.CostEstimate(flops=flops, bytes_accessed=flops // 1000, transcendentals=0)

    def exchange(local_sum, intra, inter):
        inter = swap(inter, inter_pairs)
        intra = swap(intra, intra_pairs)
        return local_sum, intra, inter

    far = [
        pltpu.with_memory_space_constraint(x, pltpu.HBM)
        for x in (tower_in, first_norm_scale, first_norm_shift, conv_weight)
    ]
    taps = [
        pltpu.VMEM((TAPS, channels, filters), jnp.bfloat16),
        pltpu.SemaphoreType.DMA((TAPS + 3,)),
    ]
    held, streams = [None] * CHUNKS, [None] * CHUNKS
    for c in range(CHUNKS):
        streams[c], *made = pl.pallas_call(
            functools.partial(entry_kernel, c * size, spans[0]),
            in_specs=[hbm] * 4,
            out_specs=[vmem] * 4,
            out_shape=[stream_shape] + emitted(0),
            scratch_shapes=[pltpu.VMEM(first_norm_scale.shape, jnp.float32)] * 2 + taps,
            compiler_params=params(),
            cost_estimate=cost(conv_flops),
        )(*far)
        held[c] = exchange(*made)
    for b in range(1, blocks):
        for c in range(CHUNKS):
            streams[c], *made = pl.pallas_call(
                functools.partial(middle_kernel, b - 1, spans),
                in_specs=[vmem] * 9 + [hbm],
                out_specs=[vmem] * 4,
                out_shape=[stream_shape] + emitted(b),
                scratch_shapes=taps,
                compiler_params=params(),
                cost_estimate=cost(conv_flops + point_flops),
            )(
                streams[c], *held[c], mid_scale, second_norm_shift, point_weight,
                first_norm_scale, first_norm_shift, conv_weight,
            )
            held[c] = exchange(*made)
    b = blocks - 1
    out = []
    for c in range(CHUNKS):
        out = [
            pl.pallas_call(
                functools.partial(last_kernel, c * size, b, spans[b]),
                in_specs=[vmem] * 7 + [hbm] * len(out),
                out_specs=hbm,
                out_shape=jax.ShapeDtypeStruct(tower_in.shape, jnp.bfloat16),
                scratch_shapes=[
                    pltpu.VMEM((size, rows, channels), jnp.bfloat16),
                    pltpu.SemaphoreType.DMA,
                ],
                input_output_aliases={7: 0} if out else {},
                compiler_params=params(),
                cost_estimate=cost(point_flops),
            )(streams[c], *held[c], mid_scale, second_norm_shift, point_weight, *out)
        ]
    return out[0]


def solution(mesh):
    placed = (P("groups", "seq", None), P(), P(), P(), P(), P(), P())
    return jax.shard_map(
        local, mesh=mesh, in_specs=placed, out_specs=P("groups", "seq", None), check_vma=False
    )
```

time: 146 us -> 56.6 us (0.39)
  matrix products: 45.4 us -> 0 us
  waiting for transfers between devices: 61 us -> 19.4 us
  Pallas kernels: 0 us -> 26.4 us
  other arithmetic: 11 us -> 0.01 us
  starting transfers between devices: 20 us -> 10.2 us
  local copies, waits for them, and re-layouts: 7.04 us -> 0.03 us
    dot_general x12 -> x0, matrix products: 45.4 us -> none  [the longest x8 25.7 us: local(): jnp.dot(window, conv_weight[block_number, kernel_tap_index], preferred_el...]
    ppermute x8 -> x16, waiting for transfers between devices: 61 us -> 19.4 us  [swap(): return lax.ppermute(value, ('groups', 'seq'), pairs)]
    pallas_call x0 -> x10, Pallas kernels: none -> 26.4 us  [the longest x6 16.1 us: local(): pl.pallas_call(functools.partial(middle_kernel, b - 1, spans), in_specs=[...]
    select_n x4 -> x0, other arithmetic: 11 us -> none  [local(): extended = jnp.where(inside, extended, jnp.zeros_like(extended))]
    ppermute x8 -> x16, starting transfers between devices: 20 us -> 10.2 us  [swap(): return lax.ppermute(value, ('groups', 'seq'), pairs)]
    slice x9 -> x0, local copies, waits for them, and re-layouts: 7.04 us -> none  [the longest x4 3.83 us: local(): extended[:, kernel_tap_index * receptive_span:kernel_tap_index * receptiv...]
  transfers between devices with their start and end apart: 8 -> 16, of which waited for: 6 -> 5; matrix products, arithmetic and copies ran while one was open for 1% -> 0% of each run, Pallas kernels for 0% -> 38%
where the time goes in v3:
time: 56.6 us; the launch traced here: 56.4 us
  Pallas kernels  26.4 us (47%)
  waiting for transfers between devices  19.4 us (34%)
  starting transfers between devices  10.2 us (18%)
    ppermute x16, waiting for transfers between devices, swap(): return lax.ppermute(value, ('groups', 'seq'), pairs)  19.4 us
    pallas_call x6, Pallas kernels, local(): pl.pallas_call(functools.partial(middle_kernel, b - 1, spans), in_specs=[...  16.1 us
    ppermute x16, starting transfers between devices, swap(): return lax.ppermute(value, ('groups', 'seq'), pairs)  10.2 us
    pallas_call x2, Pallas kernels, local(): pl.pallas_call(functools.partial(entry_kernel, c * size, spans[0]), in_sp...  7.22 us
    pallas_call x2, Pallas kernels, local(): pl.pallas_call(functools.partial(last_kernel, c * size, b, spans[b]), in_...  3.11 us
  transfers between devices with their start and end apart: 16, of which 5 were waited for; matrix products, arithmetic and copies ran while one was open for 0% of the time, Pallas kernels for 38%

profile of v3, /device:TPU:25, one launch (start us, length us, event | category | flops | bytes accessed | tf_op | source)
XLA Modules:
  0.0 56.4 jit_solution(1247783532041892729)
XLA Ops:
  0.0 3.6 %shard_map.77 = (bf16[2,256,768]{2,1,0:T(8,128)(2,1)S(1)}, f32[2,256,384]{2,1,0:T(8,128)S(1)}, bf16[2,32,384]{2,1,0:T(8,128)(2,1)S(1)}, bf16[2,32,384]{2,1,0:T(8,128)(2,1)S(1)}) custom-call(bf16[4,256,768]{2,1,0:T(8,128)(2,1)} %tower_ref.3, f32[4,768]{1,0:T(4,128)} %scale_ref.15, f32[4,768]{1,0:T(4,128)} %shift_ref.15, bf16[4,3,768,384]{3,2,1,0:T(8,128)(2,1)} %weight_ref.15), custom_call_target="tpu_custom_call" | custom-call | flops 905969664 | bytes 905969 | tf_op jit(solution)/shard_map/pallas_call | solution.py:239
  3.6 0.7 %collective-permute-start.8 = (bf16[2,32,384]{2,1,0:T(8,128)(2,1)S(1)}, bf16[2,32,384]{2,1,0:T(8,128)(2,1)S(1)}, u32[]{:S(2)}, u32[]{:S(2)}) collective-permute-start(bf16[2,32,384]{2,1,0:T(8,128)(2,1)S(1)} %get-tuple-element.55), channel_id=1, source_target_pairs={{0,1},{2,3},{4,5},{6,7},{8,9},{10,11},{12,13},{14,15},{16,17},{18,... | collective-permute-start | bytes 147464 | tf_op jit(solution)/shard_map/ppermute | solution.py:196
  4.3 0.0 copy-start.4
  4.3 1.2 %collective-permute-start.9 = (bf16[2,32,384]{2,1,0:T(8,128)(2,1)S(1)}, bf16[2,32,384]{2,1,0:T(8,128)(2,1)S(1)}, u32[]{:S(2)}, u32[]{:S(2)}) collective-permute-start(bf16[2,32,384]{2,1,0:T(8,128)(2,1)S(1)} %get-tuple-element.56), channel_id=1, source_target_pairs={{1,2},{3,4},{5,6},{7,8},{9,10},{11,12},{13,14},{17,18},{19,20},{21... | collective-permute-start | bytes 147464 | tf_op jit(solution)/shard_map/ppermute | solution.py:196
  5.6 3.7 %shard_map.73 = (bf16[2,256,768]{2,1,0:T(8,128)(2,1)S(1)}, f32[2,256,384]{2,1,0:T(8,128)S(1)}, bf16[2,32,384]{2,1,0:T(8,128)(2,1)S(1)}, bf16[2,32,384]{2,1,0:T(8,128)(2,1)S(1)}) custom-call(bf16[4,256,768]{2,1,0:T(8,128)(2,1)} %tower_ref.3, f32[4,768]{1,0:T(4,128)} %scale_ref.15, f32[4,768]{1,0:T(4,128)} %shift_ref.15, bf16[4,3,768,384]{3,2,1,0:T(8,128)(2,1)} %weight_ref.15), custom_call_target="tpu_custom_call" | custom-call | flops 905969664 | bytes 905969 | tf_op jit(solution)/shard_map/pallas_call | solution.py:239
  9.2 0.3 collective-permute-start
  9.6 1.4 %collective-permute-start.1 = (bf16[2,32,384]{2,1,0:T(8,128)(2,1)S(1)}, bf16[2,32,384]{2,1,0:T(8,128)(2,1)S(1)}, u32[]{:S(2)}, u32[]{:S(2)}) collective-permute-start(bf16[2,32,384]{2,1,0:T(8,128)(2,1)S(1)} %get-tuple-element.40), channel_id=1, source_target_pairs={{1,2},{3,4},{5,6},{7,8},{9,10},{11,12},{13,14},{17,18},{19,20},{21... | collective-permute-start | bytes 147464 | tf_op jit(solution)/shard_map/ppermute | solution.py:196
  11.1 2.6 %shard_map.78 = (bf16[2,256,768]{2,1,0:T(8,128)(2,1)S(1)}, f32[2,256,384]{2,1,0:T(8,128)S(1)}, bf16[2,64,384]{2,1,0:T(8,128)(2,1)S(1)}, bf16[2,64,384]{2,1,0:T(8,128)(2,1)S(1)}) custom-call(bf16[2,256,768]{2,1,0:T(8,128)(2,1)S(1)} %get-tuple-element.53.stream_ref, f32[2,256,384]{2,1,0:T(8,128)S(1)} %get-tuple-element.54.local_ref, ...), custom_call_target="tpu_custom_call" | custom-call | flops 1207959552 | bytes 1207959 | tf_op jit(solution)/shard_map/pallas_call | solution.py:251
  13.7 0.1 collective-permute-start.10
  13.8 0.6 %collective-permute-start.11 = (bf16[2,64,384]{2,1,0:T(8,128)(2,1)S(1)}, bf16[2,64,384]{2,1,0:T(8,128)(2,1)S(1)}, u32[]{:S(2)}, u32[]{:S(2)}) collective-permute-start(bf16[2,64,384]{2,1,0:T(8,128)(2,1)S(1)} %get-tuple-element.60), channel_id=1, source_target_pairs={{1,2},{3,4},{5,6},{7,8},{9,10},{11,12},{13,14},{17,18},{19,20},{21... | collective-permute-start | bytes 294920 | tf_op jit(solution)/shard_map/ppermute | solution.py:196
  14.4 2.6 %shard_map.74 = (bf16[2,256,768]{2,1,0:T(8,128)(2,1)S(1)}, f32[2,256,384]{2,1,0:T(8,128)S(1)}, bf16[2,64,384]{2,1,0:T(8,128)(2,1)S(1)}, bf16[2,64,384]{2,1,0:T(8,128)(2,1)S(1)}) custom-call(bf16[2,256,768]{2,1,0:T(8,128)(2,1)S(1)} %get-tuple-element.37.stream_ref, f32[2,256,384]{2,1,0:T(8,128)S(1)} %get-tuple-element.38.local_ref, ...), custom_call_target="tpu_custom_call" | custom-call | flops 1207959552 | bytes 1207959 | tf_op jit(solution)/shard_map/pallas_call | solution.py:251
  17.0 1.0 %collective-permute-start.2 = (bf16[2,64,384]{2,1,0:T(8,128)(2,1)S(1)}, bf16[2,64,384]{2,1,0:T(8,128)(2,1)S(1)}, u32[]{:S(2)}, u32[]{:S(2)}) collective-permute-start(bf16[2,64,384]{2,1,0:T(8,128)(2,1)S(1)} %get-tuple-element.43), channel_id=1, source_target_pairs={{0,1},{2,3},{4,5},{6,7},{8,9},{10,11},{12,13},{14,15},{16,17},{18,... | collective-permute-start | bytes 294920 | tf_op jit(solution)/shard_map/ppermute | solution.py:196
  18.0 0.5 collective-permute-start.3
  18.5 0.4 collective-permute-done.11.inter_ref
  18.9 2.8 %shard_map.79 = (bf16[2,256,768]{2,1,0:T(8,128)(2,1)S(1)}, f32[2,256,384]{2,1,0:T(8,128)S(1)}, bf16[2,128,384]{2,1,0:T(8,128)(2,1)S(1)}, bf16[2,128,384]{2,1,0:T(8,128)(2,1)S(1)}) custom-call(bf16[2,256,768]{2,1,0:T(8,128)(2,1)S(1)} %get-tuple-element.57.stream_ref, f32[2,256,384]{2,1,0:T(8,128)S(1)} %get-tuple-element.58.local_ref, ...), custom_call_target="tpu_custom_call" | custom-call | flops 1207959552 | bytes 1207959 | tf_op jit(solution)/shard_map/pallas_call | solution.py:251
  21.7 0.8 %collective-permute-start.12 = (bf16[2,128,384]{2,1,0:T(8,128)(2,1)S(1)}, bf16[2,128,384]{2,1,0:T(8,128)(2,1)S(1)}, u32[]{:S(2)}, u32[]{:S(2)}) collective-permute-start(bf16[2,128,384]{2,1,0:T(8,128)(2,1)S(1)} %get-tuple-element.63), channel_id=1, source_target_pairs={{0,1},{2,3},{4,5},{6,7},{8,9},{10,11},{12,13},{14,15},{16,17},{18,... | collective-permute-start | bytes 589832 | tf_op jit(solution)/shard_map/ppermute | solution.py:196
  22.6 0.2 collective-permute-start.13
  22.7 0.4 collective-permute-done.3.inter_ref
  23.1 2.6 %shard_map.75 = (bf16[2,256,768]{2,1,0:T(8,128)(2,1)S(1)}, f32[2,256,384]{2,1,0:T(8,128)S(1)}, bf16[2,128,384]{2,1,0:T(8,128)(2,1)S(1)}, bf16[2,128,384]{2,1,0:T(8,128)(2,1)S(1)}) custom-call(bf16[2,256,768]{2,1,0:T(8,128)(2,1)S(1)} %get-tuple-element.41.stream_ref, f32[2,256,384]{2,1,0:T(8,128)S(1)} %get-tuple-element.42.local_ref, ...), custom_call_target="tpu_custom_call" | custom-call | flops 1207959552 | bytes 1207959 | tf_op jit(solution)/shard_map/pallas_call | solution.py:251
  25.7 0.7 %collective-permute-start.4 = (bf16[2,128,384]{2,1,0:T(8,128)(2,1)S(1)}, bf16[2,128,384]{2,1,0:T(8,128)(2,1)S(1)}, u32[]{:S(2)}, u32[]{:S(2)}) collective-permute-start(bf16[2,128,384]{2,1,0:T(8,128)(2,1)S(1)} %get-tuple-element.47), channel_id=1, source_target_pairs={{0,1},{2,3},{4,5},{6,7},{8,9},{10,11},{12,13},{14,15},{16,17},{18,... | collective-permute-start | bytes 589832 | tf_op jit(solution)/shard_map/ppermute | solution.py:196
  26.4 0.7 %collective-permute-start.5 = (bf16[2,128,384]{2,1,0:T(8,128)(2,1)S(1)}, bf16[2,128,384]{2,1,0:T(8,128)(2,1)S(1)}, u32[]{:S(2)}, u32[]{:S(2)}) collective-permute-start(bf16[2,128,384]{2,1,0:T(8,128)(2,1)S(1)} %get-tuple-element.48), channel_id=1, source_target_pairs={{1,2},{3,4},{5,6},{7,8},{9,10},{11,12},{13,14},{17,18},{19,20},{21... | collective-permute-start | bytes 589832 | tf_op jit(solution)/shard_map/ppermute | solution.py:196
  27.1 5.0 %collective-permute-done.13.inter_ref = bf16[2,128,384]{2,1,0:T(8,128)(2,1)S(1)} collective-permute-done((bf16[2,128,384]{2,1,0:T(8,128)(2,1)S(1)}, bf16[2,128,384]{2,1,0:T(8,128)(2,1)S(1)}, u32[]{:S(2)}, u32[]{:S(2)}) %collective-permute-start.13) | collective-permute-done | bytes 196640 | tf_op jit(solution)/shard_map/ppermute | solution.py:196
  32.1 2.6 %shard_map.80 = (bf16[2,256,768]{2,1,0:T(8,128)(2,1)S(1)}, f32[2,256,384]{2,1,0:T(8,128)S(1)}, bf16[2,256,384]{2,1,0:T(8,128)(2,1)S(1)}, bf16[2,256,384]{2,1,0:T(8,128)(2,1)S(1)}) custom-call(bf16[2,256,768]{2,1,0:T(8,128)(2,1)S(1)} %get-tuple-element.61.stream_ref, f32[2,256,384]{2,1,0:T(8,128)S(1)} %get-tuple-element.62.local_ref, ...), custom_call_target="tpu_custom_call" | custom-call | flops 1207959552 | bytes 1207959 | tf_op jit(solution)/shard_map/pallas_call | solution.py:251
  34.7 0.1 collective-permute-start.14
  34.8 0.1 collective-permute-start.15
  34.9 2.8 %shard_map.76 = (bf16[2,256,768]{2,1,0:T(8,128)(2,1)S(1)}, f32[2,256,384]{2,1,0:T(8,128)S(1)}, bf16[2,256,384]{2,1,0:T(8,128)(2,1)S(1)}, bf16[2,256,384]{2,1,0:T(8,128)(2,1)S(1)}) custom-call(bf16[2,256,768]{2,1,0:T(8,128)(2,1)S(1)} %get-tuple-element.45.stream_ref, f32[2,256,384]{2,1,0:T(8,128)S(1)} %get-tuple-element.46.local_ref, ...), custom_call_target="tpu_custom_call" | custom-call | flops 1207959552 | bytes 1207959 | tf_op jit(solution)/shard_map/pallas_call | solution.py:251
  37.7 0.5 collective-permute-start.6
  38.2 1.4 %collective-permute-start.7 = (bf16[2,256,384]{2,1,0:T(8,128)(2,1)S(1)}, bf16[2,256,384]{2,1,0:T(8,128)(2,1)S(1)}, u32[]{:S(2)}, u32[]{:S(2)}) collective-permute-start(bf16[2,256,384]{2,1,0:T(8,128)(2,1)S(1)} %get-tuple-element.52), channel_id=1, source_target_pairs={{1,2},{3,4},{5,6},{7,8},{9,10},{11,12},{13,14},{17,18},{19,20},{21... | collective-permute-start | bytes 1179656 | tf_op jit(solution)/shard_map/ppermute | solution.py:196
  39.6 10.9 %collective-permute-done.15.inter_ref = bf16[2,256,384]{2,1,0:T(8,128)(2,1)S(1)} collective-permute-done((bf16[2,256,384]{2,1,0:T(8,128)(2,1)S(1)}, bf16[2,256,384]{2,1,0:T(8,128)(2,1)S(1)}, u32[]{:S(2)}, u32[]{:S(2)}) %collective-permute-start.15) | collective-permute-done | bytes 393248 | tf_op jit(solution)/shard_map/ppermute | solution.py:196
  50.5 1.6 %shard_map.81.rest_0_ = bf16[4,256,768]{2,1,0:T(8,128)(2,1)} custom-call(bf16[2,256,768]{2,1,0:T(8,128)(2,1)S(1)} %get-tuple-element.65.stream_ref, f32[2,256,384]{2,1,0:T(8,128)S(1)} %get-tuple-element.66.local_ref, bf16[2,256,384]{2,1,0:T(8,128)(2,1)S(1)} %collective-permute-done.14.intra_ref, bf16[2,256,384]{2,1,0:T(8,128)(2,1)S(1)} %collective-permute-done.15.inter_ref, ...), custom_call_target="tpu_custom_call" | custom-call | flops 301989888 | bytes 301989 | tf_op jit(solution)/shard_map/pallas_call | solution.py:268
  52.1 2.6 %collective-permute-done.7.inter_ref = bf16[2,256,384]{2,1,0:T(8,128)(2,1)S(1)} collective-permute-done((bf16[2,256,384]{2,1,0:T(8,128)(2,1)S(1)}, bf16[2,256,384]{2,1,0:T(8,128)(2,1)S(1)}, u32[]{:S(2)}, u32[]{:S(2)}) %collective-permute-start.7) | collective-permute-done | bytes 393248 | tf_op jit(solution)/shard_map/ppermute | solution.py:196
  54.7 1.6 %shard_map.82 = bf16[4,256,768]{2,1,0:T(8,128)(2,1)} custom-call(bf16[2,256,768]{2,1,0:T(8,128)(2,1)S(1)} %get-tuple-element.49.stream_ref, f32[2,256,384]{2,1,0:T(8,128)S(1)} %get-tuple-element.50.local_ref, bf16[2,256,384]{2,1,0:T(8,128)(2,1)S(1)} %collective-permute-done.6.intra_ref, ...), custom_call_target="tpu_custom_call", output_to_operand_aliasing={{}: (7, {})} | custom-call | flops 301989888 | bytes 301989 | tf_op jit(solution)/shard_map/pallas_call | solution.py:268
  (25 shorter events, 0.1 us)
Async XLA Ops:
  0.0 11.0 %slice-start = ((s8[7077888]{0:T(1024)(128)(4,1)}), s8[4194304]{0:T(1024)(128)(4,1)S(1)}, s32[]{:S(2)}) async-start(s8[7077888]{0:T(1024)(128)(4,1)} %bitcast), calls=%async_computation | async-start | bytes 8388608
  3.6 7.4 %collective-permute-start.8 = (bf16[2,32,384]{2,1,0:T(8,128)(2,1)S(1)}, bf16[2,32,384]{2,1,0:T(8,128)(2,1)S(1)}, u32[]{:S(2)}, u32[]{:S(2)}) collective-permute-start(bf16[2,32,384]{2,1,0:T(8,128)(2,1)S(1)} %get-tuple-element.55), channel_id=1, source_target_pairs={{0,1},{2,3},{4,5},{6,7},{8,9},{10,11},{12,13},{14,15},{16,17},{18,... | collective-permute-start | bytes 147464 | tf_op jit(solution)/shard_map/ppermute | solution.py:196
  4.3 6.7 %slice-start.1 = ((s8[7077888]{0:T(1024)(128)(4,1)}), s8[2883584]{0:T(1024)(128)(4,1)S(1)}, s32[]{:S(2)}) async-start(s8[7077888]{0:T(1024)(128)(4,1)} %bitcast), calls=%async_computation.1 | async-start | bytes 5767168
  4.3 6.7 %copy-start.1 = (f32[4,768]{1,0:T(4,128)S(1)}, f32[4,768]{1,0:T(4,128)}, u32[]{:S(2)}) copy-start(f32[4,768]{1,0:T(4,128)} %scale_ref.15) | copy-start | bytes 36868
  4.3 6.7 %copy-start.2 = (f32[4,768]{1,0:T(4,128)S(1)}, f32[4,768]{1,0:T(4,128)}, u32[]{:S(2)}) copy-start(f32[4,768]{1,0:T(4,128)} %shift_ref.15) | copy-start | bytes 36868
  4.3 6.7 %copy-start.3 = (f32[4,384]{1,0:T(4,128)S(1)}, f32[4,384]{1,0:T(4,128)}, u32[]{:S(2)}) copy-start(f32[4,384]{1,0:T(4,128)} %mid_scale_ref.15) | copy-start | bytes 18436
  4.3 6.7 %copy-start.4 = (f32[4,384]{1,0:T(4,128)S(1)}, f32[4,384]{1,0:T(4,128)}, u32[]{:S(2)}) copy-start(f32[4,384]{1,0:T(4,128)} %mid_shift_ref.15) | copy-start | bytes 18436
  4.3 6.6 %collective-permute-start.9 = (bf16[2,32,384]{2,1,0:T(8,128)(2,1)S(1)}, bf16[2,32,384]{2,1,0:T(8,128)(2,1)S(1)}, u32[]{:S(2)}, u32[]{:S(2)}) collective-permute-start(bf16[2,32,384]{2,1,0:T(8,128)(2,1)S(1)} %get-tuple-element.56), channel_id=1, source_target_pairs={{1,2},{3,4},{5,6},{7,8},{9,10},{11,12},{13,14},{17,18},{19,20},{21... | collective-permute-start | bytes 147464 | tf_op jit(solution)/shard_map/ppermute | solution.py:196
  5.6 5.5 %copy-start = (bf16[4,384,768]{2,1,0:T(8,128)(2,1)S(1)}, bf16[4,384,768]{2,1,0:T(8,128)(2,1)}, u32[]{:S(2)}) copy-start(bf16[4,384,768]{2,1,0:T(8,128)(2,1)} %point_ref.15) | copy-start | bytes 7077892
  9.2 5.1 %collective-permute-start = (bf16[2,32,384]{2,1,0:T(8,128)(2,1)S(1)}, bf16[2,32,384]{2,1,0:T(8,128)(2,1)S(1)}, u32[]{:S(2)}, u32[]{:S(2)}) collective-permute-start(bf16[2,32,384]{2,1,0:T(8,128)(2,1)S(1)} %get-tuple-element.39), channel_id=1, source_target_pairs={{0,1},{2,3},{4,5},{6,7},{8,9},{10,11},{12,13},{14,15},{16,17},{18,... | collective-permute-start | bytes 147464 | tf_op jit(solution)/shard_map/ppermute | solution.py:196
  9.6 4.8 %collective-permute-start.1 = (bf16[2,32,384]{2,1,0:T(8,128)(2,1)S(1)}, bf16[2,32,384]{2,1,0:T(8,128)(2,1)S(1)}, u32[]{:S(2)}, u32[]{:S(2)}) collective-permute-start(bf16[2,32,384]{2,1,0:T(8,128)(2,1)S(1)} %get-tuple-element.40), channel_id=1, source_target_pairs={{1,2},{3,4},{5,6},{7,8},{9,10},{11,12},{13,14},{17,18},{19,20},{21... | collective-permute-start | bytes 147464 | tf_op jit(solution)/shard_map/ppermute | solution.py:196
  13.7 4.8 %collective-permute-start.10 = (bf16[2,64,384]{2,1,0:T(8,128)(2,1)S(1)}, bf16[2,64,384]{2,1,0:T(8,128)(2,1)S(1)}, u32[]{:S(2)}, u32[]{:S(2)}) collective-permute-start(bf16[2,64,384]{2,1,0:T(8,128)(2,1)S(1)} %get-tuple-element.59), channel_id=1, source_target_pairs={{0,1},{2,3},{4,5},{6,7},{8,9},{10,11},{12,13},{14,15},{16,17},{18,... | collective-permute-start | bytes 294920 | tf_op jit(solution)/shard_map/ppermute | solution.py:196
  13.8 5.2 %collective-permute-start.11 = (bf16[2,64,384]{2,1,0:T(8,128)(2,1)S(1)}, bf16[2,64,384]{2,1,0:T(8,128)(2,1)S(1)}, u32[]{:S(2)}, u32[]{:S(2)}) collective-permute-start(bf16[2,64,384]{2,1,0:T(8,128)(2,1)S(1)} %get-tuple-element.60), channel_id=1, source_target_pairs={{1,2},{3,4},{5,6},{7,8},{9,10},{11,12},{13,14},{17,18},{19,20},{21... | collective-permute-start | bytes 294920 | tf_op jit(solution)/shard_map/ppermute | solution.py:196
  17.0 5.7 %collective-permute-start.2 = (bf16[2,64,384]{2,1,0:T(8,128)(2,1)S(1)}, bf16[2,64,384]{2,1,0:T(8,128)(2,1)S(1)}, u32[]{:S(2)}, u32[]{:S(2)}) collective-permute-start(bf16[2,64,384]{2,1,0:T(8,128)(2,1)S(1)} %get-tuple-element.43), channel_id=1, source_target_pairs={{0,1},{2,3},{4,5},{6,7},{8,9},{10,11},{12,13},{14,15},{16,17},{18,... | collective-permute-start | bytes 294920 | tf_op jit(solution)/shard_map/ppermute | solution.py:196
  18.0 5.1 %collective-permute-start.3 = (bf16[2,64,384]{2,1,0:T(8,128)(2,1)S(1)}, bf16[2,64,384]{2,1,0:T(8,128)(2,1)S(1)}, u32[]{:S(2)}, u32[]{:S(2)}) collective-permute-start(bf16[2,64,384]{2,1,0:T(8,128)(2,1)S(1)} %get-tuple-element.44), channel_id=1, source_target_pairs={{1,2},{3,4},{5,6},{7,8},{9,10},{11,12},{13,14},{17,18},{19,20},{21... | collective-permute-start | bytes 294920 | tf_op jit(solution)/shard_map/ppermute | solution.py:196
  21.7 5.4 %collective-permute-start.12 = (bf16[2,128,384]{2,1,0:T(8,128)(2,1)S(1)}, bf16[2,128,384]{2,1,0:T(8,128)(2,1)S(1)}, u32[]{:S(2)}, u32[]{:S(2)}) collective-permute-start(bf16[2,128,384]{2,1,0:T(8,128)(2,1)S(1)} %get-tuple-element.63), channel_id=1, source_target_pairs={{0,1},{2,3},{4,5},{6,7},{8,9},{10,11},{12,13},{14,15},{16,17},{18,... | collective-permute-start | bytes 589832 | tf_op jit(solution)/shard_map/ppermute | solution.py:196
  22.6 9.5 %collective-permute-start.13 = (bf16[2,128,384]{2,1,0:T(8,128)(2,1)S(1)}, bf16[2,128,384]{2,1,0:T(8,128)(2,1)S(1)}, u32[]{:S(2)}, u32[]{:S(2)}) collective-permute-start(bf16[2,128,384]{2,1,0:T(8,128)(2,1)S(1)} %get-tuple-element.64), channel_id=1, source_target_pairs={{1,2},{3,4},{5,6},{7,8},{9,10},{11,12},{13,14},{17,18},{19,20},{21... | collective-permute-start | bytes 589832 | tf_op jit(solution)/shard_map/ppermute | solution.py:196
  25.7 9.1 %collective-permute-start.4 = (bf16[2,128,384]{2,1,0:T(8,128)(2,1)S(1)}, bf16[2,128,384]{2,1,0:T(8,128)(2,1)S(1)}, u32[]{:S(2)}, u32[]{:S(2)}) collective-permute-start(bf16[2,128,384]{2,1,0:T(8,128)(2,1)S(1)} %get-tuple-element.47), channel_id=1, source_target_pairs={{0,1},{2,3},{4,5},{6,7},{8,9},{10,11},{12,13},{14,15},{16,17},{18,... | collective-permute-start | bytes 589832 | tf_op jit(solution)/shard_map/ppermute | solution.py:196
  26.4 8.5 %collective-permute-start.5 = (bf16[2,128,384]{2,1,0:T(8,128)(2,1)S(1)}, bf16[2,128,384]{2,1,0:T(8,128)(2,1)S(1)}, u32[]{:S(2)}, u32[]{:S(2)}) collective-permute-start(bf16[2,128,384]{2,1,0:T(8,128)(2,1)S(1)} %get-tuple-element.48), channel_id=1, source_target_pairs={{1,2},{3,4},{5,6},{7,8},{9,10},{11,12},{13,14},{17,18},{19,20},{21... | collective-permute-start | bytes 589832 | tf_op jit(solution)/shard_map/ppermute | solution.py:196
  34.7 4.9 %collective-permute-start.14 = (bf16[2,256,384]{2,1,0:T(8,128)(2,1)S(1)}, bf16[2,256,384]{2,1,0:T(8,128)(2,1)S(1)}, u32[]{:S(2)}, u32[]{:S(2)}) collective-permute-start(bf16[2,256,384]{2,1,0:T(8,128)(2,1)S(1)} %get-tuple-element.67), channel_id=1, source_target_pairs={{0,1},{2,3},{4,5},{6,7},{8,9},{10,11},{12,13},{14,15},{16,17},{18,... | collective-permute-start | bytes 1179656 | tf_op jit(solution)/shard_map/ppermute | solution.py:196
  34.8 15.7 %collective-permute-start.15 = (bf16[2,256,384]{2,1,0:T(8,128)(2,1)S(1)}, bf16[2,256,384]{2,1,0:T(8,128)(2,1)S(1)}, u32[]{:S(2)}, u32[]{:S(2)}) collective-permute-start(bf16[2,256,384]{2,1,0:T(8,128)(2,1)S(1)} %get-tuple-element.68), channel_id=1, source_target_pairs={{1,2},{3,4},{5,6},{7,8},{9,10},{11,12},{13,14},{17,18},{19,20},{21... | collective-permute-start | bytes 1179656 | tf_op jit(solution)/shard_map/ppermute | solution.py:196
  37.7 14.3 %collective-permute-start.6 = (bf16[2,256,384]{2,1,0:T(8,128)(2,1)S(1)}, bf16[2,256,384]{2,1,0:T(8,128)(2,1)S(1)}, u32[]{:S(2)}, u32[]{:S(2)}) collective-permute-start(bf16[2,256,384]{2,1,0:T(8,128)(2,1)S(1)} %get-tuple-element.51), channel_id=1, source_target_pairs={{0,1},{2,3},{4,5},{6,7},{8,9},{10,11},{12,13},{14,15},{16,17},{18,... | collective-permute-start | bytes 1179656 | tf_op jit(solution)/shard_map/ppermute | solution.py:196
  38.2 16.5 %collective-permute-start.7 = (bf16[2,256,384]{2,1,0:T(8,128)(2,1)S(1)}, bf16[2,256,384]{2,1,0:T(8,128)(2,1)S(1)}, u32[]{:S(2)}, u32[]{:S(2)}) collective-permute-start(bf16[2,256,384]{2,1,0:T(8,128)(2,1)S(1)} %get-tuple-element.52), channel_id=1, source_target_pairs={{1,2},{3,4},{5,6},{7,8},{9,10},{11,12},{13,14},{17,18},{19,20},{21... | collective-permute-start | bytes 1179656 | tf_op jit(solution)/shard_map/ppermute | solution.py:196

commit v4 on v0

v4 whole, which is shorter than its diff:
```python
import functools

import jax
import jax.numpy as jnp
from jax import lax
from jax.experimental import pallas as pl
from jax.experimental.pallas import tpu as pltpu
from jax.sharding import PartitionSpec as P

FIRST_DILATION = 32
MIB = 1024 * 1024
TAPS = 3


def place():
    index = lax.axis_index("seq")
    even = lax.rem(index, 2) == 0
    edge = jnp.logical_or(index == 0, index == lax.axis_size("seq") - 1)
    return even, edge


def both_ways(body):
    even, edge = place()
    pl.when(even)(lambda: body(True, edge))
    pl.when(jnp.logical_not(even))(lambda: body(False, edge))


def span_of(q, within, even):
    if even:
        return slice(q[0] - within[0], q[1] - within[0])
    return slice(within[1] - q[1], within[1] - q[0])


def value_term(value, within, even):
    return within, lambda q: value[span_of(q, within, even)]


def ref_term(ref, t, within, even, drop=None):
    def get(q):
        part = ref[t, span_of(q, within, even)].astype(jnp.float32)
        return part if drop is None else jnp.where(drop, 0.0, part)

    return within, get


def assemble(q, terms, even):
    cuts = sorted({q[0], q[1], *(min(max(c, q[0]), q[1]) for rows, _ in terms for c in rows)})
    pieces = []
    for low, high in zip(cuts[:-1], cuts[1:]):
        total = None
        for rows, get in terms:
            if rows[0] <= low and high <= rows[1]:
                part = get((low, high))
                total = part if total is None else total + part
        pieces.append(total)
    if not even:
        pieces = pieces[::-1]
    return pieces[0] if len(pieces) == 1 else jnp.concatenate(pieces, axis=0)


def moved(value, within, q, by, even):
    return (q[0] + by, q[1] + by), lambda to: value[
        span_of((to[0] - by, to[1] - by), within, even)
    ]


def normed_of(stream, scale, shift):
    return jnp.maximum(stream.astype(jnp.float32) * scale + shift, 0.0).astype(jnp.bfloat16)


def products_of(stream, block, even, scale_ref, shift_ref, weight_ref):
    filters = weight_ref.shape[-1]
    normed = normed_of(stream, scale_ref[block : block + 1], shift_ref[block : block + 1])
    weight = jnp.concatenate([weight_ref[block, k] for k in range(TAPS)], axis=1)
    product = jnp.dot(normed, weight, preferred_element_type=jnp.float32)
    behind, here, ahead = (product[:, k * filters : (k + 1) * filters] for k in range(TAPS))
    return (ahead, here, behind) if even else (behind, here, ahead)


def finished(stream, conv, block, scale_ref, shift_ref, point_ref):
    middle = jnp.maximum(
        conv * scale_ref[block : block + 1] + shift_ref[block : block + 1], 0.0
    ).astype(jnp.bfloat16)
    update = jnp.dot(middle, point_ref[block], preferred_element_type=jnp.float32)
    return (stream.astype(jnp.float32) + update).astype(jnp.bfloat16)


def stacked(parts):
    return jnp.concatenate(parts, axis=0)


def edge_kernel(
    span, tower_ref, scale_ref, shift_ref, weight_ref, intra_ref, inter_ref,
    low, high, scale, shift, weight, sems,
):
    tracks, rows, channels = tower_ref.shape
    sources = [
        (scale_ref, scale),
        (shift_ref, shift),
        (tower_ref.at[:, 0:span], low),
        (weight_ref.at[0, TAPS - 1], weight.at[0]),
        (tower_ref.at[:, rows - span : rows], high),
        (weight_ref.at[0, 0], weight.at[1]),
    ]
    copies = [
        pltpu.make_async_copy(source, target, sems.at[i])
        for i, (source, target) in enumerate(sources)
    ]
    for copy in copies:
        copy.start()
    for copy in copies[:3]:
        copy.wait()

    def product(stream, which):
        normed = normed_of(
            stream[...].reshape(tracks * span, channels), scale[0:1], shift[0:1]
        )
        copies[3 + 2 * which].wait()
        return (
            jnp.dot(normed, weight[which], preferred_element_type=jnp.float32)
            .astype(jnp.bfloat16)
            .reshape(tracks, span, -1)
        )

    to_last = product(low, 0)
    copies[4].wait()
    to_next = product(high, 1)

    def store(even, edge):
        inter_ref[...] = to_last if even else to_next
        intra_ref[...] = to_next if even else to_last

    both_ways(store)


def entry_kernel(span, tower_ref, scale_ref, shift_ref, weight_ref, local_ref):
    tracks, rows, channels = tower_ref.shape
    everything = (0, rows)

    def body(even, edge):
        out, here, inn = products_of(
            tower_ref[...].reshape(tracks * rows, channels),
            0, even, scale_ref, shift_ref, weight_ref,
        )
        for t in range(tracks):
            own = slice(t * rows, (t + 1) * rows)
            local_ref[t] = assemble(
                everything,
                [
                    value_term(here[own], everything, even),
                    moved(out[own], everything, (span, rows), -span, even),
                    moved(inn[own], everything, (0, rows - span), span, even),
                ],
                even,
            )

    both_ways(body)


def step_kernel(plan, *refs):
    block, q, streams, terms, sends, keep = plan
    refs = list(refs)
    take = lambda n: [refs.pop(0) for _ in range(n)]
    stream_refs, term_refs = take(len(streams)), take(len(terms))
    mid_scale_ref, mid_shift_ref, point_ref = take(3)
    scale_ref, shift_ref, weight_ref = take(3)
    refs = refs[-(1 + len(sends) + len(keep)) :]
    out_ref = refs.pop(0)
    send_refs, keep_refs = take(len(sends)), take(len(keep))
    tracks, count = out_ref.shape[0], q[1] - q[0]

    def body(even, edge):
        conv = stacked(
            [
                assemble(
                    q,
                    [
                        ref_term(ref, t, rows, even, edge if crossed else None)
                        for ref, (rows, crossed) in zip(term_refs, terms)
                    ],
                    even,
                )
                for t in range(tracks)
            ]
        )
        stream = stacked(
            [
                assemble_stream(q, stream_refs, streams, t, even)
                for t in range(tracks)
            ]
        )
        stream = finished(stream, conv, block, mid_scale_ref, mid_shift_ref, point_ref)
        out_ref[...] = stream.reshape(out_ref.shape)
        named = dict(
            zip(
                ("out", "here", "inn"),
                products_of(stream, block + 1, even, scale_ref, shift_ref, weight_ref),
            )
        )
        for t in range(tracks):
            own = slice(t * count, (t + 1) * count)
            for ref, (name, rows) in zip(send_refs, sends):
                ref[t] = named[name][own][span_of(rows, q, even)].astype(jnp.bfloat16)
            for ref, (rows, parts) in zip(keep_refs, keep):
                ref[t] = assemble(
                    rows,
                    [moved(named[name][own], q, part, by, even) for name, part, by in parts],
                    even,
                )

    both_ways(body)


def assemble_stream(q, stream_refs, streams, t, even):
    pieces = []
    for ref, within in zip(stream_refs, streams):
        low, high = max(q[0], within[0]), min(q[1], within[1])
        if low < high:
            pieces.append(ref[t, span_of((low, high), within, even)])
    if not even:
        pieces = pieces[::-1]
    return pieces[0] if len(pieces) == 1 else jnp.concatenate(pieces, axis=0)


def last_kernel(block, q, rows, stream_ref, local_ref, intra_ref, inter_ref, *refs):
    mid_scale_ref, mid_shift_ref, point_ref = refs[:3]
    out_ref, result, sems = refs[-3:]
    tracks, count, channels = stream_ref.shape

    def body(even, edge):
        conv = stacked(
            [
                local_ref[t]
                + intra_ref[t].astype(jnp.float32)
                + jnp.where(edge, 0.0, inter_ref[t].astype(jnp.float32))
                for t in range(tracks)
            ]
        )
        stream = stream_ref[...].reshape(tracks * count, channels)
        target = span_of(q, (0, rows), even)
        result[...] = finished(
            stream, conv, block, mid_scale_ref, mid_shift_ref, point_ref
        ).reshape(result.shape)
        copy = pltpu.make_async_copy(result, out_ref.at[:, target], sems.at[0])
        copy.start()
        copy.wait()

    both_ways(body)


def swaps(groups, devices):
    intra, inter = [], []
    for g in range(groups):
        base = g * devices
        intra += [(base + i, base + i + 1) for i in range(0, devices - 1, 2)]
        inter += [(base + i, base + i + 1) for i in range(1, devices - 1, 2)]
    for g in range(0, groups - 1, 2):
        for end in (0, devices - 1):
            inter.append((g * devices + end, (g + 1) * devices + end))
    return tuple(pairs + [(b, a) for a, b in pairs] for pairs in (intra, inter))


def local(
    tower_in, first_norm_scale, first_norm_shift, conv_weight, mid_scale, second_norm_shift, point_weight
):
    tracks, rows, channels = tower_in.shape
    blocks, _, _, filters = conv_weight.shape
    intra_pairs, inter_pairs = swaps(lax.axis_size("groups"), lax.axis_size("seq"))
    spans = [FIRST_DILATION * 2**b for b in range(blocks)]
    vmem = pl.BlockSpec(memory_space=pltpu.VMEM)
    hbm = pl.BlockSpec(memory_space=pltpu.HBM)
    params = pltpu.CompilerParams(vmem_limit_bytes=32 * MIB)
    norms = (first_norm_scale, first_norm_shift)
    mids = (mid_scale, second_norm_shift, point_weight)

    def cross(value):
        return lax.ppermute(value, ("groups", "seq"), inter_pairs)

    def across(value):
        return lax.ppermute(value, ("groups", "seq"), intra_pairs)

    def cost(count, conv=1, point=1):
        flops = 8 * tracks * count * channels * filters * (TAPS * conv + point)
        return pl.CostEstimate(flops=flops, bytes_accessed=flops // 1000, transcendentals=0)

    def halo(count):
        return jax.ShapeDtypeStruct((tracks, count, filters), jnp.bfloat16)

    def sums(count):
        return jax.ShapeDtypeStruct((tracks, count, filters), jnp.float32)

    def step(block, q, streams, terms, sends, keep, after=()):
        plan = (
            block, q, [r for r, _ in streams], [(r, c) for r, c, _ in terms], sends, keep,
        )
        arrays = [a for _, a in streams] + [a for _, _, a in terms]
        count = q[1] - q[0]
        made = pl.pallas_call(
            functools.partial(step_kernel, plan),
            in_specs=[vmem] * (len(arrays) + 6 + len(after)),
            out_specs=[vmem] * (1 + len(sends) + len(keep)),
            out_shape=[jax.ShapeDtypeStruct((tracks, count, channels), jnp.bfloat16)]
            + [halo(r[1] - r[0]) for _, r in sends]
            + [sums(r[1] - r[0]) for r, _ in keep],
            compiler_params=params,
            cost_estimate=cost(count),
        )(*arrays, *mids, *norms, conv_weight, *after)
        return made[0], made[1 : 1 + len(sends)], made[1 + len(sends) :]

    everything = (0, rows)
    one, two, three, four = spans

    far = [
        pltpu.with_memory_space_constraint(x, pltpu.HBM)
        for x in (tower_in, first_norm_scale, first_norm_shift, conv_weight)
    ]
    intra, inter = pl.pallas_call(
        functools.partial(edge_kernel, one),
        in_specs=[hbm] * 4,
        out_specs=[vmem] * 2,
        out_shape=[halo(one)] * 2,
        scratch_shapes=[pltpu.VMEM((tracks, one, channels), jnp.bfloat16)] * 2
        + [pltpu.VMEM(first_norm_scale.shape, jnp.float32)] * 2
        + [pltpu.VMEM((2, channels, filters), jnp.bfloat16), pltpu.SemaphoreType.DMA((6,))],
        compiler_params=params,
        cost_estimate=cost(one, point=0),
    )(*far)
    inter_0, intra_0 = cross(inter), across(intra)
    local_0 = pl.pallas_call(
        functools.partial(entry_kernel, one),
        in_specs=[vmem] * 4,
        out_specs=vmem,
        out_shape=sums(rows),
        compiler_params=params,
        cost_estimate=cost(rows, point=0),
    )(tower_in, *norms, conv_weight)

    stream_1, (inter, intra), (local_1,) = step(
        0, everything,
        [(everything, tower_in)],
        [(everything, False, local_0), ((0, one), True, inter_0), ((rows - one, rows), False, intra_0)],
        [("out", (0, two)), ("inn", (rows - two, rows))],
        [
            (
                everything,
                [
                    ("here", everything, 0),
                    ("out", (two, rows), -two),
                    ("inn", (0, rows - two), two),
                ],
            )
        ],
    )
    inter_1, intra_1 = cross(inter), across(intra)

    near = (two, rows)
    stream_2n, (inter, intra), (local_2n,) = step(
        1, near,
        [(everything, stream_1)],
        [(everything, False, local_1), ((rows - two, rows), False, intra_1)],
        [("out", (two, three)), ("inn", (rows - three, rows))],
        [
            (
                everything,
                [
                    ("here", near, 0),
                    ("out", (three, rows), -three),
                    ("inn", (two, rows - three), three),
                ],
            )
        ],
    )
    inter_2n, intra_2 = cross(inter), across(intra)
    stream_2f, (inter,), (here_2f, inn_2f) = step(
        1, (0, two),
        [(everything, stream_1)],
        [(everything, False, local_1), ((0, two), True, inter_1)],
        [("out", (0, two))],
        [((0, two), [("here", (0, two), 0)]), ((three, three + two), [("inn", (0, two), three)])],
        after=(local_2n,),
    )
    inter_2f = cross(inter)

    near = (three, rows)
    streams = [((0, two), stream_2f), ((two, rows), stream_2n)]
    stream_3n, (inter, intra), (local_3n,) = step(
        2, near,
        streams[1:],
        [
            (everything, False, local_2n),
            ((three, three + two), False, inn_2f),
            ((rows - three, rows), False, intra_2),
        ],
        [("out", near), ("inn", near)],
        [(near, [("here", near, 0)])],
    )
    inter_3n, intra_3n = cross(inter), across(intra)
    stream_3f, (inter, intra), (local_3f,) = step(
        2, (0, three),
        streams,
        [
            (everything, False, local_2n),
            ((0, two), False, here_2f),
            ((0, two), True, inter_2n),
            ((two, three), True, inter_2f),
        ],
        [("out", (0, three)), ("inn", (0, three))],
        [((0, three), [("here", (0, three), 0)])],
        after=(local_3n,),
    )
    inter_3f, intra_3f = cross(inter), across(intra)

    out = []
    for q, arrays in (
        ((0, three), (stream_3f, local_3f, intra_3n, inter_3n)),
        (near, (stream_3n, local_3n, intra_3f, inter_3f)),
    ):
        count = q[1] - q[0]
        out = [
            pl.pallas_call(
                functools.partial(last_kernel, blocks - 1, q, rows),
                in_specs=[vmem] * 7 + [hbm] * len(out),
                out_specs=hbm,
                out_shape=jax.ShapeDtypeStruct(tower_in.shape, jnp.bfloat16),
                scratch_shapes=[
                    pltpu.VMEM((tracks, count, channels), jnp.bfloat16),
                    pltpu.SemaphoreType.DMA((1,)),
                ],
                input_output_aliases={7: 0} if out else {},
                compiler_params=params,
                cost_estimate=cost(count, conv=0),
            )(*arrays, *mids, *out)
        ]
    return out[0]


def solution(mesh):
    placed = (P("groups", "seq", None), P(), P(), P(), P(), P(), P())
    return jax.shard_map(
        local, mesh=mesh, in_specs=placed, out_specs=P("groups", "seq", None), check_vma=False
    )
```

time: 146 us -> 46.2 us (0.32)
  matrix products: 45.4 us -> 0 us
  waiting for transfers between devices: 61 us -> 22.2 us
  Pallas kernels: 0 us -> 17.7 us
  starting transfers between devices: 20 us -> 5.88 us
  other arithmetic: 11 us -> 0 us
  local copies, waits for them, and re-layouts: 7.04 us -> 0.04 us
    dot_general x12 -> x0, matrix products: 45.4 us -> none  [the longest x8 25.7 us: local(): jnp.dot(window, conv_weight[block_number, kernel_tap_index], preferred_el...]
    ppermute x8 -> x11, waiting for transfers between devices: 61 us -> 22.2 us  [the longest x6 21.5 us: cross(): return lax.ppermute(value, ('groups', 'seq'), inter_pairs)]
    pallas_call x0 -> x9, Pallas kernels: none -> 17.7 us  [the longest x5 10.2 us: step(): pl.pallas_call(functools.partial(step_kernel, plan), in_specs=[vmem] * (l...]
    ppermute x8 -> x11, starting transfers between devices: 20 us -> 5.88 us  [the longest x6 4.2 us: cross(): return lax.ppermute(value, ('groups', 'seq'), inter_pairs)]
    select_n x4 -> x0, other arithmetic: 11 us -> none  [local(): extended = jnp.where(inside, extended, jnp.zeros_like(extended))]
    slice x9 -> x0, local copies, waits for them, and re-layouts: 7.04 us -> none  [the longest x4 3.83 us: local(): extended[:, kernel_tap_index * receptive_span:kernel_tap_index * receptiv...]
  transfers between devices with their start and end apart: 8 -> 11, of which waited for: 6 -> 7; matrix products, arithmetic and copies ran while one was open for 1% -> 0% of each run, Pallas kernels for 0% -> 24%
where the time goes in v4:
time: 46.2 us; the launch traced here: 46.1 us
  waiting for transfers between devices  22.2 us (48%)
  Pallas kernels  17.7 us (38%)
  starting transfers between devices  5.88 us (13%)
    ppermute x6, waiting for transfers between devices, cross(): return lax.ppermute(value, ('groups', 'seq'), inter_pairs)  21.5 us
    pallas_call x5, Pallas kernels, step(): pl.pallas_call(functools.partial(step_kernel, plan), in_specs=[vmem] * (l...  10.2 us
    ppermute x6, starting transfers between devices, cross(): return lax.ppermute(value, ('groups', 'seq'), inter_pairs)  4.2 us
    pallas_call x2, Pallas kernels, local(): pl.pallas_call(functools.partial(last_kernel, blocks - 1, q, rows), in_sp...  3.1 us
    pallas_call x1, Pallas kernels, local(): pl.pallas_call(functools.partial(entry_kernel, one), in_specs=[vmem] * 4,...  2.33 us
    pallas_call x1, Pallas kernels, local(): pl.pallas_call(functools.partial(edge_kernel, one), in_specs=[hbm] * 4, o...  2.04 us
    ppermute x5, starting transfers between devices, across(): return lax.ppermute(value, ('groups', 'seq'), intra_pairs)  1.68 us
  transfers between devices with their start and end apart: 11, of which 7 were waited for; matrix products, arithmetic and copies ran while one was open for 0% of the time, Pallas kernels for 24%

profile of v4, /device:TPU:25, one launch (start us, length us, event | category | flops | bytes accessed | tf_op | source)
XLA Modules:
  0.0 46.1 jit_solution(7094507860553363134)
XLA Ops:
  0.0 2.0 %shard_map.74 = (bf16[4,32,384]{2,1,0:T(8,128)(2,1)S(1)}, bf16[4,32,384]{2,1,0:T(8,128)(2,1)S(1)}) custom-call(bf16[4,256,768]{2,1,0:T(8,128)(2,1)} %refs_0_.3, f32[4,768]{1,0:T(4,128)} %refs_9_.5, f32[4,768]{1,0:T(4,128)} %refs_10_.1, bf16[4,3,768,384]{3,2,1,0:T(8,128)(2,1)} %refs_11_.1), custom_call_target="tpu_custom_call" | custom-call | flops 905969664 | bytes 905969 | tf_op jit(solution)/shard_map/pallas_call | solution.py:317
  2.1 1.9 %collective-permute-start = (bf16[4,32,384]{2,1,0:T(8,128)(2,1)S(1)}, bf16[4,32,384]{2,1,0:T(8,128)(2,1)S(1)}, u32[]{:S(2)}, u32[]{:S(2)}) collective-permute-start(bf16[4,32,384]{2,1,0:T(8,128)(2,1)S(1)} %get-tuple-element.27), channel_id=1, source_target_pairs={{1,2},{3,4},{5,6},{7,8},{9,10},{11,12},{13,14},{17,18},{19,20},{21... | collective-permute-start | bytes 294920 | tf_op jit(solution)/shard_map/ppermute | solution.py:277
  3.9 0.0 collective-permute-start.1
  4.0 0.0 copy-done.2
  4.0 2.3 %shard_map.73.refs_1_ = f32[4,256,384]{2,1,0:T(8,128)S(1)} custom-call(bf16[4,256,768]{2,1,0:T(8,128)(2,1)S(1)} %copy-done.2, f32[4,768]{1,0:T(4,128)S(1)} %copy-done.5, f32[4,768]{1,0:T(4,128)S(1)} %copy-done.6, bf16[4,3,768,384]{3,2,1,0:T(8,128)(2,1)S(1)} %copy-done), custom_call_target="tpu_custom_call" | custom-call | flops 7247757312 | bytes 7247757 | tf_op jit(solution)/shard_map/pallas_call | solution.py:329
  6.3 1.1 %collective-permute-done.refs_2_ = bf16[4,32,384]{2,1,0:T(8,128)(2,1)S(1)} collective-permute-done((bf16[4,32,384]{2,1,0:T(8,128)(2,1)S(1)}, bf16[4,32,384]{2,1,0:T(8,128)(2,1)S(1)}, u32[]{:S(2)}, u32[]{:S(2)}) %collective-permute-start) | collective-permute-done | bytes 98336 | tf_op jit(solution)/shard_map/ppermute | solution.py:277
  7.4 0.0 collective-permute-done.1.refs_3_
  7.4 3.2 %shard_map.75 = (bf16[4,256,768]{2,1,0:T(8,128)(2,1)S(1)}, bf16[4,64,384]{2,1,0:T(8,128)(2,1)S(1)}, bf16[4,64,384]{2,1,0:T(8,128)(2,1)S(1)}, f32[4,256,384]{2,1,0:T(8,128)S(1)}) custom-call(bf16[4,256,768]{2,1,0:T(8,128)(2,1)S(1)} %copy-done.2, f32[4,256,384]{2,1,0:T(8,128)S(1)} %shard_map.73.refs_1_, bf16[4,32,384]{2,1,0:T(8,128)(2,1)S(1)} %collective-permute-done.refs_2_, ...), custom_call_target="tpu_custom_call" | custom-call | flops 9663676416 | bytes 9663676 | tf_op jit(solution)/shard_map/pallas_call | solution.py:298
  10.6 0.5 %collective-permute-start.2 = (bf16[4,64,384]{2,1,0:T(8,128)(2,1)S(1)}, bf16[4,64,384]{2,1,0:T(8,128)(2,1)S(1)}, u32[]{:S(2)}, u32[]{:S(2)}) collective-permute-start(bf16[4,64,384]{2,1,0:T(8,128)(2,1)S(1)} %get-tuple-element.31), channel_id=1, source_target_pairs={{0,1},{2,3},{4,5},{6,7},{8,9},{10,11},{12,13},{14,15},{16,17},{18,... | collective-permute-start | bytes 589832 | tf_op jit(solution)/shard_map/ppermute | solution.py:280
  11.1 0.4 collective-permute-start.3
  11.5 0.7 %collective-permute-done.2.refs_2_ = bf16[4,64,384]{2,1,0:T(8,128)(2,1)S(1)} collective-permute-done((bf16[4,64,384]{2,1,0:T(8,128)(2,1)S(1)}, bf16[4,64,384]{2,1,0:T(8,128)(2,1)S(1)}, u32[]{:S(2)}, u32[]{:S(2)}) %collective-permute-start.2) | collective-permute-done | bytes 196640 | tf_op jit(solution)/shard_map/ppermute | solution.py:280
  12.2 2.5 %shard_map.76 = (bf16[4,192,768]{2,1,0:T(8,128)(2,1)S(1)}, bf16[4,64,384]{2,1,0:T(8,128)(2,1)S(1)}, bf16[4,128,384]{2,1,0:T(8,128)(2,1)S(1)}, f32[4,256,384]{2,1,0:T(8,128)S(1)}) custom-call(bf16[4,256,768]{2,1,0:T(8,128)(2,1)S(1)} %get-tuple-element.29.refs_0_, f32[4,256,384]{2,1,0:T(8,128)S(1)} %get-tuple-element.30.refs_1_, ...), custom_call_target="tpu_custom_call" | custom-call | flops 7247757312 | bytes 7247757 | tf_op jit(solution)/shard_map/pallas_call | solution.py:298
  14.7 0.6 %collective-permute-start.4 = (bf16[4,128,384]{2,1,0:T(8,128)(2,1)S(1)}, bf16[4,128,384]{2,1,0:T(8,128)(2,1)S(1)}, u32[]{:S(2)}, u32[]{:S(2)}) collective-permute-start(bf16[4,128,384]{2,1,0:T(8,128)(2,1)S(1)} %get-tuple-element.36), channel_id=1, source_target_pairs={{0,1},{2,3},{4,5},{6,7},{8,9},{10,11},{12,13},{14,15},{16,17},{18,... | collective-permute-start | bytes 1179656 | tf_op jit(solution)/shard_map/ppermute | solution.py:280
  15.3 0.4 collective-permute-start.5
  15.7 2.6 %collective-permute-done.3.refs_2_ = bf16[4,64,384]{2,1,0:T(8,128)(2,1)S(1)} collective-permute-done((bf16[4,64,384]{2,1,0:T(8,128)(2,1)S(1)}, bf16[4,64,384]{2,1,0:T(8,128)(2,1)S(1)}, u32[]{:S(2)}, u32[]{:S(2)}) %collective-permute-start.3) | collective-permute-done | bytes 196640 | tf_op jit(solution)/shard_map/ppermute | solution.py:277
  18.4 0.9 %shard_map.77 = (bf16[4,64,768]{2,1,0:T(8,128)(2,1)S(1)}, bf16[4,64,384]{2,1,0:T(8,128)(2,1)S(1)}, f32[4,64,384]{2,1,0:T(8,128)S(1)}, f32[4,64,384]{2,1,0:T(8,128)S(1)}) custom-call(bf16[4,256,768]{2,1,0:T(8,128)(2,1)S(1)} %get-tuple-element.29.refs_0_, f32[4,256,384]{2,1,0:T(8,128)S(1)} %get-tuple-element.30.refs_1_, ...), custom_call_target="tpu_custom_call" | custom-call | flops 2415919104 | bytes 2415919 | tf_op jit(solution)/shard_map/pallas_call | solution.py:298
  19.3 0.1 collective-permute-start.6
  19.4 0.0 collective-permute-done.4.refs_3_
  19.4 1.8 %shard_map.78 = (bf16[4,128,768]{2,1,0:T(8,128)(2,1)S(1)}, bf16[4,128,384]{2,1,0:T(8,128)(2,1)S(1)}, bf16[4,128,384]{2,1,0:T(8,128)(2,1)S(1)}, f32[4,128,384]{2,1,0:T(8,128)S(1)}) custom-call(bf16[4,192,768]{2,1,0:T(8,128)(2,1)S(1)} %get-tuple-element.32.refs_0_.refs_1_, f32[4,256,384]{2,1,0:T(8,128)S(1)} %get-tuple-element.33.refs_9_.refs_1_.refs_2_, ...), custom_call_target="tpu_custom_call" | custom-call | flops 4831838208 | bytes 4831838 | tf_op jit(solution)/shard_map/pallas_call | solution.py:298
  21.2 0.5 %collective-permute-start.9 = (bf16[4,128,384]{2,1,0:T(8,128)(2,1)S(1)}, bf16[4,128,384]{2,1,0:T(8,128)(2,1)S(1)}, u32[]{:S(2)}, u32[]{:S(2)}) collective-permute-start(bf16[4,128,384]{2,1,0:T(8,128)(2,1)S(1)} %get-tuple-element.47), channel_id=1, source_target_pairs={{0,1},{2,3},{4,5},{6,7},{8,9},{10,11},{12,13},{14,15},{16,17},{18,... | collective-permute-start | bytes 1179656 | tf_op jit(solution)/shard_map/ppermute | solution.py:280
  21.7 1.4 %collective-permute-start.10 = (bf16[4,128,384]{2,1,0:T(8,128)(2,1)S(1)}, bf16[4,128,384]{2,1,0:T(8,128)(2,1)S(1)}, u32[]{:S(2)}, u32[]{:S(2)}) collective-permute-start(bf16[4,128,384]{2,1,0:T(8,128)(2,1)S(1)} %get-tuple-element.48), channel_id=1, source_target_pairs={{1,2},{3,4},{5,6},{7,8},{9,10},{11,12},{13,14},{17,18},{19,20},{21... | collective-permute-start | bytes 1179656 | tf_op jit(solution)/shard_map/ppermute | solution.py:277
  23.0 1.7 %collective-permute-done.5.refs_4_ = bf16[4,64,384]{2,1,0:T(8,128)(2,1)S(1)} collective-permute-done((bf16[4,64,384]{2,1,0:T(8,128)(2,1)S(1)}, bf16[4,64,384]{2,1,0:T(8,128)(2,1)S(1)}, u32[]{:S(2)}, u32[]{:S(2)}) %collective-permute-start.5) | collective-permute-done | bytes 196640 | tf_op jit(solution)/shard_map/ppermute | solution.py:277
  24.7 6.3 %collective-permute-done.6.refs_5_ = bf16[4,64,384]{2,1,0:T(8,128)(2,1)S(1)} collective-permute-done((bf16[4,64,384]{2,1,0:T(8,128)(2,1)S(1)}, bf16[4,64,384]{2,1,0:T(8,128)(2,1)S(1)}, u32[]{:S(2)}, u32[]{:S(2)}) %collective-permute-start.6) | collective-permute-done | bytes 196640 | tf_op jit(solution)/shard_map/ppermute | solution.py:277
  31.0 1.8 %shard_map.79 = (bf16[4,128,768]{2,1,0:T(8,128)(2,1)S(1)}, bf16[4,128,384]{2,1,0:T(8,128)(2,1)S(1)}, bf16[4,128,384]{2,1,0:T(8,128)(2,1)S(1)}, f32[4,128,384]{2,1,0:T(8,128)S(1)}) custom-call(bf16[4,64,768]{2,1,0:T(8,128)(2,1)S(1)} %get-tuple-element.39.refs_0_, bf16[4,192,768]{2,1,0:T(8,128)(2,1)S(1)} %get-tuple-element.32.refs_0_.refs_1_, ...), custom_call_target="tpu_custom_call" | custom-call | flops 4831838208 | bytes 4831838 | tf_op jit(solution)/shard_map/pallas_call | solution.py:298
  32.8 0.1 collective-permute-start.7
  32.9 0.1 collective-permute-start.8
  33.0 0.0 collective-permute-done.9.intra_ref
  33.0 2.2 %collective-permute-done.10.inter_ref = bf16[4,128,384]{2,1,0:T(8,128)(2,1)S(1)} collective-permute-done((bf16[4,128,384]{2,1,0:T(8,128)(2,1)S(1)}, bf16[4,128,384]{2,1,0:T(8,128)(2,1)S(1)}, u32[]{:S(2)}, u32[]{:S(2)}) %collective-permute-start.10) | collective-permute-done | bytes 393248 | tf_op jit(solution)/shard_map/ppermute | solution.py:277
  35.2 1.6 %shard_map.80.refs_3_ = bf16[4,256,768]{2,1,0:T(8,128)(2,1)} custom-call(bf16[4,128,768]{2,1,0:T(8,128)(2,1)S(1)} %get-tuple-element.45.stream_ref, f32[4,128,384]{2,1,0:T(8,128)S(1)} %get-tuple-element.46.local_ref, bf16[4,128,384]{2,1,0:T(8,128)(2,1)S(1)} %collective-permute-done.9.intra_ref, bf16[4,128,384]{2,1,0:T(8,128)(2,1)S(1)} %collective-permute-done.10.inter_ref, ...), custom_call_target="tpu_custom_call" | custom-call | flops 1207959552 | bytes 1207959 | tf_op jit(solution)/shard_map/pallas_call | solution.py:420
  36.8 0.0 collective-permute-done.7.intra_ref
  36.8 7.6 %collective-permute-done.8.inter_ref = bf16[4,128,384]{2,1,0:T(8,128)(2,1)S(1)} collective-permute-done((bf16[4,128,384]{2,1,0:T(8,128)(2,1)S(1)}, bf16[4,128,384]{2,1,0:T(8,128)(2,1)S(1)}, u32[]{:S(2)}, u32[]{:S(2)}) %collective-permute-start.8) | collective-permute-done | bytes 393248 | tf_op jit(solution)/shard_map/ppermute | solution.py:277
  44.3 1.6 %shard_map.81 = bf16[4,256,768]{2,1,0:T(8,128)(2,1)} custom-call(bf16[4,128,768]{2,1,0:T(8,128)(2,1)S(1)} %get-tuple-element.37.stream_ref, f32[4,128,384]{2,1,0:T(8,128)S(1)} %get-tuple-element.38.refs_12_.local_ref, bf16[4,128,384]{2,1,0:T(8,128)(2,1)S(1)} %collective-permute-done.7.intra_ref, ...), custom_call_target="tpu_custom_call", output_to_operand_aliasing={{}: (7, {})} | custom-call | flops 1207959552 | bytes 1207959 | tf_op jit(solution)/shard_map/pallas_call | solution.py:420
  (13 shorter events, 0.0 us)
Async XLA Ops:
  0.0 4.0 %copy-start = (bf16[4,3,768,384]{3,2,1,0:T(8,128)(2,1)S(1)}, bf16[4,3,768,384]{3,2,1,0:T(8,128)(2,1)}, u32[]{:S(2)}) copy-start(bf16[4,3,768,384]{3,2,1,0:T(8,128)(2,1)} %refs_11_.1) | copy-start | bytes 21233668
  0.0 4.0 %copy-start.6 = (f32[4,768]{1,0:T(4,128)S(1)}, f32[4,768]{1,0:T(4,128)}, u32[]{:S(2)}) copy-start(f32[4,768]{1,0:T(4,128)} %refs_10_.1) | copy-start | bytes 36868
  0.0 4.0 %copy-start.5 = (f32[4,768]{1,0:T(4,128)S(1)}, f32[4,768]{1,0:T(4,128)}, u32[]{:S(2)}) copy-start(f32[4,768]{1,0:T(4,128)} %refs_9_.5) | copy-start | bytes 36868
  0.0 4.0 %copy-start.2 = (bf16[4,256,768]{2,1,0:T(8,128)(2,1)S(1)}, bf16[4,256,768]{2,1,0:T(8,128)(2,1)}, u32[]{:S(2)}) copy-start(bf16[4,256,768]{2,1,0:T(8,128)(2,1)} %refs_0_.3) | copy-start | bytes 4718596
  2.1 5.3 %collective-permute-start = (bf16[4,32,384]{2,1,0:T(8,128)(2,1)S(1)}, bf16[4,32,384]{2,1,0:T(8,128)(2,1)S(1)}, u32[]{:S(2)}, u32[]{:S(2)}) collective-permute-start(bf16[4,32,384]{2,1,0:T(8,128)(2,1)S(1)} %get-tuple-element.27), channel_id=1, source_target_pairs={{1,2},{3,4},{5,6},{7,8},{9,10},{11,12},{13,14},{17,18},{19,20},{21... | collective-permute-start | bytes 294920 | tf_op jit(solution)/shard_map/ppermute | solution.py:277
  3.9 3.5 %copy-start.1 = (bf16[4,384,768]{2,1,0:T(8,128)(2,1)S(1)}, bf16[4,384,768]{2,1,0:T(8,128)(2,1)}, u32[]{:S(2)}) copy-start(bf16[4,384,768]{2,1,0:T(8,128)(2,1)} %refs_2_.3) | copy-start | bytes 7077892
  3.9 3.5 %copy-start.3 = (f32[4,384]{1,0:T(4,128)S(1)}, f32[4,384]{1,0:T(4,128)}, u32[]{:S(2)}) copy-start(f32[4,384]{1,0:T(4,128)} %refs_0_.5) | copy-start | bytes 18436
  3.9 3.5 %copy-start.4 = (f32[4,384]{1,0:T(4,128)S(1)}, f32[4,384]{1,0:T(4,128)}, u32[]{:S(2)}) copy-start(f32[4,384]{1,0:T(4,128)} %refs_1_.3) | copy-start | bytes 18436
  3.9 3.5 %collective-permute-start.1 = (bf16[4,32,384]{2,1,0:T(8,128)(2,1)S(1)}, bf16[4,32,384]{2,1,0:T(8,128)(2,1)S(1)}, u32[]{:S(2)}, u32[]{:S(2)}) collective-permute-start(bf16[4,32,384]{2,1,0:T(8,128)(2,1)S(1)} %get-tuple-element.28), channel_id=1, source_target_pairs={{0,1},{2,3},{4,5},{6,7},{8,9},{10,11},{12,13},{14,15},{16,17},{18,... | collective-permute-start | bytes 294920 | tf_op jit(solution)/shard_map/ppermute | solution.py:280
  10.6 1.6 %collective-permute-start.2 = (bf16[4,64,384]{2,1,0:T(8,128)(2,1)S(1)}, bf16[4,64,384]{2,1,0:T(8,128)(2,1)S(1)}, u32[]{:S(2)}, u32[]{:S(2)}) collective-permute-start(bf16[4,64,384]{2,1,0:T(8,128)(2,1)S(1)} %get-tuple-element.31), channel_id=1, source_target_pairs={{0,1},{2,3},{4,5},{6,7},{8,9},{10,11},{12,13},{14,15},{16,17},{18,... | collective-permute-start | bytes 589832 | tf_op jit(solution)/shard_map/ppermute | solution.py:280
  11.1 7.2 %collective-permute-start.3 = (bf16[4,64,384]{2,1,0:T(8,128)(2,1)S(1)}, bf16[4,64,384]{2,1,0:T(8,128)(2,1)S(1)}, u32[]{:S(2)}, u32[]{:S(2)}) collective-permute-start(bf16[4,64,384]{2,1,0:T(8,128)(2,1)S(1)} %get-tuple-element.34), channel_id=1, source_target_pairs={{1,2},{3,4},{5,6},{7,8},{9,10},{11,12},{13,14},{17,18},{19,20},{21... | collective-permute-start | bytes 589832 | tf_op jit(solution)/shard_map/ppermute | solution.py:277
  14.7 4.7 %collective-permute-start.4 = (bf16[4,128,384]{2,1,0:T(8,128)(2,1)S(1)}, bf16[4,128,384]{2,1,0:T(8,128)(2,1)S(1)}, u32[]{:S(2)}, u32[]{:S(2)}) collective-permute-start(bf16[4,128,384]{2,1,0:T(8,128)(2,1)S(1)} %get-tuple-element.36), channel_id=1, source_target_pairs={{0,1},{2,3},{4,5},{6,7},{8,9},{10,11},{12,13},{14,15},{16,17},{18,... | collective-permute-start | bytes 1179656 | tf_op jit(solution)/shard_map/ppermute | solution.py:280
  15.3 9.4 %collective-permute-start.5 = (bf16[4,64,384]{2,1,0:T(8,128)(2,1)S(1)}, bf16[4,64,384]{2,1,0:T(8,128)(2,1)S(1)}, u32[]{:S(2)}, u32[]{:S(2)}) collective-permute-start(bf16[4,64,384]{2,1,0:T(8,128)(2,1)S(1)} %get-tuple-element.41), channel_id=1, source_target_pairs={{1,2},{3,4},{5,6},{7,8},{9,10},{11,12},{13,14},{17,18},{19,20},{21... | collective-permute-start | bytes 589832 | tf_op jit(solution)/shard_map/ppermute | solution.py:277
  19.3 11.7 %collective-permute-start.6 = (bf16[4,64,384]{2,1,0:T(8,128)(2,1)S(1)}, bf16[4,64,384]{2,1,0:T(8,128)(2,1)S(1)}, u32[]{:S(2)}, u32[]{:S(2)}) collective-permute-start(bf16[4,64,384]{2,1,0:T(8,128)(2,1)S(1)} %get-tuple-element.42), channel_id=1, source_target_pairs={{1,2},{3,4},{5,6},{7,8},{9,10},{11,12},{13,14},{17,18},{19,20},{21... | collective-permute-start | bytes 589832 | tf_op jit(solution)/shard_map/ppermute | solution.py:277
  21.2 11.8 %collective-permute-start.9 = (bf16[4,128,384]{2,1,0:T(8,128)(2,1)S(1)}, bf16[4,128,384]{2,1,0:T(8,128)(2,1)S(1)}, u32[]{:S(2)}, u32[]{:S(2)}) collective-permute-start(bf16[4,128,384]{2,1,0:T(8,128)(2,1)S(1)} %get-tuple-element.47), channel_id=1, source_target_pairs={{0,1},{2,3},{4,5},{6,7},{8,9},{10,11},{12,13},{14,15},{16,17},{18,... | collective-permute-start | bytes 1179656 | tf_op jit(solution)/shard_map/ppermute | solution.py:280
  21.7 13.5 %collective-permute-start.10 = (bf16[4,128,384]{2,1,0:T(8,128)(2,1)S(1)}, bf16[4,128,384]{2,1,0:T(8,128)(2,1)S(1)}, u32[]{:S(2)}, u32[]{:S(2)}) collective-permute-start(bf16[4,128,384]{2,1,0:T(8,128)(2,1)S(1)} %get-tuple-element.48), channel_id=1, source_target_pairs={{1,2},{3,4},{5,6},{7,8},{9,10},{11,12},{13,14},{17,18},{19,20},{21... | collective-permute-start | bytes 1179656 | tf_op jit(solution)/shard_map/ppermute | solution.py:277
  32.8 4.0 %collective-permute-start.7 = (bf16[4,128,384]{2,1,0:T(8,128)(2,1)S(1)}, bf16[4,128,384]{2,1,0:T(8,128)(2,1)S(1)}, u32[]{:S(2)}, u32[]{:S(2)}) collective-permute-start(bf16[4,128,384]{2,1,0:T(8,128)(2,1)S(1)} %get-tuple-element.43), channel_id=1, source_target_pairs={{0,1},{2,3},{4,5},{6,7},{8,9},{10,11},{12,13},{14,15},{16,17},{18,... | collective-permute-start | bytes 1179656 | tf_op jit(solution)/shard_map/ppermute | solution.py:280
  32.9 11.5 %collective-permute-start.8 = (bf16[4,128,384]{2,1,0:T(8,128)(2,1)S(1)}, bf16[4,128,384]{2,1,0:T(8,128)(2,1)S(1)}, u32[]{:S(2)}, u32[]{:S(2)}) collective-permute-start(bf16[4,128,384]{2,1,0:T(8,128)(2,1)S(1)} %get-tuple-element.44), channel_id=1, source_target_pairs={{1,2},{3,4},{5,6},{7,8},{9,10},{11,12},{13,14},{17,18},{19,20},{21... | collective-permute-start | bytes 1179656 | tf_op jit(solution)/shard_map/ppermute | solution.py:277

commit v5 on v4

--- a/solution.py
+++ b/solution.py
@@ -158,7 +158,7 @@
 
 
 def step_kernel(plan, *refs):
-    block, q, streams, terms, sends, keep = plan
+    block, q, first, streams, terms, sends, keep = plan
     refs = list(refs)
     take = lambda n: [refs.pop(0) for _ in range(n)]
     stream_refs, term_refs = take(len(streams)), take(len(terms))
@@ -175,7 +175,7 @@
                 assemble(
                     q,
                     [
-                        ref_term(ref, t, rows, even, edge if crossed else None)
+                        ref_term(ref, first + t, rows, even, edge if crossed else None)
                         for ref, (rows, crossed) in zip(term_refs, terms)
                     ],
                     even,
@@ -185,7 +185,7 @@
         )
         stream = stacked(
             [
-                assemble_stream(q, stream_refs, streams, t, even)
+                assemble_stream(q, stream_refs, streams, first + t, even)
                 for t in range(tracks)
             ]
         )
@@ -222,28 +222,32 @@
     return pieces[0] if len(pieces) == 1 else jnp.concatenate(pieces, axis=0)
 
 
-def last_kernel(block, q, rows, stream_ref, local_ref, intra_ref, inter_ref, *refs):
+def last_kernel(
+    block, q, rows, first, bases, stream_ref, local_ref, intra_ref, inter_ref, *refs
+):
     mid_scale_ref, mid_shift_ref, point_ref = refs[:3]
     out_ref, result, sems = refs[-3:]
-    tracks, count, channels = stream_ref.shape
 
     def body(even, edge):
-        conv = stacked(
-            [
-                local_ref[t]
-                + intra_ref[t].astype(jnp.float32)
-                + jnp.where(edge, 0.0, inter_ref[t].astype(jnp.float32))
-                for t in range(tracks)
-            ]
-        )
-        stream = stream_ref[...].reshape(tracks * count, channels)
         target = span_of(q, (0, rows), even)
-        result[...] = finished(
-            stream, conv, block, mid_scale_ref, mid_shift_ref, point_ref
-        ).reshape(result.shape)
-        copy = pltpu.make_async_copy(result, out_ref.at[:, target], sems.at[0])
-        copy.start()
-        copy.wait()
+        copies = []
+        for t in range(result.shape[0]):
+            stream, local, intra, inter = (
+                ref[base + t]
+                for ref, base in zip((stream_ref, local_ref, intra_ref, inter_ref), bases)
+            )
+            conv = (
+                local
+                + intra.astype(jnp.float32)
+                + jnp.where(edge, 0.0, inter.astype(jnp.float32))
+            )
+            result[t] = finished(stream, conv, block, mid_scale_ref, mid_shift_ref, point_ref)
+            copies.append(
+                pltpu.make_async_copy(result.at[t], out_ref.at[first + t, target], sems.at[t])
+            )
+            copies[-1].start()
+        for copy in copies:
+            copy.wait()
 
     both_ways(body)
 
@@ -279,19 +283,20 @@
     def across(value):
         return lax.ppermute(value, ("groups", "seq"), intra_pairs)
 
-    def cost(count, conv=1, point=1):
-        flops = 8 * tracks * count * channels * filters * (TAPS * conv + point)
+    def cost(count, conv=1, point=1, part=tracks):
+        flops = 20 * part * count * channels * filters * (TAPS * conv + point)
         return pl.CostEstimate(flops=flops, bytes_accessed=flops // 1000, transcendentals=0)
 
-    def halo(count):
-        return jax.ShapeDtypeStruct((tracks, count, filters), jnp.bfloat16)
-
-    def sums(count):
-        return jax.ShapeDtypeStruct((tracks, count, filters), jnp.float32)
-
-    def step(block, q, streams, terms, sends, keep, after=()):
+    def halo(count, part=tracks):
+        return jax.ShapeDtypeStruct((part, count, filters), jnp.bfloat16)
+
+    def sums(count, part=tracks):
+        return jax.ShapeDtypeStruct((part, count, filters), jnp.float32)
+
+    def step(block, q, streams, terms, sends, keep, after=(), first=0, part=tracks):
         plan = (
-            block, q, [r for r, _ in streams], [(r, c) for r, c, _ in terms], sends, keep,
+            block, q, first,
+            [r for r, _ in streams], [(r, c) for r, c, _ in terms], sends, keep,
         )
         arrays = [a for _, a in streams] + [a for _, _, a in terms]
         count = q[1] - q[0]
@@ -299,11 +304,11 @@
             functools.partial(step_kernel, plan),
             in_specs=[vmem] * (len(arrays) + 6 + len(after)),
             out_specs=[vmem] * (1 + len(sends) + len(keep)),
-            out_shape=[jax.ShapeDtypeStruct((tracks, count, channels), jnp.bfloat16)]
-            + [halo(r[1] - r[0]) for _, r in sends]
-            + [sums(r[1] - r[0]) for r, _ in keep],
+            out_shape=[jax.ShapeDtypeStruct((part, count, channels), jnp.bfloat16)]
+            + [halo(r[1] - r[0], part) for _, r in sends]
+            + [sums(r[1] - r[0], part) for r, _ in keep],
             compiler_params=params,
-            cost_estimate=cost(count),
+            cost_estimate=cost(count, part=part),
         )(*arrays, *mids, *norms, conv_weight, *after)
         return made[0], made[1 : 1 + len(sends)], made[1 + len(sends) :]
 
@@ -335,100 +340,124 @@
         cost_estimate=cost(rows, point=0),
     )(tower_in, *norms, conv_weight)
 
-    stream_1, (inter, intra), (local_1,) = step(
-        0, everything,
+    rest = (two, rows)
+    stream_1f, (inter,), (here_1f, inn_1f) = step(
+        0, (0, two),
         [(everything, tower_in)],
-        [(everything, False, local_0), ((0, one), True, inter_0), ((rows - one, rows), False, intra_0)],
-        [("out", (0, two)), ("inn", (rows - two, rows))],
+        [(everything, False, local_0), ((0, one), True, inter_0)],
+        [("out", (0, two))],
+        [((0, two), [("here", (0, two), 0)]), ((two, 2 * two), [("inn", (0, two), two)])],
+    )
+    inter_1 = cross(inter)
+    stream_1n, (intra,), (local_1n,) = step(
+        0, rest,
+        [(everything, tower_in)],
+        [(everything, False, local_0), ((rows - one, rows), False, intra_0)],
+        [("inn", (rows - two, rows))],
         [
             (
                 everything,
                 [
-                    ("here", everything, 0),
-                    ("out", (two, rows), -two),
-                    ("inn", (0, rows - two), two),
+                    ("here", rest, 0),
+                    ("out", rest, -two),
+                    ("inn", (two, rows - two), two),
                 ],
             )
         ],
-    )
-    inter_1, intra_1 = cross(inter), across(intra)
-
-    near = (two, rows)
-    stream_2n, (inter, intra), (local_2n,) = step(
+        after=(here_1f,),
+    )
+    intra_1 = across(intra)
+    streams = [((0, two), stream_1f), (rest, stream_1n)]
+
+    middle, near = (two, three), (three, rows)
+    stream_2m, (inter,), (here_2m, inn_2m) = step(
+        1, middle,
+        streams[1:],
+        [(everything, False, local_1n), ((two, 2 * two), False, inn_1f)],
+        [("out", middle)],
+        [(middle, [("here", middle, 0)]), ((two + three, rows), [("inn", middle, three)])],
+    )
+    inter_2m = cross(inter)
+    stream_2n, (intra,), (local_2n,) = step(
         1, near,
-        [(everything, stream_1)],
-        [(everything, False, local_1), ((rows - two, rows), False, intra_1)],
-        [("out", (two, three)), ("inn", (rows - three, rows))],
-        [
-            (
-                everything,
-                [
-                    ("here", near, 0),
-                    ("out", (three, rows), -three),
-                    ("inn", (two, rows - three), three),
-                ],
-            )
-        ],
-    )
-    inter_2n, intra_2 = cross(inter), across(intra)
+        streams[1:],
+        [(everything, False, local_1n), ((rows - two, rows), False, intra_1)],
+        [("inn", near)],
+        [(everything, [("here", near, 0), ("out", near, -three)])],
+        after=(here_2m,),
+    )
+    intra_2 = across(intra)
     stream_2f, (inter,), (here_2f, inn_2f) = step(
         1, (0, two),
-        [(everything, stream_1)],
-        [(everything, False, local_1), ((0, two), True, inter_1)],
+        streams[:1],
+        [
+            (everything, False, local_1n),
+            ((0, two), False, here_1f),
+            ((0, two), True, inter_1),
+        ],
         [("out", (0, two))],
         [((0, two), [("here", (0, two), 0)]), ((three, three + two), [("inn", (0, two), three)])],
         after=(local_2n,),
     )
     inter_2f = cross(inter)
 
-    near = (three, rows)
-    streams = [((0, two), stream_2f), ((two, rows), stream_2n)]
     stream_3n, (inter, intra), (local_3n,) = step(
         2, near,
-        streams[1:],
+        [(near, stream_2n)],
         [
             (everything, False, local_2n),
             ((three, three + two), False, inn_2f),
-            ((rows - three, rows), False, intra_2),
+            ((two + three, rows), False, inn_2m),
+            (near, False, intra_2),
         ],
         [("out", near), ("inn", near)],
         [(near, [("here", near, 0)])],
     )
     inter_3n, intra_3n = cross(inter), across(intra)
-    stream_3f, (inter, intra), (local_3f,) = step(
-        2, (0, three),
-        streams,
-        [
-            (everything, False, local_2n),
-            ((0, two), False, here_2f),
-            ((0, two), True, inter_2n),
-            ((two, three), True, inter_2f),
-        ],
-        [("out", (0, three)), ("inn", (0, three))],
-        [((0, three), [("here", (0, three), 0)])],
-        after=(local_3n,),
-    )
-    inter_3f, intra_3f = cross(inter), across(intra)
-
+    parts = [(0, tracks // 2), (tracks // 2, tracks - tracks // 2)]
+    ends, after = [], (local_3n,)
+    for first, part in parts:
+        stream_3f, (inter, intra), (local_3f,) = step(
+            2, (0, three),
+            [((0, two), stream_2f), (middle, stream_2m)],
+            [
+                (everything, False, local_2n),
+                ((0, two), False, here_2f),
+                (middle, False, here_2m),
+                ((0, two), True, inter_2m),
+                (middle, True, inter_2f),
+            ],
+            [("out", (0, three)), ("inn", (0, three))],
+            [((0, three), [("here", (0, three), 0)])],
+            after=after, first=first, part=part,
+        )
+        after = (local_3f,)
+        ends.append((stream_3f, local_3f, cross(inter), across(intra)))
+
+    far_ends, near_ends = [], []
+    for (first, part), (stream_3f, local_3f, inter, intra) in zip(parts, ends):
+        far_ends.append(
+            ((0, three), first, part, (0, 0, first, first), (stream_3f, local_3f, intra_3n, inter_3n))
+        )
+        near_ends.append(
+            (near, first, part, (first, first, 0, 0), (stream_3n, local_3n, intra, inter))
+        )
     out = []
-    for q, arrays in (
-        ((0, three), (stream_3f, local_3f, intra_3n, inter_3n)),
-        (near, (stream_3n, local_3n, intra_3f, inter_3f)),
-    ):
+    for q, first, part, bases, arrays in far_ends + near_ends:
         count = q[1] - q[0]
         out = [
             pl.pallas_call(
-                functools.partial(last_kernel, blocks - 1, q, rows),
+                functools.partial(last_kernel, blocks - 1, q, rows, first, bases),
                 in_specs=[vmem] * 7 + [hbm] * len(out),
                 out_specs=hbm,
                 out_shape=jax.ShapeDtypeStruct(tower_in.shape, jnp.bfloat16),
                 scratch_shapes=[
-                    pltpu.VMEM((tracks, count, channels), jnp.bfloat16),
-                    pltpu.SemaphoreType.DMA((1,)),
+                    pltpu.VMEM((part, count, channels), jnp.bfloat16),
+                    pltpu.SemaphoreType.DMA((part,)),
                 ],
                 input_output_aliases={7: 0} if out else {},
                 compiler_params=params,
-                cost_estimate=cost(count, conv=0),
+                cost_estimate=cost(count, conv=0, part=part),
             )(*arrays, *mids, *out)
         ]
     return out[0]

time: 46.2 us -> 43.8 us (0.948)
  waiting for transfers between devices: 22.2 us -> 14.4 us
  starting transfers between devices: 5.88 us -> 9.19 us
  Pallas kernels: 17.7 us -> 19.6 us
    ppermute x6 -> x7, waiting for transfers between devices: 21.5 us -> 14.4 us  [cross(): return lax.ppermute(value, ('groups', 'seq'), inter_pairs)]
    ppermute x5 -> x6, starting transfers between devices: 1.68 us -> 4.38 us  [across(): return lax.ppermute(value, ('groups', 'seq'), intra_pairs)]
    pallas_call x2 -> x4, Pallas kernels: 3.1 us -> 4.33 us  [local(): pl.pallas_call(functools.partial(last_kernel, blocks - 1, q, rows, first,...]
    pallas_call x5 -> x8, Pallas kernels: 10.2 us -> 10.9 us  [step(): pl.pallas_call(functools.partial(step_kernel, plan), in_specs=[vmem] * (l...]
    ppermute x5 -> x6, waiting for transfers between devices: 0.72 us -> 0.02 us  [across(): return lax.ppermute(value, ('groups', 'seq'), intra_pairs)]
    ppermute x6 -> x7, starting transfers between devices: 4.2 us -> 4.8 us  [cross(): return lax.ppermute(value, ('groups', 'seq'), inter_pairs)]
  transfers between devices with their start and end apart: 11 -> 13, of which waited for: 7 -> 5; matrix products, arithmetic and copies ran while one was open for 0% -> 0% of each run, Pallas kernels for 24% -> 38%
where the time goes in v5:
time: 43.8 us; the launch traced here: 43.5 us
  Pallas kernels  19.6 us (45%)
  waiting for transfers between devices  14.4 us (33%)
  starting transfers between devices  9.19 us (21%)
    ppermute x7, waiting for transfers between devices, cross(): return lax.ppermute(value, ('groups', 'seq'), inter_pairs)  14.4 us
    pallas_call x8, Pallas kernels, step(): pl.pallas_call(functools.partial(step_kernel, plan), in_specs=[vmem] * (l...  10.9 us
    ppermute x7, starting transfers between devices, cross(): return lax.ppermute(value, ('groups', 'seq'), inter_pairs)  4.8 us
    ppermute x6, starting transfers between devices, across(): return lax.ppermute(value, ('groups', 'seq'), intra_pairs)  4.38 us
    pallas_call x4, Pallas kernels, local(): pl.pallas_call(functools.partial(last_kernel, blocks - 1, q, rows, first,...  4.33 us
    pallas_call x1, Pallas kernels, local(): pl.pallas_call(functools.partial(entry_kernel, one), in_specs=[vmem] * 4,...  2.33 us
    pallas_call x1, Pallas kernels, local(): pl.pallas_call(functools.partial(edge_kernel, one), in_specs=[hbm] * 4, o...  2.04 us
  transfers between devices with their start and end apart: 13, of which 5 were waited for; matrix products, arithmetic and copies ran while one was open for 0% of the time, Pallas kernels for 38%

profile of v5, /device:TPU:25, one launch (start us, length us, event | category | flops | bytes accessed | tf_op | source)
XLA Modules:
  0.0 43.5 jit_solution(8970250353621404183)
XLA Ops:
  0.0 2.0 %shard_map.74 = (bf16[4,32,384]{2,1,0:T(8,128)(2,1)S(1)}, bf16[4,32,384]{2,1,0:T(8,128)(2,1)S(1)}) custom-call(bf16[4,256,768]{2,1,0:T(8,128)(2,1)} %refs_0_.7, f32[4,768]{1,0:T(4,128)} %refs_10_.5, f32[4,768]{1,0:T(4,128)} %refs_11_.3, bf16[4,3,768,384]{3,2,1,0:T(8,128)(2,1)} %refs_12_.3), custom_call_target="tpu_custom_call" | custom-call | flops 2264924160 | bytes 2264924 | tf_op jit(solution)/shard_map/pallas_call | solution.py:322
  2.1 0.7 %collective-permute-start = (bf16[4,32,384]{2,1,0:T(8,128)(2,1)S(1)}, bf16[4,32,384]{2,1,0:T(8,128)(2,1)S(1)}, u32[]{:S(2)}, u32[]{:S(2)}) collective-permute-start(bf16[4,32,384]{2,1,0:T(8,128)(2,1)S(1)} %get-tuple-element.37), channel_id=1, source_target_pairs={{0,1},{2,3},{4,5},{6,7},{8,9},{10,11},{12,13},{14,15},{16,17},{18,... | collective-permute-start | bytes 294920 | tf_op jit(solution)/shard_map/ppermute | solution.py:284
  2.8 1.2 %collective-permute-start.1 = (bf16[4,32,384]{2,1,0:T(8,128)(2,1)S(1)}, bf16[4,32,384]{2,1,0:T(8,128)(2,1)S(1)}, u32[]{:S(2)}, u32[]{:S(2)}) collective-permute-start(bf16[4,32,384]{2,1,0:T(8,128)(2,1)S(1)} %get-tuple-element.38), channel_id=1, source_target_pairs={{1,2},{3,4},{5,6},{7,8},{9,10},{11,12},{13,14},{17,18},{19,20},{21... | collective-permute-start | bytes 294920 | tf_op jit(solution)/shard_map/ppermute | solution.py:281
  4.1 2.3 %shard_map.73.refs_1_ = f32[4,256,384]{2,1,0:T(8,128)S(1)} custom-call(bf16[4,256,768]{2,1,0:T(8,128)(2,1)S(1)} %copy-done.2, f32[4,768]{1,0:T(4,128)S(1)} %copy-done.5, f32[4,768]{1,0:T(4,128)S(1)} %copy-done.6, bf16[4,3,768,384]{3,2,1,0:T(8,128)(2,1)S(1)} %copy-done.1), custom_call_target="tpu_custom_call" | custom-call | flops 18119393280 | bytes 18119392 | tf_op jit(solution)/shard_map/pallas_call | solution.py:334
  6.4 1.5 %collective-permute-done.1.refs_2_ = bf16[4,32,384]{2,1,0:T(8,128)(2,1)S(1)} collective-permute-done((bf16[4,32,384]{2,1,0:T(8,128)(2,1)S(1)}, bf16[4,32,384]{2,1,0:T(8,128)(2,1)S(1)}, u32[]{:S(2)}, u32[]{:S(2)}) %collective-permute-start.1) | collective-permute-done | bytes 98336 | tf_op jit(solution)/shard_map/ppermute | solution.py:281
  7.9 0.9 %shard_map.75 = (bf16[4,64,768]{2,1,0:T(8,128)(2,1)S(1)}, bf16[4,64,384]{2,1,0:T(8,128)(2,1)S(1)}, f32[4,64,384]{2,1,0:T(8,128)S(1)}, f32[4,64,384]{2,1,0:T(8,128)S(1)}) custom-call(bf16[4,256,768]{2,1,0:T(8,128)(2,1)S(1)} %copy-done.2, f32[4,256,384]{2,1,0:T(8,128)S(1)} %shard_map.73.refs_1_, bf16[4,32,384]{2,1,0:T(8,128)(2,1)S(1)} %collective-permute-done.1.refs_2_, ...), custom_call_target="tpu_custom_call" | custom-call | flops 6039797760 | bytes 6039797 | tf_op jit(solution)/shard_map/pallas_call | solution.py:303
  8.9 0.3 collective-permute-start.3
  9.2 2.5 %shard_map.76 = (bf16[4,192,768]{2,1,0:T(8,128)(2,1)S(1)}, bf16[4,64,384]{2,1,0:T(8,128)(2,1)S(1)}, f32[4,256,384]{2,1,0:T(8,128)S(1)}) custom-call(bf16[4,256,768]{2,1,0:T(8,128)(2,1)S(1)} %copy-done.2, f32[4,256,384]{2,1,0:T(8,128)S(1)} %shard_map.73.refs_1_, bf16[4,32,384]{2,1,0:T(8,128)(2,1)S(1)} %collective-permute-done.refs_2_, ...), custom_call_target="tpu_custom_call" | custom-call | flops 18119393280 | bytes 18119392 | tf_op jit(solution)/shard_map/pallas_call | solution.py:303
  11.7 1.2 %collective-permute-start.2 = (bf16[4,64,384]{2,1,0:T(8,128)(2,1)S(1)}, bf16[4,64,384]{2,1,0:T(8,128)(2,1)S(1)}, u32[]{:S(2)}, u32[]{:S(2)}) collective-permute-start(bf16[4,64,384]{2,1,0:T(8,128)(2,1)S(1)} %get-tuple-element.42), channel_id=1, source_target_pairs={{0,1},{2,3},{4,5},{6,7},{8,9},{10,11},{12,13},{14,15},{16,17},{18,... | collective-permute-start | bytes 589832 | tf_op jit(solution)/shard_map/ppermute | solution.py:284
  12.8 0.9 %shard_map.77 = (bf16[4,64,768]{2,1,0:T(8,128)(2,1)S(1)}, bf16[4,64,384]{2,1,0:T(8,128)(2,1)S(1)}, f32[4,64,384]{2,1,0:T(8,128)S(1)}, f32[4,64,384]{2,1,0:T(8,128)S(1)}) custom-call(bf16[4,192,768]{2,1,0:T(8,128)(2,1)S(1)} %get-tuple-element.40.refs_0_, f32[4,256,384]{2,1,0:T(8,128)S(1)} %get-tuple-element.41.refs_1_, ...), custom_call_target="tpu_custom_call" | custom-call | flops 6039797760 | bytes 6039797 | tf_op jit(solution)/shard_map/pallas_call | solution.py:303
  13.8 0.7 %collective-permute-start.5 = (bf16[4,64,384]{2,1,0:T(8,128)(2,1)S(1)}, bf16[4,64,384]{2,1,0:T(8,128)(2,1)S(1)}, u32[]{:S(2)}, u32[]{:S(2)}) collective-permute-start(bf16[4,64,384]{2,1,0:T(8,128)(2,1)S(1)} %get-tuple-element.57), channel_id=1, source_target_pairs={{1,2},{3,4},{5,6},{7,8},{9,10},{11,12},{13,14},{17,18},{19,20},{21... | collective-permute-start | bytes 589832 | tf_op jit(solution)/shard_map/ppermute | solution.py:281
  14.4 1.8 %shard_map.78 = (bf16[4,128,768]{2,1,0:T(8,128)(2,1)S(1)}, bf16[4,128,384]{2,1,0:T(8,128)(2,1)S(1)}, f32[4,256,384]{2,1,0:T(8,128)S(1)}) custom-call(bf16[4,192,768]{2,1,0:T(8,128)(2,1)S(1)} %get-tuple-element.40.refs_0_, f32[4,256,384]{2,1,0:T(8,128)S(1)} %get-tuple-element.41.refs_1_, bf16[4,64,384]{2,1,0:T(8,128)(2,1)S(1)} %collective-permute-done.2.refs_2_, ...), custom_call_target="tpu_custom_call" | custom-call | flops 12079595520 | bytes 12079595 | tf_op jit(solution)/shard_map/pallas_call | solution.py:303
  16.2 1.0 %collective-permute-start.4 = (bf16[4,128,384]{2,1,0:T(8,128)(2,1)S(1)}, bf16[4,128,384]{2,1,0:T(8,128)(2,1)S(1)}, u32[]{:S(2)}, u32[]{:S(2)}) collective-permute-start(bf16[4,128,384]{2,1,0:T(8,128)(2,1)S(1)} %get-tuple-element.51), channel_id=1, source_target_pairs={{0,1},{2,3},{4,5},{6,7},{8,9},{10,11},{12,13},{14,15},{16,17},{18,... | collective-permute-start | bytes 1179656 | tf_op jit(solution)/shard_map/ppermute | solution.py:284
  17.2 0.9 %shard_map.79 = (bf16[4,64,768]{2,1,0:T(8,128)(2,1)S(1)}, bf16[4,64,384]{2,1,0:T(8,128)(2,1)S(1)}, f32[4,64,384]{2,1,0:T(8,128)S(1)}, f32[4,64,384]{2,1,0:T(8,128)S(1)}) custom-call(bf16[4,64,768]{2,1,0:T(8,128)(2,1)S(1)} %get-tuple-element.47.refs_0_, f32[4,256,384]{2,1,0:T(8,128)S(1)} %get-tuple-element.41.refs_1_, ...), custom_call_target="tpu_custom_call" | custom-call | flops 6039797760 | bytes 6039797 | tf_op jit(solution)/shard_map/pallas_call | solution.py:303
  18.2 0.6 %collective-permute-start.6 = (bf16[4,64,384]{2,1,0:T(8,128)(2,1)S(1)}, bf16[4,64,384]{2,1,0:T(8,128)(2,1)S(1)}, u32[]{:S(2)}, u32[]{:S(2)}) collective-permute-start(bf16[4,64,384]{2,1,0:T(8,128)(2,1)S(1)} %get-tuple-element.58), channel_id=1, source_target_pairs={{1,2},{3,4},{5,6},{7,8},{9,10},{11,12},{13,14},{17,18},{19,20},{21... | collective-permute-start | bytes 589832 | tf_op jit(solution)/shard_map/ppermute | solution.py:281
  18.8 1.8 %shard_map.80 = (bf16[4,128,768]{2,1,0:T(8,128)(2,1)S(1)}, bf16[4,128,384]{2,1,0:T(8,128)(2,1)S(1)}, bf16[4,128,384]{2,1,0:T(8,128)(2,1)S(1)}, f32[4,128,384]{2,1,0:T(8,128)S(1)}) custom-call(bf16[4,128,768]{2,1,0:T(8,128)(2,1)S(1)} %get-tuple-element.45.refs_0_, f32[4,256,384]{2,1,0:T(8,128)S(1)} %get-tuple-element.46.refs_10_.refs_1_.refs_2_, ...), custom_call_target="tpu_custom_call" | custom-call | flops 12079595520 | bytes 12079595 | tf_op jit(solution)/shard_map/pallas_call | solution.py:303
  20.6 0.9 %collective-permute-start.11 = (bf16[4,128,384]{2,1,0:T(8,128)(2,1)S(1)}, bf16[4,128,384]{2,1,0:T(8,128)(2,1)S(1)}, u32[]{:S(2)}, u32[]{:S(2)}) collective-permute-start(bf16[4,128,384]{2,1,0:T(8,128)(2,1)S(1)} %get-tuple-element.66), channel_id=1, source_target_pairs={{0,1},{2,3},{4,5},{6,7},{8,9},{10,11},{12,13},{14,15},{16,17},{18,... | collective-permute-start | bytes 1179656 | tf_op jit(solution)/shard_map/ppermute | solution.py:284
  21.4 0.6 %collective-permute-start.12 = (bf16[4,128,384]{2,1,0:T(8,128)(2,1)S(1)}, bf16[4,128,384]{2,1,0:T(8,128)(2,1)S(1)}, u32[]{:S(2)}, u32[]{:S(2)}) collective-permute-start(bf16[4,128,384]{2,1,0:T(8,128)(2,1)S(1)} %get-tuple-element.67), channel_id=1, source_target_pairs={{1,2},{3,4},{5,6},{7,8},{9,10},{11,12},{13,14},{17,18},{19,20},{21... | collective-permute-start | bytes 1179656 | tf_op jit(solution)/shard_map/ppermute | solution.py:281
  22.0 7.7 %collective-permute-done.6.refs_6_ = bf16[4,64,384]{2,1,0:T(8,128)(2,1)S(1)} collective-permute-done((bf16[4,64,384]{2,1,0:T(8,128)(2,1)S(1)}, bf16[4,64,384]{2,1,0:T(8,128)(2,1)S(1)}, u32[]{:S(2)}, u32[]{:S(2)}) %collective-permute-start.6) | collective-permute-done | bytes 196640 | tf_op jit(solution)/shard_map/ppermute | solution.py:281
  29.7 0.9 %shard_map.81 = (bf16[2,128,768]{2,1,0:T(8,128)(2,1)S(1)}, bf16[2,128,384]{2,1,0:T(8,128)(2,1)S(1)}, bf16[2,128,384]{2,1,0:T(8,128)(2,1)S(1)}, f32[2,128,384]{2,1,0:T(8,128)S(1)}) custom-call(bf16[4,64,768]{2,1,0:T(8,128)(2,1)S(1)} %get-tuple-element.54.refs_0_, bf16[4,64,768]{2,1,0:T(8,128)(2,1)S(1)} %get-tuple-element.55.refs_1_, ...), custom_call_target="tpu_custom_call" | custom-call | flops 6039797760 | bytes 6039797 | tf_op jit(solution)/shard_map/pallas_call | solution.py:303
  30.6 0.1 collective-permute-start.9
  30.7 0.1 collective-permute-start.10
  30.7 1.2 %shard_map.82 = (bf16[2,128,768]{2,1,0:T(8,128)(2,1)S(1)}, bf16[2,128,384]{2,1,0:T(8,128)(2,1)S(1)}, bf16[2,128,384]{2,1,0:T(8,128)(2,1)S(1)}, f32[2,128,384]{2,1,0:T(8,128)S(1)}) custom-call(bf16[4,64,768]{2,1,0:T(8,128)(2,1)S(1)} %get-tuple-element.54.refs_0_, bf16[4,64,768]{2,1,0:T(8,128)(2,1)S(1)} %get-tuple-element.55.refs_1_, ...), custom_call_target="tpu_custom_call" | custom-call | flops 6039797760 | bytes 6039797 | tf_op jit(solution)/shard_map/pallas_call | solution.py:303
  31.9 0.5 %collective-permute-start.7 = (bf16[2,128,384]{2,1,0:T(8,128)(2,1)S(1)}, bf16[2,128,384]{2,1,0:T(8,128)(2,1)S(1)}, u32[]{:S(2)}, u32[]{:S(2)}) collective-permute-start(bf16[2,128,384]{2,1,0:T(8,128)(2,1)S(1)} %get-tuple-element.60), channel_id=1, source_target_pairs={{0,1},{2,3},{4,5},{6,7},{8,9},{10,11},{12,13},{14,15},{16,17},{18,... | collective-permute-start | bytes 589832 | tf_op jit(solution)/shard_map/ppermute | solution.py:284
  32.4 1.4 %collective-permute-start.8 = (bf16[2,128,384]{2,1,0:T(8,128)(2,1)S(1)}, bf16[2,128,384]{2,1,0:T(8,128)(2,1)S(1)}, u32[]{:S(2)}, u32[]{:S(2)}) collective-permute-start(bf16[2,128,384]{2,1,0:T(8,128)(2,1)S(1)} %get-tuple-element.61), channel_id=1, source_target_pairs={{1,2},{3,4},{5,6},{7,8},{9,10},{11,12},{13,14},{17,18},{19,20},{21... | collective-permute-start | bytes 589832 | tf_op jit(solution)/shard_map/ppermute | solution.py:281
  33.8 0.1 collective-permute-done.12.inter_ref
  33.9 1.1 %shard_map.83.refs_3_ = bf16[4,256,768]{2,1,0:T(8,128)(2,1)} custom-call(bf16[2,128,768]{2,1,0:T(8,128)(2,1)S(1)} %get-tuple-element.68.stream_ref, f32[2,128,384]{2,1,0:T(8,128)S(1)} %get-tuple-element.59.refs_13_.local_ref, bf16[4,128,384]{2,1,0:T(8,128)(2,1)S(1)} %collective-permute-done.11.intra_ref, ...), custom_call_target="tpu_custom_call" | custom-call | flops 1509949440 | bytes 1509949 | tf_op jit(solution)/shard_map/pallas_call | solution.py:449
  35.0 1.1 %shard_map.84.refs_3_ = bf16[4,256,768]{2,1,0:T(8,128)(2,1)} custom-call(bf16[2,128,768]{2,1,0:T(8,128)(2,1)S(1)} %get-tuple-element.64.stream_ref, f32[2,128,384]{2,1,0:T(8,128)S(1)} %get-tuple-element.65.local_ref, bf16[4,128,384]{2,1,0:T(8,128)(2,1)S(1)} %collective-permute-done.11.intra_ref, ...), custom_call_target="tpu_custom_call", output_to_operand_aliasing={{}: (7, {})} | custom-call | flops 1509949440 | bytes 1509949 | tf_op jit(solution)/shard_map/pallas_call | solution.py:449
  36.1 4.1 %collective-permute-done.10.inter_ref = bf16[2,128,384]{2,1,0:T(8,128)(2,1)S(1)} collective-permute-done((bf16[2,128,384]{2,1,0:T(8,128)(2,1)S(1)}, bf16[2,128,384]{2,1,0:T(8,128)(2,1)S(1)}, u32[]{:S(2)}, u32[]{:S(2)}) %collective-permute-start.10) | collective-permute-done | bytes 196640 | tf_op jit(solution)/shard_map/ppermute | solution.py:281
  40.2 1.1 %shard_map.85.refs_3_ = bf16[4,256,768]{2,1,0:T(8,128)(2,1)} custom-call(bf16[4,128,768]{2,1,0:T(8,128)(2,1)S(1)} %get-tuple-element.52.stream_ref, f32[4,128,384]{2,1,0:T(8,128)S(1)} %get-tuple-element.53.refs_13_.local_ref, bf16[2,128,384]{2,1,0:T(8,128)(2,1)S(1)} %collective-permute-done.9.intra_ref, ...), custom_call_target="tpu_custom_call", output_to_operand_aliasing={{}: (7, {})} | custom-call | flops 1509949440 | bytes 1509949 | tf_op jit(solution)/shard_map/pallas_call | solution.py:449
  41.3 1.0 %collective-permute-done.8.inter_ref = bf16[2,128,384]{2,1,0:T(8,128)(2,1)S(1)} collective-permute-done((bf16[2,128,384]{2,1,0:T(8,128)(2,1)S(1)}, bf16[2,128,384]{2,1,0:T(8,128)(2,1)S(1)}, u32[]{:S(2)}, u32[]{:S(2)}) %collective-permute-start.8) | collective-permute-done | bytes 196640 | tf_op jit(solution)/shard_map/ppermute | solution.py:281
  42.3 1.1 %shard_map.86 = bf16[4,256,768]{2,1,0:T(8,128)(2,1)} custom-call(bf16[4,128,768]{2,1,0:T(8,128)(2,1)S(1)} %get-tuple-element.52.stream_ref, f32[4,128,384]{2,1,0:T(8,128)S(1)} %get-tuple-element.53.refs_13_.local_ref, bf16[2,128,384]{2,1,0:T(8,128)(2,1)S(1)} %collective-permute-done.7.intra_ref, ...), custom_call_target="tpu_custom_call", output_to_operand_aliasing={{}: (7, {})} | custom-call | flops 1509949440 | bytes 1509949 | tf_op jit(solution)/shard_map/pallas_call | solution.py:449
  (22 shorter events, 0.0 us)
Async XLA Ops:
  0.0 4.1 %copy-start.1 = (bf16[4,3,768,384]{3,2,1,0:T(8,128)(2,1)S(1)}, bf16[4,3,768,384]{3,2,1,0:T(8,128)(2,1)}, u32[]{:S(2)}) copy-start(bf16[4,3,768,384]{3,2,1,0:T(8,128)(2,1)} %refs_12_.3) | copy-start | bytes 21233668
  0.0 4.1 %copy-start.6 = (f32[4,768]{1,0:T(4,128)S(1)}, f32[4,768]{1,0:T(4,128)}, u32[]{:S(2)}) copy-start(f32[4,768]{1,0:T(4,128)} %refs_11_.3) | copy-start | bytes 36868
  0.0 4.1 %copy-start.5 = (f32[4,768]{1,0:T(4,128)S(1)}, f32[4,768]{1,0:T(4,128)}, u32[]{:S(2)}) copy-start(f32[4,768]{1,0:T(4,128)} %refs_10_.5) | copy-start | bytes 36868
  0.0 4.0 %copy-start.2 = (bf16[4,256,768]{2,1,0:T(8,128)(2,1)S(1)}, bf16[4,256,768]{2,1,0:T(8,128)(2,1)}, u32[]{:S(2)}) copy-start(bf16[4,256,768]{2,1,0:T(8,128)(2,1)} %refs_0_.7) | copy-start | bytes 4718596
  2.1 7.1 %collective-permute-start = (bf16[4,32,384]{2,1,0:T(8,128)(2,1)S(1)}, bf16[4,32,384]{2,1,0:T(8,128)(2,1)S(1)}, u32[]{:S(2)}, u32[]{:S(2)}) collective-permute-start(bf16[4,32,384]{2,1,0:T(8,128)(2,1)S(1)} %get-tuple-element.37), channel_id=1, source_target_pairs={{0,1},{2,3},{4,5},{6,7},{8,9},{10,11},{12,13},{14,15},{16,17},{18,... | collective-permute-start | bytes 294920 | tf_op jit(solution)/shard_map/ppermute | solution.py:284
  2.8 5.1 %copy-start = (bf16[4,384,768]{2,1,0:T(8,128)(2,1)S(1)}, bf16[4,384,768]{2,1,0:T(8,128)(2,1)}, u32[]{:S(2)}) copy-start(bf16[4,384,768]{2,1,0:T(8,128)(2,1)} %refs_2_.7) | copy-start | bytes 7077892
  2.8 5.1 %copy-start.3 = (f32[4,384]{1,0:T(4,128)S(1)}, f32[4,384]{1,0:T(4,128)}, u32[]{:S(2)}) copy-start(f32[4,384]{1,0:T(4,128)} %refs_0_.11) | copy-start | bytes 18436
  2.8 5.1 %copy-start.4 = (f32[4,384]{1,0:T(4,128)S(1)}, f32[4,384]{1,0:T(4,128)}, u32[]{:S(2)}) copy-start(f32[4,384]{1,0:T(4,128)} %refs_1_.7) | copy-start | bytes 18436
  2.8 5.1 %collective-permute-start.1 = (bf16[4,32,384]{2,1,0:T(8,128)(2,1)S(1)}, bf16[4,32,384]{2,1,0:T(8,128)(2,1)S(1)}, u32[]{:S(2)}, u32[]{:S(2)}) collective-permute-start(bf16[4,32,384]{2,1,0:T(8,128)(2,1)S(1)} %get-tuple-element.38), channel_id=1, source_target_pairs={{1,2},{3,4},{5,6},{7,8},{9,10},{11,12},{13,14},{17,18},{19,20},{21... | collective-permute-start | bytes 294920 | tf_op jit(solution)/shard_map/ppermute | solution.py:281
  8.9 8.4 %collective-permute-start.3 = (bf16[4,64,384]{2,1,0:T(8,128)(2,1)S(1)}, bf16[4,64,384]{2,1,0:T(8,128)(2,1)S(1)}, u32[]{:S(2)}, u32[]{:S(2)}) collective-permute-start(bf16[4,64,384]{2,1,0:T(8,128)(2,1)S(1)} %get-tuple-element.48), channel_id=1, source_target_pairs={{1,2},{3,4},{5,6},{7,8},{9,10},{11,12},{13,14},{17,18},{19,20},{21... | collective-permute-start | bytes 589832 | tf_op jit(solution)/shard_map/ppermute | solution.py:281
  11.7 2.8 %collective-permute-start.2 = (bf16[4,64,384]{2,1,0:T(8,128)(2,1)S(1)}, bf16[4,64,384]{2,1,0:T(8,128)(2,1)S(1)}, u32[]{:S(2)}, u32[]{:S(2)}) collective-permute-start(bf16[4,64,384]{2,1,0:T(8,128)(2,1)S(1)} %get-tuple-element.42), channel_id=1, source_target_pairs={{0,1},{2,3},{4,5},{6,7},{8,9},{10,11},{12,13},{14,15},{16,17},{18,... | collective-permute-start | bytes 589832 | tf_op jit(solution)/shard_map/ppermute | solution.py:284
  13.8 8.2 %collective-permute-start.5 = (bf16[4,64,384]{2,1,0:T(8,128)(2,1)S(1)}, bf16[4,64,384]{2,1,0:T(8,128)(2,1)S(1)}, u32[]{:S(2)}, u32[]{:S(2)}) collective-permute-start(bf16[4,64,384]{2,1,0:T(8,128)(2,1)S(1)} %get-tuple-element.57), channel_id=1, source_target_pairs={{1,2},{3,4},{5,6},{7,8},{9,10},{11,12},{13,14},{17,18},{19,20},{21... | collective-permute-start | bytes 589832 | tf_op jit(solution)/shard_map/ppermute | solution.py:281
  16.2 2.6 %collective-permute-start.4 = (bf16[4,128,384]{2,1,0:T(8,128)(2,1)S(1)}, bf16[4,128,384]{2,1,0:T(8,128)(2,1)S(1)}, u32[]{:S(2)}, u32[]{:S(2)}) collective-permute-start(bf16[4,128,384]{2,1,0:T(8,128)(2,1)S(1)} %get-tuple-element.51), channel_id=1, source_target_pairs={{0,1},{2,3},{4,5},{6,7},{8,9},{10,11},{12,13},{14,15},{16,17},{18,... | collective-permute-start | bytes 1179656 | tf_op jit(solution)/shard_map/ppermute | solution.py:284
  18.2 11.5 %collective-permute-start.6 = (bf16[4,64,384]{2,1,0:T(8,128)(2,1)S(1)}, bf16[4,64,384]{2,1,0:T(8,128)(2,1)S(1)}, u32[]{:S(2)}, u32[]{:S(2)}) collective-permute-start(bf16[4,64,384]{2,1,0:T(8,128)(2,1)S(1)} %get-tuple-element.58), channel_id=1, source_target_pairs={{1,2},{3,4},{5,6},{7,8},{9,10},{11,12},{13,14},{17,18},{19,20},{21... | collective-permute-start | bytes 589832 | tf_op jit(solution)/shard_map/ppermute | solution.py:281
  20.6 11.8 %collective-permute-start.11 = (bf16[4,128,384]{2,1,0:T(8,128)(2,1)S(1)}, bf16[4,128,384]{2,1,0:T(8,128)(2,1)S(1)}, u32[]{:S(2)}, u32[]{:S(2)}) collective-permute-start(bf16[4,128,384]{2,1,0:T(8,128)(2,1)S(1)} %get-tuple-element.66), channel_id=1, source_target_pairs={{0,1},{2,3},{4,5},{6,7},{8,9},{10,11},{12,13},{14,15},{16,17},{18,... | collective-permute-start | bytes 1179656 | tf_op jit(solution)/shard_map/ppermute | solution.py:284
  21.4 12.4 %collective-permute-start.12 = (bf16[4,128,384]{2,1,0:T(8,128)(2,1)S(1)}, bf16[4,128,384]{2,1,0:T(8,128)(2,1)S(1)}, u32[]{:S(2)}, u32[]{:S(2)}) collective-permute-start(bf16[4,128,384]{2,1,0:T(8,128)(2,1)S(1)} %get-tuple-element.67), channel_id=1, source_target_pairs={{1,2},{3,4},{5,6},{7,8},{9,10},{11,12},{13,14},{17,18},{19,20},{21... | collective-permute-start | bytes 1179656 | tf_op jit(solution)/shard_map/ppermute | solution.py:281
  30.6 5.5 %collective-permute-start.9 = (bf16[2,128,384]{2,1,0:T(8,128)(2,1)S(1)}, bf16[2,128,384]{2,1,0:T(8,128)(2,1)S(1)}, u32[]{:S(2)}, u32[]{:S(2)}) collective-permute-start(bf16[2,128,384]{2,1,0:T(8,128)(2,1)S(1)} %get-tuple-element.62), channel_id=1, source_target_pairs={{0,1},{2,3},{4,5},{6,7},{8,9},{10,11},{12,13},{14,15},{16,17},{18,... | collective-permute-start | bytes 589832 | tf_op jit(solution)/shard_map/ppermute | solution.py:284
  30.7 9.5 %collective-permute-start.10 = (bf16[2,128,384]{2,1,0:T(8,128)(2,1)S(1)}, bf16[2,128,384]{2,1,0:T(8,128)(2,1)S(1)}, u32[]{:S(2)}, u32[]{:S(2)}) collective-permute-start(bf16[2,128,384]{2,1,0:T(8,128)(2,1)S(1)} %get-tuple-element.63), channel_id=1, source_target_pairs={{1,2},{3,4},{5,6},{7,8},{9,10},{11,12},{13,14},{17,18},{19,20},{21... | collective-permute-start | bytes 589832 | tf_op jit(solution)/shard_map/ppermute | solution.py:281
  31.9 9.4 %collective-permute-start.7 = (bf16[2,128,384]{2,1,0:T(8,128)(2,1)S(1)}, bf16[2,128,384]{2,1,0:T(8,128)(2,1)S(1)}, u32[]{:S(2)}, u32[]{:S(2)}) collective-permute-start(bf16[2,128,384]{2,1,0:T(8,128)(2,1)S(1)} %get-tuple-element.60), channel_id=1, source_target_pairs={{0,1},{2,3},{4,5},{6,7},{8,9},{10,11},{12,13},{14,15},{16,17},{18,... | collective-permute-start | bytes 589832 | tf_op jit(solution)/shard_map/ppermute | solution.py:284
  32.4 9.9 %collective-permute-start.8 = (bf16[2,128,384]{2,1,0:T(8,128)(2,1)S(1)}, bf16[2,128,384]{2,1,0:T(8,128)(2,1)S(1)}, u32[]{:S(2)}, u32[]{:S(2)}) collective-permute-start(bf16[2,128,384]{2,1,0:T(8,128)(2,1)S(1)} %get-tuple-element.61), channel_id=1, source_target_pairs={{1,2},{3,4},{5,6},{7,8},{9,10},{11,12},{13,14},{17,18},{19,20},{21... | collective-permute-start | bytes 589832 | tf_op jit(solution)/shard_map/ppermute | solution.py:281

commit v6 on v5

--- a/solution.py
+++ b/solution.py
@@ -90,50 +90,39 @@
 
 
 def edge_kernel(
-    span, tower_ref, scale_ref, shift_ref, weight_ref, intra_ref, inter_ref,
-    low, high, scale, shift, weight, sems,
+    span, tower_ref, scale_ref, shift_ref, weight_ref, inter_ref, part, scale, shift, weight, sems
 ):
     tracks, rows, channels = tower_ref.shape
-    sources = [
-        (scale_ref, scale),
-        (shift_ref, shift),
-        (tower_ref.at[:, 0:span], low),
-        (weight_ref.at[0, TAPS - 1], weight.at[0]),
-        (tower_ref.at[:, rows - span : rows], high),
-        (weight_ref.at[0, 0], weight.at[1]),
-    ]
-    copies = [
-        pltpu.make_async_copy(source, target, sems.at[i])
-        for i, (source, target) in enumerate(sources)
-    ]
-    for copy in copies:
-        copy.start()
-    for copy in copies[:3]:
-        copy.wait()
-
-    def product(stream, which):
-        normed = normed_of(
-            stream[...].reshape(tracks * span, channels), scale[0:1], shift[0:1]
-        )
-        copies[3 + 2 * which].wait()
-        return (
-            jnp.dot(normed, weight[which], preferred_element_type=jnp.float32)
+
+    def body(even, edge):
+        source = tower_ref.at[:, span_of((0, span), (0, rows), even)]
+        copies = [
+            pltpu.make_async_copy(source, target, sems.at[i])
+            for i, (source, target) in enumerate(
+                [
+                    (source, part),
+                    (weight_ref.at[0, TAPS - 1 if even else 0], weight),
+                    (scale_ref, scale),
+                    (shift_ref, shift),
+                ]
+            )
+        ]
+        for copy in copies:
+            copy.start()
+        for i in (2, 3, 0):
+            copies[i].wait()
+        normed = normed_of(part[...].reshape(tracks * span, channels), scale[0:1], shift[0:1])
+        copies[1].wait()
+        inter_ref[...] = (
+            jnp.dot(normed, weight[...], preferred_element_type=jnp.float32)
             .astype(jnp.bfloat16)
-            .reshape(tracks, span, -1)
-        )
-
-    to_last = product(low, 0)
-    copies[4].wait()
-    to_next = product(high, 1)
-
-    def store(even, edge):
-        inter_ref[...] = to_last if even else to_next
-        intra_ref[...] = to_next if even else to_last
-
-    both_ways(store)
-
-
-def entry_kernel(span, tower_ref, scale_ref, shift_ref, weight_ref, local_ref):
+            .reshape(inter_ref.shape)
+        )
+
+    both_ways(body)
+
+
+def entry_kernel(span, tower_ref, scale_ref, shift_ref, weight_ref, local_ref, intra_ref):
     tracks, rows, channels = tower_ref.shape
     everything = (0, rows)
 
@@ -144,6 +133,9 @@
         )
         for t in range(tracks):
             own = slice(t * rows, (t + 1) * rows)
+            intra_ref[t] = inn[own][span_of((rows - span, rows), everything, even)].astype(
+                jnp.bfloat16
+            )
             local_ref[t] = assemble(
                 everything,
                 [
@@ -319,26 +311,27 @@
         pltpu.with_memory_space_constraint(x, pltpu.HBM)
         for x in (tower_in, first_norm_scale, first_norm_shift, conv_weight)
     ]
-    intra, inter = pl.pallas_call(
+    inter = pl.pallas_call(
         functools.partial(edge_kernel, one),
         in_specs=[hbm] * 4,
-        out_specs=[vmem] * 2,
-        out_shape=[halo(one)] * 2,
-        scratch_shapes=[pltpu.VMEM((tracks, one, channels), jnp.bfloat16)] * 2
+        out_specs=vmem,
+        out_shape=halo(one),
+        scratch_shapes=[pltpu.VMEM((tracks, one, channels), jnp.bfloat16)]
         + [pltpu.VMEM(first_norm_scale.shape, jnp.float32)] * 2
-        + [pltpu.VMEM((2, channels, filters), jnp.bfloat16), pltpu.SemaphoreType.DMA((6,))],
+        + [pltpu.VMEM((channels, filters), jnp.bfloat16), pltpu.SemaphoreType.DMA((4,))],
         compiler_params=params,
         cost_estimate=cost(one, point=0),
     )(*far)
-    inter_0, intra_0 = cross(inter), across(intra)
-    local_0 = pl.pallas_call(
+    inter_0 = cross(inter)
+    local_0, intra = pl.pallas_call(
         functools.partial(entry_kernel, one),
         in_specs=[vmem] * 4,
-        out_specs=vmem,
-        out_shape=sums(rows),
+        out_specs=[vmem] * 2,
+        out_shape=[sums(rows), halo(one)],
         compiler_params=params,
         cost_estimate=cost(rows, point=0),
     )(tower_in, *norms, conv_weight)
+    intra_0 = across(intra)
 
     rest = (two, rows)
     stream_1f, (inter,), (here_1f, inn_1f) = step(

time: 43.8 us -> 43.4 us (level)
  waiting for transfers between devices: 14.4 us -> 13.4 us
  starting transfers between devices: 9.19 us -> 9.95 us
    ppermute x7, starting transfers between devices: 4.8 us -> 6.93 us  [cross(): return lax.ppermute(value, ('groups', 'seq'), inter_pairs)]
    ppermute x6, starting transfers between devices: 4.38 us -> 3.01 us  [across(): return lax.ppermute(value, ('groups', 'seq'), intra_pairs)]
    ppermute x7, waiting for transfers between devices: 14.4 us -> 13.1 us  [cross(): return lax.ppermute(value, ('groups', 'seq'), inter_pairs)]
  transfers between devices with their start and end apart: 13 -> 13, of which waited for: 5 -> 6; matrix products, arithmetic and copies ran while one was open for 0% -> 0% of each run, Pallas kernels for 38% -> 38%
where the time goes in v6:
time: 43.4 us; the launch traced here: 43 us
  Pallas kernels  19.2 us (44%)
  waiting for transfers between devices  13.4 us (31%)
  starting transfers between devices  9.95 us (23%)
    ppermute x7, waiting for transfers between devices, cross(): return lax.ppermute(value, ('groups', 'seq'), inter_pairs)  13.1 us
    pallas_call x8, Pallas kernels, step(): pl.pallas_call(functools.partial(step_kernel, plan), in_specs=[vmem] * (l...  10.9 us
    ppermute x7, starting transfers between devices, cross(): return lax.ppermute(value, ('groups', 'seq'), inter_pairs)  6.93 us
    pallas_call x4, Pallas kernels, local(): pl.pallas_call(functools.partial(last_kernel, blocks - 1, q, rows, first,...  4.34 us
    ppermute x6, starting transfers between devices, across(): return lax.ppermute(value, ('groups', 'seq'), intra_pairs)  3.01 us
    pallas_call x1, Pallas kernels, local(): pl.pallas_call(functools.partial(entry_kernel, one), in_specs=[vmem] * 4,...  2.3 us
    pallas_call x1, Pallas kernels, local(): pl.pallas_call(functools.partial(edge_kernel, one), in_specs=[hbm] * 4, o...  1.63 us
  transfers between devices with their start and end apart: 13, of which 6 were waited for; matrix products, arithmetic and copies ran while one was open for 0% of the time, Pallas kernels for 38%

profile of v6, /device:TPU:25, one launch (start us, length us, event | category | flops | bytes accessed | tf_op | source)
XLA Modules:
  0.0 43.0 jit_solution(17056624936535005772)
XLA Ops:
  0.0 1.6 %shard_map.74 = bf16[4,32,384]{2,1,0:T(8,128)(2,1)S(1)} custom-call(bf16[4,256,768]{2,1,0:T(8,128)(2,1)} %refs_0_.7, f32[4,768]{1,0:T(4,128)} %refs_10_.5, f32[4,768]{1,0:T(4,128)} %refs_11_.3, bf16[4,3,768,384]{3,2,1,0:T(8,128)(2,1)} %refs_12_.3), custom_call_target="tpu_custom_call" | custom-call | flops 2264924160 | bytes 2264924 | tf_op jit(solution)/shard_map/pallas_call | solution.py:314
  1.7 1.9 %collective-permute-start.1 = (bf16[4,32,384]{2,1,0:T(8,128)(2,1)S(1)}, bf16[4,32,384]{2,1,0:T(8,128)(2,1)S(1)}, u32[]{:S(2)}, u32[]{:S(2)}) collective-permute-start(bf16[4,32,384]{2,1,0:T(8,128)(2,1)S(1)} %shard_map.74), channel_id=1, source_target_pairs={{1,2},{3,4},{5,6},{7,8},{9,10},{11,12},{13,14},{17,18},{19,20},{21... | collective-permute-start | bytes 294920 | tf_op jit(solution)/shard_map/ppermute | solution.py:273
  3.6 0.2 copy-done.2
  3.8 2.3 %shard_map.73 = (f32[4,256,384]{2,1,0:T(8,128)S(1)}, bf16[4,32,384]{2,1,0:T(8,128)(2,1)S(1)}) custom-call(bf16[4,256,768]{2,1,0:T(8,128)(2,1)S(1)} %copy-done.2, f32[4,768]{1,0:T(4,128)S(1)} %copy-done.5, f32[4,768]{1,0:T(4,128)S(1)} %copy-done.6, bf16[4,3,768,384]{3,2,1,0:T(8,128)(2,1)S(1)} %copy-done.1), custom_call_target="tpu_custom_call" | custom-call | flops 18119393280 | bytes 18119392 | tf_op jit(solution)/shard_map/pallas_call | solution.py:326
  6.1 0.8 %collective-permute-start = (bf16[4,32,384]{2,1,0:T(8,128)(2,1)S(1)}, bf16[4,32,384]{2,1,0:T(8,128)(2,1)S(1)}, u32[]{:S(2)}, u32[]{:S(2)}) collective-permute-start(bf16[4,32,384]{2,1,0:T(8,128)(2,1)S(1)} %get-tuple-element.38), channel_id=1, source_target_pairs={{0,1},{2,3},{4,5},{6,7},{8,9},{10,11},{12,13},{14,15},{16,17},{18,... | collective-permute-start | bytes 294920 | tf_op jit(solution)/shard_map/ppermute | solution.py:276
  6.8 0.2 collective-permute-done.1.refs_2_
  7.0 0.9 %shard_map.75 = (bf16[4,64,768]{2,1,0:T(8,128)(2,1)S(1)}, bf16[4,64,384]{2,1,0:T(8,128)(2,1)S(1)}, f32[4,64,384]{2,1,0:T(8,128)S(1)}, f32[4,64,384]{2,1,0:T(8,128)S(1)}) custom-call(bf16[4,256,768]{2,1,0:T(8,128)(2,1)S(1)} %copy-done.2, f32[4,256,384]{2,1,0:T(8,128)S(1)} %get-tuple-element.37.refs_1_, ...), custom_call_target="tpu_custom_call" | custom-call | flops 6039797760 | bytes 6039797 | tf_op jit(solution)/shard_map/pallas_call | solution.py:295
  8.0 1.0 %collective-permute-start.3 = (bf16[4,64,384]{2,1,0:T(8,128)(2,1)S(1)}, bf16[4,64,384]{2,1,0:T(8,128)(2,1)S(1)}, u32[]{:S(2)}, u32[]{:S(2)}) collective-permute-start(bf16[4,64,384]{2,1,0:T(8,128)(2,1)S(1)} %get-tuple-element.48), channel_id=1, source_target_pairs={{1,2},{3,4},{5,6},{7,8},{9,10},{11,12},{13,14},{17,18},{19,20},{21... | collective-permute-start | bytes 589832 | tf_op jit(solution)/shard_map/ppermute | solution.py:273
  9.0 2.5 %shard_map.76 = (bf16[4,192,768]{2,1,0:T(8,128)(2,1)S(1)}, bf16[4,64,384]{2,1,0:T(8,128)(2,1)S(1)}, f32[4,256,384]{2,1,0:T(8,128)S(1)}) custom-call(bf16[4,256,768]{2,1,0:T(8,128)(2,1)S(1)} %copy-done.2, f32[4,256,384]{2,1,0:T(8,128)S(1)} %get-tuple-element.37.refs_1_, bf16[4,32,384]{2,1,0:T(8,128)(2,1)S(1)} %collective-permute-done.refs_2_, ...), custom_call_target="tpu_custom_call" | custom-call | flops 18119393280 | bytes 18119392 | tf_op jit(solution)/shard_map/pallas_call | solution.py:295
  11.5 0.4 collective-permute-start.2
  11.9 0.9 %shard_map.77 = (bf16[4,64,768]{2,1,0:T(8,128)(2,1)S(1)}, bf16[4,64,384]{2,1,0:T(8,128)(2,1)S(1)}, f32[4,64,384]{2,1,0:T(8,128)S(1)}, f32[4,64,384]{2,1,0:T(8,128)S(1)}) custom-call(bf16[4,192,768]{2,1,0:T(8,128)(2,1)S(1)} %get-tuple-element.40.refs_0_, f32[4,256,384]{2,1,0:T(8,128)S(1)} %get-tuple-element.41.refs_1_, ...), custom_call_target="tpu_custom_call" | custom-call | flops 6039797760 | bytes 6039797 | tf_op jit(solution)/shard_map/pallas_call | solution.py:295
  12.9 1.6 %collective-permute-start.5 = (bf16[4,64,384]{2,1,0:T(8,128)(2,1)S(1)}, bf16[4,64,384]{2,1,0:T(8,128)(2,1)S(1)}, u32[]{:S(2)}, u32[]{:S(2)}) collective-permute-start(bf16[4,64,384]{2,1,0:T(8,128)(2,1)S(1)} %get-tuple-element.57), channel_id=1, source_target_pairs={{1,2},{3,4},{5,6},{7,8},{9,10},{11,12},{13,14},{17,18},{19,20},{21... | collective-permute-start | bytes 589832 | tf_op jit(solution)/shard_map/ppermute | solution.py:273
  14.4 1.8 %shard_map.78 = (bf16[4,128,768]{2,1,0:T(8,128)(2,1)S(1)}, bf16[4,128,384]{2,1,0:T(8,128)(2,1)S(1)}, f32[4,256,384]{2,1,0:T(8,128)S(1)}) custom-call(bf16[4,192,768]{2,1,0:T(8,128)(2,1)S(1)} %get-tuple-element.40.refs_0_, f32[4,256,384]{2,1,0:T(8,128)S(1)} %get-tuple-element.41.refs_1_, bf16[4,64,384]{2,1,0:T(8,128)(2,1)S(1)} %collective-permute-done.2.refs_2_, ...), custom_call_target="tpu_custom_call" | custom-call | flops 12079595520 | bytes 12079595 | tf_op jit(solution)/shard_map/pallas_call | solution.py:295
  16.2 0.5 %collective-permute-start.4 = (bf16[4,128,384]{2,1,0:T(8,128)(2,1)S(1)}, bf16[4,128,384]{2,1,0:T(8,128)(2,1)S(1)}, u32[]{:S(2)}, u32[]{:S(2)}) collective-permute-start(bf16[4,128,384]{2,1,0:T(8,128)(2,1)S(1)} %get-tuple-element.51), channel_id=1, source_target_pairs={{0,1},{2,3},{4,5},{6,7},{8,9},{10,11},{12,13},{14,15},{16,17},{18,... | collective-permute-start | bytes 1179656 | tf_op jit(solution)/shard_map/ppermute | solution.py:276
  16.7 0.9 %shard_map.79 = (bf16[4,64,768]{2,1,0:T(8,128)(2,1)S(1)}, bf16[4,64,384]{2,1,0:T(8,128)(2,1)S(1)}, f32[4,64,384]{2,1,0:T(8,128)S(1)}, f32[4,64,384]{2,1,0:T(8,128)S(1)}) custom-call(bf16[4,64,768]{2,1,0:T(8,128)(2,1)S(1)} %get-tuple-element.47.refs_0_, f32[4,256,384]{2,1,0:T(8,128)S(1)} %get-tuple-element.41.refs_1_, ...), custom_call_target="tpu_custom_call" | custom-call | flops 6039797760 | bytes 6039797 | tf_op jit(solution)/shard_map/pallas_call | solution.py:295
  17.7 0.2 collective-permute-start.6
  17.9 0.2 collective-permute-done.4.refs_4_
  18.1 1.8 %shard_map.80 = (bf16[4,128,768]{2,1,0:T(8,128)(2,1)S(1)}, bf16[4,128,384]{2,1,0:T(8,128)(2,1)S(1)}, bf16[4,128,384]{2,1,0:T(8,128)(2,1)S(1)}, f32[4,128,384]{2,1,0:T(8,128)S(1)}) custom-call(bf16[4,128,768]{2,1,0:T(8,128)(2,1)S(1)} %get-tuple-element.45.refs_0_, f32[4,256,384]{2,1,0:T(8,128)S(1)} %get-tuple-element.46.refs_10_.refs_1_.refs_2_, ...), custom_call_target="tpu_custom_call" | custom-call | flops 12079595520 | bytes 12079595 | tf_op jit(solution)/shard_map/pallas_call | solution.py:295
  19.9 0.8 %collective-permute-start.11 = (bf16[4,128,384]{2,1,0:T(8,128)(2,1)S(1)}, bf16[4,128,384]{2,1,0:T(8,128)(2,1)S(1)}, u32[]{:S(2)}, u32[]{:S(2)}) collective-permute-start(bf16[4,128,384]{2,1,0:T(8,128)(2,1)S(1)} %get-tuple-element.66), channel_id=1, source_target_pairs={{0,1},{2,3},{4,5},{6,7},{8,9},{10,11},{12,13},{14,15},{16,17},{18,... | collective-permute-start | bytes 1179656 | tf_op jit(solution)/shard_map/ppermute | solution.py:276
  20.6 0.8 %collective-permute-start.12 = (bf16[4,128,384]{2,1,0:T(8,128)(2,1)S(1)}, bf16[4,128,384]{2,1,0:T(8,128)(2,1)S(1)}, u32[]{:S(2)}, u32[]{:S(2)}) collective-permute-start(bf16[4,128,384]{2,1,0:T(8,128)(2,1)S(1)} %get-tuple-element.67), channel_id=1, source_target_pairs={{1,2},{3,4},{5,6},{7,8},{9,10},{11,12},{13,14},{17,18},{19,20},{21... | collective-permute-start | bytes 1179656 | tf_op jit(solution)/shard_map/ppermute | solution.py:273
  21.4 7.7 %collective-permute-done.6.refs_6_ = bf16[4,64,384]{2,1,0:T(8,128)(2,1)S(1)} collective-permute-done((bf16[4,64,384]{2,1,0:T(8,128)(2,1)S(1)}, bf16[4,64,384]{2,1,0:T(8,128)(2,1)S(1)}, u32[]{:S(2)}, u32[]{:S(2)}) %collective-permute-start.6) | collective-permute-done | bytes 196640 | tf_op jit(solution)/shard_map/ppermute | solution.py:273
  29.2 0.9 %shard_map.81 = (bf16[2,128,768]{2,1,0:T(8,128)(2,1)S(1)}, bf16[2,128,384]{2,1,0:T(8,128)(2,1)S(1)}, bf16[2,128,384]{2,1,0:T(8,128)(2,1)S(1)}, f32[2,128,384]{2,1,0:T(8,128)S(1)}) custom-call(bf16[4,64,768]{2,1,0:T(8,128)(2,1)S(1)} %get-tuple-element.54.refs_0_, bf16[4,64,768]{2,1,0:T(8,128)(2,1)S(1)} %get-tuple-element.55.refs_1_, ...), custom_call_target="tpu_custom_call" | custom-call | flops 6039797760 | bytes 6039797 | tf_op jit(solution)/shard_map/pallas_call | solution.py:295
  30.2 1.2 %shard_map.82 = (bf16[2,128,768]{2,1,0:T(8,128)(2,1)S(1)}, bf16[2,128,384]{2,1,0:T(8,128)(2,1)S(1)}, bf16[2,128,384]{2,1,0:T(8,128)(2,1)S(1)}, f32[2,128,384]{2,1,0:T(8,128)S(1)}) custom-call(bf16[4,64,768]{2,1,0:T(8,128)(2,1)S(1)} %get-tuple-element.54.refs_0_, bf16[4,64,768]{2,1,0:T(8,128)(2,1)S(1)} %get-tuple-element.55.refs_1_, ...), custom_call_target="tpu_custom_call" | custom-call | flops 6039797760 | bytes 6039797 | tf_op jit(solution)/shard_map/pallas_call | solution.py:295
  31.4 0.5 %collective-permute-start.7 = (bf16[2,128,384]{2,1,0:T(8,128)(2,1)S(1)}, bf16[2,128,384]{2,1,0:T(8,128)(2,1)S(1)}, u32[]{:S(2)}, u32[]{:S(2)}) collective-permute-start(bf16[2,128,384]{2,1,0:T(8,128)(2,1)S(1)} %get-tuple-element.60), channel_id=1, source_target_pairs={{0,1},{2,3},{4,5},{6,7},{8,9},{10,11},{12,13},{14,15},{16,17},{18,... | collective-permute-start | bytes 589832 | tf_op jit(solution)/shard_map/ppermute | solution.py:276
  31.9 1.4 %collective-permute-start.8 = (bf16[2,128,384]{2,1,0:T(8,128)(2,1)S(1)}, bf16[2,128,384]{2,1,0:T(8,128)(2,1)S(1)}, u32[]{:S(2)}, u32[]{:S(2)}) collective-permute-start(bf16[2,128,384]{2,1,0:T(8,128)(2,1)S(1)} %get-tuple-element.61), channel_id=1, source_target_pairs={{1,2},{3,4},{5,6},{7,8},{9,10},{11,12},{13,14},{17,18},{19,20},{21... | collective-permute-start | bytes 589832 | tf_op jit(solution)/shard_map/ppermute | solution.py:273
  33.3 0.1 collective-permute-done.12.inter_ref
  33.4 1.1 %shard_map.83.refs_3_ = bf16[4,256,768]{2,1,0:T(8,128)(2,1)} custom-call(bf16[2,128,768]{2,1,0:T(8,128)(2,1)S(1)} %get-tuple-element.68.stream_ref, f32[2,128,384]{2,1,0:T(8,128)S(1)} %get-tuple-element.59.refs_13_.local_ref, bf16[4,128,384]{2,1,0:T(8,128)(2,1)S(1)} %collective-permute-done.11.intra_ref, ...), custom_call_target="tpu_custom_call" | custom-call | flops 1509949440 | bytes 1509949 | tf_op jit(solution)/shard_map/pallas_call | solution.py:442
  34.5 1.1 %shard_map.84.refs_3_ = bf16[4,256,768]{2,1,0:T(8,128)(2,1)} custom-call(bf16[2,128,768]{2,1,0:T(8,128)(2,1)S(1)} %get-tuple-element.64.stream_ref, f32[2,128,384]{2,1,0:T(8,128)S(1)} %get-tuple-element.65.local_ref, bf16[4,128,384]{2,1,0:T(8,128)(2,1)S(1)} %collective-permute-done.11.intra_ref, ...), custom_call_target="tpu_custom_call", output_to_operand_aliasing={{}: (7, {})} | custom-call | flops 1509949440 | bytes 1509949 | tf_op jit(solution)/shard_map/pallas_call | solution.py:442
  35.6 4.1 %collective-permute-done.10.inter_ref = bf16[2,128,384]{2,1,0:T(8,128)(2,1)S(1)} collective-permute-done((bf16[2,128,384]{2,1,0:T(8,128)(2,1)S(1)}, bf16[2,128,384]{2,1,0:T(8,128)(2,1)S(1)}, u32[]{:S(2)}, u32[]{:S(2)}) %collective-permute-start.10) | collective-permute-done | bytes 196640 | tf_op jit(solution)/shard_map/ppermute | solution.py:273
  39.7 1.1 %shard_map.85.refs_3_ = bf16[4,256,768]{2,1,0:T(8,128)(2,1)} custom-call(bf16[4,128,768]{2,1,0:T(8,128)(2,1)S(1)} %get-tuple-element.52.stream_ref, f32[4,128,384]{2,1,0:T(8,128)S(1)} %get-tuple-element.53.refs_13_.local_ref, bf16[2,128,384]{2,1,0:T(8,128)(2,1)S(1)} %collective-permute-done.9.intra_ref, ...), custom_call_target="tpu_custom_call", output_to_operand_aliasing={{}: (7, {})} | custom-call | flops 1509949440 | bytes 1509949 | tf_op jit(solution)/shard_map/pallas_call | solution.py:442
  40.8 1.0 %collective-permute-done.8.inter_ref = bf16[2,128,384]{2,1,0:T(8,128)(2,1)S(1)} collective-permute-done((bf16[2,128,384]{2,1,0:T(8,128)(2,1)S(1)}, bf16[2,128,384]{2,1,0:T(8,128)(2,1)S(1)}, u32[]{:S(2)}, u32[]{:S(2)}) %collective-permute-start.8) | collective-permute-done | bytes 196640 | tf_op jit(solution)/shard_map/ppermute | solution.py:273
  41.8 1.1 %shard_map.86 = bf16[4,256,768]{2,1,0:T(8,128)(2,1)} custom-call(bf16[4,128,768]{2,1,0:T(8,128)(2,1)S(1)} %get-tuple-element.52.stream_ref, f32[4,128,384]{2,1,0:T(8,128)S(1)} %get-tuple-element.53.refs_13_.local_ref, bf16[2,128,384]{2,1,0:T(8,128)(2,1)S(1)} %collective-permute-done.7.intra_ref, ...), custom_call_target="tpu_custom_call", output_to_operand_aliasing={{}: (7, {})} | custom-call | flops 1509949440 | bytes 1509949 | tf_op jit(solution)/shard_map/pallas_call | solution.py:442
  (22 shorter events, 0.2 us)
Async XLA Ops:
  0.0 3.6 %copy-start.1 = (bf16[4,3,768,384]{3,2,1,0:T(8,128)(2,1)S(1)}, bf16[4,3,768,384]{3,2,1,0:T(8,128)(2,1)}, u32[]{:S(2)}) copy-start(bf16[4,3,768,384]{3,2,1,0:T(8,128)(2,1)} %refs_12_.3) | copy-start | bytes 21233668
  0.0 3.6 %copy-start.6 = (f32[4,768]{1,0:T(4,128)S(1)}, f32[4,768]{1,0:T(4,128)}, u32[]{:S(2)}) copy-start(f32[4,768]{1,0:T(4,128)} %refs_11_.3) | copy-start | bytes 36868
  0.0 3.6 %copy-start.5 = (f32[4,768]{1,0:T(4,128)S(1)}, f32[4,768]{1,0:T(4,128)}, u32[]{:S(2)}) copy-start(f32[4,768]{1,0:T(4,128)} %refs_10_.5) | copy-start | bytes 36868
  0.0 3.7 %copy-start.2 = (bf16[4,256,768]{2,1,0:T(8,128)(2,1)S(1)}, bf16[4,256,768]{2,1,0:T(8,128)(2,1)}, u32[]{:S(2)}) copy-start(bf16[4,256,768]{2,1,0:T(8,128)(2,1)} %refs_0_.7) | copy-start | bytes 4718596
  1.7 5.4 %copy-start = (bf16[4,384,768]{2,1,0:T(8,128)(2,1)S(1)}, bf16[4,384,768]{2,1,0:T(8,128)(2,1)}, u32[]{:S(2)}) copy-start(bf16[4,384,768]{2,1,0:T(8,128)(2,1)} %refs_2_.7) | copy-start | bytes 7077892
  1.7 5.4 %copy-start.3 = (f32[4,384]{1,0:T(4,128)S(1)}, f32[4,384]{1,0:T(4,128)}, u32[]{:S(2)}) copy-start(f32[4,384]{1,0:T(4,128)} %refs_0_.11) | copy-start | bytes 18436
  1.7 5.4 %copy-start.4 = (f32[4,384]{1,0:T(4,128)S(1)}, f32[4,384]{1,0:T(4,128)}, u32[]{:S(2)}) copy-start(f32[4,384]{1,0:T(4,128)} %refs_1_.7) | copy-start | bytes 18436
  1.7 5.3 %collective-permute-start.1 = (bf16[4,32,384]{2,1,0:T(8,128)(2,1)S(1)}, bf16[4,32,384]{2,1,0:T(8,128)(2,1)S(1)}, u32[]{:S(2)}, u32[]{:S(2)}) collective-permute-start(bf16[4,32,384]{2,1,0:T(8,128)(2,1)S(1)} %shard_map.74), channel_id=1, source_target_pairs={{1,2},{3,4},{5,6},{7,8},{9,10},{11,12},{13,14},{17,18},{19,20},{21... | collective-permute-start | bytes 294920 | tf_op jit(solution)/shard_map/ppermute | solution.py:273
  6.1 2.9 %collective-permute-start = (bf16[4,32,384]{2,1,0:T(8,128)(2,1)S(1)}, bf16[4,32,384]{2,1,0:T(8,128)(2,1)S(1)}, u32[]{:S(2)}, u32[]{:S(2)}) collective-permute-start(bf16[4,32,384]{2,1,0:T(8,128)(2,1)S(1)} %get-tuple-element.38), channel_id=1, source_target_pairs={{0,1},{2,3},{4,5},{6,7},{8,9},{10,11},{12,13},{14,15},{16,17},{18,... | collective-permute-start | bytes 294920 | tf_op jit(solution)/shard_map/ppermute | solution.py:276
  8.0 8.8 %collective-permute-start.3 = (bf16[4,64,384]{2,1,0:T(8,128)(2,1)S(1)}, bf16[4,64,384]{2,1,0:T(8,128)(2,1)S(1)}, u32[]{:S(2)}, u32[]{:S(2)}) collective-permute-start(bf16[4,64,384]{2,1,0:T(8,128)(2,1)S(1)} %get-tuple-element.48), channel_id=1, source_target_pairs={{1,2},{3,4},{5,6},{7,8},{9,10},{11,12},{13,14},{17,18},{19,20},{21... | collective-permute-start | bytes 589832 | tf_op jit(solution)/shard_map/ppermute | solution.py:273
  11.5 2.9 %collective-permute-start.2 = (bf16[4,64,384]{2,1,0:T(8,128)(2,1)S(1)}, bf16[4,64,384]{2,1,0:T(8,128)(2,1)S(1)}, u32[]{:S(2)}, u32[]{:S(2)}) collective-permute-start(bf16[4,64,384]{2,1,0:T(8,128)(2,1)S(1)} %get-tuple-element.42), channel_id=1, source_target_pairs={{0,1},{2,3},{4,5},{6,7},{8,9},{10,11},{12,13},{14,15},{16,17},{18,... | collective-permute-start | bytes 589832 | tf_op jit(solution)/shard_map/ppermute | solution.py:276
  12.9 8.6 %collective-permute-start.5 = (bf16[4,64,384]{2,1,0:T(8,128)(2,1)S(1)}, bf16[4,64,384]{2,1,0:T(8,128)(2,1)S(1)}, u32[]{:S(2)}, u32[]{:S(2)}) collective-permute-start(bf16[4,64,384]{2,1,0:T(8,128)(2,1)S(1)} %get-tuple-element.57), channel_id=1, source_target_pairs={{1,2},{3,4},{5,6},{7,8},{9,10},{11,12},{13,14},{17,18},{19,20},{21... | collective-permute-start | bytes 589832 | tf_op jit(solution)/shard_map/ppermute | solution.py:273
  16.2 1.9 %collective-permute-start.4 = (bf16[4,128,384]{2,1,0:T(8,128)(2,1)S(1)}, bf16[4,128,384]{2,1,0:T(8,128)(2,1)S(1)}, u32[]{:S(2)}, u32[]{:S(2)}) collective-permute-start(bf16[4,128,384]{2,1,0:T(8,128)(2,1)S(1)} %get-tuple-element.51), channel_id=1, source_target_pairs={{0,1},{2,3},{4,5},{6,7},{8,9},{10,11},{12,13},{14,15},{16,17},{18,... | collective-permute-start | bytes 1179656 | tf_op jit(solution)/shard_map/ppermute | solution.py:276
  17.7 11.5 %collective-permute-start.6 = (bf16[4,64,384]{2,1,0:T(8,128)(2,1)S(1)}, bf16[4,64,384]{2,1,0:T(8,128)(2,1)S(1)}, u32[]{:S(2)}, u32[]{:S(2)}) collective-permute-start(bf16[4,64,384]{2,1,0:T(8,128)(2,1)S(1)} %get-tuple-element.58), channel_id=1, source_target_pairs={{1,2},{3,4},{5,6},{7,8},{9,10},{11,12},{13,14},{17,18},{19,20},{21... | collective-permute-start | bytes 589832 | tf_op jit(solution)/shard_map/ppermute | solution.py:273
  19.9 12.0 %collective-permute-start.11 = (bf16[4,128,384]{2,1,0:T(8,128)(2,1)S(1)}, bf16[4,128,384]{2,1,0:T(8,128)(2,1)S(1)}, u32[]{:S(2)}, u32[]{:S(2)}) collective-permute-start(bf16[4,128,384]{2,1,0:T(8,128)(2,1)S(1)} %get-tuple-element.66), channel_id=1, source_target_pairs={{0,1},{2,3},{4,5},{6,7},{8,9},{10,11},{12,13},{14,15},{16,17},{18,... | collective-permute-start | bytes 1179656 | tf_op jit(solution)/shard_map/ppermute | solution.py:276
  20.6 12.7 %collective-permute-start.12 = (bf16[4,128,384]{2,1,0:T(8,128)(2,1)S(1)}, bf16[4,128,384]{2,1,0:T(8,128)(2,1)S(1)}, u32[]{:S(2)}, u32[]{:S(2)}) collective-permute-start(bf16[4,128,384]{2,1,0:T(8,128)(2,1)S(1)} %get-tuple-element.67), channel_id=1, source_target_pairs={{1,2},{3,4},{5,6},{7,8},{9,10},{11,12},{13,14},{17,18},{19,20},{21... | collective-permute-start | bytes 1179656 | tf_op jit(solution)/shard_map/ppermute | solution.py:273
  30.1 5.5 %collective-permute-start.9 = (bf16[2,128,384]{2,1,0:T(8,128)(2,1)S(1)}, bf16[2,128,384]{2,1,0:T(8,128)(2,1)S(1)}, u32[]{:S(2)}, u32[]{:S(2)}) collective-permute-start(bf16[2,128,384]{2,1,0:T(8,128)(2,1)S(1)} %get-tuple-element.62), channel_id=1, source_target_pairs={{0,1},{2,3},{4,5},{6,7},{8,9},{10,11},{12,13},{14,15},{16,17},{18,... | collective-permute-start | bytes 589832 | tf_op jit(solution)/shard_map/ppermute | solution.py:276
  30.2 9.5 %collective-permute-start.10 = (bf16[2,128,384]{2,1,0:T(8,128)(2,1)S(1)}, bf16[2,128,384]{2,1,0:T(8,128)(2,1)S(1)}, u32[]{:S(2)}, u32[]{:S(2)}) collective-permute-start(bf16[2,128,384]{2,1,0:T(8,128)(2,1)S(1)} %get-tuple-element.63), channel_id=1, source_target_pairs={{1,2},{3,4},{5,6},{7,8},{9,10},{11,12},{13,14},{17,18},{19,20},{21... | collective-permute-start | bytes 589832 | tf_op jit(solution)/shard_map/ppermute | solution.py:273
  31.4 9.4 %collective-permute-start.7 = (bf16[2,128,384]{2,1,0:T(8,128)(2,1)S(1)}, bf16[2,128,384]{2,1,0:T(8,128)(2,1)S(1)}, u32[]{:S(2)}, u32[]{:S(2)}) collective-permute-start(bf16[2,128,384]{2,1,0:T(8,128)(2,1)S(1)} %get-tuple-element.60), channel_id=1, source_target_pairs={{0,1},{2,3},{4,5},{6,7},{8,9},{10,11},{12,13},{14,15},{16,17},{18,... | collective-permute-start | bytes 589832 | tf_op jit(solution)/shard_map/ppermute | solution.py:276
  31.9 9.9 %collective-permute-start.8 = (bf16[2,128,384]{2,1,0:T(8,128)(2,1)S(1)}, bf16[2,128,384]{2,1,0:T(8,128)(2,1)S(1)}, u32[]{:S(2)}, u32[]{:S(2)}) collective-permute-start(bf16[2,128,384]{2,1,0:T(8,128)(2,1)S(1)} %get-tuple-element.61), channel_id=1, source_target_pairs={{1,2},{3,4},{5,6},{7,8},{9,10},{11,12},{13,14},{17,18},{19,20},{21... | collective-permute-start | bytes 589832 | tf_op jit(solution)/shard_map/ppermute | solution.py:273

commit v7 on v6

--- a/solution.py
+++ b/solution.py
@@ -68,13 +68,16 @@
     return jnp.maximum(stream.astype(jnp.float32) * scale + shift, 0.0).astype(jnp.bfloat16)
 
 
-def products_of(stream, block, even, scale_ref, shift_ref, weight_ref):
+def products_of(stream, block, even, names, scale_ref, shift_ref, weight_ref):
     filters = weight_ref.shape[-1]
     normed = normed_of(stream, scale_ref[block : block + 1], shift_ref[block : block + 1])
-    weight = jnp.concatenate([weight_ref[block, k] for k in range(TAPS)], axis=1)
+    order = ("inn", "here", "out") if even else ("out", "here", "inn")
+    chosen = [(k, name) for k, name in enumerate(order) if name in names]
+    weight = jnp.concatenate([weight_ref[block, k] for k, _ in chosen], axis=1)
     product = jnp.dot(normed, weight, preferred_element_type=jnp.float32)
-    behind, here, ahead = (product[:, k * filters : (k + 1) * filters] for k in range(TAPS))
-    return (ahead, here, behind) if even else (behind, here, ahead)
+    return {
+        name: product[:, i * filters : (i + 1) * filters] for i, (_, name) in enumerate(chosen)
+    }
 
 
 def finished(stream, conv, block, scale_ref, shift_ref, point_ref):
@@ -127,10 +130,11 @@
     everything = (0, rows)
 
     def body(even, edge):
-        out, here, inn = products_of(
+        named = products_of(
             tower_ref[...].reshape(tracks * rows, channels),
-            0, even, scale_ref, shift_ref, weight_ref,
-        )
+            0, even, ("out", "here", "inn"), scale_ref, shift_ref, weight_ref,
+        )
+        out, here, inn = named["out"], named["here"], named["inn"]
         for t in range(tracks):
             own = slice(t * rows, (t + 1) * rows)
             intra_ref[t] = inn[own][span_of((rows - span, rows), everything, even)].astype(
@@ -150,15 +154,16 @@
 
 
 def step_kernel(plan, *refs):
-    block, q, first, streams, terms, sends, keep = plan
+    block, q, first, streams, terms, sends, keep, late = plan
     refs = list(refs)
     take = lambda n: [refs.pop(0) for _ in range(n)]
-    stream_refs, term_refs = take(len(streams)), take(len(terms))
+    stream_refs, term_refs, late_refs = take(len(streams)), take(len(terms)), take(len(late))
     mid_scale_ref, mid_shift_ref, point_ref = take(3)
     scale_ref, shift_ref, weight_ref = take(3)
-    refs = refs[-(1 + len(sends) + len(keep)) :]
+    refs = refs[-(1 + len(sends) + len(keep) + sum(len(kept) for _, kept in late)) :]
     out_ref = refs.pop(0)
     send_refs, keep_refs = take(len(sends)), take(len(keep))
+    late_keep_refs = [take(len(kept)) for _, kept in late]
     tracks, count = out_ref.shape[0], q[1] - q[0]
 
     def body(even, edge):
@@ -183,16 +188,23 @@
         )
         stream = finished(stream, conv, block, mid_scale_ref, mid_shift_ref, point_ref)
         out_ref[...] = stream.reshape(out_ref.shape)
-        named = dict(
-            zip(
-                ("out", "here", "inn"),
-                products_of(stream, block + 1, even, scale_ref, shift_ref, weight_ref),
-            )
-        )
+        names = {name for name, _ in sends} | {name for _, parts in keep for name, _, _ in parts}
+        named = products_of(stream, block + 1, even, names, scale_ref, shift_ref, weight_ref)
         for t in range(tracks):
             own = slice(t * count, (t + 1) * count)
             for ref, (name, rows) in zip(send_refs, sends):
                 ref[t] = named[name][own][span_of(rows, q, even)].astype(jnp.bfloat16)
+        store(named, q, keep_refs, keep, even)
+        for ref, kept_refs, (rows, kept) in zip(late_refs, late_keep_refs, late):
+            stream = ref[...].reshape(-1, ref.shape[-1])
+            names = {name for _, parts in kept for name, _, _ in parts}
+            named = products_of(stream, block + 1, even, names, scale_ref, shift_ref, weight_ref)
+            store(named, rows, kept_refs, kept, even)
+
+    def store(named, q, keep_refs, keep, even):
+        count = q[1] - q[0]
+        for t in range(tracks):
+            own = slice(t * count, (t + 1) * count)
             for ref, (rows, parts) in zip(keep_refs, keep):
                 ref[t] = assemble(
                     rows,
@@ -285,20 +297,22 @@
     def sums(count, part=tracks):
         return jax.ShapeDtypeStruct((part, count, filters), jnp.float32)
 
-    def step(block, q, streams, terms, sends, keep, after=(), first=0, part=tracks):
+    def step(block, q, streams, terms, sends, keep, after=(), first=0, part=tracks, late=()):
         plan = (
             block, q, first,
             [r for r, _ in streams], [(r, c) for r, c, _ in terms], sends, keep,
-        )
-        arrays = [a for _, a in streams] + [a for _, _, a in terms]
+            [(r, kept) for r, _, kept in late],
+        )
+        arrays = [a for _, a in streams] + [a for _, _, a in terms] + [a for _, a, _ in late]
+        kept_rows = [r for r, _ in keep] + [r for _, _, kept in late for r, _ in kept]
         count = q[1] - q[0]
         made = pl.pallas_call(
             functools.partial(step_kernel, plan),
             in_specs=[vmem] * (len(arrays) + 6 + len(after)),
-            out_specs=[vmem] * (1 + len(sends) + len(keep)),
+            out_specs=[vmem] * (1 + len(sends) + len(kept_rows)),
             out_shape=[jax.ShapeDtypeStruct((part, count, channels), jnp.bfloat16)]
             + [halo(r[1] - r[0], part) for _, r in sends]
-            + [sums(r[1] - r[0], part) for r, _ in keep],
+            + [sums(r[1] - r[0], part) for r in kept_rows],
             compiler_params=params,
             cost_estimate=cost(count, part=part),
         )(*arrays, *mids, *norms, conv_weight, *after)
@@ -363,21 +377,26 @@
     streams = [((0, two), stream_1f), (rest, stream_1n)]
 
     middle, near = (two, three), (three, rows)
-    stream_2m, (inter,), (here_2m, inn_2m) = step(
+    stream_2m, (inter,), _ = step(
         1, middle,
         streams[1:],
         [(everything, False, local_1n), ((two, 2 * two), False, inn_1f)],
         [("out", middle)],
-        [(middle, [("here", middle, 0)]), ((two + three, rows), [("inn", middle, three)])],
+        [],
     )
     inter_2m = cross(inter)
-    stream_2n, (intra,), (local_2n,) = step(
+    stream_2n, (intra,), (local_2n, here_2m, inn_2m) = step(
         1, near,
         streams[1:],
         [(everything, False, local_1n), ((rows - two, rows), False, intra_1)],
         [("inn", near)],
         [(everything, [("here", near, 0), ("out", near, -three)])],
-        after=(here_2m,),
+        late=[
+            (
+                middle, stream_2m,
+                [(middle, [("here", middle, 0)]), ((two + three, rows), [("inn", middle, three)])],
+            )
+        ],
     )
     intra_2 = across(intra)
     stream_2f, (inter,), (here_2f, inn_2f) = step(

time: 43.4 us -> 43.1 us (level)
  transfers between devices with their start and end apart: 13 -> 13, of which waited for: 6 -> 5; matrix products, arithmetic and copies ran while one was open for 0% -> 0% of each run, Pallas kernels for 38% -> 38%
where the time goes in v7:
time: 43.1 us; the launch traced here: 42.8 us
  Pallas kernels  19.1 us (44%)
  waiting for transfers between devices  13.1 us (30%)
  starting transfers between devices  9.97 us (23%)
    ppermute x7, waiting for transfers between devices, cross(): return lax.ppermute(value, ('groups', 'seq'), inter_pairs)  13.1 us
    pallas_call x8, Pallas kernels, step(): pl.pallas_call(functools.partial(step_kernel, plan), in_specs=[vmem] * (l...  10.8 us
    ppermute x7, starting transfers between devices, cross(): return lax.ppermute(value, ('groups', 'seq'), inter_pairs)  6.94 us
    pallas_call x4, Pallas kernels, local(): pl.pallas_call(functools.partial(last_kernel, blocks - 1, q, rows, first,...  4.34 us
    ppermute x6, starting transfers between devices, across(): return lax.ppermute(value, ('groups', 'seq'), intra_pairs)  3.03 us
    pallas_call x1, Pallas kernels, local(): pl.pallas_call(functools.partial(entry_kernel, one), in_specs=[vmem] * 4,...  2.3 us
    pallas_call x1, Pallas kernels, local(): pl.pallas_call(functools.partial(edge_kernel, one), in_specs=[hbm] * 4, o...  1.63 us
  transfers between devices with their start and end apart: 13, of which 5 were waited for; matrix products, arithmetic and copies ran while one was open for 0% of the time, Pallas kernels for 38%

profile of v7, /device:TPU:25, one launch (start us, length us, event | category | flops | bytes accessed | tf_op | source)
XLA Modules:
  0.0 42.8 jit_solution(2797712458737892243)
XLA Ops:
  0.0 1.6 %shard_map.74 = bf16[4,32,384]{2,1,0:T(8,128)(2,1)S(1)} custom-call(bf16[4,256,768]{2,1,0:T(8,128)(2,1)} %refs_0_.7, f32[4,768]{1,0:T(4,128)} %refs_10_.5, f32[4,768]{1,0:T(4,128)} %refs_11_.3, bf16[4,3,768,384]{3,2,1,0:T(8,128)(2,1)} %refs_12_.3), custom_call_target="tpu_custom_call" | custom-call | flops 2264924160 | bytes 2264924 | tf_op jit(solution)/shard_map/pallas_call | solution.py:328
  1.7 1.9 %collective-permute-start.1 = (bf16[4,32,384]{2,1,0:T(8,128)(2,1)S(1)}, bf16[4,32,384]{2,1,0:T(8,128)(2,1)S(1)}, u32[]{:S(2)}, u32[]{:S(2)}) collective-permute-start(bf16[4,32,384]{2,1,0:T(8,128)(2,1)S(1)} %shard_map.74), channel_id=1, source_target_pairs={{1,2},{3,4},{5,6},{7,8},{9,10},{11,12},{13,14},{17,18},{19,20},{21... | collective-permute-start | bytes 294920 | tf_op jit(solution)/shard_map/ppermute | solution.py:285
  3.6 0.2 copy-done.2
  3.8 2.3 %shard_map.73 = (f32[4,256,384]{2,1,0:T(8,128)S(1)}, bf16[4,32,384]{2,1,0:T(8,128)(2,1)S(1)}) custom-call(bf16[4,256,768]{2,1,0:T(8,128)(2,1)S(1)} %copy-done.2, f32[4,768]{1,0:T(4,128)S(1)} %copy-done.5, f32[4,768]{1,0:T(4,128)S(1)} %copy-done.6, bf16[4,3,768,384]{3,2,1,0:T(8,128)(2,1)S(1)} %copy-done.1), custom_call_target="tpu_custom_call" | custom-call | flops 18119393280 | bytes 18119392 | tf_op jit(solution)/shard_map/pallas_call | solution.py:340
  6.1 0.8 %collective-permute-start = (bf16[4,32,384]{2,1,0:T(8,128)(2,1)S(1)}, bf16[4,32,384]{2,1,0:T(8,128)(2,1)S(1)}, u32[]{:S(2)}, u32[]{:S(2)}) collective-permute-start(bf16[4,32,384]{2,1,0:T(8,128)(2,1)S(1)} %get-tuple-element.38), channel_id=1, source_target_pairs={{0,1},{2,3},{4,5},{6,7},{8,9},{10,11},{12,13},{14,15},{16,17},{18,... | collective-permute-start | bytes 294920 | tf_op jit(solution)/shard_map/ppermute | solution.py:288
  6.8 0.2 collective-permute-done.1.refs_2_
  7.0 0.9 %shard_map.75 = (bf16[4,64,768]{2,1,0:T(8,128)(2,1)S(1)}, bf16[4,64,384]{2,1,0:T(8,128)(2,1)S(1)}, f32[4,64,384]{2,1,0:T(8,128)S(1)}, f32[4,64,384]{2,1,0:T(8,128)S(1)}) custom-call(bf16[4,256,768]{2,1,0:T(8,128)(2,1)S(1)} %copy-done.2, f32[4,256,384]{2,1,0:T(8,128)S(1)} %get-tuple-element.37.refs_1_, ...), custom_call_target="tpu_custom_call" | custom-call | flops 6039797760 | bytes 6039797 | tf_op jit(solution)/shard_map/pallas_call | solution.py:309
  8.0 1.0 %collective-permute-start.3 = (bf16[4,64,384]{2,1,0:T(8,128)(2,1)S(1)}, bf16[4,64,384]{2,1,0:T(8,128)(2,1)S(1)}, u32[]{:S(2)}, u32[]{:S(2)}) collective-permute-start(bf16[4,64,384]{2,1,0:T(8,128)(2,1)S(1)} %get-tuple-element.48), channel_id=1, source_target_pairs={{1,2},{3,4},{5,6},{7,8},{9,10},{11,12},{13,14},{17,18},{19,20},{21... | collective-permute-start | bytes 589832 | tf_op jit(solution)/shard_map/ppermute | solution.py:285
  9.0 2.5 %shard_map.76 = (bf16[4,192,768]{2,1,0:T(8,128)(2,1)S(1)}, bf16[4,64,384]{2,1,0:T(8,128)(2,1)S(1)}, f32[4,256,384]{2,1,0:T(8,128)S(1)}) custom-call(bf16[4,256,768]{2,1,0:T(8,128)(2,1)S(1)} %copy-done.2, f32[4,256,384]{2,1,0:T(8,128)S(1)} %get-tuple-element.37.refs_1_, bf16[4,32,384]{2,1,0:T(8,128)(2,1)S(1)} %collective-permute-done.refs_2_, ...), custom_call_target="tpu_custom_call" | custom-call | flops 18119393280 | bytes 18119392 | tf_op jit(solution)/shard_map/pallas_call | solution.py:309
  11.5 0.4 %collective-permute-start.2 = (bf16[4,64,384]{2,1,0:T(8,128)(2,1)S(1)}, bf16[4,64,384]{2,1,0:T(8,128)(2,1)S(1)}, u32[]{:S(2)}, u32[]{:S(2)}) collective-permute-start(bf16[4,64,384]{2,1,0:T(8,128)(2,1)S(1)} %get-tuple-element.42), channel_id=1, source_target_pairs={{0,1},{2,3},{4,5},{6,7},{8,9},{10,11},{12,13},{14,15},{16,17},{18,... | collective-permute-start | bytes 589832 | tf_op jit(solution)/shard_map/ppermute | solution.py:288
  11.9 0.7 %shard_map.77 = (bf16[4,64,768]{2,1,0:T(8,128)(2,1)S(1)}, bf16[4,64,384]{2,1,0:T(8,128)(2,1)S(1)}) custom-call(bf16[4,192,768]{2,1,0:T(8,128)(2,1)S(1)} %get-tuple-element.40.refs_0_, f32[4,256,384]{2,1,0:T(8,128)S(1)} %get-tuple-element.41.refs_1_, f32[4,64,384]{2,1,0:T(8,128)S(1)} %get-tuple-element.43.refs_2_, f32[4,384]{1,0:T(4,128)S(1)} %copy-done.3, ...), custom_call_target="tpu_custom_call" | custom-call | flops 6039797760 | bytes 6039797 | tf_op jit(solution)/shard_map/pallas_call | solution.py:309
  12.6 1.4 %collective-permute-start.5 = (bf16[4,64,384]{2,1,0:T(8,128)(2,1)S(1)}, bf16[4,64,384]{2,1,0:T(8,128)(2,1)S(1)}, u32[]{:S(2)}, u32[]{:S(2)}) collective-permute-start(bf16[4,64,384]{2,1,0:T(8,128)(2,1)S(1)} %get-tuple-element.57), channel_id=1, source_target_pairs={{1,2},{3,4},{5,6},{7,8},{9,10},{11,12},{13,14},{17,18},{19,20},{21... | collective-permute-start | bytes 589832 | tf_op jit(solution)/shard_map/ppermute | solution.py:285
  14.0 1.9 %shard_map.78 = (bf16[4,128,768]{2,1,0:T(8,128)(2,1)S(1)}, bf16[4,128,384]{2,1,0:T(8,128)(2,1)S(1)}, f32[4,256,384]{2,1,0:T(8,128)S(1)}, f32[4,64,384]{2,1,0:T(8,128)S(1)}, f32[4,64,384]{2,1,0:T(8,128)S(1)}) custom-call(bf16[4,192,768]{2,1,0:T(8,128)(2,1)S(1)} %get-tuple-element.40.refs_0_, f32[4,256,384]{2,1,0:T(8,128)S(1)} %get-tuple-element.41.refs_1_, ...), custom_call_target="tpu_custom_call" | custom-call | flops 12079595520 | bytes 12079595 | tf_op jit(solution)/shard_map/pallas_call | solution.py:309
  15.9 0.5 %collective-permute-start.4 = (bf16[4,128,384]{2,1,0:T(8,128)(2,1)S(1)}, bf16[4,128,384]{2,1,0:T(8,128)(2,1)S(1)}, u32[]{:S(2)}, u32[]{:S(2)}) collective-permute-start(bf16[4,128,384]{2,1,0:T(8,128)(2,1)S(1)} %get-tuple-element.51), channel_id=1, source_target_pairs={{0,1},{2,3},{4,5},{6,7},{8,9},{10,11},{12,13},{14,15},{16,17},{18,... | collective-permute-start | bytes 1179656 | tf_op jit(solution)/shard_map/ppermute | solution.py:288
  16.5 0.9 %shard_map.79 = (bf16[4,64,768]{2,1,0:T(8,128)(2,1)S(1)}, bf16[4,64,384]{2,1,0:T(8,128)(2,1)S(1)}, f32[4,64,384]{2,1,0:T(8,128)S(1)}, f32[4,64,384]{2,1,0:T(8,128)S(1)}) custom-call(bf16[4,64,768]{2,1,0:T(8,128)(2,1)S(1)} %get-tuple-element.47.refs_0_, f32[4,256,384]{2,1,0:T(8,128)S(1)} %get-tuple-element.41.refs_1_, ...), custom_call_target="tpu_custom_call" | custom-call | flops 6039797760 | bytes 6039797 | tf_op jit(solution)/shard_map/pallas_call | solution.py:309
  17.4 0.4 collective-permute-start.6
  17.8 1.8 %shard_map.80 = (bf16[4,128,768]{2,1,0:T(8,128)(2,1)S(1)}, bf16[4,128,384]{2,1,0:T(8,128)(2,1)S(1)}, bf16[4,128,384]{2,1,0:T(8,128)(2,1)S(1)}, f32[4,128,384]{2,1,0:T(8,128)S(1)}) custom-call(bf16[4,128,768]{2,1,0:T(8,128)(2,1)S(1)} %get-tuple-element.45.refs_0_, f32[4,256,384]{2,1,0:T(8,128)S(1)} %get-tuple-element.46.refs_10_.refs_1_.refs_2_, ...), custom_call_target="tpu_custom_call" | custom-call | flops 12079595520 | bytes 12079595 | tf_op jit(solution)/shard_map/pallas_call | solution.py:309
  19.6 0.8 %collective-permute-start.11 = (bf16[4,128,384]{2,1,0:T(8,128)(2,1)S(1)}, bf16[4,128,384]{2,1,0:T(8,128)(2,1)S(1)}, u32[]{:S(2)}, u32[]{:S(2)}) collective-permute-start(bf16[4,128,384]{2,1,0:T(8,128)(2,1)S(1)} %get-tuple-element.66), channel_id=1, source_target_pairs={{0,1},{2,3},{4,5},{6,7},{8,9},{10,11},{12,13},{14,15},{16,17},{18,... | collective-permute-start | bytes 1179656 | tf_op jit(solution)/shard_map/ppermute | solution.py:288
  20.4 0.8 %collective-permute-start.12 = (bf16[4,128,384]{2,1,0:T(8,128)(2,1)S(1)}, bf16[4,128,384]{2,1,0:T(8,128)(2,1)S(1)}, u32[]{:S(2)}, u32[]{:S(2)}) collective-permute-start(bf16[4,128,384]{2,1,0:T(8,128)(2,1)S(1)} %get-tuple-element.67), channel_id=1, source_target_pairs={{1,2},{3,4},{5,6},{7,8},{9,10},{11,12},{13,14},{17,18},{19,20},{21... | collective-permute-start | bytes 1179656 | tf_op jit(solution)/shard_map/ppermute | solution.py:285
  21.1 7.7 %collective-permute-done.6.refs_6_ = bf16[4,64,384]{2,1,0:T(8,128)(2,1)S(1)} collective-permute-done((bf16[4,64,384]{2,1,0:T(8,128)(2,1)S(1)}, bf16[4,64,384]{2,1,0:T(8,128)(2,1)S(1)}, u32[]{:S(2)}, u32[]{:S(2)}) %collective-permute-start.6) | collective-permute-done | bytes 196640 | tf_op jit(solution)/shard_map/ppermute | solution.py:285
  28.9 0.9 %shard_map.81 = (bf16[2,128,768]{2,1,0:T(8,128)(2,1)S(1)}, bf16[2,128,384]{2,1,0:T(8,128)(2,1)S(1)}, bf16[2,128,384]{2,1,0:T(8,128)(2,1)S(1)}, f32[2,128,384]{2,1,0:T(8,128)S(1)}) custom-call(bf16[4,64,768]{2,1,0:T(8,128)(2,1)S(1)} %get-tuple-element.54.refs_0_, bf16[4,64,768]{2,1,0:T(8,128)(2,1)S(1)} %get-tuple-element.44.refs_3_.refs_1_, ...), custom_call_target="tpu_custom_call" | custom-call | flops 6039797760 | bytes 6039797 | tf_op jit(solution)/shard_map/pallas_call | solution.py:309
  29.8 0.1 collective-permute-start.9
  30.0 1.2 %shard_map.82 = (bf16[2,128,768]{2,1,0:T(8,128)(2,1)S(1)}, bf16[2,128,384]{2,1,0:T(8,128)(2,1)S(1)}, bf16[2,128,384]{2,1,0:T(8,128)(2,1)S(1)}, f32[2,128,384]{2,1,0:T(8,128)S(1)}) custom-call(bf16[4,64,768]{2,1,0:T(8,128)(2,1)S(1)} %get-tuple-element.54.refs_0_, bf16[4,64,768]{2,1,0:T(8,128)(2,1)S(1)} %get-tuple-element.44.refs_3_.refs_1_, ...), custom_call_target="tpu_custom_call" | custom-call | flops 6039797760 | bytes 6039797 | tf_op jit(solution)/shard_map/pallas_call | solution.py:309
  31.1 0.5 %collective-permute-start.7 = (bf16[2,128,384]{2,1,0:T(8,128)(2,1)S(1)}, bf16[2,128,384]{2,1,0:T(8,128)(2,1)S(1)}, u32[]{:S(2)}, u32[]{:S(2)}) collective-permute-start(bf16[2,128,384]{2,1,0:T(8,128)(2,1)S(1)} %get-tuple-element.60), channel_id=1, source_target_pairs={{0,1},{2,3},{4,5},{6,7},{8,9},{10,11},{12,13},{14,15},{16,17},{18,... | collective-permute-start | bytes 589832 | tf_op jit(solution)/shard_map/ppermute | solution.py:288
  31.6 1.4 %collective-permute-start.8 = (bf16[2,128,384]{2,1,0:T(8,128)(2,1)S(1)}, bf16[2,128,384]{2,1,0:T(8,128)(2,1)S(1)}, u32[]{:S(2)}, u32[]{:S(2)}) collective-permute-start(bf16[2,128,384]{2,1,0:T(8,128)(2,1)S(1)} %get-tuple-element.61), channel_id=1, source_target_pairs={{1,2},{3,4},{5,6},{7,8},{9,10},{11,12},{13,14},{17,18},{19,20},{21... | collective-permute-start | bytes 589832 | tf_op jit(solution)/shard_map/ppermute | solution.py:285
  33.0 0.1 collective-permute-done.12.inter_ref
  33.1 1.1 %shard_map.83.refs_3_ = bf16[4,256,768]{2,1,0:T(8,128)(2,1)} custom-call(bf16[2,128,768]{2,1,0:T(8,128)(2,1)S(1)} %get-tuple-element.68.stream_ref, f32[2,128,384]{2,1,0:T(8,128)S(1)} %get-tuple-element.59.refs_13_.local_ref, bf16[4,128,384]{2,1,0:T(8,128)(2,1)S(1)} %collective-permute-done.11.intra_ref, ...), custom_call_target="tpu_custom_call" | custom-call | flops 1509949440 | bytes 1509949 | tf_op jit(solution)/shard_map/pallas_call | solution.py:461
  34.2 1.1 %shard_map.84.refs_3_ = bf16[4,256,768]{2,1,0:T(8,128)(2,1)} custom-call(bf16[2,128,768]{2,1,0:T(8,128)(2,1)S(1)} %get-tuple-element.64.stream_ref, f32[2,128,384]{2,1,0:T(8,128)S(1)} %get-tuple-element.65.local_ref, bf16[4,128,384]{2,1,0:T(8,128)(2,1)S(1)} %collective-permute-done.11.intra_ref, ...), custom_call_target="tpu_custom_call", output_to_operand_aliasing={{}: (7, {})} | custom-call | flops 1509949440 | bytes 1509949 | tf_op jit(solution)/shard_map/pallas_call | solution.py:461
  35.3 4.1 %collective-permute-done.10.inter_ref = bf16[2,128,384]{2,1,0:T(8,128)(2,1)S(1)} collective-permute-done((bf16[2,128,384]{2,1,0:T(8,128)(2,1)S(1)}, bf16[2,128,384]{2,1,0:T(8,128)(2,1)S(1)}, u32[]{:S(2)}, u32[]{:S(2)}) %collective-permute-start.10) | collective-permute-done | bytes 196640 | tf_op jit(solution)/shard_map/ppermute | solution.py:285
  39.4 1.1 %shard_map.85.refs_3_ = bf16[4,256,768]{2,1,0:T(8,128)(2,1)} custom-call(bf16[4,128,768]{2,1,0:T(8,128)(2,1)S(1)} %get-tuple-element.52.stream_ref, f32[4,128,384]{2,1,0:T(8,128)S(1)} %get-tuple-element.53.refs_13_.local_ref, bf16[2,128,384]{2,1,0:T(8,128)(2,1)S(1)} %collective-permute-done.9.intra_ref, ...), custom_call_target="tpu_custom_call", output_to_operand_aliasing={{}: (7, {})} | custom-call | flops 1509949440 | bytes 1509949 | tf_op jit(solution)/shard_map/pallas_call | solution.py:461
  40.5 1.0 %collective-permute-done.8.inter_ref = bf16[2,128,384]{2,1,0:T(8,128)(2,1)S(1)} collective-permute-done((bf16[2,128,384]{2,1,0:T(8,128)(2,1)S(1)}, bf16[2,128,384]{2,1,0:T(8,128)(2,1)S(1)}, u32[]{:S(2)}, u32[]{:S(2)}) %collective-permute-start.8) | collective-permute-done | bytes 196640 | tf_op jit(solution)/shard_map/ppermute | solution.py:285
  41.5 1.1 %shard_map.86 = bf16[4,256,768]{2,1,0:T(8,128)(2,1)} custom-call(bf16[4,128,768]{2,1,0:T(8,128)(2,1)S(1)} %get-tuple-element.52.stream_ref, f32[4,128,384]{2,1,0:T(8,128)S(1)} %get-tuple-element.53.refs_13_.local_ref, bf16[2,128,384]{2,1,0:T(8,128)(2,1)S(1)} %collective-permute-done.7.intra_ref, ...), custom_call_target="tpu_custom_call", output_to_operand_aliasing={{}: (7, {})} | custom-call | flops 1509949440 | bytes 1509949 | tf_op jit(solution)/shard_map/pallas_call | solution.py:461
  (22 shorter events, 0.1 us)
Async XLA Ops:
  0.0 3.6 %copy-start.1 = (bf16[4,3,768,384]{3,2,1,0:T(8,128)(2,1)S(1)}, bf16[4,3,768,384]{3,2,1,0:T(8,128)(2,1)}, u32[]{:S(2)}) copy-start(bf16[4,3,768,384]{3,2,1,0:T(8,128)(2,1)} %refs_12_.3) | copy-start | bytes 21233668
  0.0 3.6 %copy-start.6 = (f32[4,768]{1,0:T(4,128)S(1)}, f32[4,768]{1,0:T(4,128)}, u32[]{:S(2)}) copy-start(f32[4,768]{1,0:T(4,128)} %refs_11_.3) | copy-start | bytes 36868
  0.0 3.6 %copy-start.5 = (f32[4,768]{1,0:T(4,128)S(1)}, f32[4,768]{1,0:T(4,128)}, u32[]{:S(2)}) copy-start(f32[4,768]{1,0:T(4,128)} %refs_10_.5) | copy-start | bytes 36868
  0.0 3.7 %copy-start.2 = (bf16[4,256,768]{2,1,0:T(8,128)(2,1)S(1)}, bf16[4,256,768]{2,1,0:T(8,128)(2,1)}, u32[]{:S(2)}) copy-start(bf16[4,256,768]{2,1,0:T(8,128)(2,1)} %refs_0_.7) | copy-start | bytes 4718596
  1.7 5.4 %copy-start = (bf16[4,384,768]{2,1,0:T(8,128)(2,1)S(1)}, bf16[4,384,768]{2,1,0:T(8,128)(2,1)}, u32[]{:S(2)}) copy-start(bf16[4,384,768]{2,1,0:T(8,128)(2,1)} %refs_2_.7) | copy-start | bytes 7077892
  1.7 5.4 %copy-start.3 = (f32[4,384]{1,0:T(4,128)S(1)}, f32[4,384]{1,0:T(4,128)}, u32[]{:S(2)}) copy-start(f32[4,384]{1,0:T(4,128)} %refs_0_.11) | copy-start | bytes 18436
  1.7 5.4 %copy-start.4 = (f32[4,384]{1,0:T(4,128)S(1)}, f32[4,384]{1,0:T(4,128)}, u32[]{:S(2)}) copy-start(f32[4,384]{1,0:T(4,128)} %refs_1_.7) | copy-start | bytes 18436
  1.7 5.3 %collective-permute-start.1 = (bf16[4,32,384]{2,1,0:T(8,128)(2,1)S(1)}, bf16[4,32,384]{2,1,0:T(8,128)(2,1)S(1)}, u32[]{:S(2)}, u32[]{:S(2)}) collective-permute-start(bf16[4,32,384]{2,1,0:T(8,128)(2,1)S(1)} %shard_map.74), channel_id=1, source_target_pairs={{1,2},{3,4},{5,6},{7,8},{9,10},{11,12},{13,14},{17,18},{19,20},{21... | collective-permute-start | bytes 294920 | tf_op jit(solution)/shard_map/ppermute | solution.py:285
  6.1 2.9 %collective-permute-start = (bf16[4,32,384]{2,1,0:T(8,128)(2,1)S(1)}, bf16[4,32,384]{2,1,0:T(8,128)(2,1)S(1)}, u32[]{:S(2)}, u32[]{:S(2)}) collective-permute-start(bf16[4,32,384]{2,1,0:T(8,128)(2,1)S(1)} %get-tuple-element.38), channel_id=1, source_target_pairs={{0,1},{2,3},{4,5},{6,7},{8,9},{10,11},{12,13},{14,15},{16,17},{18,... | collective-permute-start | bytes 294920 | tf_op jit(solution)/shard_map/ppermute | solution.py:288
  8.0 8.5 %collective-permute-start.3 = (bf16[4,64,384]{2,1,0:T(8,128)(2,1)S(1)}, bf16[4,64,384]{2,1,0:T(8,128)(2,1)S(1)}, u32[]{:S(2)}, u32[]{:S(2)}) collective-permute-start(bf16[4,64,384]{2,1,0:T(8,128)(2,1)S(1)} %get-tuple-element.48), channel_id=1, source_target_pairs={{1,2},{3,4},{5,6},{7,8},{9,10},{11,12},{13,14},{17,18},{19,20},{21... | collective-permute-start | bytes 589832 | tf_op jit(solution)/shard_map/ppermute | solution.py:285
  11.5 2.5 %collective-permute-start.2 = (bf16[4,64,384]{2,1,0:T(8,128)(2,1)S(1)}, bf16[4,64,384]{2,1,0:T(8,128)(2,1)S(1)}, u32[]{:S(2)}, u32[]{:S(2)}) collective-permute-start(bf16[4,64,384]{2,1,0:T(8,128)(2,1)S(1)} %get-tuple-element.42), channel_id=1, source_target_pairs={{0,1},{2,3},{4,5},{6,7},{8,9},{10,11},{12,13},{14,15},{16,17},{18,... | collective-permute-start | bytes 589832 | tf_op jit(solution)/shard_map/ppermute | solution.py:288
  12.6 8.6 %collective-permute-start.5 = (bf16[4,64,384]{2,1,0:T(8,128)(2,1)S(1)}, bf16[4,64,384]{2,1,0:T(8,128)(2,1)S(1)}, u32[]{:S(2)}, u32[]{:S(2)}) collective-permute-start(bf16[4,64,384]{2,1,0:T(8,128)(2,1)S(1)} %get-tuple-element.57), channel_id=1, source_target_pairs={{1,2},{3,4},{5,6},{7,8},{9,10},{11,12},{13,14},{17,18},{19,20},{21... | collective-permute-start | bytes 589832 | tf_op jit(solution)/shard_map/ppermute | solution.py:285
  15.9 1.9 %collective-permute-start.4 = (bf16[4,128,384]{2,1,0:T(8,128)(2,1)S(1)}, bf16[4,128,384]{2,1,0:T(8,128)(2,1)S(1)}, u32[]{:S(2)}, u32[]{:S(2)}) collective-permute-start(bf16[4,128,384]{2,1,0:T(8,128)(2,1)S(1)} %get-tuple-element.51), channel_id=1, source_target_pairs={{0,1},{2,3},{4,5},{6,7},{8,9},{10,11},{12,13},{14,15},{16,17},{18,... | collective-permute-start | bytes 1179656 | tf_op jit(solution)/shard_map/ppermute | solution.py:288
  17.4 11.5 %collective-permute-start.6 = (bf16[4,64,384]{2,1,0:T(8,128)(2,1)S(1)}, bf16[4,64,384]{2,1,0:T(8,128)(2,1)S(1)}, u32[]{:S(2)}, u32[]{:S(2)}) collective-permute-start(bf16[4,64,384]{2,1,0:T(8,128)(2,1)S(1)} %get-tuple-element.58), channel_id=1, source_target_pairs={{1,2},{3,4},{5,6},{7,8},{9,10},{11,12},{13,14},{17,18},{19,20},{21... | collective-permute-start | bytes 589832 | tf_op jit(solution)/shard_map/ppermute | solution.py:285
  19.6 12.0 %collective-permute-start.11 = (bf16[4,128,384]{2,1,0:T(8,128)(2,1)S(1)}, bf16[4,128,384]{2,1,0:T(8,128)(2,1)S(1)}, u32[]{:S(2)}, u32[]{:S(2)}) collective-permute-start(bf16[4,128,384]{2,1,0:T(8,128)(2,1)S(1)} %get-tuple-element.66), channel_id=1, source_target_pairs={{0,1},{2,3},{4,5},{6,7},{8,9},{10,11},{12,13},{14,15},{16,17},{18,... | collective-permute-start | bytes 1179656 | tf_op jit(solution)/shard_map/ppermute | solution.py:288
  20.4 12.7 %collective-permute-start.12 = (bf16[4,128,384]{2,1,0:T(8,128)(2,1)S(1)}, bf16[4,128,384]{2,1,0:T(8,128)(2,1)S(1)}, u32[]{:S(2)}, u32[]{:S(2)}) collective-permute-start(bf16[4,128,384]{2,1,0:T(8,128)(2,1)S(1)} %get-tuple-element.67), channel_id=1, source_target_pairs={{1,2},{3,4},{5,6},{7,8},{9,10},{11,12},{13,14},{17,18},{19,20},{21... | collective-permute-start | bytes 1179656 | tf_op jit(solution)/shard_map/ppermute | solution.py:285
  29.8 5.5 %collective-permute-start.9 = (bf16[2,128,384]{2,1,0:T(8,128)(2,1)S(1)}, bf16[2,128,384]{2,1,0:T(8,128)(2,1)S(1)}, u32[]{:S(2)}, u32[]{:S(2)}) collective-permute-start(bf16[2,128,384]{2,1,0:T(8,128)(2,1)S(1)} %get-tuple-element.62), channel_id=1, source_target_pairs={{0,1},{2,3},{4,5},{6,7},{8,9},{10,11},{12,13},{14,15},{16,17},{18,... | collective-permute-start | bytes 589832 | tf_op jit(solution)/shard_map/ppermute | solution.py:288
  29.9 9.5 %collective-permute-start.10 = (bf16[2,128,384]{2,1,0:T(8,128)(2,1)S(1)}, bf16[2,128,384]{2,1,0:T(8,128)(2,1)S(1)}, u32[]{:S(2)}, u32[]{:S(2)}) collective-permute-start(bf16[2,128,384]{2,1,0:T(8,128)(2,1)S(1)} %get-tuple-element.63), channel_id=1, source_target_pairs={{1,2},{3,4},{5,6},{7,8},{9,10},{11,12},{13,14},{17,18},{19,20},{21... | collective-permute-start | bytes 589832 | tf_op jit(solution)/shard_map/ppermute | solution.py:285
  31.1 9.4 %collective-permute-start.7 = (bf16[2,128,384]{2,1,0:T(8,128)(2,1)S(1)}, bf16[2,128,384]{2,1,0:T(8,128)(2,1)S(1)}, u32[]{:S(2)}, u32[]{:S(2)}) collective-permute-start(bf16[2,128,384]{2,1,0:T(8,128)(2,1)S(1)} %get-tuple-element.60), channel_id=1, source_target_pairs={{0,1},{2,3},{4,5},{6,7},{8,9},{10,11},{12,13},{14,15},{16,17},{18,... | collective-permute-start | bytes 589832 | tf_op jit(solution)/shard_map/ppermute | solution.py:288
  31.6 9.9 %collective-permute-start.8 = (bf16[2,128,384]{2,1,0:T(8,128)(2,1)S(1)}, bf16[2,128,384]{2,1,0:T(8,128)(2,1)S(1)}, u32[]{:S(2)}, u32[]{:S(2)}) collective-permute-start(bf16[2,128,384]{2,1,0:T(8,128)(2,1)S(1)} %get-tuple-element.61), channel_id=1, source_target_pairs={{1,2},{3,4},{5,6},{7,8},{9,10},{11,12},{13,14},{17,18},{19,20},{21... | collective-permute-start | bytes 589832 | tf_op jit(solution)/shard_map/ppermute | solution.py:285

commit v8 on v7

--- a/solution.py
+++ b/solution.py
@@ -347,48 +347,64 @@
     )(tower_in, *norms, conv_weight)
     intra_0 = across(intra)
 
-    rest = (two, rows)
+    edges, middle, inner, ends = (0, two), (two, three), (three, rows - two), (rows - two, rows)
+    near = (three, rows)
+    stream_1p, _, (local_1p,) = step(
+        0, inner,
+        [(everything, tower_in)],
+        [(everything, False, local_0)],
+        [],
+        [((two, rows), [("here", inner, 0), ("out", inner, -two), ("inn", inner, two)])],
+    )
     stream_1f, (inter,), (here_1f, inn_1f) = step(
-        0, (0, two),
+        0, edges,
         [(everything, tower_in)],
         [(everything, False, local_0), ((0, one), True, inter_0)],
-        [("out", (0, two))],
-        [((0, two), [("here", (0, two), 0)]), ((two, 2 * two), [("inn", (0, two), two)])],
+        [("out", edges)],
+        [(edges, [("here", edges, 0)]), (middle, [("inn", edges, two)])],
+        after=(local_1p,),
     )
     inter_1 = cross(inter)
-    stream_1n, (intra,), (local_1n,) = step(
-        0, rest,
+    stream_1m, _, (local_1m,) = step(
+        0, middle,
+        [(everything, tower_in)],
+        [(everything, False, local_0)],
+        [],
+        [((0, rows - two), [("here", middle, 0), ("out", middle, -two), ("inn", middle, two)])],
+        after=(here_1f,),
+    )
+    stream_1e, (intra,), (local_1e,) = step(
+        0, ends,
         [(everything, tower_in)],
         [(everything, False, local_0), ((rows - one, rows), False, intra_0)],
-        [("inn", (rows - two, rows))],
-        [
-            (
-                everything,
-                [
-                    ("here", rest, 0),
-                    ("out", rest, -two),
-                    ("inn", (two, rows - two), two),
-                ],
-            )
-        ],
-        after=(here_1f,),
+        [("inn", ends)],
+        [((three, rows), [("here", ends, 0), ("out", ends, -two)])],
+        after=(local_1m,),
     )
     intra_1 = across(intra)
-    streams = [((0, two), stream_1f), (rest, stream_1n)]
-
-    middle, near = (two, three), (three, rows)
+
     stream_2m, (inter,), _ = step(
         1, middle,
-        streams[1:],
-        [(everything, False, local_1n), ((two, 2 * two), False, inn_1f)],
+        [(middle, stream_1m)],
+        [
+            ((two, rows), False, local_1p),
+            ((0, rows - two), False, local_1m),
+            (middle, False, inn_1f),
+        ],
         [("out", middle)],
         [],
+        after=(local_1e,),
     )
     inter_2m = cross(inter)
     stream_2n, (intra,), (local_2n, here_2m, inn_2m) = step(
         1, near,
-        streams[1:],
-        [(everything, False, local_1n), ((rows - two, rows), False, intra_1)],
+        [(inner, stream_1p), (ends, stream_1e)],
+        [
+            ((two, rows), False, local_1p),
+            ((0, rows - two), False, local_1m),
+            (near, False, local_1e),
+            (ends, False, intra_1),
+        ],
         [("inn", near)],
         [(everything, [("here", near, 0), ("out", near, -three)])],
         late=[
@@ -400,15 +416,15 @@
     )
     intra_2 = across(intra)
     stream_2f, (inter,), (here_2f, inn_2f) = step(
-        1, (0, two),
-        streams[:1],
+        1, edges,
+        [(edges, stream_1f)],
         [
-            (everything, False, local_1n),
-            ((0, two), False, here_1f),
-            ((0, two), True, inter_1),
+            ((0, rows - two), False, local_1m),
+            (edges, False, here_1f),
+            (edges, True, inter_1),
         ],
-        [("out", (0, two))],
-        [((0, two), [("here", (0, two), 0)]), ((three, three + two), [("inn", (0, two), three)])],
+        [("out", edges)],
+        [(edges, [("here", edges, 0)]), ((three, three + two), [("inn", edges, three)])],
         after=(local_2n,),
     )
     inter_2f = cross(inter)
@@ -427,7 +443,7 @@
     )
     inter_3n, intra_3n = cross(inter), across(intra)
     parts = [(0, tracks // 2), (tracks // 2, tracks - tracks // 2)]
-    ends, after = [], (local_3n,)
+    last, after = [], (local_3n,)
     for first, part in parts:
         stream_3f, (inter, intra), (local_3f,) = step(
             2, (0, three),
@@ -444,10 +460,10 @@
             after=after, first=first, part=part,
         )
         after = (local_3f,)
-        ends.append((stream_3f, local_3f, cross(inter), across(intra)))
+        last.append((stream_3f, local_3f, cross(inter), across(intra)))
 
     far_ends, near_ends = [], []
-    for (first, part), (stream_3f, local_3f, inter, intra) in zip(parts, ends):
+    for (first, part), (stream_3f, local_3f, inter, intra) in zip(parts, last):
         far_ends.append(
             ((0, three), first, part, (0, 0, first, first), (stream_3f, local_3f, intra_3n, inter_3n))
         )

time: 43.1 us -> 43 us (level)
    pallas_call x8 -> x10, Pallas kernels: 10.8 us -> 11.1 us  [step(): pl.pallas_call(functools.partial(step_kernel, plan), in_specs=[vmem] * (l...]
  transfers between devices with their start and end apart: 13 -> 13, of which waited for: 5 -> 5; matrix products, arithmetic and copies ran while one was open for 0% -> 0% of each run, Pallas kernels for 38% -> 39%
where the time goes in v8:
time: 43 us; the launch traced here: 42.8 us
  Pallas kernels  19.4 us (45%)
  waiting for transfers between devices  13 us (30%)
  starting transfers between devices  9.74 us (23%)
    ppermute x7, waiting for transfers between devices, cross(): return lax.ppermute(value, ('groups', 'seq'), inter_pairs)  12.8 us
    pallas_call x10, Pallas kernels, step(): pl.pallas_call(functools.partial(step_kernel, plan), in_specs=[vmem] * (l...  11.1 us
    ppermute x7, starting transfers between devices, cross(): return lax.ppermute(value, ('groups', 'seq'), inter_pairs)  7.09 us
    pallas_call x4, Pallas kernels, local(): pl.pallas_call(functools.partial(last_kernel, blocks - 1, q, rows, first,...  4.36 us
    ppermute x6, starting transfers between devices, across(): return lax.ppermute(value, ('groups', 'seq'), intra_pairs)  2.65 us
    pallas_call x1, Pallas kernels, local(): pl.pallas_call(functools.partial(entry_kernel, one), in_specs=[vmem] * 4,...  2.31 us
    pallas_call x1, Pallas kernels, local(): pl.pallas_call(functools.partial(edge_kernel, one), in_specs=[hbm] * 4, o...  1.63 us
  transfers between devices with their start and end apart: 13, of which 5 were waited for; matrix products, arithmetic and copies ran while one was open for 0% of the time, Pallas kernels for 39%

profile of v8, /device:TPU:25, one launch (start us, length us, event | category | flops | bytes accessed | tf_op | source)
XLA Modules:
  0.0 42.8 jit_solution(14878884692676484292)
XLA Ops:
  0.0 1.6 %shard_map.75 = bf16[4,32,384]{2,1,0:T(8,128)(2,1)S(1)} custom-call(bf16[4,256,768]{2,1,0:T(8,128)(2,1)} %refs_0_.11, f32[4,768]{1,0:T(4,128)} %refs_10_.7, f32[4,768]{1,0:T(4,128)} %refs_11_.5, bf16[4,3,768,384]{3,2,1,0:T(8,128)(2,1)} %refs_12_.5), custom_call_target="tpu_custom_call" | custom-call | flops 2264924160 | bytes 2264924 | tf_op jit(solution)/shard_map/pallas_call | solution.py:328
  1.7 1.9 %collective-permute-start.1 = (bf16[4,32,384]{2,1,0:T(8,128)(2,1)S(1)}, bf16[4,32,384]{2,1,0:T(8,128)(2,1)S(1)}, u32[]{:S(2)}, u32[]{:S(2)}) collective-permute-start(bf16[4,32,384]{2,1,0:T(8,128)(2,1)S(1)} %shard_map.75), channel_id=1, source_target_pairs={{1,2},{3,4},{5,6},{7,8},{9,10},{11,12},{13,14},{17,18},{19,20},{21... | collective-permute-start | bytes 294920 | tf_op jit(solution)/shard_map/ppermute | solution.py:285
  3.6 0.2 copy-done.2
  3.8 2.3 %shard_map.73 = (f32[4,256,384]{2,1,0:T(8,128)S(1)}, bf16[4,32,384]{2,1,0:T(8,128)(2,1)S(1)}) custom-call(bf16[4,256,768]{2,1,0:T(8,128)(2,1)S(1)} %copy-done.2, f32[4,768]{1,0:T(4,128)S(1)} %copy-done.5, f32[4,768]{1,0:T(4,128)S(1)} %copy-done.6, bf16[4,3,768,384]{3,2,1,0:T(8,128)(2,1)S(1)} %copy-done.1), custom_call_target="tpu_custom_call" | custom-call | flops 18119393280 | bytes 18119392 | tf_op jit(solution)/shard_map/pallas_call | solution.py:340
  6.1 0.7 %collective-permute-start = (bf16[4,32,384]{2,1,0:T(8,128)(2,1)S(1)}, bf16[4,32,384]{2,1,0:T(8,128)(2,1)S(1)}, u32[]{:S(2)}, u32[]{:S(2)}) collective-permute-start(bf16[4,32,384]{2,1,0:T(8,128)(2,1)S(1)} %get-tuple-element.43), channel_id=1, source_target_pairs={{0,1},{2,3},{4,5},{6,7},{8,9},{10,11},{12,13},{14,15},{16,17},{18,... | collective-permute-start | bytes 294920 | tf_op jit(solution)/shard_map/ppermute | solution.py:288
  6.8 0.9 %shard_map.74 = (bf16[4,64,768]{2,1,0:T(8,128)(2,1)S(1)}, f32[4,192,384]{2,1,0:T(8,128)S(1)}) custom-call(bf16[4,256,768]{2,1,0:T(8,128)(2,1)S(1)} %copy-done.2, f32[4,256,384]{2,1,0:T(8,128)S(1)} %get-tuple-element.41.refs_1_, f32[4,384]{1,0:T(4,128)S(1)} %copy-done.3, f32[4,384]{1,0:T(4,128)S(1)} %copy-done.4, bf16[4,384,768]{2,1,0:T(8,128)(2,1)S(1)} %copy-done, ...), custom_call_target="tpu_custom_call" | custom-call | flops 6039797760 | bytes 6039797 | tf_op jit(solution)/shard_map/pallas_call | solution.py:309
  7.8 0.9 %shard_map.76 = (bf16[4,64,768]{2,1,0:T(8,128)(2,1)S(1)}, bf16[4,64,384]{2,1,0:T(8,128)(2,1)S(1)}, f32[4,64,384]{2,1,0:T(8,128)S(1)}, f32[4,64,384]{2,1,0:T(8,128)S(1)}) custom-call(bf16[4,256,768]{2,1,0:T(8,128)(2,1)S(1)} %copy-done.2, f32[4,256,384]{2,1,0:T(8,128)S(1)} %get-tuple-element.41.refs_1_, ...), custom_call_target="tpu_custom_call" | custom-call | flops 6039797760 | bytes 6039797 | tf_op jit(solution)/shard_map/pallas_call | solution.py:309
  8.7 1.2 %collective-permute-start.3 = (bf16[4,64,384]{2,1,0:T(8,128)(2,1)S(1)}, bf16[4,64,384]{2,1,0:T(8,128)(2,1)S(1)}, u32[]{:S(2)}, u32[]{:S(2)}) collective-permute-start(bf16[4,64,384]{2,1,0:T(8,128)(2,1)S(1)} %get-tuple-element.56), channel_id=1, source_target_pairs={{1,2},{3,4},{5,6},{7,8},{9,10},{11,12},{13,14},{17,18},{19,20},{21... | collective-permute-start | bytes 589832 | tf_op jit(solution)/shard_map/ppermute | solution.py:285
  9.9 0.9 %shard_map.77 = (bf16[4,64,768]{2,1,0:T(8,128)(2,1)S(1)}, f32[4,192,384]{2,1,0:T(8,128)S(1)}) custom-call(bf16[4,256,768]{2,1,0:T(8,128)(2,1)S(1)} %copy-done.2, f32[4,256,384]{2,1,0:T(8,128)S(1)} %get-tuple-element.41.refs_1_, f32[4,384]{1,0:T(4,128)S(1)} %copy-done.3, f32[4,384]{1,0:T(4,128)S(1)} %copy-done.4, bf16[4,384,768]{2,1,0:T(8,128)(2,1)S(1)} %copy-done, ...), custom_call_target="tpu_custom_call" | custom-call | flops 6039797760 | bytes 6039797 | tf_op jit(solution)/shard_map/pallas_call | solution.py:309
  10.8 0.9 %shard_map.78 = (bf16[4,64,768]{2,1,0:T(8,128)(2,1)S(1)}, bf16[4,64,384]{2,1,0:T(8,128)(2,1)S(1)}, f32[4,128,384]{2,1,0:T(8,128)S(1)}) custom-call(bf16[4,256,768]{2,1,0:T(8,128)(2,1)S(1)} %copy-done.2, f32[4,256,384]{2,1,0:T(8,128)S(1)} %get-tuple-element.41.refs_1_, bf16[4,32,384]{2,1,0:T(8,128)(2,1)S(1)} %collective-permute-done.refs_2_, ...), custom_call_target="tpu_custom_call" | custom-call | flops 6039797760 | bytes 6039797 | tf_op jit(solution)/shard_map/pallas_call | solution.py:309
  11.8 0.4 collective-permute-start.2
  12.2 0.7 %shard_map.79 = (bf16[4,64,768]{2,1,0:T(8,128)(2,1)S(1)}, bf16[4,64,384]{2,1,0:T(8,128)(2,1)S(1)}) custom-call(bf16[4,64,768]{2,1,0:T(8,128)(2,1)S(1)} %get-tuple-element.50.refs_0_, f32[4,192,384]{2,1,0:T(8,128)S(1)} %get-tuple-element.44.refs_9_.refs_1_.refs_2_, f32[4,192,384]{2,1,0:T(8,128)S(1)} %get-tuple-element.46.refs_9_.refs_2_.refs_3_.refs_1_, ...), custom_call_target="tpu_custom_call" | custom-call | flops 6039797760 | bytes 6039797 | tf_op jit(solution)/shard_map/pallas_call | solution.py:309
  12.9 1.6 %collective-permute-start.5 = (bf16[4,64,384]{2,1,0:T(8,128)(2,1)S(1)}, bf16[4,64,384]{2,1,0:T(8,128)(2,1)S(1)}, u32[]{:S(2)}, u32[]{:S(2)}) collective-permute-start(bf16[4,64,384]{2,1,0:T(8,128)(2,1)S(1)} %get-tuple-element.65), channel_id=1, source_target_pairs={{1,2},{3,4},{5,6},{7,8},{9,10},{11,12},{13,14},{17,18},{19,20},{21... | collective-permute-start | bytes 589832 | tf_op jit(solution)/shard_map/ppermute | solution.py:285
  14.4 1.9 %shard_map.80 = (bf16[4,128,768]{2,1,0:T(8,128)(2,1)S(1)}, bf16[4,128,384]{2,1,0:T(8,128)(2,1)S(1)}, f32[4,256,384]{2,1,0:T(8,128)S(1)}, f32[4,64,384]{2,1,0:T(8,128)S(1)}, f32[4,64,384]{2,1,0:T(8,128)S(1)}) custom-call(bf16[4,64,768]{2,1,0:T(8,128)(2,1)S(1)} %get-tuple-element.42.refs_0_, bf16[4,64,768]{2,1,0:T(8,128)(2,1)S(1)} %get-tuple-element.47.refs_1_, ...), custom_call_target="tpu_custom_call" | custom-call | flops 12079595520 | bytes 12079595 | tf_op jit(solution)/shard_map/pallas_call | solution.py:309
  16.5 0.9 %shard_map.81 = (bf16[4,64,768]{2,1,0:T(8,128)(2,1)S(1)}, bf16[4,64,384]{2,1,0:T(8,128)(2,1)S(1)}, f32[4,64,384]{2,1,0:T(8,128)S(1)}, f32[4,64,384]{2,1,0:T(8,128)S(1)}) custom-call(bf16[4,64,768]{2,1,0:T(8,128)(2,1)S(1)} %get-tuple-element.55.refs_0_, f32[4,192,384]{2,1,0:T(8,128)S(1)} %get-tuple-element.46.refs_9_.refs_2_.refs_3_.refs_1_, ...), custom_call_target="tpu_custom_call" | custom-call | flops 6039797760 | bytes 6039797 | tf_op jit(solution)/shard_map/pallas_call | solution.py:309
  17.4 0.5 %collective-permute-start.6 = (bf16[4,64,384]{2,1,0:T(8,128)(2,1)S(1)}, bf16[4,64,384]{2,1,0:T(8,128)(2,1)S(1)}, u32[]{:S(2)}, u32[]{:S(2)}) collective-permute-start(bf16[4,64,384]{2,1,0:T(8,128)(2,1)S(1)} %get-tuple-element.66), channel_id=1, source_target_pairs={{1,2},{3,4},{5,6},{7,8},{9,10},{11,12},{13,14},{17,18},{19,20},{21... | collective-permute-start | bytes 589832 | tf_op jit(solution)/shard_map/ppermute | solution.py:285
  18.0 0.2 collective-permute-done.4.refs_4_
  18.2 1.8 %shard_map.82 = (bf16[4,128,768]{2,1,0:T(8,128)(2,1)S(1)}, bf16[4,128,384]{2,1,0:T(8,128)(2,1)S(1)}, bf16[4,128,384]{2,1,0:T(8,128)(2,1)S(1)}, f32[4,128,384]{2,1,0:T(8,128)S(1)}) custom-call(bf16[4,128,768]{2,1,0:T(8,128)(2,1)S(1)} %get-tuple-element.53.refs_0_, f32[4,256,384]{2,1,0:T(8,128)S(1)} %get-tuple-element.54.refs_10_.refs_1_.refs_2_, ...), custom_call_target="tpu_custom_call" | custom-call | flops 12079595520 | bytes 12079595 | tf_op jit(solution)/shard_map/pallas_call | solution.py:309
  20.0 0.9 %collective-permute-start.11 = (bf16[4,128,384]{2,1,0:T(8,128)(2,1)S(1)}, bf16[4,128,384]{2,1,0:T(8,128)(2,1)S(1)}, u32[]{:S(2)}, u32[]{:S(2)}) collective-permute-start(bf16[4,128,384]{2,1,0:T(8,128)(2,1)S(1)} %get-tuple-element.74), channel_id=1, source_target_pairs={{0,1},{2,3},{4,5},{6,7},{8,9},{10,11},{12,13},{14,15},{16,17},{18,... | collective-permute-start | bytes 1179656 | tf_op jit(solution)/shard_map/ppermute | solution.py:288
  20.8 0.4 %collective-permute-start.12 = (bf16[4,128,384]{2,1,0:T(8,128)(2,1)S(1)}, bf16[4,128,384]{2,1,0:T(8,128)(2,1)S(1)}, u32[]{:S(2)}, u32[]{:S(2)}) collective-permute-start(bf16[4,128,384]{2,1,0:T(8,128)(2,1)S(1)} %get-tuple-element.75), channel_id=1, source_target_pairs={{1,2},{3,4},{5,6},{7,8},{9,10},{11,12},{13,14},{17,18},{19,20},{21... | collective-permute-start | bytes 1179656 | tf_op jit(solution)/shard_map/ppermute | solution.py:285
  21.3 7.6 %collective-permute-done.6.refs_6_ = bf16[4,64,384]{2,1,0:T(8,128)(2,1)S(1)} collective-permute-done((bf16[4,64,384]{2,1,0:T(8,128)(2,1)S(1)}, bf16[4,64,384]{2,1,0:T(8,128)(2,1)S(1)}, u32[]{:S(2)}, u32[]{:S(2)}) %collective-permute-start.6) | collective-permute-done | bytes 196640 | tf_op jit(solution)/shard_map/ppermute | solution.py:285
  28.9 0.9 %shard_map.83 = (bf16[2,128,768]{2,1,0:T(8,128)(2,1)S(1)}, bf16[2,128,384]{2,1,0:T(8,128)(2,1)S(1)}, bf16[2,128,384]{2,1,0:T(8,128)(2,1)S(1)}, f32[2,128,384]{2,1,0:T(8,128)S(1)}) custom-call(bf16[4,64,768]{2,1,0:T(8,128)(2,1)S(1)} %get-tuple-element.62.refs_0_, bf16[4,64,768]{2,1,0:T(8,128)(2,1)S(1)} %get-tuple-element.52.refs_6_.refs_1_, ...), custom_call_target="tpu_custom_call" | custom-call | flops 6039797760 | bytes 6039797 | tf_op jit(solution)/shard_map/pallas_call | solution.py:309
  30.0 1.2 %shard_map.84 = (bf16[2,128,768]{2,1,0:T(8,128)(2,1)S(1)}, bf16[2,128,384]{2,1,0:T(8,128)(2,1)S(1)}, bf16[2,128,384]{2,1,0:T(8,128)(2,1)S(1)}, f32[2,128,384]{2,1,0:T(8,128)S(1)}) custom-call(bf16[4,64,768]{2,1,0:T(8,128)(2,1)S(1)} %get-tuple-element.62.refs_0_, bf16[4,64,768]{2,1,0:T(8,128)(2,1)S(1)} %get-tuple-element.52.refs_6_.refs_1_, ...), custom_call_target="tpu_custom_call" | custom-call | flops 6039797760 | bytes 6039797 | tf_op jit(solution)/shard_map/pallas_call | solution.py:309
  31.2 0.5 %collective-permute-start.7 = (bf16[2,128,384]{2,1,0:T(8,128)(2,1)S(1)}, bf16[2,128,384]{2,1,0:T(8,128)(2,1)S(1)}, u32[]{:S(2)}, u32[]{:S(2)}) collective-permute-start(bf16[2,128,384]{2,1,0:T(8,128)(2,1)S(1)} %get-tuple-element.68), channel_id=1, source_target_pairs={{0,1},{2,3},{4,5},{6,7},{8,9},{10,11},{12,13},{14,15},{16,17},{18,... | collective-permute-start | bytes 589832 | tf_op jit(solution)/shard_map/ppermute | solution.py:288
  31.6 1.4 %collective-permute-start.8 = (bf16[2,128,384]{2,1,0:T(8,128)(2,1)S(1)}, bf16[2,128,384]{2,1,0:T(8,128)(2,1)S(1)}, u32[]{:S(2)}, u32[]{:S(2)}) collective-permute-start(bf16[2,128,384]{2,1,0:T(8,128)(2,1)S(1)} %get-tuple-element.69), channel_id=1, source_target_pairs={{1,2},{3,4},{5,6},{7,8},{9,10},{11,12},{13,14},{17,18},{19,20},{21... | collective-permute-start | bytes 589832 | tf_op jit(solution)/shard_map/ppermute | solution.py:285
  33.0 0.1 collective-permute-done.12.inter_ref
  33.1 1.1 %shard_map.85.refs_3_ = bf16[4,256,768]{2,1,0:T(8,128)(2,1)} custom-call(bf16[2,128,768]{2,1,0:T(8,128)(2,1)S(1)} %get-tuple-element.76.stream_ref, f32[2,128,384]{2,1,0:T(8,128)S(1)} %get-tuple-element.67.refs_13_.local_ref, bf16[4,128,384]{2,1,0:T(8,128)(2,1)S(1)} %collective-permute-done.11.intra_ref, ...), custom_call_target="tpu_custom_call" | custom-call | flops 1509949440 | bytes 1509949 | tf_op jit(solution)/shard_map/pallas_call | solution.py:477
  34.2 1.1 %shard_map.86.refs_3_ = bf16[4,256,768]{2,1,0:T(8,128)(2,1)} custom-call(bf16[2,128,768]{2,1,0:T(8,128)(2,1)S(1)} %get-tuple-element.72.stream_ref, f32[2,128,384]{2,1,0:T(8,128)S(1)} %get-tuple-element.73.local_ref, bf16[4,128,384]{2,1,0:T(8,128)(2,1)S(1)} %collective-permute-done.11.intra_ref, ...), custom_call_target="tpu_custom_call", output_to_operand_aliasing={{}: (7, {})} | custom-call | flops 1509949440 | bytes 1509949 | tf_op jit(solution)/shard_map/pallas_call | solution.py:477
  35.3 4.1 %collective-permute-done.10.inter_ref = bf16[2,128,384]{2,1,0:T(8,128)(2,1)S(1)} collective-permute-done((bf16[2,128,384]{2,1,0:T(8,128)(2,1)S(1)}, bf16[2,128,384]{2,1,0:T(8,128)(2,1)S(1)}, u32[]{:S(2)}, u32[]{:S(2)}) %collective-permute-start.10) | collective-permute-done | bytes 196640 | tf_op jit(solution)/shard_map/ppermute | solution.py:285
  39.4 1.1 %shard_map.87.refs_3_ = bf16[4,256,768]{2,1,0:T(8,128)(2,1)} custom-call(bf16[4,128,768]{2,1,0:T(8,128)(2,1)S(1)} %get-tuple-element.60.stream_ref, f32[4,128,384]{2,1,0:T(8,128)S(1)} %get-tuple-element.61.refs_13_.local_ref, bf16[2,128,384]{2,1,0:T(8,128)(2,1)S(1)} %collective-permute-done.9.intra_ref, ...), custom_call_target="tpu_custom_call", output_to_operand_aliasing={{}: (7, {})} | custom-call | flops 1509949440 | bytes 1509949 | tf_op jit(solution)/shard_map/pallas_call | solution.py:477
  40.5 1.0 %collective-permute-done.8.inter_ref = bf16[2,128,384]{2,1,0:T(8,128)(2,1)S(1)} collective-permute-done((bf16[2,128,384]{2,1,0:T(8,128)(2,1)S(1)}, bf16[2,128,384]{2,1,0:T(8,128)(2,1)S(1)}, u32[]{:S(2)}, u32[]{:S(2)}) %collective-permute-start.8) | collective-permute-done | bytes 196640 | tf_op jit(solution)/shard_map/ppermute | solution.py:285
  41.5 1.1 %shard_map.88 = bf16[4,256,768]{2,1,0:T(8,128)(2,1)} custom-call(bf16[4,128,768]{2,1,0:T(8,128)(2,1)S(1)} %get-tuple-element.60.stream_ref, f32[4,128,384]{2,1,0:T(8,128)S(1)} %get-tuple-element.61.refs_13_.local_ref, bf16[2,128,384]{2,1,0:T(8,128)(2,1)S(1)} %collective-permute-done.7.intra_ref, ...), custom_call_target="tpu_custom_call", output_to_operand_aliasing={{}: (7, {})} | custom-call | flops 1509949440 | bytes 1509949 | tf_op jit(solution)/shard_map/pallas_call | solution.py:477
  (24 shorter events, 0.3 us)
Async XLA Ops:
  0.0 3.6 %copy-start.1 = (bf16[4,3,768,384]{3,2,1,0:T(8,128)(2,1)S(1)}, bf16[4,3,768,384]{3,2,1,0:T(8,128)(2,1)}, u32[]{:S(2)}) copy-start(bf16[4,3,768,384]{3,2,1,0:T(8,128)(2,1)} %refs_12_.5) | copy-start | bytes 21233668
  0.0 3.6 %copy-start.6 = (f32[4,768]{1,0:T(4,128)S(1)}, f32[4,768]{1,0:T(4,128)}, u32[]{:S(2)}) copy-start(f32[4,768]{1,0:T(4,128)} %refs_11_.5) | copy-start | bytes 36868
  0.0 3.6 %copy-start.5 = (f32[4,768]{1,0:T(4,128)S(1)}, f32[4,768]{1,0:T(4,128)}, u32[]{:S(2)}) copy-start(f32[4,768]{1,0:T(4,128)} %refs_10_.7) | copy-start | bytes 36868
  0.0 3.7 %copy-start.2 = (bf16[4,256,768]{2,1,0:T(8,128)(2,1)S(1)}, bf16[4,256,768]{2,1,0:T(8,128)(2,1)}, u32[]{:S(2)}) copy-start(bf16[4,256,768]{2,1,0:T(8,128)(2,1)} %refs_0_.11) | copy-start | bytes 4718596
  1.7 5.2 %copy-start = (bf16[4,384,768]{2,1,0:T(8,128)(2,1)S(1)}, bf16[4,384,768]{2,1,0:T(8,128)(2,1)}, u32[]{:S(2)}) copy-start(bf16[4,384,768]{2,1,0:T(8,128)(2,1)} %refs_2_.11) | copy-start | bytes 7077892
  1.7 5.2 %copy-start.3 = (f32[4,384]{1,0:T(4,128)S(1)}, f32[4,384]{1,0:T(4,128)}, u32[]{:S(2)}) copy-start(f32[4,384]{1,0:T(4,128)} %refs_0_.15) | copy-start | bytes 18436
  1.7 5.2 %copy-start.4 = (f32[4,384]{1,0:T(4,128)S(1)}, f32[4,384]{1,0:T(4,128)}, u32[]{:S(2)}) copy-start(f32[4,384]{1,0:T(4,128)} %refs_1_.7) | copy-start | bytes 18436
  1.7 6.1 %collective-permute-start.1 = (bf16[4,32,384]{2,1,0:T(8,128)(2,1)S(1)}, bf16[4,32,384]{2,1,0:T(8,128)(2,1)S(1)}, u32[]{:S(2)}, u32[]{:S(2)}) collective-permute-start(bf16[4,32,384]{2,1,0:T(8,128)(2,1)S(1)} %shard_map.75), channel_id=1, source_target_pairs={{1,2},{3,4},{5,6},{7,8},{9,10},{11,12},{13,14},{17,18},{19,20},{21... | collective-permute-start | bytes 294920 | tf_op jit(solution)/shard_map/ppermute | solution.py:285
  6.1 4.7 %collective-permute-start = (bf16[4,32,384]{2,1,0:T(8,128)(2,1)S(1)}, bf16[4,32,384]{2,1,0:T(8,128)(2,1)S(1)}, u32[]{:S(2)}, u32[]{:S(2)}) collective-permute-start(bf16[4,32,384]{2,1,0:T(8,128)(2,1)S(1)} %get-tuple-element.43), channel_id=1, source_target_pairs={{0,1},{2,3},{4,5},{6,7},{8,9},{10,11},{12,13},{14,15},{16,17},{18,... | collective-permute-start | bytes 294920 | tf_op jit(solution)/shard_map/ppermute | solution.py:288
  8.7 7.8 %collective-permute-start.3 = (bf16[4,64,384]{2,1,0:T(8,128)(2,1)S(1)}, bf16[4,64,384]{2,1,0:T(8,128)(2,1)S(1)}, u32[]{:S(2)}, u32[]{:S(2)}) collective-permute-start(bf16[4,64,384]{2,1,0:T(8,128)(2,1)S(1)} %get-tuple-element.56), channel_id=1, source_target_pairs={{1,2},{3,4},{5,6},{7,8},{9,10},{11,12},{13,14},{17,18},{19,20},{21... | collective-permute-start | bytes 589832 | tf_op jit(solution)/shard_map/ppermute | solution.py:285
  11.8 2.7 %collective-permute-start.2 = (bf16[4,64,384]{2,1,0:T(8,128)(2,1)S(1)}, bf16[4,64,384]{2,1,0:T(8,128)(2,1)S(1)}, u32[]{:S(2)}, u32[]{:S(2)}) collective-permute-start(bf16[4,64,384]{2,1,0:T(8,128)(2,1)S(1)} %get-tuple-element.49), channel_id=1, source_target_pairs={{0,1},{2,3},{4,5},{6,7},{8,9},{10,11},{12,13},{14,15},{16,17},{18,... | collective-permute-start | bytes 589832 | tf_op jit(solution)/shard_map/ppermute | solution.py:288
  12.9 8.4 %collective-permute-start.5 = (bf16[4,64,384]{2,1,0:T(8,128)(2,1)S(1)}, bf16[4,64,384]{2,1,0:T(8,128)(2,1)S(1)}, u32[]{:S(2)}, u32[]{:S(2)}) collective-permute-start(bf16[4,64,384]{2,1,0:T(8,128)(2,1)S(1)} %get-tuple-element.65), channel_id=1, source_target_pairs={{1,2},{3,4},{5,6},{7,8},{9,10},{11,12},{13,14},{17,18},{19,20},{21... | collective-permute-start | bytes 589832 | tf_op jit(solution)/shard_map/ppermute | solution.py:285
  16.4 1.8 %collective-permute-start.4 = (bf16[4,128,384]{2,1,0:T(8,128)(2,1)S(1)}, bf16[4,128,384]{2,1,0:T(8,128)(2,1)S(1)}, u32[]{:S(2)}, u32[]{:S(2)}) collective-permute-start(bf16[4,128,384]{2,1,0:T(8,128)(2,1)S(1)} %get-tuple-element.59), channel_id=1, source_target_pairs={{0,1},{2,3},{4,5},{6,7},{8,9},{10,11},{12,13},{14,15},{16,17},{18,... | collective-permute-start | bytes 1179656 | tf_op jit(solution)/shard_map/ppermute | solution.py:288
  17.4 11.5 %collective-permute-start.6 = (bf16[4,64,384]{2,1,0:T(8,128)(2,1)S(1)}, bf16[4,64,384]{2,1,0:T(8,128)(2,1)S(1)}, u32[]{:S(2)}, u32[]{:S(2)}) collective-permute-start(bf16[4,64,384]{2,1,0:T(8,128)(2,1)S(1)} %get-tuple-element.66), channel_id=1, source_target_pairs={{1,2},{3,4},{5,6},{7,8},{9,10},{11,12},{13,14},{17,18},{19,20},{21... | collective-permute-start | bytes 589832 | tf_op jit(solution)/shard_map/ppermute | solution.py:285
  20.0 11.7 %collective-permute-start.11 = (bf16[4,128,384]{2,1,0:T(8,128)(2,1)S(1)}, bf16[4,128,384]{2,1,0:T(8,128)(2,1)S(1)}, u32[]{:S(2)}, u32[]{:S(2)}) collective-permute-start(bf16[4,128,384]{2,1,0:T(8,128)(2,1)S(1)} %get-tuple-element.74), channel_id=1, source_target_pairs={{0,1},{2,3},{4,5},{6,7},{8,9},{10,11},{12,13},{14,15},{16,17},{18,... | collective-permute-start | bytes 1179656 | tf_op jit(solution)/shard_map/ppermute | solution.py:288
  20.8 12.3 %collective-permute-start.12 = (bf16[4,128,384]{2,1,0:T(8,128)(2,1)S(1)}, bf16[4,128,384]{2,1,0:T(8,128)(2,1)S(1)}, u32[]{:S(2)}, u32[]{:S(2)}) collective-permute-start(bf16[4,128,384]{2,1,0:T(8,128)(2,1)S(1)} %get-tuple-element.75), channel_id=1, source_target_pairs={{1,2},{3,4},{5,6},{7,8},{9,10},{11,12},{13,14},{17,18},{19,20},{21... | collective-permute-start | bytes 1179656 | tf_op jit(solution)/shard_map/ppermute | solution.py:285
  29.8 5.5 %collective-permute-start.9 = (bf16[2,128,384]{2,1,0:T(8,128)(2,1)S(1)}, bf16[2,128,384]{2,1,0:T(8,128)(2,1)S(1)}, u32[]{:S(2)}, u32[]{:S(2)}) collective-permute-start(bf16[2,128,384]{2,1,0:T(8,128)(2,1)S(1)} %get-tuple-element.70), channel_id=1, source_target_pairs={{0,1},{2,3},{4,5},{6,7},{8,9},{10,11},{12,13},{14,15},{16,17},{18,... | collective-permute-start | bytes 589832 | tf_op jit(solution)/shard_map/ppermute | solution.py:288
  29.9 9.5 %collective-permute-start.10 = (bf16[2,128,384]{2,1,0:T(8,128)(2,1)S(1)}, bf16[2,128,384]{2,1,0:T(8,128)(2,1)S(1)}, u32[]{:S(2)}, u32[]{:S(2)}) collective-permute-start(bf16[2,128,384]{2,1,0:T(8,128)(2,1)S(1)} %get-tuple-element.71), channel_id=1, source_target_pairs={{1,2},{3,4},{5,6},{7,8},{9,10},{11,12},{13,14},{17,18},{19,20},{21... | collective-permute-start | bytes 589832 | tf_op jit(solution)/shard_map/ppermute | solution.py:285
  31.2 9.4 %collective-permute-start.7 = (bf16[2,128,384]{2,1,0:T(8,128)(2,1)S(1)}, bf16[2,128,384]{2,1,0:T(8,128)(2,1)S(1)}, u32[]{:S(2)}, u32[]{:S(2)}) collective-permute-start(bf16[2,128,384]{2,1,0:T(8,128)(2,1)S(1)} %get-tuple-element.68), channel_id=1, source_target_pairs={{0,1},{2,3},{4,5},{6,7},{8,9},{10,11},{12,13},{14,15},{16,17},{18,... | collective-permute-start | bytes 589832 | tf_op jit(solution)/shard_map/ppermute | solution.py:288
  31.6 9.9 %collective-permute-start.8 = (bf16[2,128,384]{2,1,0:T(8,128)(2,1)S(1)}, bf16[2,128,384]{2,1,0:T(8,128)(2,1)S(1)}, u32[]{:S(2)}, u32[]{:S(2)}) collective-permute-start(bf16[2,128,384]{2,1,0:T(8,128)(2,1)S(1)} %get-tuple-element.69), channel_id=1, source_target_pairs={{1,2},{3,4},{5,6},{7,8},{9,10},{11,12},{13,14},{17,18},{19,20},{21... | collective-permute-start | bytes 589832 | tf_op jit(solution)/shard_map/ppermute | solution.py:285

commit v9 on v8

--- a/solution.py
+++ b/solution.py
@@ -441,7 +441,7 @@
         [("out", near), ("inn", near)],
         [(near, [("here", near, 0)])],
     )
-    inter_3n, intra_3n = cross(inter), across(intra)
+    inter_3n, kept_3n = cross(inter), intra
     parts = [(0, tracks // 2), (tracks // 2, tracks - tracks // 2)]
     last, after = [], (local_3n,)
     for first, part in parts:
@@ -460,6 +460,9 @@
             after=after, first=first, part=part,
         )
         after = (local_3f,)
+        if first == 0:
+            kept_3n, intra = lax.optimization_barrier((kept_3n, intra))
+            intra_3n = across(kept_3n)
         last.append((stream_3f, local_3f, cross(inter), across(intra)))
 
     far_ends, near_ends = [], []

time: 43 us -> 43 us (level)
  waiting for transfers between devices: 13 us -> 14.5 us
  starting transfers between devices: 9.74 us -> 8.67 us
    ppermute x7, waiting for transfers between devices: 12.8 us -> 14.2 us  [cross(): return lax.ppermute(value, ('groups', 'seq'), inter_pairs)]
    ppermute x7, starting transfers between devices: 7.09 us -> 6.48 us  [cross(): return lax.ppermute(value, ('groups', 'seq'), inter_pairs)]
    ppermute x6, starting transfers between devices: 2.65 us -> 2.19 us  [across(): return lax.ppermute(value, ('groups', 'seq'), intra_pairs)]
  transfers between devices with their start and end apart: 13 -> 13, of which waited for: 5 -> 5; matrix products, arithmetic and copies ran while one was open for 0% -> 0% of each run, Pallas kernels for 39% -> 38%
where the time goes in v9:
time: 43 us; the launch traced here: 42.8 us
  Pallas kernels  19 us (44%)
  waiting for transfers between devices  14.5 us (34%)
  starting transfers between devices  8.67 us (20%)
    ppermute x7, waiting for transfers between devices, cross(): return lax.ppermute(value, ('groups', 'seq'), inter_pairs)  14.2 us
    pallas_call x10, Pallas kernels, step(): pl.pallas_call(functools.partial(step_kernel, plan), in_specs=[vmem] * (l...  10.8 us
    ppermute x7, starting transfers between devices, cross(): return lax.ppermute(value, ('groups', 'seq'), inter_pairs)  6.48 us
    pallas_call x4, Pallas kernels, local(): pl.pallas_call(functools.partial(last_kernel, blocks - 1, q, rows, first,...  4.32 us
    pallas_call x1, Pallas kernels, local(): pl.pallas_call(functools.partial(entry_kernel, one), in_specs=[vmem] * 4,...  2.31 us
    ppermute x6, starting transfers between devices, across(): return lax.ppermute(value, ('groups', 'seq'), intra_pairs)  2.19 us
    pallas_call x1, Pallas kernels, local(): pl.pallas_call(functools.partial(edge_kernel, one), in_specs=[hbm] * 4, o...  1.63 us
  transfers between devices with their start and end apart: 13, of which 5 were waited for; matrix products, arithmetic and copies ran while one was open for 0% of the time, Pallas kernels for 38%

profile of v9, /device:TPU:25, one launch (start us, length us, event | category | flops | bytes accessed | tf_op | source)
XLA Modules:
  0.0 42.8 jit_solution(15960340004227025084)
XLA Ops:
  0.0 1.6 %shard_map.75 = bf16[4,32,384]{2,1,0:T(8,128)(2,1)S(1)} custom-call(bf16[4,256,768]{2,1,0:T(8,128)(2,1)} %refs_0_.11, f32[4,768]{1,0:T(4,128)} %refs_10_.7, f32[4,768]{1,0:T(4,128)} %refs_11_.5, bf16[4,3,768,384]{3,2,1,0:T(8,128)(2,1)} %refs_12_.5), custom_call_target="tpu_custom_call" | custom-call | flops 2264924160 | bytes 2264924 | tf_op jit(solution)/shard_map/pallas_call | solution.py:328
  1.7 1.9 %collective-permute-start.1 = (bf16[4,32,384]{2,1,0:T(8,128)(2,1)S(1)}, bf16[4,32,384]{2,1,0:T(8,128)(2,1)S(1)}, u32[]{:S(2)}, u32[]{:S(2)}) collective-permute-start(bf16[4,32,384]{2,1,0:T(8,128)(2,1)S(1)} %shard_map.75), channel_id=1, source_target_pairs={{1,2},{3,4},{5,6},{7,8},{9,10},{11,12},{13,14},{17,18},{19,20},{21... | collective-permute-start | bytes 294920 | tf_op jit(solution)/shard_map/ppermute | solution.py:285
  3.6 0.2 copy-done.2
  3.8 2.3 %shard_map.73 = (f32[4,256,384]{2,1,0:T(8,128)S(1)}, bf16[4,32,384]{2,1,0:T(8,128)(2,1)S(1)}) custom-call(bf16[4,256,768]{2,1,0:T(8,128)(2,1)S(1)} %copy-done.2, f32[4,768]{1,0:T(4,128)S(1)} %copy-done.5, f32[4,768]{1,0:T(4,128)S(1)} %copy-done.6, bf16[4,3,768,384]{3,2,1,0:T(8,128)(2,1)S(1)} %copy-done.1), custom_call_target="tpu_custom_call" | custom-call | flops 18119393280 | bytes 18119392 | tf_op jit(solution)/shard_map/pallas_call | solution.py:340
  6.1 0.7 %collective-permute-start = (bf16[4,32,384]{2,1,0:T(8,128)(2,1)S(1)}, bf16[4,32,384]{2,1,0:T(8,128)(2,1)S(1)}, u32[]{:S(2)}, u32[]{:S(2)}) collective-permute-start(bf16[4,32,384]{2,1,0:T(8,128)(2,1)S(1)} %get-tuple-element.45), channel_id=1, source_target_pairs={{0,1},{2,3},{4,5},{6,7},{8,9},{10,11},{12,13},{14,15},{16,17},{18,... | collective-permute-start | bytes 294920 | tf_op jit(solution)/shard_map/ppermute | solution.py:288
  6.8 0.9 %shard_map.74 = (bf16[4,64,768]{2,1,0:T(8,128)(2,1)S(1)}, f32[4,192,384]{2,1,0:T(8,128)S(1)}) custom-call(bf16[4,256,768]{2,1,0:T(8,128)(2,1)S(1)} %copy-done.2, f32[4,256,384]{2,1,0:T(8,128)S(1)} %get-tuple-element.43.refs_1_, f32[4,384]{1,0:T(4,128)S(1)} %copy-done.3, f32[4,384]{1,0:T(4,128)S(1)} %copy-done.4, bf16[4,384,768]{2,1,0:T(8,128)(2,1)S(1)} %copy-done, ...), custom_call_target="tpu_custom_call" | custom-call | flops 6039797760 | bytes 6039797 | tf_op jit(solution)/shard_map/pallas_call | solution.py:309
  7.8 0.9 %shard_map.76 = (bf16[4,64,768]{2,1,0:T(8,128)(2,1)S(1)}, bf16[4,64,384]{2,1,0:T(8,128)(2,1)S(1)}, f32[4,64,384]{2,1,0:T(8,128)S(1)}, f32[4,64,384]{2,1,0:T(8,128)S(1)}) custom-call(bf16[4,256,768]{2,1,0:T(8,128)(2,1)S(1)} %copy-done.2, f32[4,256,384]{2,1,0:T(8,128)S(1)} %get-tuple-element.43.refs_1_, ...), custom_call_target="tpu_custom_call" | custom-call | flops 6039797760 | bytes 6039797 | tf_op jit(solution)/shard_map/pallas_call | solution.py:309
  8.7 1.2 %collective-permute-start.3 = (bf16[4,64,384]{2,1,0:T(8,128)(2,1)S(1)}, bf16[4,64,384]{2,1,0:T(8,128)(2,1)S(1)}, u32[]{:S(2)}, u32[]{:S(2)}) collective-permute-start(bf16[4,64,384]{2,1,0:T(8,128)(2,1)S(1)} %get-tuple-element.58), channel_id=1, source_target_pairs={{1,2},{3,4},{5,6},{7,8},{9,10},{11,12},{13,14},{17,18},{19,20},{21... | collective-permute-start | bytes 589832 | tf_op jit(solution)/shard_map/ppermute | solution.py:285
  9.9 0.9 %shard_map.77 = (bf16[4,64,768]{2,1,0:T(8,128)(2,1)S(1)}, f32[4,192,384]{2,1,0:T(8,128)S(1)}) custom-call(bf16[4,256,768]{2,1,0:T(8,128)(2,1)S(1)} %copy-done.2, f32[4,256,384]{2,1,0:T(8,128)S(1)} %get-tuple-element.43.refs_1_, f32[4,384]{1,0:T(4,128)S(1)} %copy-done.3, f32[4,384]{1,0:T(4,128)S(1)} %copy-done.4, bf16[4,384,768]{2,1,0:T(8,128)(2,1)S(1)} %copy-done, ...), custom_call_target="tpu_custom_call" | custom-call | flops 6039797760 | bytes 6039797 | tf_op jit(solution)/shard_map/pallas_call | solution.py:309
  10.8 0.9 %shard_map.78 = (bf16[4,64,768]{2,1,0:T(8,128)(2,1)S(1)}, bf16[4,64,384]{2,1,0:T(8,128)(2,1)S(1)}, f32[4,128,384]{2,1,0:T(8,128)S(1)}) custom-call(bf16[4,256,768]{2,1,0:T(8,128)(2,1)S(1)} %copy-done.2, f32[4,256,384]{2,1,0:T(8,128)S(1)} %get-tuple-element.43.refs_1_, bf16[4,32,384]{2,1,0:T(8,128)(2,1)S(1)} %collective-permute-done.refs_2_, ...), custom_call_target="tpu_custom_call" | custom-call | flops 6039797760 | bytes 6039797 | tf_op jit(solution)/shard_map/pallas_call | solution.py:309
  11.8 0.4 %collective-permute-start.2 = (bf16[4,64,384]{2,1,0:T(8,128)(2,1)S(1)}, bf16[4,64,384]{2,1,0:T(8,128)(2,1)S(1)}, u32[]{:S(2)}, u32[]{:S(2)}) collective-permute-start(bf16[4,64,384]{2,1,0:T(8,128)(2,1)S(1)} %get-tuple-element.51), channel_id=1, source_target_pairs={{0,1},{2,3},{4,5},{6,7},{8,9},{10,11},{12,13},{14,15},{16,17},{18,... | collective-permute-start | bytes 589832 | tf_op jit(solution)/shard_map/ppermute | solution.py:288
  12.2 0.7 %shard_map.79 = (bf16[4,64,768]{2,1,0:T(8,128)(2,1)S(1)}, bf16[4,64,384]{2,1,0:T(8,128)(2,1)S(1)}) custom-call(bf16[4,64,768]{2,1,0:T(8,128)(2,1)S(1)} %get-tuple-element.52.refs_0_, f32[4,192,384]{2,1,0:T(8,128)S(1)} %get-tuple-element.46.refs_9_.refs_1_.refs_2_, f32[4,192,384]{2,1,0:T(8,128)S(1)} %get-tuple-element.48.refs_9_.refs_2_.refs_3_.refs_1_, ...), custom_call_target="tpu_custom_call" | custom-call | flops 6039797760 | bytes 6039797 | tf_op jit(solution)/shard_map/pallas_call | solution.py:309
  12.9 1.6 %collective-permute-start.5 = (bf16[4,64,384]{2,1,0:T(8,128)(2,1)S(1)}, bf16[4,64,384]{2,1,0:T(8,128)(2,1)S(1)}, u32[]{:S(2)}, u32[]{:S(2)}) collective-permute-start(bf16[4,64,384]{2,1,0:T(8,128)(2,1)S(1)} %get-tuple-element.67), channel_id=1, source_target_pairs={{1,2},{3,4},{5,6},{7,8},{9,10},{11,12},{13,14},{17,18},{19,20},{21... | collective-permute-start | bytes 589832 | tf_op jit(solution)/shard_map/ppermute | solution.py:285
  14.4 1.9 %shard_map.80 = (bf16[4,128,768]{2,1,0:T(8,128)(2,1)S(1)}, bf16[4,128,384]{2,1,0:T(8,128)(2,1)S(1)}, f32[4,256,384]{2,1,0:T(8,128)S(1)}, f32[4,64,384]{2,1,0:T(8,128)S(1)}, f32[4,64,384]{2,1,0:T(8,128)S(1)}) custom-call(bf16[4,64,768]{2,1,0:T(8,128)(2,1)S(1)} %get-tuple-element.44.refs_0_, bf16[4,64,768]{2,1,0:T(8,128)(2,1)S(1)} %get-tuple-element.49.refs_1_, ...), custom_call_target="tpu_custom_call" | custom-call | flops 12079595520 | bytes 12079595 | tf_op jit(solution)/shard_map/pallas_call | solution.py:309
  16.4 0.9 %shard_map.81 = (bf16[4,64,768]{2,1,0:T(8,128)(2,1)S(1)}, bf16[4,64,384]{2,1,0:T(8,128)(2,1)S(1)}, f32[4,64,384]{2,1,0:T(8,128)S(1)}, f32[4,64,384]{2,1,0:T(8,128)S(1)}) custom-call(bf16[4,64,768]{2,1,0:T(8,128)(2,1)S(1)} %get-tuple-element.57.refs_0_, f32[4,192,384]{2,1,0:T(8,128)S(1)} %get-tuple-element.48.refs_9_.refs_2_.refs_3_.refs_1_, ...), custom_call_target="tpu_custom_call" | custom-call | flops 6039797760 | bytes 6039797 | tf_op jit(solution)/shard_map/pallas_call | solution.py:309
  17.4 0.5 %collective-permute-start.6 = (bf16[4,64,384]{2,1,0:T(8,128)(2,1)S(1)}, bf16[4,64,384]{2,1,0:T(8,128)(2,1)S(1)}, u32[]{:S(2)}, u32[]{:S(2)}) collective-permute-start(bf16[4,64,384]{2,1,0:T(8,128)(2,1)S(1)} %get-tuple-element.68), channel_id=1, source_target_pairs={{1,2},{3,4},{5,6},{7,8},{9,10},{11,12},{13,14},{17,18},{19,20},{21... | collective-permute-start | bytes 589832 | tf_op jit(solution)/shard_map/ppermute | solution.py:285
  17.9 0.2 collective-permute-done.4.refs_4_
  18.1 1.8 %shard_map.82 = (bf16[4,128,768]{2,1,0:T(8,128)(2,1)S(1)}, bf16[4,128,384]{2,1,0:T(8,128)(2,1)S(1)}, bf16[4,128,384]{2,1,0:T(8,128)(2,1)S(1)}, f32[4,128,384]{2,1,0:T(8,128)S(1)}) custom-call(bf16[4,128,768]{2,1,0:T(8,128)(2,1)S(1)} %get-tuple-element.55.refs_0_, f32[4,256,384]{2,1,0:T(8,128)S(1)} %get-tuple-element.56.refs_10_.refs_1_.refs_2_, ...), custom_call_target="tpu_custom_call" | custom-call | flops 12079595520 | bytes 12079595 | tf_op jit(solution)/shard_map/pallas_call | solution.py:309
  19.9 1.1 %collective-permute-start.12 = (bf16[4,128,384]{2,1,0:T(8,128)(2,1)S(1)}, bf16[4,128,384]{2,1,0:T(8,128)(2,1)S(1)}, u32[]{:S(2)}, u32[]{:S(2)}) collective-permute-start(bf16[4,128,384]{2,1,0:T(8,128)(2,1)S(1)} %get-tuple-element.79), channel_id=1, source_target_pairs={{1,2},{3,4},{5,6},{7,8},{9,10},{11,12},{13,14},{17,18},{19,20},{21... | collective-permute-start | bytes 1179656 | tf_op jit(solution)/shard_map/ppermute | solution.py:285
  21.1 7.8 %collective-permute-done.6.refs_6_ = bf16[4,64,384]{2,1,0:T(8,128)(2,1)S(1)} collective-permute-done((bf16[4,64,384]{2,1,0:T(8,128)(2,1)S(1)}, bf16[4,64,384]{2,1,0:T(8,128)(2,1)S(1)}, u32[]{:S(2)}, u32[]{:S(2)}) %collective-permute-start.6) | collective-permute-done | bytes 196640 | tf_op jit(solution)/shard_map/ppermute | solution.py:285
  28.9 0.9 %shard_map.83 = (bf16[2,128,768]{2,1,0:T(8,128)(2,1)S(1)}, bf16[2,128,384]{2,1,0:T(8,128)(2,1)S(1)}, bf16[2,128,384]{2,1,0:T(8,128)(2,1)S(1)}, f32[2,128,384]{2,1,0:T(8,128)S(1)}) custom-call(bf16[4,64,768]{2,1,0:T(8,128)(2,1)S(1)} %get-tuple-element.64.refs_0_, bf16[4,64,768]{2,1,0:T(8,128)(2,1)S(1)} %get-tuple-element.54.refs_6_.refs_1_, ...), custom_call_target="tpu_custom_call" | custom-call | flops 6039797760 | bytes 6039797 | tf_op jit(solution)/shard_map/pallas_call | solution.py:309
  29.9 0.4 collective-permute-start.11
  30.4 0.9 %shard_map.84 = (bf16[2,128,768]{2,1,0:T(8,128)(2,1)S(1)}, bf16[2,128,384]{2,1,0:T(8,128)(2,1)S(1)}, bf16[2,128,384]{2,1,0:T(8,128)(2,1)S(1)}, f32[2,128,384]{2,1,0:T(8,128)S(1)}) custom-call(bf16[4,64,768]{2,1,0:T(8,128)(2,1)S(1)} %get-tuple-element.64.refs_0_, bf16[4,64,768]{2,1,0:T(8,128)(2,1)S(1)} %get-tuple-element.54.refs_6_.refs_1_, ...), custom_call_target="tpu_custom_call" | custom-call | flops 6039797760 | bytes 6039797 | tf_op jit(solution)/shard_map/pallas_call | solution.py:309
  31.3 0.4 %collective-permute-start.7 = (bf16[2,128,384]{2,1,0:T(8,128)(2,1)S(1)}, bf16[2,128,384]{2,1,0:T(8,128)(2,1)S(1)}, u32[]{:S(2)}, u32[]{:S(2)}) collective-permute-start(bf16[2,128,384]{2,1,0:T(8,128)(2,1)S(1)} %get-tuple-element.70), channel_id=1, source_target_pairs={{0,1},{2,3},{4,5},{6,7},{8,9},{10,11},{12,13},{14,15},{16,17},{18,... | collective-permute-start | bytes 589832 | tf_op jit(solution)/shard_map/ppermute | solution.py:288
  31.7 1.4 %collective-permute-done.12.inter_ref = bf16[4,128,384]{2,1,0:T(8,128)(2,1)S(1)} collective-permute-done((bf16[4,128,384]{2,1,0:T(8,128)(2,1)S(1)}, bf16[4,128,384]{2,1,0:T(8,128)(2,1)S(1)}, u32[]{:S(2)}, u32[]{:S(2)}) %collective-permute-start.12) | collective-permute-done | bytes 393248 | tf_op jit(solution)/shard_map/ppermute | solution.py:285
  33.1 0.1 collective-permute-start.8
  33.2 1.1 %shard_map.85.refs_3_ = bf16[4,256,768]{2,1,0:T(8,128)(2,1)} custom-call(bf16[2,128,768]{2,1,0:T(8,128)(2,1)S(1)} %get-tuple-element.80.stream_ref, f32[2,128,384]{2,1,0:T(8,128)S(1)} %get-tuple-element.69.refs_13_.local_ref, bf16[4,128,384]{2,1,0:T(8,128)(2,1)S(1)} %collective-permute-done.11.intra_ref, ...), custom_call_target="tpu_custom_call" | custom-call | flops 1509949440 | bytes 1509949 | tf_op jit(solution)/shard_map/pallas_call | solution.py:480
  34.2 1.1 %shard_map.86.refs_3_ = bf16[4,256,768]{2,1,0:T(8,128)(2,1)} custom-call(bf16[2,128,768]{2,1,0:T(8,128)(2,1)S(1)} %get-tuple-element.76.stream_ref, f32[2,128,384]{2,1,0:T(8,128)S(1)} %get-tuple-element.77.local_ref, bf16[4,128,384]{2,1,0:T(8,128)(2,1)S(1)} %collective-permute-done.11.intra_ref, ...), custom_call_target="tpu_custom_call", output_to_operand_aliasing={{}: (7, {})} | custom-call | flops 1509949440 | bytes 1509949 | tf_op jit(solution)/shard_map/pallas_call | solution.py:480
  35.4 4.0 %collective-permute-done.10.inter_ref = bf16[2,128,384]{2,1,0:T(8,128)(2,1)S(1)} collective-permute-done((bf16[2,128,384]{2,1,0:T(8,128)(2,1)S(1)}, bf16[2,128,384]{2,1,0:T(8,128)(2,1)S(1)}, u32[]{:S(2)}, u32[]{:S(2)}) %collective-permute-start.10) | collective-permute-done | bytes 196640 | tf_op jit(solution)/shard_map/ppermute | solution.py:285
  39.4 1.1 %shard_map.87.refs_3_ = bf16[4,256,768]{2,1,0:T(8,128)(2,1)} custom-call(bf16[4,128,768]{2,1,0:T(8,128)(2,1)S(1)} %get-tuple-element.62.stream_ref, f32[4,128,384]{2,1,0:T(8,128)S(1)} %get-tuple-element.63.refs_13_.local_ref, bf16[2,128,384]{2,1,0:T(8,128)(2,1)S(1)} %collective-permute-done.9.intra_ref, ...), custom_call_target="tpu_custom_call", output_to_operand_aliasing={{}: (7, {})} | custom-call | flops 1509949440 | bytes 1509949 | tf_op jit(solution)/shard_map/pallas_call | solution.py:480
  40.5 1.0 %collective-permute-done.8.inter_ref = bf16[2,128,384]{2,1,0:T(8,128)(2,1)S(1)} collective-permute-done((bf16[2,128,384]{2,1,0:T(8,128)(2,1)S(1)}, bf16[2,128,384]{2,1,0:T(8,128)(2,1)S(1)}, u32[]{:S(2)}, u32[]{:S(2)}) %collective-permute-start.8) | collective-permute-done | bytes 196640 | tf_op jit(solution)/shard_map/ppermute | solution.py:285
  41.5 1.1 %shard_map.88 = bf16[4,256,768]{2,1,0:T(8,128)(2,1)} custom-call(bf16[4,128,768]{2,1,0:T(8,128)(2,1)S(1)} %get-tuple-element.62.stream_ref, f32[4,128,384]{2,1,0:T(8,128)S(1)} %get-tuple-element.63.refs_13_.local_ref, bf16[2,128,384]{2,1,0:T(8,128)(2,1)S(1)} %collective-permute-done.7.intra_ref, ...), custom_call_target="tpu_custom_call", output_to_operand_aliasing={{}: (7, {})} | custom-call | flops 1509949440 | bytes 1509949 | tf_op jit(solution)/shard_map/pallas_call | solution.py:480
  (24 shorter events, 0.3 us)
Async XLA Ops:
  0.0 3.6 %copy-start.1 = (bf16[4,3,768,384]{3,2,1,0:T(8,128)(2,1)S(1)}, bf16[4,3,768,384]{3,2,1,0:T(8,128)(2,1)}, u32[]{:S(2)}) copy-start(bf16[4,3,768,384]{3,2,1,0:T(8,128)(2,1)} %refs_12_.5) | copy-start | bytes 21233668
  0.0 3.6 %copy-start.6 = (f32[4,768]{1,0:T(4,128)S(1)}, f32[4,768]{1,0:T(4,128)}, u32[]{:S(2)}) copy-start(f32[4,768]{1,0:T(4,128)} %refs_11_.5) | copy-start | bytes 36868
  0.0 3.6 %copy-start.5 = (f32[4,768]{1,0:T(4,128)S(1)}, f32[4,768]{1,0:T(4,128)}, u32[]{:S(2)}) copy-start(f32[4,768]{1,0:T(4,128)} %refs_10_.7) | copy-start | bytes 36868
  0.0 3.7 %copy-start.2 = (bf16[4,256,768]{2,1,0:T(8,128)(2,1)S(1)}, bf16[4,256,768]{2,1,0:T(8,128)(2,1)}, u32[]{:S(2)}) copy-start(bf16[4,256,768]{2,1,0:T(8,128)(2,1)} %refs_0_.11) | copy-start | bytes 4718596
  1.7 5.2 %copy-start = (bf16[4,384,768]{2,1,0:T(8,128)(2,1)S(1)}, bf16[4,384,768]{2,1,0:T(8,128)(2,1)}, u32[]{:S(2)}) copy-start(bf16[4,384,768]{2,1,0:T(8,128)(2,1)} %refs_2_.11) | copy-start | bytes 7077892
  1.7 5.2 %copy-start.3 = (f32[4,384]{1,0:T(4,128)S(1)}, f32[4,384]{1,0:T(4,128)}, u32[]{:S(2)}) copy-start(f32[4,384]{1,0:T(4,128)} %refs_0_.15) | copy-start | bytes 18436
  1.7 5.2 %copy-start.4 = (f32[4,384]{1,0:T(4,128)S(1)}, f32[4,384]{1,0:T(4,128)}, u32[]{:S(2)}) copy-start(f32[4,384]{1,0:T(4,128)} %refs_1_.7) | copy-start | bytes 18436
  1.7 6.1 %collective-permute-start.1 = (bf16[4,32,384]{2,1,0:T(8,128)(2,1)S(1)}, bf16[4,32,384]{2,1,0:T(8,128)(2,1)S(1)}, u32[]{:S(2)}, u32[]{:S(2)}) collective-permute-start(bf16[4,32,384]{2,1,0:T(8,128)(2,1)S(1)} %shard_map.75), channel_id=1, source_target_pairs={{1,2},{3,4},{5,6},{7,8},{9,10},{11,12},{13,14},{17,18},{19,20},{21... | collective-permute-start | bytes 294920 | tf_op jit(solution)/shard_map/ppermute | solution.py:285
  6.1 4.7 %collective-permute-start = (bf16[4,32,384]{2,1,0:T(8,128)(2,1)S(1)}, bf16[4,32,384]{2,1,0:T(8,128)(2,1)S(1)}, u32[]{:S(2)}, u32[]{:S(2)}) collective-permute-start(bf16[4,32,384]{2,1,0:T(8,128)(2,1)S(1)} %get-tuple-element.45), channel_id=1, source_target_pairs={{0,1},{2,3},{4,5},{6,7},{8,9},{10,11},{12,13},{14,15},{16,17},{18,... | collective-permute-start | bytes 294920 | tf_op jit(solution)/shard_map/ppermute | solution.py:288
  8.7 7.8 %collective-permute-start.3 = (bf16[4,64,384]{2,1,0:T(8,128)(2,1)S(1)}, bf16[4,64,384]{2,1,0:T(8,128)(2,1)S(1)}, u32[]{:S(2)}, u32[]{:S(2)}) collective-permute-start(bf16[4,64,384]{2,1,0:T(8,128)(2,1)S(1)} %get-tuple-element.58), channel_id=1, source_target_pairs={{1,2},{3,4},{5,6},{7,8},{9,10},{11,12},{13,14},{17,18},{19,20},{21... | collective-permute-start | bytes 589832 | tf_op jit(solution)/shard_map/ppermute | solution.py:285
  11.8 2.7 %collective-permute-start.2 = (bf16[4,64,384]{2,1,0:T(8,128)(2,1)S(1)}, bf16[4,64,384]{2,1,0:T(8,128)(2,1)S(1)}, u32[]{:S(2)}, u32[]{:S(2)}) collective-permute-start(bf16[4,64,384]{2,1,0:T(8,128)(2,1)S(1)} %get-tuple-element.51), channel_id=1, source_target_pairs={{0,1},{2,3},{4,5},{6,7},{8,9},{10,11},{12,13},{14,15},{16,17},{18,... | collective-permute-start | bytes 589832 | tf_op jit(solution)/shard_map/ppermute | solution.py:288
  12.9 8.2 %collective-permute-start.5 = (bf16[4,64,384]{2,1,0:T(8,128)(2,1)S(1)}, bf16[4,64,384]{2,1,0:T(8,128)(2,1)S(1)}, u32[]{:S(2)}, u32[]{:S(2)}) collective-permute-start(bf16[4,64,384]{2,1,0:T(8,128)(2,1)S(1)} %get-tuple-element.67), channel_id=1, source_target_pairs={{1,2},{3,4},{5,6},{7,8},{9,10},{11,12},{13,14},{17,18},{19,20},{21... | collective-permute-start | bytes 589832 | tf_op jit(solution)/shard_map/ppermute | solution.py:285
  16.4 1.8 %collective-permute-start.4 = (bf16[4,128,384]{2,1,0:T(8,128)(2,1)S(1)}, bf16[4,128,384]{2,1,0:T(8,128)(2,1)S(1)}, u32[]{:S(2)}, u32[]{:S(2)}) collective-permute-start(bf16[4,128,384]{2,1,0:T(8,128)(2,1)S(1)} %get-tuple-element.61), channel_id=1, source_target_pairs={{0,1},{2,3},{4,5},{6,7},{8,9},{10,11},{12,13},{14,15},{16,17},{18,... | collective-permute-start | bytes 1179656 | tf_op jit(solution)/shard_map/ppermute | solution.py:288
  17.4 11.5 %collective-permute-start.6 = (bf16[4,64,384]{2,1,0:T(8,128)(2,1)S(1)}, bf16[4,64,384]{2,1,0:T(8,128)(2,1)S(1)}, u32[]{:S(2)}, u32[]{:S(2)}) collective-permute-start(bf16[4,64,384]{2,1,0:T(8,128)(2,1)S(1)} %get-tuple-element.68), channel_id=1, source_target_pairs={{1,2},{3,4},{5,6},{7,8},{9,10},{11,12},{13,14},{17,18},{19,20},{21... | collective-permute-start | bytes 589832 | tf_op jit(solution)/shard_map/ppermute | solution.py:285
  19.9 13.2 %collective-permute-start.12 = (bf16[4,128,384]{2,1,0:T(8,128)(2,1)S(1)}, bf16[4,128,384]{2,1,0:T(8,128)(2,1)S(1)}, u32[]{:S(2)}, u32[]{:S(2)}) collective-permute-start(bf16[4,128,384]{2,1,0:T(8,128)(2,1)S(1)} %get-tuple-element.79), channel_id=1, source_target_pairs={{1,2},{3,4},{5,6},{7,8},{9,10},{11,12},{13,14},{17,18},{19,20},{21... | collective-permute-start | bytes 1179656 | tf_op jit(solution)/shard_map/ppermute | solution.py:285
  29.8 5.6 %collective-permute-start.9 = (bf16[2,128,384]{2,1,0:T(8,128)(2,1)S(1)}, bf16[2,128,384]{2,1,0:T(8,128)(2,1)S(1)}, u32[]{:S(2)}, u32[]{:S(2)}) collective-permute-start(bf16[2,128,384]{2,1,0:T(8,128)(2,1)S(1)} %get-tuple-element.74), channel_id=1, source_target_pairs={{0,1},{2,3},{4,5},{6,7},{8,9},{10,11},{12,13},{14,15},{16,17},{18,... | collective-permute-start | bytes 589832 | tf_op jit(solution)/shard_map/ppermute | solution.py:288
  29.9 9.5 %collective-permute-start.10 = (bf16[2,128,384]{2,1,0:T(8,128)(2,1)S(1)}, bf16[2,128,384]{2,1,0:T(8,128)(2,1)S(1)}, u32[]{:S(2)}, u32[]{:S(2)}) collective-permute-start(bf16[2,128,384]{2,1,0:T(8,128)(2,1)S(1)} %get-tuple-element.75), channel_id=1, source_target_pairs={{1,2},{3,4},{5,6},{7,8},{9,10},{11,12},{13,14},{17,18},{19,20},{21... | collective-permute-start | bytes 589832 | tf_op jit(solution)/shard_map/ppermute | solution.py:285
  29.9 3.2 %collective-permute-start.11 = (bf16[4,128,384]{2,1,0:T(8,128)(2,1)S(1)}, bf16[4,128,384]{2,1,0:T(8,128)(2,1)S(1)}, u32[]{:S(2)}, u32[]{:S(2)}) collective-permute-start(bf16[4,128,384]{2,1,0:T(8,128)(2,1)S(1)} %get-tuple-element.78), channel_id=1, source_target_pairs={{0,1},{2,3},{4,5},{6,7},{8,9},{10,11},{12,13},{14,15},{16,17},{18,... | collective-permute-start | bytes 1179656 | tf_op jit(solution)/shard_map/ppermute | solution.py:288
  31.3 9.2 %collective-permute-start.7 = (bf16[2,128,384]{2,1,0:T(8,128)(2,1)S(1)}, bf16[2,128,384]{2,1,0:T(8,128)(2,1)S(1)}, u32[]{:S(2)}, u32[]{:S(2)}) collective-permute-start(bf16[2,128,384]{2,1,0:T(8,128)(2,1)S(1)} %get-tuple-element.70), channel_id=1, source_target_pairs={{0,1},{2,3},{4,5},{6,7},{8,9},{10,11},{12,13},{14,15},{16,17},{18,... | collective-permute-start | bytes 589832 | tf_op jit(solution)/shard_map/ppermute | solution.py:288
  33.1 8.4 %collective-permute-start.8 = (bf16[2,128,384]{2,1,0:T(8,128)(2,1)S(1)}, bf16[2,128,384]{2,1,0:T(8,128)(2,1)S(1)}, u32[]{:S(2)}, u32[]{:S(2)}) collective-permute-start(bf16[2,128,384]{2,1,0:T(8,128)(2,1)S(1)} %get-tuple-element.71), channel_id=1, source_target_pairs={{1,2},{3,4},{5,6},{7,8},{9,10},{11,12},{13,14},{17,18},{19,20},{21... | collective-permute-start | bytes 589832 | tf_op jit(solution)/shard_map/ppermute | solution.py:285

commit v10 on v9

--- a/solution.py
+++ b/solution.py
@@ -226,30 +226,34 @@
     return pieces[0] if len(pieces) == 1 else jnp.concatenate(pieces, axis=0)
 
 
-def last_kernel(
-    block, q, rows, first, bases, stream_ref, local_ref, intra_ref, inter_ref, *refs
-):
-    mid_scale_ref, mid_shift_ref, point_ref = refs[:3]
+def last_kernel(block, q, rows, groups, *refs):
+    count = 4 * len(groups)
+    mid_scale_ref, mid_shift_ref, point_ref = refs[count : count + 3]
     out_ref, result, sems = refs[-3:]
 
     def body(even, edge):
         target = span_of(q, (0, rows), even)
         copies = []
-        for t in range(result.shape[0]):
-            stream, local, intra, inter = (
-                ref[base + t]
-                for ref, base in zip((stream_ref, local_ref, intra_ref, inter_ref), bases)
-            )
-            conv = (
-                local
-                + intra.astype(jnp.float32)
-                + jnp.where(edge, 0.0, inter.astype(jnp.float32))
-            )
-            result[t] = finished(stream, conv, block, mid_scale_ref, mid_shift_ref, point_ref)
-            copies.append(
-                pltpu.make_async_copy(result.at[t], out_ref.at[first + t, target], sems.at[t])
-            )
-            copies[-1].start()
+        for i, (first, part, bases) in enumerate(groups):
+            for t in range(part):
+                stream, local, intra, inter = (
+                    ref[base + t] for ref, base in zip(refs[4 * i : 4 * i + 4], bases)
+                )
+                conv = (
+                    local
+                    + intra.astype(jnp.float32)
+                    + jnp.where(edge, 0.0, inter.astype(jnp.float32))
+                )
+                done = len(copies)
+                result[done] = finished(
+                    stream, conv, block, mid_scale_ref, mid_shift_ref, point_ref
+                )
+                copies.append(
+                    pltpu.make_async_copy(
+                        result.at[done], out_ref.at[first + t, target], sems.at[done]
+                    )
+                )
+                copies[-1].start()
         for copy in copies:
             copy.wait()
 
@@ -468,27 +472,28 @@
     far_ends, near_ends = [], []
     for (first, part), (stream_3f, local_3f, inter, intra) in zip(parts, last):
         far_ends.append(
-            ((0, three), first, part, (0, 0, first, first), (stream_3f, local_3f, intra_3n, inter_3n))
-        )
-        near_ends.append(
-            (near, first, part, (first, first, 0, 0), (stream_3n, local_3n, intra, inter))
-        )
+            (first, part, (0, 0, first, first), (stream_3f, local_3f, intra_3n, inter_3n))
+        )
+        near_ends.append((first, part, (first, first, 0, 0), (stream_3n, local_3n, intra, inter)))
     out = []
-    for q, first, part, bases, arrays in far_ends + near_ends:
-        count = q[1] - q[0]
+    for q, chosen in [((0, three), far_ends)] + [(near, [end]) for end in near_ends]:
+        count, total = q[1] - q[0], sum(part for _, part, _, _ in chosen)
+        arrays = [array for *_, group in chosen for array in group]
         out = [
             pl.pallas_call(
-                functools.partial(last_kernel, blocks - 1, q, rows, first, bases),
-                in_specs=[vmem] * 7 + [hbm] * len(out),
+                functools.partial(
+                    last_kernel, blocks - 1, q, rows, [end[:3] for end in chosen]
+                ),
+                in_specs=[vmem] * (len(arrays) + 3) + [hbm] * len(out),
                 out_specs=hbm,
                 out_shape=jax.ShapeDtypeStruct(tower_in.shape, jnp.bfloat16),
                 scratch_shapes=[
-                    pltpu.VMEM((part, count, channels), jnp.bfloat16),
-                    pltpu.SemaphoreType.DMA((part,)),
+                    pltpu.VMEM((total, count, channels), jnp.bfloat16),
+                    pltpu.SemaphoreType.DMA((total,)),
                 ],
-                input_output_aliases={7: 0} if out else {},
+                input_output_aliases={len(arrays) + 3: 0} if out else {},
                 compiler_params=params,
-                cost_estimate=cost(count, conv=0, part=part),
+                cost_estimate=cost(count, conv=0, part=total),
             )(*arrays, *mids, *out)
         ]
     return out[0]

time: 43 us -> 43 us (level)
  Pallas kernels: 19 us -> 18.2 us
  waiting for transfers between devices: 14.5 us -> 15.3 us
    ppermute x7, waiting for transfers between devices: 14.2 us -> 15.1 us  [cross(): return lax.ppermute(value, ('groups', 'seq'), inter_pairs)]
    pallas_call x4 -> x3, Pallas kernels: 4.32 us -> 3.47 us  [local(): pl.pallas_call(functools.partial(last_kernel, blocks - 1, q, rows, [end[:...]
  transfers between devices with their start and end apart: 13 -> 13, of which waited for: 5 -> 5; matrix products, arithmetic and copies ran while one was open for 0% -> 0% of each run, Pallas kernels for 38% -> 36%
where the time goes in v10:
time: 43 us; the launch traced here: 42.8 us
  Pallas kernels  18.2 us (42%)
  waiting for transfers between devices  15.3 us (36%)
  starting transfers between devices  8.66 us (20%)
    ppermute x7, waiting for transfers between devices, cross(): return lax.ppermute(value, ('groups', 'seq'), inter_pairs)  15.1 us
    pallas_call x10, Pallas kernels, step(): pl.pallas_call(functools.partial(step_kernel, plan), in_specs=[vmem] * (l...  10.8 us
    ppermute x7, starting transfers between devices, cross(): return lax.ppermute(value, ('groups', 'seq'), inter_pairs)  6.48 us
    pallas_call x3, Pallas kernels, local(): pl.pallas_call(functools.partial(last_kernel, blocks - 1, q, rows, [end[:...  3.47 us
    pallas_call x1, Pallas kernels, local(): pl.pallas_call(functools.partial(entry_kernel, one), in_specs=[vmem] * 4,...  2.31 us
    ppermute x6, starting transfers between devices, across(): return lax.ppermute(value, ('groups', 'seq'), intra_pairs)  2.18 us
    pallas_call x1, Pallas kernels, local(): pl.pallas_call(functools.partial(edge_kernel, one), in_specs=[hbm] * 4, o...  1.63 us
  transfers between devices with their start and end apart: 13, of which 5 were waited for; matrix products, arithmetic and copies ran while one was open for 0% of the time, Pallas kernels for 36%

profile of v10, /device:TPU:25, one launch (start us, length us, event | category | flops | bytes accessed | tf_op | source)
XLA Modules:
  0.0 42.8 jit_solution(12150743787464582196)
XLA Ops:
  0.0 1.6 %shard_map.75 = bf16[4,32,384]{2,1,0:T(8,128)(2,1)S(1)} custom-call(bf16[4,256,768]{2,1,0:T(8,128)(2,1)} %refs_0_.7, f32[4,768]{1,0:T(4,128)} %refs_10_.8, f32[4,768]{1,0:T(4,128)} %refs_11_.5, bf16[4,3,768,384]{3,2,1,0:T(8,128)(2,1)} %refs_12_.5), custom_call_target="tpu_custom_call" | custom-call | flops 2264924160 | bytes 2264924 | tf_op jit(solution)/shard_map/pallas_call | solution.py:332
  1.7 1.9 %collective-permute-start.1 = (bf16[4,32,384]{2,1,0:T(8,128)(2,1)S(1)}, bf16[4,32,384]{2,1,0:T(8,128)(2,1)S(1)}, u32[]{:S(2)}, u32[]{:S(2)}) collective-permute-start(bf16[4,32,384]{2,1,0:T(8,128)(2,1)S(1)} %shard_map.75), channel_id=1, source_target_pairs={{1,2},{3,4},{5,6},{7,8},{9,10},{11,12},{13,14},{17,18},{19,20},{21... | collective-permute-start | bytes 294920 | tf_op jit(solution)/shard_map/ppermute | solution.py:289
  3.6 0.2 copy-done.2
  3.8 2.3 %shard_map.73 = (f32[4,256,384]{2,1,0:T(8,128)S(1)}, bf16[4,32,384]{2,1,0:T(8,128)(2,1)S(1)}) custom-call(bf16[4,256,768]{2,1,0:T(8,128)(2,1)S(1)} %copy-done.2, f32[4,768]{1,0:T(4,128)S(1)} %copy-done.5, f32[4,768]{1,0:T(4,128)S(1)} %copy-done.6, bf16[4,3,768,384]{3,2,1,0:T(8,128)(2,1)S(1)} %copy-done.1), custom_call_target="tpu_custom_call" | custom-call | flops 18119393280 | bytes 18119392 | tf_op jit(solution)/shard_map/pallas_call | solution.py:344
  6.1 0.7 %collective-permute-start = (bf16[4,32,384]{2,1,0:T(8,128)(2,1)S(1)}, bf16[4,32,384]{2,1,0:T(8,128)(2,1)S(1)}, u32[]{:S(2)}, u32[]{:S(2)}) collective-permute-start(bf16[4,32,384]{2,1,0:T(8,128)(2,1)S(1)} %get-tuple-element.45), channel_id=1, source_target_pairs={{0,1},{2,3},{4,5},{6,7},{8,9},{10,11},{12,13},{14,15},{16,17},{18,... | collective-permute-start | bytes 294920 | tf_op jit(solution)/shard_map/ppermute | solution.py:292
  6.8 0.9 %shard_map.74 = (bf16[4,64,768]{2,1,0:T(8,128)(2,1)S(1)}, f32[4,192,384]{2,1,0:T(8,128)S(1)}) custom-call(bf16[4,256,768]{2,1,0:T(8,128)(2,1)S(1)} %copy-done.2, f32[4,256,384]{2,1,0:T(8,128)S(1)} %get-tuple-element.43.refs_1_, f32[4,384]{1,0:T(4,128)S(1)} %copy-done.3, f32[4,384]{1,0:T(4,128)S(1)} %copy-done.4, bf16[4,384,768]{2,1,0:T(8,128)(2,1)S(1)} %copy-done, ...), custom_call_target="tpu_custom_call" | custom-call | flops 6039797760 | bytes 6039797 | tf_op jit(solution)/shard_map/pallas_call | solution.py:313
  7.8 0.9 %shard_map.76 = (bf16[4,64,768]{2,1,0:T(8,128)(2,1)S(1)}, bf16[4,64,384]{2,1,0:T(8,128)(2,1)S(1)}, f32[4,64,384]{2,1,0:T(8,128)S(1)}, f32[4,64,384]{2,1,0:T(8,128)S(1)}) custom-call(bf16[4,256,768]{2,1,0:T(8,128)(2,1)S(1)} %copy-done.2, f32[4,256,384]{2,1,0:T(8,128)S(1)} %get-tuple-element.43.refs_1_, ...), custom_call_target="tpu_custom_call" | custom-call | flops 6039797760 | bytes 6039797 | tf_op jit(solution)/shard_map/pallas_call | solution.py:313
  8.7 1.2 %collective-permute-start.3 = (bf16[4,64,384]{2,1,0:T(8,128)(2,1)S(1)}, bf16[4,64,384]{2,1,0:T(8,128)(2,1)S(1)}, u32[]{:S(2)}, u32[]{:S(2)}) collective-permute-start(bf16[4,64,384]{2,1,0:T(8,128)(2,1)S(1)} %get-tuple-element.58), channel_id=1, source_target_pairs={{1,2},{3,4},{5,6},{7,8},{9,10},{11,12},{13,14},{17,18},{19,20},{21... | collective-permute-start | bytes 589832 | tf_op jit(solution)/shard_map/ppermute | solution.py:289
  9.9 0.9 %shard_map.77 = (bf16[4,64,768]{2,1,0:T(8,128)(2,1)S(1)}, f32[4,192,384]{2,1,0:T(8,128)S(1)}) custom-call(bf16[4,256,768]{2,1,0:T(8,128)(2,1)S(1)} %copy-done.2, f32[4,256,384]{2,1,0:T(8,128)S(1)} %get-tuple-element.43.refs_1_, f32[4,384]{1,0:T(4,128)S(1)} %copy-done.3, f32[4,384]{1,0:T(4,128)S(1)} %copy-done.4, bf16[4,384,768]{2,1,0:T(8,128)(2,1)S(1)} %copy-done, ...), custom_call_target="tpu_custom_call" | custom-call | flops 6039797760 | bytes 6039797 | tf_op jit(solution)/shard_map/pallas_call | solution.py:313
  10.8 0.9 %shard_map.78 = (bf16[4,64,768]{2,1,0:T(8,128)(2,1)S(1)}, bf16[4,64,384]{2,1,0:T(8,128)(2,1)S(1)}, f32[4,128,384]{2,1,0:T(8,128)S(1)}) custom-call(bf16[4,256,768]{2,1,0:T(8,128)(2,1)S(1)} %copy-done.2, f32[4,256,384]{2,1,0:T(8,128)S(1)} %get-tuple-element.43.refs_1_, bf16[4,32,384]{2,1,0:T(8,128)(2,1)S(1)} %collective-permute-done.refs_2_, ...), custom_call_target="tpu_custom_call" | custom-call | flops 6039797760 | bytes 6039797 | tf_op jit(solution)/shard_map/pallas_call | solution.py:313
  11.8 0.4 collective-permute-start.2
  12.2 0.7 %shard_map.79 = (bf16[4,64,768]{2,1,0:T(8,128)(2,1)S(1)}, bf16[4,64,384]{2,1,0:T(8,128)(2,1)S(1)}) custom-call(bf16[4,64,768]{2,1,0:T(8,128)(2,1)S(1)} %get-tuple-element.52.refs_0_, f32[4,192,384]{2,1,0:T(8,128)S(1)} %get-tuple-element.46.refs_9_.refs_1_.refs_2_, f32[4,192,384]{2,1,0:T(8,128)S(1)} %get-tuple-element.48.refs_9_.refs_2_.refs_3_.refs_1_, ...), custom_call_target="tpu_custom_call" | custom-call | flops 6039797760 | bytes 6039797 | tf_op jit(solution)/shard_map/pallas_call | solution.py:313
  12.9 1.6 %collective-permute-start.5 = (bf16[4,64,384]{2,1,0:T(8,128)(2,1)S(1)}, bf16[4,64,384]{2,1,0:T(8,128)(2,1)S(1)}, u32[]{:S(2)}, u32[]{:S(2)}) collective-permute-start(bf16[4,64,384]{2,1,0:T(8,128)(2,1)S(1)} %get-tuple-element.67), channel_id=1, source_target_pairs={{1,2},{3,4},{5,6},{7,8},{9,10},{11,12},{13,14},{17,18},{19,20},{21... | collective-permute-start | bytes 589832 | tf_op jit(solution)/shard_map/ppermute | solution.py:289
  14.4 1.9 %shard_map.80 = (bf16[4,128,768]{2,1,0:T(8,128)(2,1)S(1)}, bf16[4,128,384]{2,1,0:T(8,128)(2,1)S(1)}, f32[4,256,384]{2,1,0:T(8,128)S(1)}, f32[4,64,384]{2,1,0:T(8,128)S(1)}, f32[4,64,384]{2,1,0:T(8,128)S(1)}) custom-call(bf16[4,64,768]{2,1,0:T(8,128)(2,1)S(1)} %get-tuple-element.44.refs_0_, bf16[4,64,768]{2,1,0:T(8,128)(2,1)S(1)} %get-tuple-element.49.refs_1_, ...), custom_call_target="tpu_custom_call" | custom-call | flops 12079595520 | bytes 12079595 | tf_op jit(solution)/shard_map/pallas_call | solution.py:313
  16.4 0.1 collective-permute-start.4
  16.4 0.9 %shard_map.81 = (bf16[4,64,768]{2,1,0:T(8,128)(2,1)S(1)}, bf16[4,64,384]{2,1,0:T(8,128)(2,1)S(1)}, f32[4,64,384]{2,1,0:T(8,128)S(1)}, f32[4,64,384]{2,1,0:T(8,128)S(1)}) custom-call(bf16[4,64,768]{2,1,0:T(8,128)(2,1)S(1)} %get-tuple-element.57.refs_0_, f32[4,192,384]{2,1,0:T(8,128)S(1)} %get-tuple-element.48.refs_9_.refs_2_.refs_3_.refs_1_, ...), custom_call_target="tpu_custom_call" | custom-call | flops 6039797760 | bytes 6039797 | tf_op jit(solution)/shard_map/pallas_call | solution.py:313
  17.4 0.5 %collective-permute-start.6 = (bf16[4,64,384]{2,1,0:T(8,128)(2,1)S(1)}, bf16[4,64,384]{2,1,0:T(8,128)(2,1)S(1)}, u32[]{:S(2)}, u32[]{:S(2)}) collective-permute-start(bf16[4,64,384]{2,1,0:T(8,128)(2,1)S(1)} %get-tuple-element.68), channel_id=1, source_target_pairs={{1,2},{3,4},{5,6},{7,8},{9,10},{11,12},{13,14},{17,18},{19,20},{21... | collective-permute-start | bytes 589832 | tf_op jit(solution)/shard_map/ppermute | solution.py:289
  17.9 0.2 collective-permute-done.4.refs_4_
  18.1 1.8 %shard_map.82 = (bf16[4,128,768]{2,1,0:T(8,128)(2,1)S(1)}, bf16[4,128,384]{2,1,0:T(8,128)(2,1)S(1)}, bf16[4,128,384]{2,1,0:T(8,128)(2,1)S(1)}, f32[4,128,384]{2,1,0:T(8,128)S(1)}) custom-call(bf16[4,128,768]{2,1,0:T(8,128)(2,1)S(1)} %get-tuple-element.55.refs_0_, f32[4,256,384]{2,1,0:T(8,128)S(1)} %get-tuple-element.56.refs_10_.refs_1_.refs_2_, ...), custom_call_target="tpu_custom_call" | custom-call | flops 12079595520 | bytes 12079595 | tf_op jit(solution)/shard_map/pallas_call | solution.py:313
  19.9 1.1 %collective-permute-start.12 = (bf16[4,128,384]{2,1,0:T(8,128)(2,1)S(1)}, bf16[4,128,384]{2,1,0:T(8,128)(2,1)S(1)}, u32[]{:S(2)}, u32[]{:S(2)}) collective-permute-start(bf16[4,128,384]{2,1,0:T(8,128)(2,1)S(1)} %get-tuple-element.78), channel_id=1, source_target_pairs={{1,2},{3,4},{5,6},{7,8},{9,10},{11,12},{13,14},{17,18},{19,20},{21... | collective-permute-start | bytes 1179656 | tf_op jit(solution)/shard_map/ppermute | solution.py:289
  21.1 7.8 %collective-permute-done.6.refs_6_ = bf16[4,64,384]{2,1,0:T(8,128)(2,1)S(1)} collective-permute-done((bf16[4,64,384]{2,1,0:T(8,128)(2,1)S(1)}, bf16[4,64,384]{2,1,0:T(8,128)(2,1)S(1)}, u32[]{:S(2)}, u32[]{:S(2)}) %collective-permute-start.6) | collective-permute-done | bytes 196640 | tf_op jit(solution)/shard_map/ppermute | solution.py:289
  28.9 0.9 %shard_map.83 = (bf16[2,128,768]{2,1,0:T(8,128)(2,1)S(1)}, bf16[2,128,384]{2,1,0:T(8,128)(2,1)S(1)}, bf16[2,128,384]{2,1,0:T(8,128)(2,1)S(1)}, f32[2,128,384]{2,1,0:T(8,128)S(1)}) custom-call(bf16[4,64,768]{2,1,0:T(8,128)(2,1)S(1)} %get-tuple-element.64.refs_0_, bf16[4,64,768]{2,1,0:T(8,128)(2,1)S(1)} %get-tuple-element.54.refs_6_.refs_1_, ...), custom_call_target="tpu_custom_call" | custom-call | flops 6039797760 | bytes 6039797 | tf_op jit(solution)/shard_map/pallas_call | solution.py:313
  29.9 0.4 collective-permute-start.11
  30.4 0.9 %shard_map.84 = (bf16[2,128,768]{2,1,0:T(8,128)(2,1)S(1)}, bf16[2,128,384]{2,1,0:T(8,128)(2,1)S(1)}, bf16[2,128,384]{2,1,0:T(8,128)(2,1)S(1)}, f32[2,128,384]{2,1,0:T(8,128)S(1)}) custom-call(bf16[4,64,768]{2,1,0:T(8,128)(2,1)S(1)} %get-tuple-element.64.refs_0_, bf16[4,64,768]{2,1,0:T(8,128)(2,1)S(1)} %get-tuple-element.54.refs_6_.refs_1_, ...), custom_call_target="tpu_custom_call" | custom-call | flops 6039797760 | bytes 6039797 | tf_op jit(solution)/shard_map/pallas_call | solution.py:313
  31.3 0.4 %collective-permute-start.7 = (bf16[2,128,384]{2,1,0:T(8,128)(2,1)S(1)}, bf16[2,128,384]{2,1,0:T(8,128)(2,1)S(1)}, u32[]{:S(2)}, u32[]{:S(2)}) collective-permute-start(bf16[2,128,384]{2,1,0:T(8,128)(2,1)S(1)} %get-tuple-element.70), channel_id=1, source_target_pairs={{0,1},{2,3},{4,5},{6,7},{8,9},{10,11},{12,13},{14,15},{16,17},{18,... | collective-permute-start | bytes 589832 | tf_op jit(solution)/shard_map/ppermute | solution.py:292
  31.7 1.4 %collective-permute-done.12.refs_3_.refs_7_ = bf16[4,128,384]{2,1,0:T(8,128)(2,1)S(1)} collective-permute-done((bf16[4,128,384]{2,1,0:T(8,128)(2,1)S(1)}, bf16[4,128,384]{2,1,0:T(8,128)(2,1)S(1)}, u32[]{:S(2)}, u32[]{:S(2)}) %collective-permute-start.12) | collective-permute-done | bytes 393248 | tf_op jit(solution)/shard_map/ppermute | solution.py:289
  33.1 0.1 collective-permute-start.8
  33.2 1.3 %shard_map.85.refs_7_ = bf16[4,256,768]{2,1,0:T(8,128)(2,1)} custom-call(bf16[2,128,768]{2,1,0:T(8,128)(2,1)S(1)} %get-tuple-element.76.refs_0_, f32[2,128,384]{2,1,0:T(8,128)S(1)} %get-tuple-element.69.refs_13_.refs_1_, bf16[4,128,384]{2,1,0:T(8,128)(2,1)S(1)} %collective-permute-done.11.refs_2_.refs_6_, ...), custom_call_target="tpu_custom_call" | custom-call | flops 3019898880 | bytes 3019898 | tf_op jit(solution)/shard_map/pallas_call | solution.py:483
  34.5 4.9 %collective-permute-done.10.refs_3_ = bf16[2,128,384]{2,1,0:T(8,128)(2,1)S(1)} collective-permute-done((bf16[2,128,384]{2,1,0:T(8,128)(2,1)S(1)}, bf16[2,128,384]{2,1,0:T(8,128)(2,1)S(1)}, u32[]{:S(2)}, u32[]{:S(2)}) %collective-permute-start.10) | collective-permute-done | bytes 196640 | tf_op jit(solution)/shard_map/ppermute | solution.py:289
  39.4 1.1 %shard_map.86.refs_7_ = bf16[4,256,768]{2,1,0:T(8,128)(2,1)} custom-call(bf16[4,128,768]{2,1,0:T(8,128)(2,1)S(1)} %get-tuple-element.62.refs_0_, f32[4,128,384]{2,1,0:T(8,128)S(1)} %get-tuple-element.63.refs_13_.refs_1_, bf16[2,128,384]{2,1,0:T(8,128)(2,1)S(1)} %collective-permute-done.9.refs_2_, ...), custom_call_target="tpu_custom_call", output_to_operand_aliasing={{}: (7, {})} | custom-call | flops 1509949440 | bytes 1509949 | tf_op jit(solution)/shard_map/pallas_call | solution.py:483
  40.5 1.0 %collective-permute-done.8.refs_3_ = bf16[2,128,384]{2,1,0:T(8,128)(2,1)S(1)} collective-permute-done((bf16[2,128,384]{2,1,0:T(8,128)(2,1)S(1)}, bf16[2,128,384]{2,1,0:T(8,128)(2,1)S(1)}, u32[]{:S(2)}, u32[]{:S(2)}) %collective-permute-start.8) | collective-permute-done | bytes 196640 | tf_op jit(solution)/shard_map/ppermute | solution.py:289
  41.5 1.1 %shard_map.87 = bf16[4,256,768]{2,1,0:T(8,128)(2,1)} custom-call(bf16[4,128,768]{2,1,0:T(8,128)(2,1)S(1)} %get-tuple-element.62.refs_0_, f32[4,128,384]{2,1,0:T(8,128)S(1)} %get-tuple-element.63.refs_13_.refs_1_, bf16[2,128,384]{2,1,0:T(8,128)(2,1)S(1)} %collective-permute-done.7.refs_2_, ...), custom_call_target="tpu_custom_call", output_to_operand_aliasing={{}: (7, {})} | custom-call | flops 1509949440 | bytes 1509949 | tf_op jit(solution)/shard_map/pallas_call | solution.py:483
  (23 shorter events, 0.2 us)
Async XLA Ops:
  0.0 3.6 %copy-start.1 = (bf16[4,3,768,384]{3,2,1,0:T(8,128)(2,1)S(1)}, bf16[4,3,768,384]{3,2,1,0:T(8,128)(2,1)}, u32[]{:S(2)}) copy-start(bf16[4,3,768,384]{3,2,1,0:T(8,128)(2,1)} %refs_12_.5) | copy-start | bytes 21233668
  0.0 3.6 %copy-start.6 = (f32[4,768]{1,0:T(4,128)S(1)}, f32[4,768]{1,0:T(4,128)}, u32[]{:S(2)}) copy-start(f32[4,768]{1,0:T(4,128)} %refs_11_.5) | copy-start | bytes 36868
  0.0 3.6 %copy-start.5 = (f32[4,768]{1,0:T(4,128)S(1)}, f32[4,768]{1,0:T(4,128)}, u32[]{:S(2)}) copy-start(f32[4,768]{1,0:T(4,128)} %refs_10_.8) | copy-start | bytes 36868
  0.0 3.7 %copy-start.2 = (bf16[4,256,768]{2,1,0:T(8,128)(2,1)S(1)}, bf16[4,256,768]{2,1,0:T(8,128)(2,1)}, u32[]{:S(2)}) copy-start(bf16[4,256,768]{2,1,0:T(8,128)(2,1)} %refs_0_.7) | copy-start | bytes 4718596
  1.7 5.2 %copy-start = (bf16[4,384,768]{2,1,0:T(8,128)(2,1)S(1)}, bf16[4,384,768]{2,1,0:T(8,128)(2,1)}, u32[]{:S(2)}) copy-start(bf16[4,384,768]{2,1,0:T(8,128)(2,1)} %refs_6_.17) | copy-start | bytes 7077892
  1.7 5.2 %copy-start.3 = (f32[4,384]{1,0:T(4,128)S(1)}, f32[4,384]{1,0:T(4,128)}, u32[]{:S(2)}) copy-start(f32[4,384]{1,0:T(4,128)} %refs_4_.15) | copy-start | bytes 18436
  1.7 5.2 %copy-start.4 = (f32[4,384]{1,0:T(4,128)S(1)}, f32[4,384]{1,0:T(4,128)}, u32[]{:S(2)}) copy-start(f32[4,384]{1,0:T(4,128)} %refs_5_.17) | copy-start | bytes 18436
  1.7 6.1 %collective-permute-start.1 = (bf16[4,32,384]{2,1,0:T(8,128)(2,1)S(1)}, bf16[4,32,384]{2,1,0:T(8,128)(2,1)S(1)}, u32[]{:S(2)}, u32[]{:S(2)}) collective-permute-start(bf16[4,32,384]{2,1,0:T(8,128)(2,1)S(1)} %shard_map.75), channel_id=1, source_target_pairs={{1,2},{3,4},{5,6},{7,8},{9,10},{11,12},{13,14},{17,18},{19,20},{21... | collective-permute-start | bytes 294920 | tf_op jit(solution)/shard_map/ppermute | solution.py:289
  6.1 4.8 %collective-permute-start = (bf16[4,32,384]{2,1,0:T(8,128)(2,1)S(1)}, bf16[4,32,384]{2,1,0:T(8,128)(2,1)S(1)}, u32[]{:S(2)}, u32[]{:S(2)}) collective-permute-start(bf16[4,32,384]{2,1,0:T(8,128)(2,1)S(1)} %get-tuple-element.45), channel_id=1, source_target_pairs={{0,1},{2,3},{4,5},{6,7},{8,9},{10,11},{12,13},{14,15},{16,17},{18,... | collective-permute-start | bytes 294920 | tf_op jit(solution)/shard_map/ppermute | solution.py:292
  8.7 7.8 %collective-permute-start.3 = (bf16[4,64,384]{2,1,0:T(8,128)(2,1)S(1)}, bf16[4,64,384]{2,1,0:T(8,128)(2,1)S(1)}, u32[]{:S(2)}, u32[]{:S(2)}) collective-permute-start(bf16[4,64,384]{2,1,0:T(8,128)(2,1)S(1)} %get-tuple-element.58), channel_id=1, source_target_pairs={{1,2},{3,4},{5,6},{7,8},{9,10},{11,12},{13,14},{17,18},{19,20},{21... | collective-permute-start | bytes 589832 | tf_op jit(solution)/shard_map/ppermute | solution.py:289
  11.8 2.7 %collective-permute-start.2 = (bf16[4,64,384]{2,1,0:T(8,128)(2,1)S(1)}, bf16[4,64,384]{2,1,0:T(8,128)(2,1)S(1)}, u32[]{:S(2)}, u32[]{:S(2)}) collective-permute-start(bf16[4,64,384]{2,1,0:T(8,128)(2,1)S(1)} %get-tuple-element.51), channel_id=1, source_target_pairs={{0,1},{2,3},{4,5},{6,7},{8,9},{10,11},{12,13},{14,15},{16,17},{18,... | collective-permute-start | bytes 589832 | tf_op jit(solution)/shard_map/ppermute | solution.py:292
  12.9 8.2 %collective-permute-start.5 = (bf16[4,64,384]{2,1,0:T(8,128)(2,1)S(1)}, bf16[4,64,384]{2,1,0:T(8,128)(2,1)S(1)}, u32[]{:S(2)}, u32[]{:S(2)}) collective-permute-start(bf16[4,64,384]{2,1,0:T(8,128)(2,1)S(1)} %get-tuple-element.67), channel_id=1, source_target_pairs={{1,2},{3,4},{5,6},{7,8},{9,10},{11,12},{13,14},{17,18},{19,20},{21... | collective-permute-start | bytes 589832 | tf_op jit(solution)/shard_map/ppermute | solution.py:289
  16.4 1.8 %collective-permute-start.4 = (bf16[4,128,384]{2,1,0:T(8,128)(2,1)S(1)}, bf16[4,128,384]{2,1,0:T(8,128)(2,1)S(1)}, u32[]{:S(2)}, u32[]{:S(2)}) collective-permute-start(bf16[4,128,384]{2,1,0:T(8,128)(2,1)S(1)} %get-tuple-element.61), channel_id=1, source_target_pairs={{0,1},{2,3},{4,5},{6,7},{8,9},{10,11},{12,13},{14,15},{16,17},{18,... | collective-permute-start | bytes 1179656 | tf_op jit(solution)/shard_map/ppermute | solution.py:292
  17.4 11.5 %collective-permute-start.6 = (bf16[4,64,384]{2,1,0:T(8,128)(2,1)S(1)}, bf16[4,64,384]{2,1,0:T(8,128)(2,1)S(1)}, u32[]{:S(2)}, u32[]{:S(2)}) collective-permute-start(bf16[4,64,384]{2,1,0:T(8,128)(2,1)S(1)} %get-tuple-element.68), channel_id=1, source_target_pairs={{1,2},{3,4},{5,6},{7,8},{9,10},{11,12},{13,14},{17,18},{19,20},{21... | collective-permute-start | bytes 589832 | tf_op jit(solution)/shard_map/ppermute | solution.py:289
  19.9 13.1 %collective-permute-start.12 = (bf16[4,128,384]{2,1,0:T(8,128)(2,1)S(1)}, bf16[4,128,384]{2,1,0:T(8,128)(2,1)S(1)}, u32[]{:S(2)}, u32[]{:S(2)}) collective-permute-start(bf16[4,128,384]{2,1,0:T(8,128)(2,1)S(1)} %get-tuple-element.78), channel_id=1, source_target_pairs={{1,2},{3,4},{5,6},{7,8},{9,10},{11,12},{13,14},{17,18},{19,20},{21... | collective-permute-start | bytes 1179656 | tf_op jit(solution)/shard_map/ppermute | solution.py:289
  29.8 4.7 %collective-permute-start.9 = (bf16[2,128,384]{2,1,0:T(8,128)(2,1)S(1)}, bf16[2,128,384]{2,1,0:T(8,128)(2,1)S(1)}, u32[]{:S(2)}, u32[]{:S(2)}) collective-permute-start(bf16[2,128,384]{2,1,0:T(8,128)(2,1)S(1)} %get-tuple-element.74), channel_id=1, source_target_pairs={{0,1},{2,3},{4,5},{6,7},{8,9},{10,11},{12,13},{14,15},{16,17},{18,... | collective-permute-start | bytes 589832 | tf_op jit(solution)/shard_map/ppermute | solution.py:292
  29.9 9.5 %collective-permute-start.10 = (bf16[2,128,384]{2,1,0:T(8,128)(2,1)S(1)}, bf16[2,128,384]{2,1,0:T(8,128)(2,1)S(1)}, u32[]{:S(2)}, u32[]{:S(2)}) collective-permute-start(bf16[2,128,384]{2,1,0:T(8,128)(2,1)S(1)} %get-tuple-element.75), channel_id=1, source_target_pairs={{1,2},{3,4},{5,6},{7,8},{9,10},{11,12},{13,14},{17,18},{19,20},{21... | collective-permute-start | bytes 589832 | tf_op jit(solution)/shard_map/ppermute | solution.py:289
  29.9 3.2 %collective-permute-start.11 = (bf16[4,128,384]{2,1,0:T(8,128)(2,1)S(1)}, bf16[4,128,384]{2,1,0:T(8,128)(2,1)S(1)}, u32[]{:S(2)}, u32[]{:S(2)}) collective-permute-start(bf16[4,128,384]{2,1,0:T(8,128)(2,1)S(1)} %get-tuple-element.77), channel_id=1, source_target_pairs={{0,1},{2,3},{4,5},{6,7},{8,9},{10,11},{12,13},{14,15},{16,17},{18,... | collective-permute-start | bytes 1179656 | tf_op jit(solution)/shard_map/ppermute | solution.py:292
  31.3 9.2 %collective-permute-start.7 = (bf16[2,128,384]{2,1,0:T(8,128)(2,1)S(1)}, bf16[2,128,384]{2,1,0:T(8,128)(2,1)S(1)}, u32[]{:S(2)}, u32[]{:S(2)}) collective-permute-start(bf16[2,128,384]{2,1,0:T(8,128)(2,1)S(1)} %get-tuple-element.70), channel_id=1, source_target_pairs={{0,1},{2,3},{4,5},{6,7},{8,9},{10,11},{12,13},{14,15},{16,17},{18,... | collective-permute-start | bytes 589832 | tf_op jit(solution)/shard_map/ppermute | solution.py:292
  33.1 8.4 %collective-permute-start.8 = (bf16[2,128,384]{2,1,0:T(8,128)(2,1)S(1)}, bf16[2,128,384]{2,1,0:T(8,128)(2,1)S(1)}, u32[]{:S(2)}, u32[]{:S(2)}) collective-permute-start(bf16[2,128,384]{2,1,0:T(8,128)(2,1)S(1)} %get-tuple-element.71), channel_id=1, source_target_pairs={{1,2},{3,4},{5,6},{7,8},{9,10},{11,12},{13,14},{17,18},{19,20},{21... | collective-permute-start | bytes 589832 | tf_op jit(solution)/shard_map/ppermute | solution.py:289
